TPU v7x, 32 devices: a whole 2x2x4 slice. The times are simulated.
32 devices in a mesh: ens: 2 (over x), tile: 16 (over z, y, core).
Axes of the slice: x: 2, y: 2, z: 4, core: 2. Of those that a mesh axis runs over, the one named last changes fastest.
Arguments:
- thermal_snapshot: float32 [32, 30, 8100], P(('ens', 'tile')), parts along dimension 0, may hold values from -4 to 4
- layer_boundary_stirring_factor: float32 [16, 30, 8100], P('tile'), may hold values from 0.05 to 20
- flooded_layer_number: int32 [16, 8100], P('tile'), may hold values from 0 to 30
- adjacent_patch: int32 [16, 4], P('tile'), may hold values from -1 to 15, as said below
- joint_facing_flag: int32 [16, 4], P('tile'), may hold values from 0 to 7, as said below
- elevation_operator_main_entry: float32 [16, 8100], P('tile'), may hold values from 0.05 to 0.2
- scalar_adjoint_sensitivity: float32 [32, 30, 8100], P(('ens', 'tile')), parts along dimension 0, may hold values from -4 to 4
- elevation_adjoint_sensitivity: float32 [32, 8100], P(('ens', 'tile')), parts along dimension 0, may hold values from -4 to 4
Outputs:
- surface_height: float32 [32, 8100], P(('ens', 'tile')), parts along dimension 0
- temp_gradient: float32 [32, 30, 8100], P(('ens', 'tile')), parts along dimension 0
There are 2 independent parts, one for each index of `ens`. A program takes and returns all parts, laid end to end along the dimension named above; an argument that names none is the same for every part. Nothing has to cross between parts.
Inputs may be any that keep to these rules, and one draw needn't show every extreme that they name: adjacent_patch[t, s] is the tile across side s of tile t, or -1 where land or the window's edge closes it; when not -1 it is one of t - 1, t + 1, t - 8, t + 8, t - 8, t + 8. Seams pair up: if side s of tile t meets side s2 of tile u with joint_facing_flag[t, s] = 2 s2 + f, then adjacent_patch[u, s2] = t and joint_facing_flag[u, s2] = 2 s + f. joint_facing_flag[t, s] = 2 s2 + f: s2 is the side of the neighbour that is met, f = 1 reverses the order along the seam.
All inputs are finite; a program needn't handle non-finite values.
Results may differ from a plain program's by a relative error of at most 0.0003.
Values sent between devices are 32-bit elements; how exact they have to be, the bound alone decides.
No kernel may reach another device: no remote copies, remote signals or barrier semaphores. Data moves between devices by JAX's collectives and lax.ppermute only.
A program may use at most 128 MiB of HBM per device.

v0:
```python
import math

import jax
import jax.numpy as jnp
from jax import lax
from jax.sharding import PartitionSpec as P

ITERS = 4


scalar_spreading_increment = 0.2


def edge_strips(field):
    cells = field.shape[-1]
    tile_size = math.isqrt(cells)
    return jnp.stack(
        [
            field[..., :tile_size],
            field[..., cells - tile_size :],
            field[..., ::tile_size],
            field[..., tile_size - 1 :: tile_size],
        ],
        axis=1,
    )


def pick_range(all_strips, adjacent_patch, joint_facing_flag, first_row):
    row_count = all_strips.shape[0]
    present = (adjacent_patch >= first_row) & (adjacent_patch < first_row + row_count)
    source_rows = jnp.clip(adjacent_patch - first_row, 0, row_count - 1)
    flat_strips = all_strips.reshape((row_count * 4,) + all_strips.shape[2:])
    flat_index = (source_rows * 4 + joint_facing_flag // 2).reshape(-1)
    fetched = jnp.take(flat_strips, flat_index, axis=0).reshape(
        adjacent_patch.shape + all_strips.shape[2:]
    )
    reverse_mask = (joint_facing_flag % 2 == 1)[:, :, None, None]
    fetched = jnp.where(reverse_mask, fetched[..., ::-1], fetched)
    return jnp.where(present[:, :, None, None], fetched, jnp.zeros_like(fetched))


def place_side(edge_strip, side_index, tile_size, cells):
    leading = [(0, 0)] * (edge_strip.ndim - 1)
    if side_index == 0:
        return jnp.pad(edge_strip, leading + [(0, cells - tile_size)])
    if side_index == 1:
        return jnp.pad(edge_strip, leading + [(cells - tile_size, 0)])
    before = 0 if side_index == 2 else tile_size - 1
    padded = jnp.pad(edge_strip[..., None], leading + [(0, 0), (before, tile_size - 1 - before)])
    return padded.reshape(edge_strip.shape[:-1] + (cells,))


def spread_scalar_field(field, flooded_point_flags, ghost_cells, halo_flooded_flags):
    cells = field.shape[-1]
    tile_size = ghost_cells.shape[-1]
    leading = [(0, 0)] * (field.ndim - 1)
    column_keep = (jnp.arange(cells - 1) % tile_size != tile_size - 1).astype(jnp.float32)
    flux_along = (
        flooded_point_flags[..., 1:]
        * flooded_point_flags[..., :-1]
        * column_keep
        * (field[..., 1:] - field[..., :-1])
    )
    flux_across = (
        flooded_point_flags[..., tile_size:]
        * flooded_point_flags[..., :-tile_size]
        * (field[..., tile_size:] - field[..., :-tile_size])
    )
    tendency = jnp.pad(flux_along, leading + [(0, 1)]) - jnp.pad(flux_along, leading + [(1, 0)])
    tendency = (
        tendency
        + jnp.pad(flux_across, leading + [(0, tile_size)])
        - jnp.pad(flux_across, leading + [(tile_size, 0)])
    )
    seam_flux = (
        edge_strips(flooded_point_flags) * halo_flooded_flags * (ghost_cells - edge_strips(field))
    )
    for side_index in range(4):
        tendency = tendency + place_side(seam_flux[:, side_index], side_index, tile_size, cells)
    return tendency


def column_solve(source, layer_boundary_stirring_factor, flooded_point_flags):
    below_wet = jnp.concatenate(
        [flooded_point_flags[:, 1:], jnp.zeros_like(flooded_point_flags[:, :1])], axis=1
    )
    coupling = layer_boundary_stirring_factor * flooded_point_flags * below_wet
    upper_link = jnp.concatenate([jnp.zeros_like(coupling[:, :1]), coupling[:, :-1]], axis=1)
    diagonal = 1.0 + upper_link + coupling

    def forward_sweep(carry, inputs):
        ratio_prev, value_prev = carry
        link_above, center, link_below, rhs_level = inputs
        denominator = center + link_above * ratio_prev
        ratio_next = -link_below / denominator
        value_next = (rhs_level + link_above * value_prev) / denominator
        return ((ratio_next, value_next), (ratio_next, value_next))

    def back_sweep(later, inputs):
        ratio_here, value_here = inputs
        current = value_here - ratio_here * later
        return (current, current)

    starting = jnp.zeros((source.shape[0], source.shape[2]), jnp.float32)
    sweep_inputs = (
        jnp.moveaxis(upper_link, 1, 0),
        jnp.moveaxis(diagonal, 1, 0),
        jnp.moveaxis(coupling, 1, 0),
        jnp.moveaxis(source, 1, 0),
    )
    carried, (ratios, values) = lax.scan(forward_sweep, (starting, starting), sweep_inputs)
    carried, solved = lax.scan(back_sweep, starting, (ratios, values), reverse=True)
    return jnp.moveaxis(solved, 0, 1)


def residual_norm(residual):
    return lax.psum(jnp.sum(residual * residual), "tile")


def surface_solve(rhs, apply_operator):
    solution = jnp.zeros_like(rhs)
    residual = rhs
    direction = rhs
    norm_now = residual_norm(residual)
    for iteration in range(ITERS):
        product_field = apply_operator(direction)
        step_length = norm_now / lax.psum(jnp.sum(direction * product_field), "tile")
        solution = solution + step_length * direction
        residual = residual - step_length * product_field
        norm_next = residual_norm(residual)
        direction = residual + norm_next / norm_now * direction
        norm_now = norm_next
    return solution


def shards(
    thermal_snapshot,
    layer_boundary_stirring_factor,
    flooded_layer_number,
    adjacent_patch,
    joint_facing_flag,
    elevation_operator_main_entry,
    scalar_adjoint_sensitivity,
    elevation_adjoint_sensitivity,
):
    flooded_layer_total = thermal_snapshot.shape[1]
    flooded_point_flags = (
        jnp.arange(flooded_layer_total)[None, :, None] < flooded_layer_number[:, None, :]
    ).astype(jnp.float32)
    depth_strips = lax.all_gather(
        edge_strips(flooded_layer_number[:, None, :]), "tile", axis=0, tiled=True
    )
    ghost_depth = pick_range(depth_strips, adjacent_patch, joint_facing_flag, 0)
    halo_flooded_flags = (
        jnp.arange(flooded_layer_total)[None, None, :, None] < ghost_depth
    ).astype(jnp.float32)
    surface_wet = flooded_point_flags[:, :1]
    surface_ghost_wet = halo_flooded_flags[:, :, :1]

    def halo_points_per_layer(field):
        own_strips = edge_strips(field)
        every_strip = lax.all_gather(own_strips, "tile", axis=0, tiled=True)
        found = pick_range(every_strip, adjacent_patch, joint_facing_flag, 0)
        return found

    def surface_ghosts(field):
        own_strips = edge_strips(field)
        every_strip = lax.all_gather(own_strips, "tile", axis=0, tiled=True)
        found = pick_range(every_strip, adjacent_patch, joint_facing_flag, 0)
        return found

    def apply_operator(field):
        return elevation_operator_main_entry[:, None, :] * field - spread_scalar_field(
            field, surface_wet, surface_ghosts(field), surface_ghost_wet
        )

    level_scale = 1.0 / math.sqrt(flooded_layer_total)
    stirred_sea_elevation = thermal_snapshot + scalar_spreading_increment * spread_scalar_field(
        thermal_snapshot,
        flooded_point_flags,
        halo_points_per_layer(thermal_snapshot),
        halo_flooded_flags,
    )
    mixed = column_solve(stirred_sea_elevation, layer_boundary_stirring_factor, flooded_point_flags)
    forcing = jnp.sum(flooded_point_flags * mixed, axis=1, keepdims=True) * level_scale
    surface_height = surface_solve(forcing, apply_operator)
    forcing_adjoint = surface_solve(elevation_adjoint_sensitivity[:, None, :], apply_operator)
    mixed_adjoint = scalar_adjoint_sensitivity + flooded_point_flags * forcing_adjoint * level_scale
    mixed_h_adjoint = column_solve(
        mixed_adjoint, layer_boundary_stirring_factor, flooded_point_flags
    )
    temp_gradient = mixed_h_adjoint + scalar_spreading_increment * spread_scalar_field(
        mixed_h_adjoint,
        flooded_point_flags,
        halo_points_per_layer(mixed_h_adjoint),
        halo_flooded_flags,
    )
    return (surface_height[:, 0], temp_gradient)


def solution(mesh):
    placed = (
        P(("ens", "tile"), None, None),
        P("tile", None, None),
        P("tile", None),
        P("tile", None),
        P("tile", None),
        P("tile", None),
        P(("ens", "tile"), None, None),
        P(("ens", "tile"), None),
    )
    return jax.shard_map(
        shards,
        mesh=mesh,
        in_specs=placed,
        out_specs=(P(("ens", "tile"), None), P(("ens", "tile"), None, None)),
        check_vma=False,
    )
```

profile of v0, /device:TPU:0, one launch (start us, length us, event | category | flops | bytes accessed | tf_op | source)
XLA Modules:
  0.0 719.2 jit_solution(2737533783459266020)
XLA Ops:
  3.5 26.0 %all_gather.34 = f32[16,4,30,90]{3,1,2,0:T(4,128)S(1)} all-gather(f32[1,4,30,90]{3,1,2,0:T(4,128)S(1)} %copy.363), channel_id=1, replica_groups=mesh['ens'=2,'tile'=16] {'tile'}, dimensions={0}, use_global_device_ids=true | all-gather | bytes 734400 | tf_op jit(solution)/shard_map/all_gather | solution.py:162
  31.7 18.1 %all_gather.33 = s32[16,4,1,90]{3,1,2,0:T(4,128)S(1)} all-gather(s32[1,4,1,90]{3,1,2,0:T(4,128)S(1)} %bitcast.573), channel_id=1, replica_groups=mesh['ens'=2,'tile'=16] {'tile'}, dimensions={0}, use_global_device_ids=true | all-gather | bytes 24480 | tf_op jit(solution)/shard_map/all_gather | solution.py:150
  53.4 2.6 pad.264.clone
  56.0 2.2 reshape.1994
  59.9 2.9 pad.265.clone
  62.8 3.2 reshape.1995
  68.1 2.0 add_bitcast_fusion
  73.2 2.0 copy.376
  76.2 1.9 broadcast.1038.clone.1
  78.1 1.9 broadcast.1038.clone.2
  79.9 70.7 %while.68 = (s32[]{:T(128)}, f32[1,8100]{1,0:T(1,128)S(1)}, f32[1,8100]{1,0:T(1,128)S(1)}, f32[30,1,8100]{2,1,0:T(1,128)}, f32[30,1,8100]{2,1,0:T(1,128)}, /*ind...) while((s32[]{:T(128)}, f32[1,8100]{1,0:T(1,128)S(1)}, ...), condition=%wide.region_1.3_spmd.clone, body=%wide.region_0.2_spmd.clone.sunk | while | flops 72903 | bytes 391415 | solution.py:111
  80.1 1.7 bitcast_dynamic-update-slice_fusion.12
  89.5 1.7 bitcast_dynamic-update-slice_fusion.12
  94.2 1.7 bitcast_dynamic-update-slice_fusion.12
  113.0 1.7 bitcast_dynamic-update-slice_fusion.12
  122.4 1.7 bitcast_dynamic-update-slice_fusion.12
  127.1 1.7 bitcast_dynamic-update-slice_fusion.12
  136.5 1.7 bitcast_dynamic-update-slice_fusion.12
  152.4 26.3 %while.69 = (s32[]{:T(128)}, f32[1,8100]{1,0:T(1,128)S(1)}, f32[30,1,8100]{2,1,0:T(1,128)S(1)}, f32[30,1,8100]{2,1,0:T(1,128)}, f32[30,1,8100]{2,1,0:T(1,128)}, /*index=5*/s32[]{:T(128)}, s32[]{:T(128)}, s32[]{:T(128)}) while((s32[]{:T(128)}, f32[1,8100]{1,0:T(1,128)S(1)}, f32[30,1,8100]{2,1,0:T(1,128)S(1)}, ...), condition=%wide.region_3.5_spmd.clone, body=%wide.region_2.4_spmd.clone.sunk | while | flops 24304 | bytes 163215 | solution.py:112
  181.3 18.8 %all_gather.35 = f32[16,4,1,90]{3,1,2,0:T(4,128)S(1)} all-gather(f32[1,4,1,90]{3,1,2,0:T(4,128)S(1)} %pad_maximum_fusion.2), channel_id=1, replica_groups=mesh['ens'=2,'tile'=16] {'tile'}, dimensions={0}, use_global_device_ids=true | all-gather | bytes 24480 | tf_op jit(solution)/shard_map/all_gather | solution.py:168
  201.2 17.5 %all_gather.39 = f32[16,4,1,90]{3,1,2,0:T(4,128)S(1)} all-gather(f32[1,4,1,90]{3,1,2,0:T(4,128)S(1)} %pad_maximum_fusion.6), channel_id=1, replica_groups=mesh['ens'=2,'tile'=16] {'tile'}, dimensions={0}, use_global_device_ids=true | all-gather | bytes 24480 | tf_op jit(solution)/shard_map/all_gather | solution.py:168
  223.1 31.7 %all-reduce.88 = (f32[]{:T(128)}, f32[]{:T(128)}, f32[]{:T(128)}, f32[]{:T(128)}) all-reduce(f32[]{:T(128)} %get-tuple-element.648, f32[]{:T(128)} %get-tuple-element.646, f32[]{:T(128)} %multiply_reduce_fusion.6, f32[]{:T(128)} %get-tuple-element.588), channel_id=1, replica_groups=mesh['ens'=2,'tile'=16] {'tile'}, use_global_device_ids=true, to_apply=%region_6.8 | all-reduce | flops 4 | bytes 32 | tf_op jit(solution)/shard_map/psum | solution.py:117
  258.7 30.1 %all-reduce.87 = (f32[]{:T(128)}, f32[]{:T(128)}) all-reduce(f32[]{:T(128)} %get-tuple-element.586, f32[]{:T(128)} %multiply_reduce_fusion.4), channel_id=1, replica_groups=mesh['ens'=2,'tile'=16] {'tile'}, use_global_device_ids=true, to_apply=%region_10.13 | all-reduce | flops 2 | bytes 16 | tf_op jit(solution)/shard_map/psum | solution.py:117
  292.4 17.2 %all_gather.36 = f32[16,4,1,90]{3,1,2,0:T(4,128)S(1)} all-gather(f32[1,4,1,90]{3,1,2,0:T(4,128)S(1)} %pad_maximum_fusion.3), channel_id=1, replica_groups=mesh['ens'=2,'tile'=16] {'tile'}, dimensions={0}, use_global_device_ids=true | all-gather | bytes 24480 | tf_op jit(solution)/shard_map/all_gather | solution.py:168
  310.6 19.2 %all_gather.40 = f32[16,4,1,90]{3,1,2,0:T(4,128)S(1)} all-gather(f32[1,4,1,90]{3,1,2,0:T(4,128)S(1)} %pad_maximum_fusion.7), channel_id=1, replica_groups=mesh['ens'=2,'tile'=16] {'tile'}, dimensions={0}, use_global_device_ids=true | all-gather | bytes 24480 | tf_op jit(solution)/shard_map/all_gather | solution.py:168
  333.0 30.5 %all-reduce.86 = (f32[]{:T(128)}, f32[]{:T(128)}) all-reduce(f32[]{:T(128)} %get-tuple-element.638, f32[]{:T(128)} %get-tuple-element.582), channel_id=1, replica_groups=mesh['ens'=2,'tile'=16] {'tile'}, use_global_device_ids=true, to_apply=%region_12.15 | all-reduce | flops 2 | bytes 16 | tf_op jit(solution)/shard_map/psum | solution.py:127
  367.5 30.2 %all-reduce.85 = (f32[]{:T(128)}, f32[]{:T(128)}) all-reduce(f32[]{:T(128)} %get-tuple-element.580, f32[]{:T(128)} %get-tuple-element.578), channel_id=1, replica_groups=mesh['ens'=2,'tile'=16] {'tile'}, use_global_device_ids=true, to_apply=%region_14.17 | all-reduce | flops 2 | bytes 16 | tf_op jit(solution)/shard_map/psum | solution.py:117
  401.3 17.2 %all_gather.37 = f32[16,4,1,90]{3,1,2,0:T(4,128)S(1)} all-gather(f32[1,4,1,90]{3,1,2,0:T(4,128)S(1)} %pad_maximum_fusion.4), channel_id=1, replica_groups=mesh['ens'=2,'tile'=16] {'tile'}, dimensions={0}, use_global_device_ids=true | all-gather | bytes 24480 | tf_op jit(solution)/shard_map/all_gather | solution.py:168
  419.6 19.2 %all_gather.41 = f32[16,4,1,90]{3,1,2,0:T(4,128)S(1)} all-gather(f32[1,4,1,90]{3,1,2,0:T(4,128)S(1)} %pad_maximum_fusion.8), channel_id=1, replica_groups=mesh['ens'=2,'tile'=16] {'tile'}, dimensions={0}, use_global_device_ids=true | all-gather | bytes 24480 | tf_op jit(solution)/shard_map/all_gather | solution.py:168
  441.9 30.4 %all-reduce.84 = (f32[]{:T(128)}, f32[]{:T(128)}) all-reduce(f32[]{:T(128)} %get-tuple-element.630, f32[]{:T(128)} %get-tuple-element.574), channel_id=1, replica_groups=mesh['ens'=2,'tile'=16] {'tile'}, use_global_device_ids=true, to_apply=%region_16.19 | all-reduce | flops 2 | bytes 16 | tf_op jit(solution)/shard_map/psum | solution.py:127
  476.3 30.1 %all-reduce.83 = (f32[]{:T(128)}, f32[]{:T(128)}) all-reduce(f32[]{:T(128)} %multiply_reduce_fusion.7, f32[]{:T(128)} %multiply_reduce_fusion), channel_id=1, replica_groups=mesh['ens'=2,'tile'=16] {'tile'}, use_global_device_ids=true, to_apply=%region_18.21 | all-reduce | flops 2 | bytes 16 | tf_op jit(solution)/shard_map/psum | solution.py:117
  510.0 17.4 %all_gather.42 = f32[16,4,1,90]{3,1,2,0:T(4,128)S(1)} all-gather(f32[1,4,1,90]{3,1,2,0:T(4,128)S(1)} %pad_maximum_fusion.9), channel_id=1, replica_groups=mesh['ens'=2,'tile'=16] {'tile'}, dimensions={0}, use_global_device_ids=true | all-gather | bytes 24480 | tf_op jit(solution)/shard_map/all_gather | solution.py:168
  528.4 19.2 %all_gather.38 = f32[16,4,1,90]{3,1,2,0:T(4,128)S(1)} all-gather(f32[1,4,1,90]{3,1,2,0:T(4,128)S(1)} %pad_maximum_fusion.5), channel_id=1, replica_groups=mesh['ens'=2,'tile'=16] {'tile'}, dimensions={0}, use_global_device_ids=true | all-gather | bytes 24480 | tf_op jit(solution)/shard_map/all_gather | solution.py:168
  550.8 30.5 %all-reduce.82 = (f32[]{:T(128)}, f32[]{:T(128)}) all-reduce(f32[]{:T(128)} %get-tuple-element.487, f32[]{:T(128)} %get-tuple-element.486), channel_id=1, replica_groups=mesh['ens'=2,'tile'=16] {'tile'}, use_global_device_ids=true, to_apply=%region_20.23 | all-reduce | flops 2 | bytes 16 | tf_op jit(solution)/shard_map/psum | solution.py:127
  582.6 2.8 fusion.17
  586.3 1.9 broadcast.1038.clone.4
  588.1 52.8 %while.70 = (s32[]{:T(128)}, f32[1,8100]{1,0:T(1,128)S(1)}, f32[1,8100]{1,0:T(1,128)S(1)}, f32[30,1,8100]{2,1,0:T(1,128)S(1)}, f32[30,1,8100]{2,1,0:T(1,128)}, /...) while((s32[]{:T(128)}, f32[1,8100]{1,0:T(1,128)S(1)}, ...), condition=%wide.region_38.41_spmd.clone, body=%wide.region_37.40_spmd.clone.sunk | while | flops 72903 | bytes 392379 | solution.py:111
  589.9 1.7 bitcast_dynamic-update-slice_fusion.15
  591.6 1.7 bitcast_dynamic-update-slice_fusion.15
  593.4 1.7 bitcast_dynamic-update-slice_fusion.15
  642.7 26.3 %while.71 = (s32[]{:T(128)}, f32[1,8100]{1,0:T(1,128)S(1)}, f32[30,1,8100]{2,1,0:T(1,128)S(1)}, f32[30,1,8100]{2,1,0:T(1,128)}, f32[30,1,8100]{2,1,0:T(1,128)}, /*index=5*/s32[]{:T(128)}, s32[]{:T(128)}, s32[]{:T(128)}) while((s32[]{:T(128)}, f32[1,8100]{1,0:T(1,128)S(1)}, f32[30,1,8100]{2,1,0:T(1,128)S(1)}, ...), condition=%wide.region_40.43_spmd.clone, body=%wide.region_39.42_spmd.clone.sunk | while | flops 24304 | bytes 163215 | solution.py:112
  671.2 20.6 %all_gather.43 = f32[16,4,30,90]{3,1,2,0:T(4,128)S(1)} all-gather(f32[1,4,30,90]{3,1,2,0:T(4,128)S(1)} %copy.444), channel_id=1, replica_groups=mesh['ens'=2,'tile'=16] {'tile'}, dimensions={0}, use_global_device_ids=true | all-gather | bytes 734400 | tf_op jit(solution)/shard_map/all_gather | solution.py:162
  693.7 1.9 gather_fusion.10
  698.4 2.6 pad.336.clone
  701.0 3.2 reshape.1996
  705.8 2.9 pad.337.clone
  708.7 3.2 reshape.1997
  715.1 2.0 copy.455
  (428 shorter events, 218.2 us)
Async XLA Ops:
  0.6 1.2 copy-start.3
  29.8 0.7 copy-start.17
  29.8 0.7 copy-start.18
  29.8 1.4 copy-start.9
  30.5 517.1 %copy-start.16 = (s32[1024]{0:T(1024)}, s32[1024]{0:T(1024)S(1)}, u32[]{:S(2)}) copy-start(s32[1024]{0:T(1024)S(1)} %pad_clamp_fusion) | copy-start | bytes 12292
  31.1 517.1 %copy-start.11 = (pred[4]{0:T(512)(128)(4,1)}, pred[4]{0:T(512)(128)(4,1)S(1)}, u32[]{:S(2)}) copy-start(pred[4]{0:T(512)(128)(4,1)S(1)} %compare_and_fusion) | copy-start | bytes 16
  50.5 497.9 %copy-start.13 = (pred[4]{0:T(512)(128)(4,1)}, pred[4]{0:T(512)(128)(4,1)S(1)}, u32[]{:S(2)}) copy-start(pred[4]{0:T(512)(128)(4,1)S(1)} %get-tuple-element.708) | copy-start | bytes 16
  50.5 497.9 %copy-start.14 = (pred[4]{0:T(512)(128)(4,1)}, pred[4]{0:T(512)(128)(4,1)S(1)}, u32[]{:S(2)}) copy-start(pred[4]{0:T(512)(128)(4,1)S(1)} %get-tuple-element.709) | copy-start | bytes 16
  50.6 169.2 %copy-start.15 = (s32[4,90]{1,0:T(4,128)}, s32[4,90]{1,0:T(4,128)S(1)}, u32[]{:S(2)}) copy-start(s32[4,90]{1,0:T(4,128)S(1)} %fusion.82) | copy-start | bytes 4324
  66.6 1.2 copy-start.2
  66.6 1.5 copy-start.4
  70.1 1.2 copy-start.8
  150.6 1.0 copy-start.6
  151.6 28.6 %copy-start.5 = (f32[1,8100]{1,0:T(1,128)S(1)}, f32[1,8100]{1,0:T(1,128)}, u32[]{:S(2)}) copy-start(f32[1,8100]{1,0:T(1,128)} %param.27) | copy-start | bytes 97204
  178.8 42.7 %copy-start.10 = (f32[1,8100]{1,0:T(1,128)S(1)}, f32[1,8100]{1,0:T(1,128)}, u32[]{:S(2)}) copy-start(f32[1,8100]{1,0:T(1,128)} %param.25) | copy-start | bytes 97204
  640.9 0.9 copy-start.7
  692.1 3.5 copy-start.12
  712.5 1.2 copy-start
  712.5 1.5 copy-start.1
where the time goes:
time: 728 us; the launch traced here: 719 us
  blocking collectives  424 us (58%)
  other arithmetic  200 us (27%)
  local copies, waits for them, and re-layouts  74.4 us (10%)
  between operations  19.9 us (3%)
    dynamic_update_slice x180, other arithmetic, column_solve(): lax.scan(forward_sweep, (starting, starting), sweep_inputs)  175 us
    all_gather x8, blocking collectives, surface_ghosts(): every_strip = lax.all_gather(own_strips, 'tile', axis=0, tiled=True)  146 us
    psum x4, blocking collectives, residual_norm(): return lax.psum(jnp.sum(residual * residual), 'tile')  122 us
    psum x3, blocking collectives, surface_solve(): lax.psum(jnp.sum(direction * product_field), 'tile')  91.4 us
    all_gather x2, blocking collectives, halo_points_per_layer(): every_strip = lax.all_gather(own_strips, 'tile', axis=0, tiled=True)  46.7 us
    unnamed x67, local copies, waits for them, and re-layouts  20.2 us
    all_gather x1, blocking collectives, shards(): lax.all_gather(edge_strips(flooded_layer_number[:, None, :]), 'tile', axi...  18.1 us

commit v1 on v0

v1 whole, which is shorter than its diff:
```python
import functools
import math

import jax
import jax.numpy as jnp
from jax import lax
from jax.experimental import pallas as pl
from jax.experimental.pallas import tpu as pltpu
from jax.sharding import PartitionSpec as P

SIDE = 90
CELLS = SIDE * SIDE
ROWS = 64
LANES = 128
ITERS = 4
ROW_TILES = 8
SPREAD = 0.2
CENTRE = 4.1
BLOCK = 72
F32 = jnp.float32
I32 = jnp.int32


def grid_iotas():
    row = lax.broadcasted_iota(I32, (ROWS, LANES), 0)
    lane = lax.broadcasted_iota(I32, (ROWS, LANES), 1)
    cell = row * LANES + lane
    i = (cell * 46604) >> 22
    j = cell - SIDE * i
    return row, lane, cell, i, j


def ahead(x, n):
    lane = lax.broadcasted_iota(I32, x.shape, 1)
    y = pltpu.roll(x, LANES - n, 1)
    return jnp.where(lane < LANES - n, y, pltpu.roll(y, ROWS - 1, 0))


def behind(x, n):
    lane = lax.broadcasted_iota(I32, x.shape, 1)
    y = pltpu.roll(x, n, 1)
    return jnp.where(lane >= n, y, pltpu.roll(y, 1, 0))


def take(x, index):
    pieces = []
    for first in range(0, x.shape[0], 8):
        part = index if index.shape[0] == 8 else index[first : first + 8]
        pieces.append(jnp.take_along_axis(x[first : first + 8], part, axis=1, mode="promise_in_bounds"))
    return pieces[0] if len(pieces) == 1 else jnp.concatenate(pieces, axis=0)


def lanes8():
    return lax.broadcasted_iota(I32, (8, LANES), 1)


def column_owner(lane):
    odd = lane & 1
    half = (lane - 89 * odd) >> 1
    return (37 * half) & 63


def lines_23(za, zb, depth_row):
    lane = lanes8()
    near = (SIDE * lane + depth_row) & 127
    far = (SIDE * lane + SIDE - 1 - depth_row) & 127
    wide = lax.broadcasted_iota(I32, za.shape, 1)
    first = wide < 64
    return (
        jnp.where(first, take(za, near), take(zb, near)),
        jnp.where(first, take(za, far), take(zb, far)),
    )


def spread_lines(side2, side3, side1):
    lane = lanes8()
    owner = column_owner(lane)
    later = (owner + 64) & 127
    even = (lax.broadcasted_iota(I32, side2.shape, 1) & 1) == 0
    wa = jnp.where(even, take(side2, owner), take(side3, owner))
    wb = jnp.where(even, take(side2, later), take(side3, later))
    return wa, wb, pltpu.roll(side1, 74, 1)


def scatter_masks():
    row, lane, cell, i, j = grid_iotas()
    column = (j == 0) | (j == SIDE - 1)
    return (
        column & (i < 64),
        column & (i >= 64) & (i < SIDE),
        cell < SIDE,
        i == SIDE - 1,
    )


def scatter_rows(masks, wa, wb, side0, w1):
    zero = jnp.zeros((ROWS, LANES), F32)
    out = jnp.where(masks[0], wa, zero) + jnp.where(masks[1], wb, zero)
    return out + jnp.where(masks[2], side0, zero) + jnp.where(masks[3], w1, zero)


def scatter_lines(masks, lines):
    wa, wb, w1 = spread_lines(
        jnp.broadcast_to(lines[2:3], (8, LANES)),
        jnp.broadcast_to(lines[3:4], (8, LANES)),
        jnp.broadcast_to(lines[1:2], (8, LANES)),
    )
    return scatter_rows(masks, wa[0:1], wb[0:1], lines[0:1], w1[0:1])


def row_line(ref, base, first_cell):
    row, off = divmod(first_cell, LANES)
    top = ref[pl.ds(base + row, 1), :]
    if off == 0:
        return top
    lane = lax.broadcasted_iota(I32, (1, LANES), 1)
    top = pltpu.roll(top, LANES - off, 1)
    if off + SIDE <= LANES:
        return top
    low = pltpu.roll(ref[pl.ds(base + row + 1, 1), :], LANES - off, 1)
    return jnp.where(lane < LANES - off, top, low)


def write_frames(field_ref, base, out_ref, first_row, za_ref, zb_ref):
    field = field_ref[base : base + ROWS, :]
    row, lane, cell, i, j = grid_iotas()
    zero = jnp.zeros_like(field)
    for depth in range(4):
        column = (j == depth) | (j == SIDE - 1 - depth)
        za = jnp.where(column & (i < 64), field, zero)
        zb = jnp.where(column & (i >= 64), field, zero)
        za_ref[depth : depth + 1, :] = jnp.sum(za, axis=0, keepdims=True)
        zb_ref[depth : depth + 1, :] = jnp.sum(zb, axis=0, keepdims=True)
        out_ref[first_row + depth * 4 : first_row + depth * 4 + 1, :] = row_line(
            field_ref, base, depth * SIDE
        )
        out_ref[first_row + depth * 4 + 1 : first_row + depth * 4 + 2, :] = row_line(
            field_ref, base, (SIDE - 1 - depth) * SIDE
        )
    for depth in range(4, 8):
        za_ref[depth : depth + 1, :] = jnp.zeros((1, LANES), F32)
        zb_ref[depth : depth + 1, :] = jnp.zeros((1, LANES), F32)
    depth_row = lax.broadcasted_iota(I32, (8, LANES), 0) & 3
    side2, side3 = lines_23(za_ref[0:8, :], zb_ref[0:8, :], depth_row)
    for depth in range(4):
        at = first_row + depth * 4
        out_ref[at + 2 : at + 3, :] = side2[depth : depth + 1]
        out_ref[at + 3 : at + 4, :] = side3[depth : depth + 1]


def tail_row(ref, rows):
    window = ref[rows, CELLS - LANES : CELLS]
    return pltpu.roll(window, CELLS - (ROWS - 1) * LANES, 1)


def edges_kernel(adj_ref, flag_ref, t_ref, depth_ref, d_ref, b_ref, ts_ref, blk_ref, dense_ref, z_ref):
    row, lane, cell, i, j = grid_iotas()
    inside = cell < CELLS
    for number, ref in enumerate((b_ref, d_ref, depth_ref)):
        base = number * ROWS
        for l in range(ROWS - 1):
            dense_ref[base + l : base + l + 1, :] = ref[:, l * LANES : (l + 1) * LANES].astype(F32)
        dense_ref[base + ROWS - 1 : base + ROWS, :] = tail_row(ref, slice(0, 1)).astype(F32)
        dense_ref[base : base + ROWS, :] = jnp.where(inside, dense_ref[base : base + ROWS, :], 0.0)
        write_frames(dense_ref, base, blk_ref, number * 16, z_ref.at[0], z_ref.at[1])
    at = 48
    for sides in ((0, 1, 2, 3), (2, 2, 0, 0), (3, 3, 1, 1)):
        for ref in (adj_ref, flag_ref):
            for side in sides:
                blk_ref[at : at + 1, :] = jnp.full((1, LANES), ref[0, side], I32).astype(F32)
                at += 1
    levels = t_ref.shape[1]
    for first in range(0, levels, 8):
        size = min(8, levels - first)
        lane8 = lax.broadcasted_iota(I32, (size, LANES), 1)
        odd = lane8 & 1
        owner = column_owner(lane8)
        la = (SIDE * owner + 89 * odd) >> 7
        lb = jnp.where(owner + 64 < SIDE, (SIDE * (owner + 64) + 89 * odd) >> 7, -1)
        za = jnp.zeros((size, LANES), F32)
        zb = za
        for l in range(ROWS):
            if l < ROWS - 1:
                x = t_ref[0, first : first + size, l * LANES : (l + 1) * LANES]
            else:
                x = pltpu.roll(
                    t_ref[0, first : first + size, CELLS - LANES : CELLS], CELLS - (ROWS - 1) * LANES, 1
                )
            if l <= (SIDE * 63 + 89) // LANES:
                za = jnp.where(la == l, x, za)
            if l >= (SIDE * 64) // LANES:
                zb = jnp.where(lb == l, x, zb)
        z_ref[0, first : first + size, :] = za
        z_ref[1, first : first + size, :] = zb
        ts_ref[0, first : first + size, :] = t_ref[0, first : first + size, 0:LANES]
        window = t_ref[0, first : first + size, CELLS - LANES : CELLS]
        ts_ref[1, first : first + size, :] = pltpu.roll(window, SIDE, 1)
    side2, side3 = lines_23(z_ref[0], z_ref[1], 0)
    ts_ref[2] = side2
    ts_ref[3] = side3
    for side in range(4):
        ts_ref[side, levels : levels + 1, :] = blk_ref[32 + side : 33 + side, :]
        ts_ref[side, levels + 1 : levels + 2, :] = jnp.zeros((1, LANES), F32)


def to_dense(src_ref, dst_ref, levels):
    for first in range(0, levels, 8):
        size = min(8, levels - first)
        for l in range(ROWS):
            if l < ROWS - 1:
                x = src_ref[0, first : first + size, l * LANES : (l + 1) * LANES]
            else:
                x = pltpu.roll(
                    src_ref[0, first : first + size, CELLS - LANES : CELLS], CELLS - (ROWS - 1) * LANES, 1
                )
            dst_ref[pl.ds(first * ROWS + l, size, stride=ROWS), :] = x


def interior_reach(depth):
    row, lane, cell, i, j = grid_iotas()
    zero = jnp.zeros_like(depth)
    along = jnp.where(j < SIDE - 1, jnp.minimum(depth, ahead(depth, 1)), zero)
    across = jnp.where(cell < CELLS - SIDE, jnp.minimum(depth, ahead(depth, SIDE)), zero)
    return along, across


def interior_spread(x, along, across, level):
    zero = jnp.zeros_like(x)
    flux1 = jnp.where(along > level, ahead(x, 1) - x, zero)
    flux2 = jnp.where(across > level, ahead(x, SIDE) - x, zero)
    return (flux1 - behind(flux1, 1)) + (flux2 - behind(flux2, SIDE))


def columns_kernel(levels, k_ref, s_ref, t_ref, dense_ref, a_ref, q_ref, f_ref, aq_ref, g_ref, v_ref, td_ref, z_ref):
    to_dense(k_ref, g_ref, levels)
    to_dense(s_ref, v_ref, levels)
    to_dense(t_ref, td_ref, levels)
    depth = dense_ref[2 * ROWS : 3 * ROWS, :]
    along, across = interior_reach(depth)
    zero = jnp.zeros((ROWS, LANES), F32)

    def down(level, carry):
        link, below, va, vq = carry
        at = pl.ds(pl.multiple_of(level * ROWS, ROWS), ROWS)
        here = level.astype(F32)
        r = jnp.where(depth > here + 1.0, g_ref[at, :], zero)
        wet = jnp.where(depth > here, 1.0, zero)
        upper = 1.0 + below
        inverse = 1.0 / (upper + r)
        ratio = r * inverse
        va = (v_ref[at, :] + link * va) * inverse
        vq = (wet + link * vq) * inverse
        g_ref[at, :] = ratio
        v_ref[at, :] = va
        q_ref[at, :] = vq
        return r, upper * ratio, va, vq

    lax.fori_loop(0, levels, down, (zero, zero, zero, zero))
    row, lane, cell, i, j = grid_iotas()
    column = (j == 0) | (j == SIDE - 1)
    first = column & (i < 64)
    second = column & (i >= 64) & (i < SIDE)

    def up(step, carry):
        xa, xq, total = carry
        level = levels - 1 - step
        at = pl.ds(pl.multiple_of(level * ROWS, ROWS), ROWS)
        ratio = g_ref[at, :]
        xa = v_ref[at, :] + ratio * xa
        xq = q_ref[at, :] + ratio * xq
        a_ref[at, :] = xa
        q_ref[at, :] = xq
        here = pl.ds(level, 1)
        for number, x in enumerate((xa, xq)):
            z_ref[number * 4, here, :] = jnp.sum(jnp.where(first, x, zero), axis=0, keepdims=True)
            z_ref[number * 4 + 1, here, :] = jnp.sum(jnp.where(second, x, zero), axis=0, keepdims=True)
            aq_ref[number * 4, here, :] = x[0:1]
            z_ref[number * 4 + 2, here, :] = x[ROWS - 2 : ROWS - 1]
            z_ref[number * 4 + 3, here, :] = x[ROWS - 1 : ROWS]
        t = td_ref[at, :]
        mixed_h = t + SPREAD * interior_spread(t, along, across, level.astype(F32))
        return xa, xq, total + xq * mixed_h

    xa, xq, total = lax.fori_loop(0, levels, up, (zero, zero, zero))
    f_ref[...] = jnp.where(cell < CELLS, total, zero)
    spare = z_ref.shape[1] - levels
    for number in range(2):
        for part in range(4):
            z_ref[number * 4 + part, levels:, :] = jnp.zeros((spare, LANES), F32)
        aq_ref[number * 4, levels:, :] = jnp.zeros((spare, LANES), F32)
        side2, side3 = lines_23(z_ref[number * 4], z_ref[number * 4 + 1], 0)
        aq_ref[number * 4 + 2] = side2
        aq_ref[number * 4 + 3] = side3
        low, high = z_ref[number * 4 + 2], z_ref[number * 4 + 3]
        wide = lax.broadcasted_iota(I32, low.shape, 1)
        aq_ref[number * 4 + 1] = jnp.where(wide < 54, pltpu.roll(low, 54, 1), pltpu.roll(high, 54, 1))


def pick(refs, shifts, tiles, me, neighbour, first, side_met):
    value = refs[0][first + side_met]
    for number in range(1, len(shifts)):
        hit = neighbour == lax.rem(me + tiles - shifts[number], tiles)
        value = jnp.where(hit, refs[number][first + side_met], value)
    return value


def seam_index(flag):
    lane = lanes8()
    return jnp.where((flag & 1) == 1, SIDE - 1 - lane, lane) & 127


def forcing_kernel(shifts, tiles, levels, me_ref, adj_ref, flag_ref, f_ref, ts_ref, aq_ref, *rest):
    refs = rest[: len(shifts)]
    out_ref, frame_ref, reach_ref, za_ref, zb_ref = rest[len(shifts) :]
    me = me_ref[0]
    level = lax.broadcasted_iota(I32, (32, LANES), 0).astype(F32)
    lines = []
    for side in range(4):
        neighbour = adj_ref[0, side]
        flag = flag_ref[0, side]
        other = take(pick(refs, shifts, tiles, me, neighbour, 0, flag >> 1), seam_index(flag))
        own = ts_ref[side]
        reach = jnp.minimum(other[levels : levels + 1], own[levels : levels + 1])
        reach = jnp.where(neighbour >= 0, reach, 0.0)
        reach_ref[side : side + 1, :] = reach
        flux = jnp.where(reach > level, other - own, 0.0)
        lines.append(jnp.sum(aq_ref[4 + side] * flux, axis=0, keepdims=True))
    reach_ref[4:8, :] = jnp.zeros((4, LANES), F32)
    seams = scatter_lines(scatter_masks(), jnp.concatenate(lines + lines, axis=0))
    out_ref[...] = (f_ref[...] + SPREAD * seams) * (1.0 / math.sqrt(levels))
    write_frames(out_ref, 0, frame_ref, 0, za_ref, zb_ref)


def block_rows(refs, counts, block, first, size):
    position = 0
    for ref, count in zip(refs, counts):
        for number in range(count):
            at = number * block + first
            yield position, ref[at : at + size, :]
            position += 1


def gather_lines(p, lines):
    high = lines.astype(jnp.bfloat16)
    rest = lines - high.astype(F32)
    middle = rest.astype(jnp.bfloat16)
    low = (rest - middle.astype(F32)).astype(jnp.bfloat16)
    out = jnp.dot(p, high, preferred_element_type=F32)
    out = out + jnp.dot(p, middle, preferred_element_type=F32)
    return out + jnp.dot(p, low, preferred_element_type=F32)


def ends(x, low, high, low_parity, high_parity, depth):
    lane = lax.broadcasted_iota(I32, x.shape, 1)
    low_end = take(low, jnp.where(low_parity == 1, SIDE - 1 - depth, depth))
    high_end = take(high, jnp.where(high_parity == 1, SIDE - 1 - depth, depth))
    return (
        jnp.where(lane == 0, low_end, pltpu.roll(x, 1, 1)),
        jnp.where(lane == SIDE - 1, high_end, pltpu.roll(x, LANES - 1, 1)),
    )


def prepare_kernel(counts, lines, me_ref, dense_ref, *rest):
    refs = rest[: len(counts)]
    p_ref, index_ref, frame_ref, own_ref, seam_ref, work_ref, depth_ref, d_ref = rest[len(counts) :]
    me = me_ref[0]
    for number in range(6):
        for position, rows in block_rows(refs, counts, BLOCK, 48 + 4 * number, 4):
            work_ref[number, position * 4 : position * 4 + 4, :] = rows
    for depth in range(4):
        for position, rows in block_rows(refs, counts, BLOCK, 16 + 4 * depth, 4):
            d_ref[depth, position * 4 : position * 4 + 4, :] = rows
        for position, rows in block_rows(refs, counts, BLOCK, 32 + 4 * depth, 4):
            depth_ref[depth, position * 4 : position * 4 + 4, :] = rows
    lane = lax.broadcasted_iota(I32, (lines, LANES), 1)
    odd = lax.broadcasted_iota(I32, (lines, LANES), 0) & 1
    column = lax.broadcasted_iota(I32, (lines, lines), 1)
    for number in range(3):
        tile = work_ref[2 * number, :, 0:1].astype(I32)
        flag = work_ref[2 * number + 1, :, 0:1].astype(I32)
        at = jnp.where(tile >= 0, 4 * (tile ^ me) + (flag >> 1), -1)
        p = jnp.where(jnp.broadcast_to(at, (lines, lines)) == column, 1.0, 0.0)
        p_ref[number * lines : (number + 1) * lines, :] = p.astype(jnp.bfloat16)
        parity = work_ref[2 * number + 1].astype(I32) & 1
        if number == 0:
            index_ref[0:lines, :] = jnp.where(parity == 1, SIDE - 1 - lane, lane) & 127
        else:
            index_ref[number * lines : (number + 1) * lines, :] = parity ^ odd
    wet = [jnp.where(depth_ref[depth] > 0.0, 1.0, 0.0) for depth in range(4)]
    met = gather_lines(p_ref[...], wet[0])
    facing = take(met[0:lines], index_ref[0:lines, :])
    for depth in range(3):
        low, high = ends(
            wet[depth],
            met[lines : 2 * lines],
            met[2 * lines : 3 * lines],
            index_ref[lines : 2 * lines, :],
            index_ref[2 * lines : 3 * lines, :],
            depth,
        )
        masks = [
            wet[depth] * (facing if depth == 0 else wet[depth - 1]),
            wet[depth] * wet[depth + 1],
            wet[depth] * low,
            wet[depth] * high,
        ]
        frame_ref[depth, 0] = d_ref[depth] + ((masks[0] + masks[1]) + (masks[2] + masks[3]))
        for number in range(4):
            frame_ref[depth, 1 + number] = masks[number]
        if depth == 0:
            seam_ref[...] = masks[0][0:8]
    surface = jnp.minimum(dense_ref[2 * ROWS : 3 * ROWS, :], 1.0)
    along, across = interior_reach(surface)
    degree = (along + behind(along, 1)) + (across + behind(across, SIDE))
    degree = degree + scatter_lines(scatter_masks(), seam_ref[...])
    own_ref[0] = dense_ref[ROWS : 2 * ROWS, :] + degree
    own_ref[1] = along
    own_ref[2] = across


def krylov_kernel(
    counts, block, lines, b_ref, p_ref, index_ref, frame_ref, own_ref, seam_ref, *rest
):
    refs = rest[: len(counts)]
    v_ref, line_ref, gram_ref, x_ref = rest[len(counts) :]
    for depth in range(4):
        for position, rows in block_rows(refs, counts, block, 4 * depth, 4):
            x_ref[depth, position * 4 : position * 4 + 4, :] = rows
    p = p_ref[...]
    facing_at = index_ref[0:lines, :]
    low_parity = index_ref[lines : 2 * lines, :]
    high_parity = index_ref[2 * lines : 3 * lines, :]
    scale = 2.0 / CENTRE
    masks = scatter_masks()
    row, lane, cell, i, j = grid_iotas()
    inside = cell < CELLS
    diagonal, along, across = own_ref[0], own_ref[1], own_ref[2]
    seam = seam_ref[...]
    frames = [[x_ref[depth] for depth in range(4)]]
    own = [b_ref[0:ROWS, :]]
    for step in range(ITERS):
        x = frames[-1]
        met = gather_lines(p, x[0])
        facing = take(met[0:lines], facing_at)
        line_ref[step] = facing[0:8]
        mine = own[-1]
        flow = (along * ahead(mine, 1) + behind(along * mine, 1)) + (
            across * ahead(mine, SIDE) + behind(across * mine, SIDE)
        )
        image = diagonal * mine - flow - scatter_lines(masks, seam * facing[0:8])
        image = jnp.where(inside, scale * image - 2.0 * mine, 0.0)
        own.append(0.5 * image if step == 0 else image - own[-2])
        following = []
        for depth in range(ITERS - 1 - step):
            low, high = ends(
                x[depth],
                met[lines : 2 * lines],
                met[2 * lines : 3 * lines],
                low_parity,
                high_parity,
                depth,
            )
            before = facing if depth == 0 else x[depth - 1]
            flow = (frame_ref[depth, 1] * before + frame_ref[depth, 2] * x[depth + 1]) + (
                frame_ref[depth, 3] * low + frame_ref[depth, 4] * high
            )
            image = scale * (frame_ref[depth, 0] * x[depth] - flow) - 2.0 * x[depth]
            following.append(0.5 * image if step == 0 else image - frames[-2][depth])
        frames.append(following)
        if step < ITERS - 1:
            v_ref[step] = own[-1]
    at = 0
    for first in range(ITERS + 1):
        for second in range(first + 1):
            gram_ref[at : at + 1, :] = jnp.sum(own[first] * own[second], axis=0, keepdims=True)
            at += 1
    gram_ref[15:16, :] = jnp.zeros((1, LANES), F32)


def image_of(p):
    out = [None] * (len(p) + 1)

    def add(at, value):
        out[at] = value if out[at] is None else out[at] + value

    for at, value in enumerate(p):
        add(at, CENTRE * value)
        if at == 0:
            add(1, CENTRE * value)
        else:
            add(at + 1, 0.5 * CENTRE * value)
            add(at - 1, 0.5 * CENTRE * value)
    return out


def form(left, gram, right):
    total = None
    for first, x in enumerate(left):
        inner = None
        for second, y in enumerate(right):
            term = gram[max(first, second)][min(first, second)] * y
            inner = term if inner is None else inner + term
        total = x * inner if total is None else total + x * inner
    return total


def coefficients(refs, sum_ref):
    total = refs[0][...]
    for ref in refs[1:]:
        total = total + ref[...]
    sum_ref[...] = jnp.broadcast_to(jnp.sum(total, axis=1, keepdims=True), (16, LANES))
    gram = []
    at = 0
    for first in range(ITERS + 1):
        gram.append([sum_ref[at + second : at + second + 1, :] for second in range(first + 1)])
        at += first + 1
    one = jnp.ones((1, LANES), F32)
    x = []
    r = [one]
    p = [one]
    rr = gram[0][0]
    for step in range(ITERS):
        image = image_of(p)
        curve = form(p, gram, image)
        alpha = jnp.where(curve > 0.0, rr / curve, 0.0)
        x = [x[n] + alpha * p[n] if n < len(x) else alpha * p[n] for n in range(len(p))]
        r = [r[n] - alpha * image[n] if n < len(r) else -alpha * image[n] for n in range(len(image))]
        if step < ITERS - 1:
            new = jnp.maximum(form(r, gram, r), 0.0)
            beta = jnp.where(rr > 0.0, new / rr, 0.0)
            p = [r[n] + beta * p[n] if n < len(p) else r[n] for n in range(len(r))]
            rr = new
    return x


def combine(x, b_ref, v_ref):
    out = x[0] * b_ref[0:ROWS, :]
    for number in range(1, ITERS):
        out = out + x[number] * v_ref[number - 1]
    return out


def gradient_kernel(shifts, tiles, levels, grams, me_ref, adj_ref, flag_ref, *rest):
    gram_refs = rest[:grams]
    rest = rest[grams:]
    dense_ref, v_ref, line_ref, blk_ref, reach_ref, a_ref, q_ref, aq_ref = rest[:8]
    refs = rest[8 : 8 + len(shifts)]
    out_ref, sum_ref, w_ref, h_ref = rest[8 + len(shifts) :]
    me = me_ref[0]
    x = coefficients(gram_refs, sum_ref)
    level_scale = 1.0 / math.sqrt(levels)
    adjoint = combine(x, dense_ref, v_ref) * level_scale
    own_line = x[0] * blk_ref[0:8, :]
    met_line = x[0] * line_ref[0]
    w_ref[4, 0:ROWS // 2, :] = jnp.zeros((ROWS // 2, LANES), F32)
    own_sides = []
    depth = dense_ref[2 * ROWS : 3 * ROWS, :]
    along, across = interior_reach(depth)
    sum_ref[0:8, :] = met_line + x[1] * line_ref[1] + x[2] * line_ref[2] + x[3] * line_ref[3]
    h_ref[0:ROWS, :] = adjoint
    w_ref[4, 8:9, :] = h_ref[0:1, :]
    w_ref[4, 9:10, :] = row_line(h_ref, 0, (SIDE - 1) * SIDE)
    row, lane, cell, i, j = grid_iotas()
    column = (j == 0) | (j == SIDE - 1)
    zero = jnp.zeros((ROWS, LANES), F32)
    za = jnp.sum(jnp.where(column & (i < 64), adjoint, zero), axis=0, keepdims=True)
    zb = jnp.sum(jnp.where(column & (i >= 64), adjoint, zero), axis=0, keepdims=True)
    side2, side3 = lines_23(jnp.broadcast_to(za, (8, LANES)), jnp.broadcast_to(zb, (8, LANES)), 0)
    w_ref[4, 10:11, :] = side2[0:1]
    w_ref[4, 11:12, :] = side3[0:1]
    level = lax.broadcasted_iota(I32, (32, LANES), 0).astype(F32)
    fluxes = []
    for side in range(4):
        neighbour = adj_ref[0, side]
        flag = flag_ref[0, side]
        index = seam_index(flag)
        a_other = take(pick(refs, shifts, tiles, me, neighbour, 0, flag >> 1), index)
        q_other = take(pick(refs, shifts, tiles, me, neighbour, 4, flag >> 1), index)
        other = a_other + (sum_ref[side : side + 1, :] * level_scale) * q_other
        own = aq_ref[side] + w_ref[4, 8 + side : 9 + side, :] * aq_ref[4 + side]
        fluxes.append(jnp.where(reach_ref[side : side + 1, :] > level, other - own, 0.0))
    wa, wb, w1 = spread_lines(fluxes[2], fluxes[3], fluxes[1])
    w_ref[0] = wa
    w_ref[1] = wb
    w_ref[2] = fluxes[0]
    w_ref[3] = w1
    masks = scatter_masks()

    def per_level(number, carry):
        at = pl.ds(pl.multiple_of(number * ROWS, ROWS), ROWS)
        here = pl.ds(number, 1)
        h = a_ref[at, :] + adjoint * q_ref[at, :]
        spread = interior_spread(h, along, across, number.astype(F32))
        spread = spread + scatter_rows(
            masks, w_ref[0, here, :], w_ref[1, here, :], w_ref[2, here, :], w_ref[3, here, :]
        )
        h_ref[at, :] = h + SPREAD * spread
        return carry

    lax.fori_loop(0, levels, per_level, 0)
    for first in range(0, levels, 8):
        size = min(8, levels - first)
        for l in range(ROWS):
            width = min(LANES, CELLS - l * LANES)
            x_tile = h_ref[pl.ds(first * ROWS + l, size, stride=ROWS), :]
            out_ref[0, first : first + size, l * LANES : l * LANES + width] = x_tile[:, 0:width]


def height_kernel(grams, *rest):
    gram_refs = rest[:grams]
    b_ref, v_ref, out_ref, sum_ref, x_ref = rest[grams:]
    x_ref[...] = combine(coefficients(gram_refs, sum_ref), b_ref, v_ref)
    for l in range(ROWS):
        width = min(LANES, CELLS - l * LANES)
        out_ref[:, l * LANES : l * LANES + width] = x_ref[l : l + 1, 0:width]


def rounds(tiles):
    out = []
    stride = 1
    while stride < tiles:
        radix = 4 if (tiles // stride) % 4 == 0 else 2
        out.append((stride, radix))
        stride *= radix
    return out


def swap(x, tiles, offset):
    return lax.ppermute(x, "tile", [(t, t ^ offset) for t in range(tiles)])


def gather_tiles(block, tiles):
    held = [block]
    counts = [1]
    for stride, radix in rounds(tiles):
        whole = held[0] if len(held) == 1 else jnp.concatenate(held, axis=0)
        for number in range(1, radix):
            held.append(swap(whole, tiles, number * stride))
            counts.append(stride)
    return held, tuple(counts)


def sum_tiles(block, tiles):
    held = [block]
    for stride, radix in rounds(tiles):
        whole = functools.reduce(jnp.add, held)
        held = [whole] + [swap(whole, tiles, number * stride) for number in range(1, radix)]
    return held


def shards(thermal, stirring, depth, adjacent, flags, main_entry, sensitivity, elevation, tiles):
    levels = thermal.shape[1]
    me = lax.axis_index("tile").astype(I32).reshape(1)
    smem = pl.BlockSpec(memory_space=pltpu.SMEM)
    vmem = pl.BlockSpec(memory_space=pltpu.VMEM)
    params = pltpu.CompilerParams(vmem_limit_bytes=48 * 1024 * 1024)

    def shape(*dims):
        return jax.ShapeDtypeStruct(dims, F32)

    def call(kernel, outs, scratch, scalars, arrays, name, flops=1e6, traffic=1e6):
        return pl.pallas_call(
            kernel,
            out_shape=outs,
            in_specs=[smem] * len(scalars) + [vmem] * len(arrays),
            out_specs=jax.tree.map(lambda _: vmem, outs),
            scratch_shapes=scratch,
            compiler_params=params,
            cost_estimate=pl.CostEstimate(flops=int(flops), bytes_accessed=int(traffic), transcendentals=0),
            name=name,
        )(*scalars, *arrays)

    offsets = []
    for offset in (1, -1, ROW_TILES, -ROW_TILES, tiles // 2):
        if offset % tiles not in [o % tiles for o in offsets] and offset % tiles:
            offsets.append(offset)
    shifts = tuple(offset % tiles for offset in offsets)

    def to_neighbours(x):
        out = []
        for offset in offsets:
            pairs = [(t, t + offset) for t in range(tiles) if 0 <= t + offset < tiles]
            if 2 * offset == tiles or 2 * offset == -tiles:
                pairs = [(t, (t + offset) % tiles) for t in range(tiles)]
            out.append(lax.ppermute(x, "tile", pairs))
        return out

    strips, block, dense = call(
        edges_kernel,
        (shape(4, 32, LANES), shape(BLOCK, LANES), shape(3 * ROWS, LANES)),
        [pltpu.VMEM((2, 32, LANES), F32)],
        (adjacent, flags),
        (thermal, depth, main_entry, elevation),
        "edges",
    )
    strips_met = to_neighbours(strips)
    blocks, counts = gather_tiles(block, tiles)
    big = pltpu.VMEM((levels * ROWS, LANES), F32)
    solved, weight, forcing_inside, edge_lines = call(
        functools.partial(columns_kernel, levels),
        (shape(levels * ROWS, LANES), shape(levels * ROWS, LANES), shape(ROWS, LANES), shape(8, 32, LANES)),
        [big, big, big, pltpu.VMEM((8, 32, LANES), F32)],
        (),
        (stirring, sensitivity, thermal, dense),
        "columns",
        2e7,
        8e6,
    )
    edge_lines_met = to_neighbours(edge_lines)
    forcing, forcing_frames, reach = call(
        functools.partial(forcing_kernel, shifts, tiles, levels),
        (shape(ROWS, LANES), shape(16, LANES), shape(8, LANES)),
        [pltpu.VMEM((8, LANES), F32), pltpu.VMEM((8, LANES), F32)],
        (me, adjacent, flags),
        (forcing_inside, strips, edge_lines, *strips_met),
        "forcing",
    )
    forcing_blocks, _ = gather_tiles(forcing_frames, tiles)
    lines = 4 * tiles
    frame = pltpu.VMEM((4, lines, LANES), F32)
    prepared = call(
        functools.partial(prepare_kernel, counts, lines),
        (
            jax.ShapeDtypeStruct((3 * lines, lines), jnp.bfloat16),
            jax.ShapeDtypeStruct((3 * lines, LANES), I32),
            shape(3, 5, lines, LANES),
            shape(3, ROWS, LANES),
            shape(8, LANES),
        ),
        [pltpu.VMEM((6, lines, LANES), F32), frame, frame],
        (me,),
        (dense, *blocks),
        "prepare",
    )

    def krylov(rhs, rhs_blocks, rows, name):
        return call(
            functools.partial(krylov_kernel, counts, rows, lines),
            (shape(ITERS - 1, ROWS, LANES), shape(ITERS, 8, LANES), shape(16, LANES)),
            [frame],
            (),
            (rhs, *prepared, *rhs_blocks),
            name,
        )

    basis_b, lines_b, gram_b = krylov(dense, blocks, BLOCK, "krylov_adjoint")
    grams_b = sum_tiles(gram_b, tiles)
    basis_a, _, gram_a = krylov(forcing, forcing_blocks, 16, "krylov_forward")
    grams_a = sum_tiles(gram_a, tiles)
    gradient = call(
        functools.partial(gradient_kernel, shifts, tiles, levels, len(grams_b)),
        jax.ShapeDtypeStruct(thermal.shape, F32),
        [pltpu.VMEM((16, LANES), F32), pltpu.VMEM((5, 32, LANES), F32), big],
        (me, adjacent, flags),
        (*grams_b, dense, basis_b, lines_b, block, reach, solved, weight, edge_lines, *edge_lines_met),
        "gradient",
        1e7,
        4e6,
    )
    height = call(
        functools.partial(height_kernel, len(grams_a)),
        jax.ShapeDtypeStruct(elevation.shape, F32),
        [pltpu.VMEM((16, LANES), F32), pltpu.VMEM((ROWS, LANES), F32)],
        (),
        (*grams_a, forcing, basis_a),
        "height",
    )
    return height, gradient


def solution(mesh):
    placed = (
        P(("ens", "tile"), None, None),
        P("tile", None, None),
        P("tile", None),
        P("tile", None),
        P("tile", None),
        P("tile", None),
        P(("ens", "tile"), None, None),
        P(("ens", "tile"), None),
    )
    return jax.shard_map(
        functools.partial(shards, tiles=mesh.shape["tile"]),
        mesh=mesh,
        in_specs=placed,
        out_specs=(P(("ens", "tile"), None), P(("ens", "tile"), None, None)),
        check_vma=False,
    )
```

time: 728 us -> 81.2 us (0.11); the launches traced: 719 us -> 81 us
  blocking collectives: 424 us -> 0 us
  other arithmetic: 200 us -> 0.01 us
  local copies, waits for them, and re-layouts: 74.4 us -> 5.58 us
  starting transfers between devices: 0 us -> 45.1 us
  Pallas kernels: 0 us -> 21 us
  between operations: 19.9 us -> 0.87 us
  waiting for transfers between devices: 0 us -> 8.35 us
    psum x7 -> x0, blocking collectives: 214 us -> none  [the longest x4 122 us: residual_norm(): return lax.psum(jnp.sum(residual * residual), 'tile')]
    all_gather x11 -> x0, blocking collectives: 210 us -> none  [the longest x8 146 us: surface_ghosts(): every_strip = lax.all_gather(own_strips, 'tile', axis=0, tiled=True)]
    dynamic_update_slice x180 -> x0, other arithmetic: 175 us -> none  [column_solve(): lax.scan(forward_sweep, (starting, starting), sweep_inputs)]
    ppermute x0 -> x30, starting transfers between devices: none -> 45.1 us  [the longest x24 29.6 us: swap(): return lax.ppermute(x, 'tile', [(t, t ^ offset) for t in range(tiles)])]
    pallas_call x0 -> x8, Pallas kernels: none -> 21 us  [call(): pl.pallas_call(kernel, out_shape=outs, in_specs=[smem] * len(scalars) + [...]
    reshape x22 -> x0, local copies, waits for them, and re-layouts: 16.4 us -> none  [the longest x20 14.2 us: place_side(): return padded.reshape(edge_strip.shape[:-1] + (cells,))]
    unnamed x67 -> x24, local copies, waits for them, and re-layouts: 20.2 us -> 5.57 us
    pad x20 -> x0, local copies, waits for them, and re-layouts: 11.8 us -> none  [place_side(): jnp.pad(edge_strip[..., None], leading + [(0, 0), (before, tile_size - 1...]
  transfers between devices with their start and end apart: 0 -> 30, of which waited for: 0 -> 6; matrix products, arithmetic and copies ran while one was open for 0% -> 4% of each run, Pallas kernels for 0% -> 24%
where the time goes in v1:
time: 81.2 us; the launch traced here: 81 us
  starting transfers between devices  45.1 us (56%)
  Pallas kernels  21 us (26%)
  waiting for transfers between devices  8.35 us (10%)
  local copies, waits for them, and re-layouts  5.58 us (7%)
  between operations  0.87 us (1%)
    ppermute x24, starting transfers between devices, swap(): return lax.ppermute(x, 'tile', [(t, t ^ offset) for t in range(tiles)])  29.6 us
    pallas_call x8, Pallas kernels, call(): pl.pallas_call(kernel, out_shape=outs, in_specs=[smem] * len(scalars) + [...  21 us
    ppermute x6, starting transfers between devices, to_neighbours(): out.append(lax.ppermute(x, 'tile', pairs))  15.6 us
    ppermute x24, waiting for transfers between devices, swap(): return lax.ppermute(x, 'tile', [(t, t ^ offset) for t in range(tiles)])  6.22 us
    unnamed x24, local copies, waits for them, and re-layouts  5.57 us
    ppermute x6, waiting for transfers between devices, to_neighbours(): out.append(lax.ppermute(x, 'tile', pairs))  2.13 us
  transfers between devices with their start and end apart: 30, of which 6 were waited for; matrix products, arithmetic and copies ran while one was open for 4% of the time, Pallas kernels for 24%

profile of v1, /device:TPU:0, one launch (start us, length us, event | category | flops | bytes accessed | tf_op | source)
XLA Modules:
  0.0 81.0 jit_solution(10849599884678427426)
XLA Ops:
  0.7 1.8 %copy.13.t_ref = f32[1,30,8100]{2,1,0:T(8,128)S(1)} copy(f32[1,30,8100]{2,0,1:T(1,128)} %param.8) | data formatting | bytes 1944000 | tf_op args[0]
  2.5 0.0 copy-start.5
  2.6 0.9 %edges.1 = (f32[4,32,128]{2,1,0:T(8,128)S(1)}, f32[72,128]{1,0:T(8,128)S(1)}, f32[192,128]{1,0:T(8,128)S(1)}) custom-call(s32[1,4]{1,0:T(1,128)S(1)} %copy-done.3, s32[1,4]{1,0:T(1,128)S(1)} %copy-done.4, f32[1,30,8100]{2,1,0:T(8,128)S(1)} %copy.13.t_ref, s32[1,8100]{1,0:T(1,128)S(1)} %copy-done, f32[1,8100]{1,0:T(1,128)S(1)} %copy-done.1, ...), custom_call_target="tpu_custom_call" | custom-call | flops 1000000 | bytes 1000000 | tf_op jit(solution)/shard_map/edges/pallas_call | solution.py:662
  3.5 2.4 %collective-permute-start = (f32[4,32,128]{2,1,0:T(8,128)S(1)}, f32[4,32,128]{2,1,0:T(8,128)S(1)}, u32[]{:S(2)}, u32[]{:S(2)}) collective-permute-start(f32[4,32,128]{2,1,0:T(8,128)S(1)} %get-tuple-element.24.ts_ref), channel_id=1, source_target_pairs={{0,1},{1,2},{2,3},{3,4},{4,5},{5,6},{6,7},{7,8},{8,9},{9,10},{10,1... | collective-permute-start | bytes 196616 | tf_op jit(solution)/shard_map/ppermute | solution.py:685
  5.8 1.3 %collective-permute-start.1 = (f32[4,32,128]{2,1,0:T(8,128)S(1)}, f32[4,32,128]{2,1,0:T(8,128)S(1)}, u32[]{:S(2)}, u32[]{:S(2)}) collective-permute-start(f32[4,32,128]{2,1,0:T(8,128)S(1)} %get-tuple-element.24.ts_ref), channel_id=1, source_target_pairs={{1,0},{2,1},{3,2},{4,3},{5,4},{6,5},{7,6},{8,7},{9,8},{10,9},{11,1... | collective-permute-start | bytes 196616 | tf_op jit(solution)/shard_map/ppermute | solution.py:685
  7.1 6.9 %collective-permute-start.2 = (f32[4,32,128]{2,1,0:T(8,128)S(1)}, f32[4,32,128]{2,1,0:T(8,128)S(1)}, u32[]{:S(2)}, u32[]{:S(2)}) collective-permute-start(f32[4,32,128]{2,1,0:T(8,128)S(1)} %get-tuple-element.24.ts_ref), channel_id=1, source_target_pairs={{0,8},{1,9},{2,10},{3,11},{4,12},{5,13},{6,14},{7,15},{8,0},{9,1},... | collective-permute-start | bytes 196616 | tf_op jit(solution)/shard_map/ppermute | solution.py:685
  14.0 0.6 collective-permute-start.4
  14.7 0.6 copy.11.k_ref
  15.3 0.6 copy-done.6
  15.9 0.6 copy.12.s_ref
  16.4 7.7 %columns.1 = (f32[1920,128]{1,0:T(8,128)S(1)}, f32[1920,128]{1,0:T(8,128)S(1)}, f32[64,128]{1,0:T(8,128)S(1)}, f32[8,32,128]{2,1,0:T(8,128)S(1)}) custom-call(f32[1,30,8100]{2,1,0:T(8,128)S(1)} %copy.11.k_ref, f32[1,30,8100]{2,1,0:T(8,128)S(1)} %copy.12.s_ref, f32[1,30,8100]{2,1,0:T(8,128)S(1)} %copy.13.t_ref, ...), custom_call_target="tpu_custom_call" | custom-call | flops 20000000 | bytes 8000000 | tf_op jit(solution)/shard_map/columns/pallas_call | solution.py:662
  24.2 1.3 %collective-permute-start.5 = (f32[72,128]{1,0:T(8,128)S(1)}, f32[72,128]{1,0:T(8,128)S(1)}, u32[]{:S(2)}, u32[]{:S(2)}) collective-permute-start(f32[72,128]{1,0:T(8,128)S(1)} %get-tuple-element.27.rest_0_.rest_7_), channel_id=1, source_target_pairs={{0,3},{1,2},{2,1},{3,0},{4,7},{5,6},{6,5},{7,4},{8,11},{9,10},{10,... | collective-permute-start | bytes 110600 | tf_op jit(solution)/shard_map/ppermute | solution.py:629
  25.5 2.1 %collective-permute-done.5.rest_3_ = f32[72,128]{1,0:T(8,128)S(1)} collective-permute-done((f32[72,128]{1,0:T(8,128)S(1)}, f32[72,128]{1,0:T(8,128)S(1)}, u32[]{:S(2)}, u32[]{:S(2)}) %collective-permute-start.5) | collective-permute-done | bytes 36896 | tf_op jit(solution)/shard_map/ppermute | solution.py:629
  27.7 1.6 %collective-permute-start.6 = (f32[288,128]{1,0:T(8,128)S(1)}, f32[288,128]{1,0:T(8,128)S(1)}, u32[]{:S(2)}, u32[]{:S(2)}) collective-permute-start(f32[288,128]{1,0:T(8,128)S(1)} %constant_dynamic-update-slice_fusion), channel_id=1, source_target_pairs={{0,4},{1,5},{2,6},{3,7},{4,0},{5,1},{6,2},{7,3},{8,12},{9,13},{10,... | collective-permute-start | bytes 442376 | tf_op jit(solution)/shard_map/ppermute | solution.py:629
  29.2 0.3 collective-permute-start.7
  29.6 2.5 %collective-permute-start.8 = (f32[288,128]{1,0:T(8,128)S(1)}, f32[288,128]{1,0:T(8,128)S(1)}, u32[]{:S(2)}, u32[]{:S(2)}) collective-permute-start(f32[288,128]{1,0:T(8,128)S(1)} %constant_dynamic-update-slice_fusion), channel_id=1, source_target_pairs={{0,12},{1,13},{2,14},{3,15},{4,8},{5,9},{6,10},{7,11},{8,4},{9,5},... | collective-permute-start | bytes 442376 | tf_op jit(solution)/shard_map/ppermute | solution.py:629
  32.1 0.9 %forcing.1 = (f32[64,128]{1,0:T(8,128)S(1)}, f32[16,128]{1,0:T(8,128)S(1)}, f32[8,128]{1,0:T(8,128)S(1)}) custom-call(s32[1]{0:T(128)} %bitcast.me_ref, s32[1,4]{1,0:T(1,128)S(1)} %copy-done.3, s32[1,4]{1,0:T(1,128)S(1)} %copy-done.4, f32[64,128]{1,0:T(8,128)S(1)} %get-tuple-element.23.f_ref, f32[4,32,128]{2,1,0:T(8,128)S(1)} %get-tuple-element.24.ts_ref, ...), custom_call_target="tpu_custom_call" | custom-call | flops 1000000 | bytes 1000000 | tf_op jit(solution)/shard_map/forcing/pallas_call | solution.py:662
  32.9 0.1 collective-permute-start.9
  33.0 1.5 %collective-permute-start.10 = (f32[16,128]{1,0:T(8,128)S(1)}, f32[16,128]{1,0:T(8,128)S(1)}, u32[]{:S(2)}, u32[]{:S(2)}) collective-permute-start(f32[16,128]{1,0:T(8,128)S(1)} %get-tuple-element.33.rest_0_), channel_id=1, source_target_pairs={{0,2},{1,3},{2,0},{3,1},{4,6},{5,7},{6,4},{7,5},{8,10},{9,11},{10,... | collective-permute-start | bytes 24584 | tf_op jit(solution)/shard_map/ppermute | solution.py:629
  34.5 0.9 %collective-permute-start.11 = (f32[16,128]{1,0:T(8,128)S(1)}, f32[16,128]{1,0:T(8,128)S(1)}, u32[]{:S(2)}, u32[]{:S(2)}) collective-permute-start(f32[16,128]{1,0:T(8,128)S(1)} %get-tuple-element.33.rest_0_), channel_id=1, source_target_pairs={{0,3},{1,2},{2,1},{3,0},{4,7},{5,6},{6,5},{7,4},{8,11},{9,10},{10,... | collective-permute-start | bytes 24584 | tf_op jit(solution)/shard_map/ppermute | solution.py:629
  35.3 1.4 %collective-permute-done.10.rest_2_ = f32[16,128]{1,0:T(8,128)S(1)} collective-permute-done((f32[16,128]{1,0:T(8,128)S(1)}, f32[16,128]{1,0:T(8,128)S(1)}, u32[]{:S(2)}, u32[]{:S(2)}) %collective-permute-start.10) | collective-permute-done | bytes 8224 | tf_op jit(solution)/shard_map/ppermute | solution.py:629
  36.7 0.8 %collective-permute-done.11.rest_3_ = f32[16,128]{1,0:T(8,128)S(1)} collective-permute-done((f32[16,128]{1,0:T(8,128)S(1)}, f32[16,128]{1,0:T(8,128)S(1)}, u32[]{:S(2)}, u32[]{:S(2)}) %collective-permute-start.11) | collective-permute-done | bytes 8224 | tf_op jit(solution)/shard_map/ppermute | solution.py:629
  37.6 0.7 collective-permute-start.12
  38.2 1.2 %collective-permute-start.13 = (f32[64,128]{1,0:T(8,128)S(1)}, f32[64,128]{1,0:T(8,128)S(1)}, u32[]{:S(2)}, u32[]{:S(2)}) collective-permute-start(f32[64,128]{1,0:T(8,128)S(1)} %constant_dynamic-update-slice_fusion.4), channel_id=1, source_target_pairs={{0,8},{1,9},{2,10},{3,11},{4,12},{5,13},{6,14},{7,15},{8,0},{9,1},... | collective-permute-start | bytes 98312 | tf_op jit(solution)/shard_map/ppermute | solution.py:629
  39.5 2.5 %collective-permute-start.14 = (f32[64,128]{1,0:T(8,128)S(1)}, f32[64,128]{1,0:T(8,128)S(1)}, u32[]{:S(2)}, u32[]{:S(2)}) collective-permute-start(f32[64,128]{1,0:T(8,128)S(1)} %constant_dynamic-update-slice_fusion.4), channel_id=1, source_target_pairs={{0,12},{1,13},{2,14},{3,15},{4,8},{5,9},{6,10},{7,11},{8,4},{9,5},... | collective-permute-start | bytes 98312 | tf_op jit(solution)/shard_map/ppermute | solution.py:629
  42.0 0.7 collective-permute-done.7.rest_5_
  42.7 0.5 prepare.1
  43.2 1.5 %krylov_adjoint.1 = (f32[3,64,128]{2,1,0:T(8,128)S(1)}, f32[4,8,128]{2,1,0:T(8,128)S(1)}, f32[16,128]{1,0:T(8,128)S(1)}) custom-call(f32[192,128]{1,0:T(8,128)S(1)} %get-tuple-element.22.dense_ref.b_ref.rest_4_, bf16[192,64]{1,0:T(8,128)(2,1)S(1)} %get-tuple-element.28.p_ref, s32[192,128]{1,0:T(8,128)S(1)} %get-tuple-element.29.index_ref, ...), custom_call_target="tpu_custom_call" | custom-call | flops 1000000 | bytes 1000000 | tf_op jit(solution)/shard_map/krylov_adjoint/pallas_call | solution.py:662
  44.7 0.1 collective-permute-start.23
  44.9 1.7 %collective-permute-start.22 = (f32[16,128]{1,0:T(8,128)S(1)}, f32[16,128]{1,0:T(8,128)S(1)}, u32[]{:S(2)}, u32[]{:S(2)}) collective-permute-start(f32[16,128]{1,0:T(8,128)S(1)} %get-tuple-element.36), channel_id=1, source_target_pairs={{0,2},{1,3},{2,0},{3,1},{4,6},{5,7},{6,4},{7,5},{8,10},{9,11},{10,... | collective-permute-start | bytes 24584 | tf_op jit(solution)/shard_map/ppermute | solution.py:629
  46.6 0.1 collective-permute-start.21
  46.7 1.1 %collective-permute-done.13.rest_5_ = f32[64,128]{1,0:T(8,128)S(1)} collective-permute-done((f32[64,128]{1,0:T(8,128)S(1)}, f32[64,128]{1,0:T(8,128)S(1)}, u32[]{:S(2)}, u32[]{:S(2)}) %collective-permute-start.13) | collective-permute-done | bytes 32800 | tf_op jit(solution)/shard_map/ppermute | solution.py:629
  47.8 1.3 %collective-permute-start.27 = (f32[8,32,128]{2,1,0:T(8,128)S(1)}, f32[8,32,128]{2,1,0:T(8,128)S(1)}, u32[]{:S(2)}, u32[]{:S(2)}) collective-permute-start(f32[8,32,128]{2,1,0:T(8,128)S(1)} %get-tuple-element.25.aq_ref.rest_11_), channel_id=1, source_target_pairs={{0,1},{1,2},{2,3},{3,4},{4,5},{5,6},{6,7},{7,8},{8,9},{9,10},{10,1... | collective-permute-start | bytes 393224 | tf_op jit(solution)/shard_map/ppermute | solution.py:685
  49.1 1.3 %collective-permute-start.28 = (f32[8,32,128]{2,1,0:T(8,128)S(1)}, f32[8,32,128]{2,1,0:T(8,128)S(1)}, u32[]{:S(2)}, u32[]{:S(2)}) collective-permute-start(f32[8,32,128]{2,1,0:T(8,128)S(1)} %get-tuple-element.25.aq_ref.rest_11_), channel_id=1, source_target_pairs={{1,0},{2,1},{3,2},{4,3},{5,4},{6,5},{7,6},{8,7},{9,8},{10,9},{11,1... | collective-permute-start | bytes 393224 | tf_op jit(solution)/shard_map/ppermute | solution.py:685
  50.4 2.0 %krylov_forward.1 = (f32[3,64,128]{2,1,0:T(8,128)S(1)}, f32[4,8,128]{2,1,0:T(8,128)}, f32[16,128]{1,0:T(8,128)S(1)}) custom-call(f32[64,128]{1,0:T(8,128)S(1)} %get-tuple-element.26.b_ref.rest_4_, bf16[192,64]{1,0:T(8,128)(2,1)S(1)} %get-tuple-element.28.p_ref, s32[192,128]{1,0:T(8,128)S(1)} %get-tuple-element.29.index_ref, ...), custom_call_target="tpu_custom_call" | custom-call | flops 1000000 | bytes 1000000 | tf_op jit(solution)/shard_map/krylov_forward/pallas_call | solution.py:662
  52.4 6.4 %collective-permute-start.17 = (f32[16,128]{1,0:T(8,128)S(1)}, f32[16,128]{1,0:T(8,128)S(1)}, u32[]{:S(2)}, u32[]{:S(2)}) collective-permute-start(f32[16,128]{1,0:T(8,128)S(1)} %get-tuple-element.34), channel_id=1, source_target_pairs={{0,3},{1,2},{2,1},{3,0},{4,7},{5,6},{6,5},{7,4},{8,11},{9,10},{10,... | collective-permute-start | bytes 24584 | tf_op jit(solution)/shard_map/ppermute | solution.py:629
  58.8 0.2 collective-permute-start.15
  59.0 2.4 %collective-permute-start.29 = (f32[8,32,128]{2,1,0:T(8,128)S(1)}, f32[8,32,128]{2,1,0:T(8,128)S(1)}, u32[]{:S(2)}, u32[]{:S(2)}) collective-permute-start(f32[8,32,128]{2,1,0:T(8,128)S(1)} %get-tuple-element.25.aq_ref.rest_11_), channel_id=1, source_target_pairs={{0,8},{1,9},{2,10},{3,11},{4,12},{5,13},{6,14},{7,15},{8,0},{9,1},... | collective-permute-start | bytes 393224 | tf_op jit(solution)/shard_map/ppermute | solution.py:685
  61.4 1.9 %collective-permute-start.24 = (f32[16,128]{1,0:T(8,128)S(1)}, f32[16,128]{1,0:T(8,128)S(1)}, u32[]{:S(2)}, u32[]{:S(2)}) collective-permute-start(f32[16,128]{1,0:T(8,128)S(1)} %add_add_fusion.rest_0_), channel_id=1, source_target_pairs={{0,4},{1,5},{2,6},{3,7},{4,0},{5,1},{6,2},{7,3},{8,12},{9,13},{10,... | collective-permute-start | bytes 24584 | tf_op jit(solution)/shard_map/ppermute | solution.py:629
  63.3 1.8 %collective-permute-start.25 = (f32[16,128]{1,0:T(8,128)S(1)}, f32[16,128]{1,0:T(8,128)S(1)}, u32[]{:S(2)}, u32[]{:S(2)}) collective-permute-start(f32[16,128]{1,0:T(8,128)S(1)} %add_add_fusion.rest_0_), channel_id=1, source_target_pairs={{0,8},{1,9},{2,10},{3,11},{4,12},{5,13},{6,14},{7,15},{8,0},{9,1},... | collective-permute-start | bytes 24584 | tf_op jit(solution)/shard_map/ppermute | solution.py:629
  65.1 1.2 %collective-permute-start.26 = (f32[16,128]{1,0:T(8,128)S(1)}, f32[16,128]{1,0:T(8,128)S(1)}, u32[]{:S(2)}, u32[]{:S(2)}) collective-permute-start(f32[16,128]{1,0:T(8,128)S(1)} %add_add_fusion.rest_0_), channel_id=1, source_target_pairs={{0,12},{1,13},{2,14},{3,15},{4,8},{5,9},{6,10},{7,11},{8,4},{9,5},... | collective-permute-start | bytes 24584 | tf_op jit(solution)/shard_map/ppermute | solution.py:629
  66.4 0.5 collective-permute-start.18
  66.9 2.1 %collective-permute-done.29.rest_14_ = f32[8,32,128]{2,1,0:T(8,128)S(1)} collective-permute-done((f32[8,32,128]{2,1,0:T(8,128)S(1)}, f32[8,32,128]{2,1,0:T(8,128)S(1)}, u32[]{:S(2)}, u32[]{:S(2)}) %collective-permute-start.29) | collective-permute-done | bytes 131104 | tf_op jit(solution)/shard_map/ppermute | solution.py:685
  69.0 0.6 collective-permute-start.19
  69.6 1.9 %collective-permute-start.20 = (f32[16,128]{1,0:T(8,128)S(1)}, f32[16,128]{1,0:T(8,128)S(1)}, u32[]{:S(2)}, u32[]{:S(2)}) collective-permute-start(f32[16,128]{1,0:T(8,128)S(1)} %add_add_fusion.1.rest_0_), channel_id=1, source_target_pairs={{0,12},{1,13},{2,14},{3,15},{4,8},{5,9},{6,10},{7,11},{8,4},{9,5},... | collective-permute-start | bytes 24584 | tf_op jit(solution)/shard_map/ppermute | solution.py:629
  71.5 6.6 %gradient.1 = f32[1,30,8100]{2,1,0:T(8,128)S(1)} custom-call(s32[1]{0:T(128)} %bitcast.me_ref, s32[1,4]{1,0:T(1,128)S(1)} %copy-done.3, s32[1,4]{1,0:T(1,128)S(1)} %copy-done.4, f32[16,128]{1,0:T(8,128)S(1)} %add_add_fusion.rest_0_, f32[16,128]{1,0:T(8,128)S(1)} %collective-permute-done.24.rest_1_, f32[16,128]{1,0:T(8,128)S(1)} %collective-permute-done.25.rest_2_, ...), custom_call_target="tpu_custom_call" | custom-call | flops 10000000 | bytes 4000000 | tf_op jit(solution)/shard_map/gradient/pallas_call | solution.py:662
  78.1 2.0 %copy.14 = f32[1,30,8100]{2,0,1:T(1,128)} copy(f32[1,30,8100]{2,1,0:T(8,128)S(1)} %gradient.1) | data formatting | bytes 1944000
  80.1 0.8 %height.1 = f32[1,8100]{1,0:T(1,128)} custom-call(f32[16,128]{1,0:T(8,128)S(1)} %add_add_fusion.1.rest_0_, f32[16,128]{1,0:T(8,128)S(1)} %collective-permute-done.18.rest_1_, f32[16,128]{1,0:T(8,128)S(1)} %collective-permute-done.19.rest_2_, f32[16,128]{1,0:T(8,128)S(1)} %collective-permute-done.20.rest_3_, f32[64,128]{1,0:T(8,128)S(1)} %get-tuple-element.26.b_ref.rest_4_, ...), custom_call_target="tpu_custom_call" | custom-call | flops 1000000 | bytes 1000000 | tf_op jit(solution)/shard_map/height/pallas_call | solution.py:662
  (48 shorter events, 0.1 us)
Async XLA Ops:
  0.6 1.9 %copy-start.3 = (s32[1,4]{1,0:T(1,128)S(1)}, s32[1,4]{1,0:T(1,128)}, u32[]{:S(2)}) copy-start(s32[1,4]{1,0:T(1,128)} %adj_ref.5) | copy-start | bytes 52
  0.6 1.9 %copy-start.4 = (s32[1,4]{1,0:T(1,128)S(1)}, s32[1,4]{1,0:T(1,128)}, u32[]{:S(2)}) copy-start(s32[1,4]{1,0:T(1,128)} %flag_ref.5) | copy-start | bytes 52
  0.7 1.9 %copy-start = (s32[1,8100]{1,0:T(1,128)S(1)}, s32[1,8100]{1,0:T(1,128)}, u32[]{:S(2)}) copy-start(s32[1,8100]{1,0:T(1,128)} %depth_ref.1) | copy-start | bytes 97204
  0.7 1.9 %copy-start.1 = (f32[1,8100]{1,0:T(1,128)S(1)}, f32[1,8100]{1,0:T(1,128)}, u32[]{:S(2)}) copy-start(f32[1,8100]{1,0:T(1,128)} %d_ref.1) | copy-start | bytes 97204
  0.7 1.9 %copy-start.2 = (f32[1,8100]{1,0:T(1,128)S(1)}, f32[1,8100]{1,0:T(1,128)}, u32[]{:S(2)}) copy-start(f32[1,8100]{1,0:T(1,128)} %b_ref.1) | copy-start | bytes 97204
  2.5 12.1 %copy-start.5 = (f32[1,30,8100]{2,0,1:T(1,128)S(1)}, f32[1,30,8100]{2,0,1:T(1,128)}, u32[]{:S(2)}) copy-start(f32[1,30,8100]{2,0,1:T(1,128)} %param.9) | copy-start | bytes 2916004
  3.5 26.1 %collective-permute-start = (f32[4,32,128]{2,1,0:T(8,128)S(1)}, f32[4,32,128]{2,1,0:T(8,128)S(1)}, u32[]{:S(2)}, u32[]{:S(2)}) collective-permute-start(f32[4,32,128]{2,1,0:T(8,128)S(1)} %get-tuple-element.24.ts_ref), channel_id=1, source_target_pairs={{0,1},{1,2},{2,3},{3,4},{4,5},{5,6},{6,7},{7,8},{8,9},{9,10},{10,1... | collective-permute-start | bytes 196616 | tf_op jit(solution)/shard_map/ppermute | solution.py:685
  5.8 26.2 %collective-permute-start.1 = (f32[4,32,128]{2,1,0:T(8,128)S(1)}, f32[4,32,128]{2,1,0:T(8,128)S(1)}, u32[]{:S(2)}, u32[]{:S(2)}) collective-permute-start(f32[4,32,128]{2,1,0:T(8,128)S(1)} %get-tuple-element.24.ts_ref), channel_id=1, source_target_pairs={{1,0},{2,1},{3,2},{4,3},{5,4},{6,5},{7,6},{8,7},{9,8},{10,9},{11,1... | collective-permute-start | bytes 196616 | tf_op jit(solution)/shard_map/ppermute | solution.py:685
  7.1 24.9 %collective-permute-start.2 = (f32[4,32,128]{2,1,0:T(8,128)S(1)}, f32[4,32,128]{2,1,0:T(8,128)S(1)}, u32[]{:S(2)}, u32[]{:S(2)}) collective-permute-start(f32[4,32,128]{2,1,0:T(8,128)S(1)} %get-tuple-element.24.ts_ref), channel_id=1, source_target_pairs={{0,8},{1,9},{2,10},{3,11},{4,12},{5,13},{6,14},{7,15},{8,0},{9,1},... | collective-permute-start | bytes 196616 | tf_op jit(solution)/shard_map/ppermute | solution.py:685
  14.0 10.2 %collective-permute-start.3 = (f32[72,128]{1,0:T(8,128)S(1)}, f32[72,128]{1,0:T(8,128)S(1)}, u32[]{:S(2)}, u32[]{:S(2)}) collective-permute-start(f32[72,128]{1,0:T(8,128)S(1)} %get-tuple-element.27.rest_0_.rest_7_), channel_id=1, source_target_pairs={{0,1},{1,0},{2,3},{3,2},{4,5},{5,4},{6,7},{7,6},{8,9},{9,8},{10,11... | collective-permute-start | bytes 110600 | tf_op jit(solution)/shard_map/ppermute | solution.py:629
  14.0 11.5 %collective-permute-start.4 = (f32[72,128]{1,0:T(8,128)S(1)}, f32[72,128]{1,0:T(8,128)S(1)}, u32[]{:S(2)}, u32[]{:S(2)}) collective-permute-start(f32[72,128]{1,0:T(8,128)S(1)} %get-tuple-element.27.rest_0_.rest_7_), channel_id=1, source_target_pairs={{0,2},{1,3},{2,0},{3,1},{4,6},{5,7},{6,4},{7,5},{8,10},{9,11},{10,... | collective-permute-start | bytes 110600 | tf_op jit(solution)/shard_map/ppermute | solution.py:629
  14.7 1.2 %copy-start.6 = (f32[1,30,8100]{2,0,1:T(1,128)S(1)}, f32[1,30,8100]{2,0,1:T(1,128)}, u32[]{:S(2)}) copy-start(f32[1,30,8100]{2,0,1:T(1,128)} %param.14) | copy-start | bytes 2916004
  24.2 3.4 %collective-permute-start.5 = (f32[72,128]{1,0:T(8,128)S(1)}, f32[72,128]{1,0:T(8,128)S(1)}, u32[]{:S(2)}, u32[]{:S(2)}) collective-permute-start(f32[72,128]{1,0:T(8,128)S(1)} %get-tuple-element.27.rest_0_.rest_7_), channel_id=1, source_target_pairs={{0,3},{1,2},{2,1},{3,0},{4,7},{5,6},{6,5},{7,4},{8,11},{9,10},{10,... | collective-permute-start | bytes 110600 | tf_op jit(solution)/shard_map/ppermute | solution.py:629
  27.7 11.8 %collective-permute-start.6 = (f32[288,128]{1,0:T(8,128)S(1)}, f32[288,128]{1,0:T(8,128)S(1)}, u32[]{:S(2)}, u32[]{:S(2)}) collective-permute-start(f32[288,128]{1,0:T(8,128)S(1)} %constant_dynamic-update-slice_fusion), channel_id=1, source_target_pairs={{0,4},{1,5},{2,6},{3,7},{4,0},{5,1},{6,2},{7,3},{8,12},{9,13},{10,... | collective-permute-start | bytes 442376 | tf_op jit(solution)/shard_map/ppermute | solution.py:629
  29.2 13.4 %collective-permute-start.7 = (f32[288,128]{1,0:T(8,128)S(1)}, f32[288,128]{1,0:T(8,128)S(1)}, u32[]{:S(2)}, u32[]{:S(2)}) collective-permute-start(f32[288,128]{1,0:T(8,128)S(1)} %constant_dynamic-update-slice_fusion), channel_id=1, source_target_pairs={{0,8},{1,9},{2,10},{3,11},{4,12},{5,13},{6,14},{7,15},{8,0},{9,1},... | collective-permute-start | bytes 442376 | tf_op jit(solution)/shard_map/ppermute | solution.py:629
  29.6 13.1 %collective-permute-start.8 = (f32[288,128]{1,0:T(8,128)S(1)}, f32[288,128]{1,0:T(8,128)S(1)}, u32[]{:S(2)}, u32[]{:S(2)}) collective-permute-start(f32[288,128]{1,0:T(8,128)S(1)} %constant_dynamic-update-slice_fusion), channel_id=1, source_target_pairs={{0,12},{1,13},{2,14},{3,15},{4,8},{5,9},{6,10},{7,11},{8,4},{9,5},... | collective-permute-start | bytes 442376 | tf_op jit(solution)/shard_map/ppermute | solution.py:629
  32.9 1.6 %collective-permute-start.9 = (f32[16,128]{1,0:T(8,128)S(1)}, f32[16,128]{1,0:T(8,128)S(1)}, u32[]{:S(2)}, u32[]{:S(2)}) collective-permute-start(f32[16,128]{1,0:T(8,128)S(1)} %get-tuple-element.33.rest_0_), channel_id=1, source_target_pairs={{0,1},{1,0},{2,3},{3,2},{4,5},{5,4},{6,7},{7,6},{8,9},{9,8},{10,11... | collective-permute-start | bytes 24584 | tf_op jit(solution)/shard_map/ppermute | solution.py:629
  33.0 3.7 %collective-permute-start.10 = (f32[16,128]{1,0:T(8,128)S(1)}, f32[16,128]{1,0:T(8,128)S(1)}, u32[]{:S(2)}, u32[]{:S(2)}) collective-permute-start(f32[16,128]{1,0:T(8,128)S(1)} %get-tuple-element.33.rest_0_), channel_id=1, source_target_pairs={{0,2},{1,3},{2,0},{3,1},{4,6},{5,7},{6,4},{7,5},{8,10},{9,11},{10,... | collective-permute-start | bytes 24584 | tf_op jit(solution)/shard_map/ppermute | solution.py:629
  34.5 3.1 %collective-permute-start.11 = (f32[16,128]{1,0:T(8,128)S(1)}, f32[16,128]{1,0:T(8,128)S(1)}, u32[]{:S(2)}, u32[]{:S(2)}) collective-permute-start(f32[16,128]{1,0:T(8,128)S(1)} %get-tuple-element.33.rest_0_), channel_id=1, source_target_pairs={{0,3},{1,2},{2,1},{3,0},{4,7},{5,6},{6,5},{7,4},{8,11},{9,10},{10,... | collective-permute-start | bytes 24584 | tf_op jit(solution)/shard_map/ppermute | solution.py:629
  37.6 9.0 %collective-permute-start.12 = (f32[64,128]{1,0:T(8,128)S(1)}, f32[64,128]{1,0:T(8,128)S(1)}, u32[]{:S(2)}, u32[]{:S(2)}) collective-permute-start(f32[64,128]{1,0:T(8,128)S(1)} %constant_dynamic-update-slice_fusion.4), channel_id=1, source_target_pairs={{0,4},{1,5},{2,6},{3,7},{4,0},{5,1},{6,2},{7,3},{8,12},{9,13},{10,... | collective-permute-start | bytes 98312 | tf_op jit(solution)/shard_map/ppermute | solution.py:629
  38.2 9.5 %collective-permute-start.13 = (f32[64,128]{1,0:T(8,128)S(1)}, f32[64,128]{1,0:T(8,128)S(1)}, u32[]{:S(2)}, u32[]{:S(2)}) collective-permute-start(f32[64,128]{1,0:T(8,128)S(1)} %constant_dynamic-update-slice_fusion.4), channel_id=1, source_target_pairs={{0,8},{1,9},{2,10},{3,11},{4,12},{5,13},{6,14},{7,15},{8,0},{9,1},... | collective-permute-start | bytes 98312 | tf_op jit(solution)/shard_map/ppermute | solution.py:629
  39.5 9.6 %collective-permute-start.14 = (f32[64,128]{1,0:T(8,128)S(1)}, f32[64,128]{1,0:T(8,128)S(1)}, u32[]{:S(2)}, u32[]{:S(2)}) collective-permute-start(f32[64,128]{1,0:T(8,128)S(1)} %constant_dynamic-update-slice_fusion.4), channel_id=1, source_target_pairs={{0,12},{1,13},{2,14},{3,15},{4,8},{5,9},{6,10},{7,11},{8,4},{9,5},... | collective-permute-start | bytes 98312 | tf_op jit(solution)/shard_map/ppermute | solution.py:629
  44.7 7.7 %collective-permute-start.23 = (f32[16,128]{1,0:T(8,128)S(1)}, f32[16,128]{1,0:T(8,128)S(1)}, u32[]{:S(2)}, u32[]{:S(2)}) collective-permute-start(f32[16,128]{1,0:T(8,128)S(1)} %get-tuple-element.36), channel_id=1, source_target_pairs={{0,3},{1,2},{2,1},{3,0},{4,7},{5,6},{6,5},{7,4},{8,11},{9,10},{10,... | collective-permute-start | bytes 24584 | tf_op jit(solution)/shard_map/ppermute | solution.py:629
  44.9 14.0 %collective-permute-start.22 = (f32[16,128]{1,0:T(8,128)S(1)}, f32[16,128]{1,0:T(8,128)S(1)}, u32[]{:S(2)}, u32[]{:S(2)}) collective-permute-start(f32[16,128]{1,0:T(8,128)S(1)} %get-tuple-element.36), channel_id=1, source_target_pairs={{0,2},{1,3},{2,0},{3,1},{4,6},{5,7},{6,4},{7,5},{8,10},{9,11},{10,... | collective-permute-start | bytes 24584 | tf_op jit(solution)/shard_map/ppermute | solution.py:629
  46.6 12.2 %collective-permute-start.21 = (f32[16,128]{1,0:T(8,128)S(1)}, f32[16,128]{1,0:T(8,128)S(1)}, u32[]{:S(2)}, u32[]{:S(2)}) collective-permute-start(f32[16,128]{1,0:T(8,128)S(1)} %get-tuple-element.36), channel_id=1, source_target_pairs={{0,1},{1,0},{2,3},{3,2},{4,5},{5,4},{6,7},{7,6},{8,9},{9,8},{10,11... | collective-permute-start | bytes 24584 | tf_op jit(solution)/shard_map/ppermute | solution.py:629
  47.8 11.2 %collective-permute-start.27 = (f32[8,32,128]{2,1,0:T(8,128)S(1)}, f32[8,32,128]{2,1,0:T(8,128)S(1)}, u32[]{:S(2)}, u32[]{:S(2)}) collective-permute-start(f32[8,32,128]{2,1,0:T(8,128)S(1)} %get-tuple-element.25.aq_ref.rest_11_), channel_id=1, source_target_pairs={{0,1},{1,2},{2,3},{3,4},{4,5},{5,6},{6,7},{7,8},{8,9},{9,10},{10,1... | collective-permute-start | bytes 393224 | tf_op jit(solution)/shard_map/ppermute | solution.py:685
  49.1 17.3 %collective-permute-start.28 = (f32[8,32,128]{2,1,0:T(8,128)S(1)}, f32[8,32,128]{2,1,0:T(8,128)S(1)}, u32[]{:S(2)}, u32[]{:S(2)}) collective-permute-start(f32[8,32,128]{2,1,0:T(8,128)S(1)} %get-tuple-element.25.aq_ref.rest_11_), channel_id=1, source_target_pairs={{1,0},{2,1},{3,2},{4,3},{5,4},{6,5},{7,6},{8,7},{9,8},{10,9},{11,1... | collective-permute-start | bytes 393224 | tf_op jit(solution)/shard_map/ppermute | solution.py:685
  52.4 9.1 %collective-permute-start.17 = (f32[16,128]{1,0:T(8,128)S(1)}, f32[16,128]{1,0:T(8,128)S(1)}, u32[]{:S(2)}, u32[]{:S(2)}) collective-permute-start(f32[16,128]{1,0:T(8,128)S(1)} %get-tuple-element.34), channel_id=1, source_target_pairs={{0,3},{1,2},{2,1},{3,0},{4,7},{5,6},{6,5},{7,4},{8,11},{9,10},{10,... | collective-permute-start | bytes 24584 | tf_op jit(solution)/shard_map/ppermute | solution.py:629
  58.8 4.5 %collective-permute-start.16 = (f32[16,128]{1,0:T(8,128)S(1)}, f32[16,128]{1,0:T(8,128)S(1)}, u32[]{:S(2)}, u32[]{:S(2)}) collective-permute-start(f32[16,128]{1,0:T(8,128)S(1)} %get-tuple-element.34), channel_id=1, source_target_pairs={{0,2},{1,3},{2,0},{3,1},{4,6},{5,7},{6,4},{7,5},{8,10},{9,11},{10,... | collective-permute-start | bytes 24584 | tf_op jit(solution)/shard_map/ppermute | solution.py:629
  58.8 6.3 %collective-permute-start.15 = (f32[16,128]{1,0:T(8,128)S(1)}, f32[16,128]{1,0:T(8,128)S(1)}, u32[]{:S(2)}, u32[]{:S(2)}) collective-permute-start(f32[16,128]{1,0:T(8,128)S(1)} %get-tuple-element.34), channel_id=1, source_target_pairs={{0,1},{1,0},{2,3},{3,2},{4,5},{5,4},{6,7},{7,6},{8,9},{9,8},{10,11... | collective-permute-start | bytes 24584 | tf_op jit(solution)/shard_map/ppermute | solution.py:629
  59.0 10.0 %collective-permute-start.29 = (f32[8,32,128]{2,1,0:T(8,128)S(1)}, f32[8,32,128]{2,1,0:T(8,128)S(1)}, u32[]{:S(2)}, u32[]{:S(2)}) collective-permute-start(f32[8,32,128]{2,1,0:T(8,128)S(1)} %get-tuple-element.25.aq_ref.rest_11_), channel_id=1, source_target_pairs={{0,8},{1,9},{2,10},{3,11},{4,12},{5,13},{6,14},{7,15},{8,0},{9,1},... | collective-permute-start | bytes 393224 | tf_op jit(solution)/shard_map/ppermute | solution.py:685
  61.4 8.2 %collective-permute-start.24 = (f32[16,128]{1,0:T(8,128)S(1)}, f32[16,128]{1,0:T(8,128)S(1)}, u32[]{:S(2)}, u32[]{:S(2)}) collective-permute-start(f32[16,128]{1,0:T(8,128)S(1)} %add_add_fusion.rest_0_), channel_id=1, source_target_pairs={{0,4},{1,5},{2,6},{3,7},{4,0},{5,1},{6,2},{7,3},{8,12},{9,13},{10,... | collective-permute-start | bytes 24584 | tf_op jit(solution)/shard_map/ppermute | solution.py:629
  63.3 8.2 %collective-permute-start.25 = (f32[16,128]{1,0:T(8,128)S(1)}, f32[16,128]{1,0:T(8,128)S(1)}, u32[]{:S(2)}, u32[]{:S(2)}) collective-permute-start(f32[16,128]{1,0:T(8,128)S(1)} %add_add_fusion.rest_0_), channel_id=1, source_target_pairs={{0,8},{1,9},{2,10},{3,11},{4,12},{5,13},{6,14},{7,15},{8,0},{9,1},... | collective-permute-start | bytes 24584 | tf_op jit(solution)/shard_map/ppermute | solution.py:629
  65.1 6.4 %collective-permute-start.26 = (f32[16,128]{1,0:T(8,128)S(1)}, f32[16,128]{1,0:T(8,128)S(1)}, u32[]{:S(2)}, u32[]{:S(2)}) collective-permute-start(f32[16,128]{1,0:T(8,128)S(1)} %add_add_fusion.rest_0_), channel_id=1, source_target_pairs={{0,12},{1,13},{2,14},{3,15},{4,8},{5,9},{6,10},{7,11},{8,4},{9,5},... | collective-permute-start | bytes 24584 | tf_op jit(solution)/shard_map/ppermute | solution.py:629
  66.4 13.7 %collective-permute-start.18 = (f32[16,128]{1,0:T(8,128)S(1)}, f32[16,128]{1,0:T(8,128)S(1)}, u32[]{:S(2)}, u32[]{:S(2)}) collective-permute-start(f32[16,128]{1,0:T(8,128)S(1)} %add_add_fusion.1.rest_0_), channel_id=1, source_target_pairs={{0,4},{1,5},{2,6},{3,7},{4,0},{5,1},{6,2},{7,3},{8,12},{9,13},{10,... | collective-permute-start | bytes 24584 | tf_op jit(solution)/shard_map/ppermute | solution.py:629
  69.0 11.1 %collective-permute-start.19 = (f32[16,128]{1,0:T(8,128)S(1)}, f32[16,128]{1,0:T(8,128)S(1)}, u32[]{:S(2)}, u32[]{:S(2)}) collective-permute-start(f32[16,128]{1,0:T(8,128)S(1)} %add_add_fusion.1.rest_0_), channel_id=1, source_target_pairs={{0,8},{1,9},{2,10},{3,11},{4,12},{5,13},{6,14},{7,15},{8,0},{9,1},... | collective-permute-start | bytes 24584 | tf_op jit(solution)/shard_map/ppermute | solution.py:629
  69.6 10.5 %collective-permute-start.20 = (f32[16,128]{1,0:T(8,128)S(1)}, f32[16,128]{1,0:T(8,128)S(1)}, u32[]{:S(2)}, u32[]{:S(2)}) collective-permute-start(f32[16,128]{1,0:T(8,128)S(1)} %add_add_fusion.1.rest_0_), channel_id=1, source_target_pairs={{0,12},{1,13},{2,14},{3,15},{4,8},{5,9},{6,10},{7,11},{8,4},{9,5},... | collective-permute-start | bytes 24584 | tf_op jit(solution)/shard_map/ppermute | solution.py:629

commit v2 on v1

--- a/solution.py
+++ b/solution.py
@@ -16,7 +16,7 @@
 ROW_TILES = 8
 SPREAD = 0.2
 CENTRE = 4.1
-BLOCK = 72
+BLOCK = 88
 F32 = jnp.float32
 I32 = jnp.int32
 
@@ -148,93 +148,81 @@
         out_ref[at + 3 : at + 4, :] = side3[depth : depth + 1]
 
 
-def tail_row(ref, rows):
-    window = ref[rows, CELLS - LANES : CELLS]
-    return pltpu.roll(window, CELLS - (ROWS - 1) * LANES, 1)
-
-
-def edges_kernel(adj_ref, flag_ref, t_ref, depth_ref, d_ref, b_ref, ts_ref, blk_ref, dense_ref, z_ref):
+def level_rows(ref, level):
+    whole = (CELLS // LANES // 8) * 8
+    rows = CELLS // LANES
+    window = ref[level, :, CELLS - LANES : CELLS]
+    return jnp.concatenate(
+        [
+            ref[level, :, 0 : whole * LANES].reshape(whole, LANES),
+            ref[level, :, whole * LANES : rows * LANES].reshape(rows - whole, LANES),
+            pltpu.roll(window, CELLS - rows * LANES, 1),
+        ],
+        axis=0,
+    )
+
+
+def surface_rows(ref):
+    whole = (CELLS // LANES // 8) * 8
+    rows = CELLS // LANES
+    window = ref[:, CELLS - LANES : CELLS]
+    return jnp.concatenate(
+        [
+            ref[:, 0 : whole * LANES].reshape(whole, LANES),
+            ref[:, whole * LANES : rows * LANES].reshape(rows - whole, LANES),
+            pltpu.roll(window, CELLS - rows * LANES, 1),
+        ],
+        axis=0,
+    )
+
+
+def interior_reach(depth):
+    row, lane, cell, i, j = grid_iotas()
+    zero = jnp.zeros_like(depth)
+    along = jnp.where(j < SIDE - 1, jnp.minimum(depth, ahead(depth, 1)), zero)
+    across = jnp.where(cell < CELLS - SIDE, jnp.minimum(depth, ahead(depth, SIDE)), zero)
+    return along, across
+
+
+def interior_spread(x, along, across, level):
+    zero = jnp.zeros_like(x)
+    flux1 = jnp.where(along > level, ahead(x, 1) - x, zero)
+    flux2 = jnp.where(across > level, ahead(x, SIDE) - x, zero)
+    return (flux1 - behind(flux1, 1)) + (flux2 - behind(flux2, SIDE))
+
+
+def columns_kernel(
+    levels,
+    adj_ref,
+    flag_ref,
+    k_ref,
+    s_ref,
+    t_ref,
+    depth_ref,
+    d_ref,
+    b_ref,
+    a_ref,
+    q_ref,
+    f_ref,
+    ts_ref,
+    aq_ref,
+    blk_ref,
+    dense_ref,
+    g_ref,
+    z_ref,
+):
     row, lane, cell, i, j = grid_iotas()
     inside = cell < CELLS
     for number, ref in enumerate((b_ref, d_ref, depth_ref)):
-        base = number * ROWS
-        for l in range(ROWS - 1):
-            dense_ref[base + l : base + l + 1, :] = ref[:, l * LANES : (l + 1) * LANES].astype(F32)
-        dense_ref[base + ROWS - 1 : base + ROWS, :] = tail_row(ref, slice(0, 1)).astype(F32)
-        dense_ref[base : base + ROWS, :] = jnp.where(inside, dense_ref[base : base + ROWS, :], 0.0)
-        write_frames(dense_ref, base, blk_ref, number * 16, z_ref.at[0], z_ref.at[1])
+        rows = slice(number * ROWS, (number + 1) * ROWS)
+        dense_ref[rows, :] = jnp.where(inside, surface_rows(ref).astype(F32), 0.0)
+        write_frames(dense_ref, number * ROWS, blk_ref, number * 16, z_ref.at[0], z_ref.at[1])
     at = 48
     for sides in ((0, 1, 2, 3), (2, 2, 0, 0), (3, 3, 1, 1)):
         for ref in (adj_ref, flag_ref):
             for side in sides:
                 blk_ref[at : at + 1, :] = jnp.full((1, LANES), ref[0, side], I32).astype(F32)
                 at += 1
-    levels = t_ref.shape[1]
-    for first in range(0, levels, 8):
-        size = min(8, levels - first)
-        lane8 = lax.broadcasted_iota(I32, (size, LANES), 1)
-        odd = lane8 & 1
-        owner = column_owner(lane8)
-        la = (SIDE * owner + 89 * odd) >> 7
-        lb = jnp.where(owner + 64 < SIDE, (SIDE * (owner + 64) + 89 * odd) >> 7, -1)
-        za = jnp.zeros((size, LANES), F32)
-        zb = za
-        for l in range(ROWS):
-            if l < ROWS - 1:
-                x = t_ref[0, first : first + size, l * LANES : (l + 1) * LANES]
-            else:
-                x = pltpu.roll(
-                    t_ref[0, first : first + size, CELLS - LANES : CELLS], CELLS - (ROWS - 1) * LANES, 1
-                )
-            if l <= (SIDE * 63 + 89) // LANES:
-                za = jnp.where(la == l, x, za)
-            if l >= (SIDE * 64) // LANES:
-                zb = jnp.where(lb == l, x, zb)
-        z_ref[0, first : first + size, :] = za
-        z_ref[1, first : first + size, :] = zb
-        ts_ref[0, first : first + size, :] = t_ref[0, first : first + size, 0:LANES]
-        window = t_ref[0, first : first + size, CELLS - LANES : CELLS]
-        ts_ref[1, first : first + size, :] = pltpu.roll(window, SIDE, 1)
-    side2, side3 = lines_23(z_ref[0], z_ref[1], 0)
-    ts_ref[2] = side2
-    ts_ref[3] = side3
-    for side in range(4):
-        ts_ref[side, levels : levels + 1, :] = blk_ref[32 + side : 33 + side, :]
-        ts_ref[side, levels + 1 : levels + 2, :] = jnp.zeros((1, LANES), F32)
-
-
-def to_dense(src_ref, dst_ref, levels):
-    for first in range(0, levels, 8):
-        size = min(8, levels - first)
-        for l in range(ROWS):
-            if l < ROWS - 1:
-                x = src_ref[0, first : first + size, l * LANES : (l + 1) * LANES]
-            else:
-                x = pltpu.roll(
-                    src_ref[0, first : first + size, CELLS - LANES : CELLS], CELLS - (ROWS - 1) * LANES, 1
-                )
-            dst_ref[pl.ds(first * ROWS + l, size, stride=ROWS), :] = x
-
-
-def interior_reach(depth):
-    row, lane, cell, i, j = grid_iotas()
-    zero = jnp.zeros_like(depth)
-    along = jnp.where(j < SIDE - 1, jnp.minimum(depth, ahead(depth, 1)), zero)
-    across = jnp.where(cell < CELLS - SIDE, jnp.minimum(depth, ahead(depth, SIDE)), zero)
-    return along, across
-
-
-def interior_spread(x, along, across, level):
-    zero = jnp.zeros_like(x)
-    flux1 = jnp.where(along > level, ahead(x, 1) - x, zero)
-    flux2 = jnp.where(across > level, ahead(x, SIDE) - x, zero)
-    return (flux1 - behind(flux1, 1)) + (flux2 - behind(flux2, SIDE))
-
-
-def columns_kernel(levels, k_ref, s_ref, t_ref, dense_ref, a_ref, q_ref, f_ref, aq_ref, g_ref, v_ref, td_ref, z_ref):
-    to_dense(k_ref, g_ref, levels)
-    to_dense(s_ref, v_ref, levels)
-    to_dense(t_ref, td_ref, levels)
     depth = dense_ref[2 * ROWS : 3 * ROWS, :]
     along, across = interior_reach(depth)
     zero = jnp.zeros((ROWS, LANES), F32)
@@ -243,57 +231,62 @@
         link, below, va, vq = carry
         at = pl.ds(pl.multiple_of(level * ROWS, ROWS), ROWS)
         here = level.astype(F32)
-        r = jnp.where(depth > here + 1.0, g_ref[at, :], zero)
+        r = jnp.where(depth > here + 1.0, level_rows(k_ref, level), zero)
         wet = jnp.where(depth > here, 1.0, zero)
         upper = 1.0 + below
         inverse = 1.0 / (upper + r)
         ratio = r * inverse
-        va = (v_ref[at, :] + link * va) * inverse
+        va = (level_rows(s_ref, level) + link * va) * inverse
         vq = (wet + link * vq) * inverse
         g_ref[at, :] = ratio
-        v_ref[at, :] = va
+        a_ref[at, :] = va
         q_ref[at, :] = vq
         return r, upper * ratio, va, vq
 
-    lax.fori_loop(0, levels, down, (zero, zero, zero, zero))
-    row, lane, cell, i, j = grid_iotas()
-    column = (j == 0) | (j == SIDE - 1)
-    first = column & (i < 64)
-    second = column & (i >= 64) & (i < SIDE)
+    lax.fori_loop(0, levels, down, (zero, zero, zero, zero), unroll=2)
+    column = ((j == 0) | (j == SIDE - 1)) & (i < SIDE)
+    first = (column & (i < 64))[0:48]
+    second = (column & (i >= 64))[40:ROWS]
 
     def up(step, carry):
         xa, xq, total = carry
         level = levels - 1 - step
         at = pl.ds(pl.multiple_of(level * ROWS, ROWS), ROWS)
         ratio = g_ref[at, :]
-        xa = v_ref[at, :] + ratio * xa
+        xa = a_ref[at, :] + ratio * xa
         xq = q_ref[at, :] + ratio * xq
         a_ref[at, :] = xa
         q_ref[at, :] = xq
+        t = level_rows(t_ref, level)
         here = pl.ds(level, 1)
-        for number, x in enumerate((xa, xq)):
-            z_ref[number * 4, here, :] = jnp.sum(jnp.where(first, x, zero), axis=0, keepdims=True)
-            z_ref[number * 4 + 1, here, :] = jnp.sum(jnp.where(second, x, zero), axis=0, keepdims=True)
-            aq_ref[number * 4, here, :] = x[0:1]
-            z_ref[number * 4 + 2, here, :] = x[ROWS - 2 : ROWS - 1]
-            z_ref[number * 4 + 3, here, :] = x[ROWS - 1 : ROWS]
-        t = td_ref[at, :]
+        for number, x in enumerate((t, xa, xq)):
+            base = number * 4
+            z_ref[base, here, :] = jnp.sum(jnp.where(first, x[0:48], 0.0), axis=0, keepdims=True)
+            z_ref[base + 1, here, :] = jnp.sum(jnp.where(second, x[40:ROWS], 0.0), axis=0, keepdims=True)
+            out, side0 = (ts_ref, 0) if number == 0 else (aq_ref, (number - 1) * 4)
+            out[side0, here, :] = x[0:1]
+            z_ref[base + 2, here, :] = x[ROWS - 2 : ROWS - 1]
+            z_ref[base + 3, here, :] = x[ROWS - 1 : ROWS]
         mixed_h = t + SPREAD * interior_spread(t, along, across, level.astype(F32))
         return xa, xq, total + xq * mixed_h
 
-    xa, xq, total = lax.fori_loop(0, levels, up, (zero, zero, zero))
-    f_ref[...] = jnp.where(cell < CELLS, total, zero)
+    xa, xq, total = lax.fori_loop(0, levels, up, (zero, zero, zero), unroll=2)
+    f_ref[...] = jnp.where(inside, total, zero)
     spare = z_ref.shape[1] - levels
-    for number in range(2):
+    for number in range(3):
+        base = number * 4
+        out, at = (ts_ref, 0) if number == 0 else (aq_ref, (number - 1) * 4)
         for part in range(4):
-            z_ref[number * 4 + part, levels:, :] = jnp.zeros((spare, LANES), F32)
-        aq_ref[number * 4, levels:, :] = jnp.zeros((spare, LANES), F32)
-        side2, side3 = lines_23(z_ref[number * 4], z_ref[number * 4 + 1], 0)
-        aq_ref[number * 4 + 2] = side2
-        aq_ref[number * 4 + 3] = side3
-        low, high = z_ref[number * 4 + 2], z_ref[number * 4 + 3]
+            z_ref[base + part, levels:, :] = jnp.zeros((spare, LANES), F32)
+        out[at, levels:, :] = jnp.zeros((spare, LANES), F32)
+        side2, side3 = lines_23(z_ref[base], z_ref[base + 1], 0)
+        out[at + 2] = side2
+        out[at + 3] = side3
+        low, high = z_ref[base + 2], z_ref[base + 3]
         wide = lax.broadcasted_iota(I32, low.shape, 1)
-        aq_ref[number * 4 + 1] = jnp.where(wide < 54, pltpu.roll(low, 54, 1), pltpu.roll(high, 54, 1))
+        out[at + 1] = jnp.where(wide < 54, pltpu.roll(low, 54, 1), pltpu.roll(high, 54, 1))
+    for side in range(4):
+        ts_ref[side, levels : levels + 1, :] = blk_ref[32 + side : 33 + side, :]
 
 
 def pick(refs, shifts, tiles, me, neighbour, first, side_met):
@@ -309,7 +302,7 @@
     return jnp.where((flag & 1) == 1, SIDE - 1 - lane, lane) & 127
 
 
-def forcing_kernel(shifts, tiles, levels, me_ref, adj_ref, flag_ref, f_ref, ts_ref, aq_ref, *rest):
+def forcing_kernel(shifts, tiles, levels, me_ref, adj_ref, flag_ref, f_ref, ts_ref, aq_ref, blk_ref, *rest):
     refs = rest[: len(shifts)]
     out_ref, frame_ref, reach_ref, za_ref, zb_ref = rest[len(shifts) :]
     me = me_ref[0]
@@ -328,7 +321,8 @@
     reach_ref[4:8, :] = jnp.zeros((4, LANES), F32)
     seams = scatter_lines(scatter_masks(), jnp.concatenate(lines + lines, axis=0))
     out_ref[...] = (f_ref[...] + SPREAD * seams) * (1.0 / math.sqrt(levels))
-    write_frames(out_ref, 0, frame_ref, 0, za_ref, zb_ref)
+    frame_ref[0:72, :] = blk_ref[...]
+    write_frames(out_ref, 0, frame_ref, 72, za_ref, zb_ref)
 
 
 def block_rows(refs, counts, block, first, size):
@@ -360,9 +354,10 @@
     )
 
 
-def prepare_kernel(counts, lines, me_ref, dense_ref, *rest):
+def krylov_kernel(counts, lines, me_ref, dense_ref, forcing_ref, *rest):
     refs = rest[: len(counts)]
-    p_ref, index_ref, frame_ref, own_ref, seam_ref, work_ref, depth_ref, d_ref = rest[len(counts) :]
+    va_ref, vb_ref, line_ref, gram_ref = rest[len(counts) : len(counts) + 4]
+    p_ref, index_ref, frame_ref, work_ref, depth_ref, d_ref, x_ref = rest[len(counts) + 4 :]
     me = me_ref[0]
     for number in range(6):
         for position, rows in block_rows(refs, counts, BLOCK, 48 + 4 * number, 4):
@@ -408,73 +403,67 @@
         for number in range(4):
             frame_ref[depth, 1 + number] = masks[number]
         if depth == 0:
-            seam_ref[...] = masks[0][0:8]
+            seam = masks[0][0:8]
     surface = jnp.minimum(dense_ref[2 * ROWS : 3 * ROWS, :], 1.0)
     along, across = interior_reach(surface)
     degree = (along + behind(along, 1)) + (across + behind(across, SIDE))
-    degree = degree + scatter_lines(scatter_masks(), seam_ref[...])
-    own_ref[0] = dense_ref[ROWS : 2 * ROWS, :] + degree
-    own_ref[1] = along
-    own_ref[2] = across
-
-
-def krylov_kernel(
-    counts, block, lines, b_ref, p_ref, index_ref, frame_ref, own_ref, seam_ref, *rest
-):
-    refs = rest[: len(counts)]
-    v_ref, line_ref, gram_ref, x_ref = rest[len(counts) :]
-    for depth in range(4):
-        for position, rows in block_rows(refs, counts, block, 4 * depth, 4):
-            x_ref[depth, position * 4 : position * 4 + 4, :] = rows
+    masks = scatter_masks()
+    diagonal = dense_ref[ROWS : 2 * ROWS, :] + (degree + scatter_lines(masks, seam))
     p = p_ref[...]
     facing_at = index_ref[0:lines, :]
     low_parity = index_ref[lines : 2 * lines, :]
     high_parity = index_ref[2 * lines : 3 * lines, :]
     scale = 2.0 / CENTRE
-    masks = scatter_masks()
     row, lane, cell, i, j = grid_iotas()
     inside = cell < CELLS
-    diagonal, along, across = own_ref[0], own_ref[1], own_ref[2]
-    seam = seam_ref[...]
-    frames = [[x_ref[depth] for depth in range(4)]]
-    own = [b_ref[0:ROWS, :]]
+    frames = []
+    own = []
+    for solve, first in enumerate((0, 72)):
+        for depth in range(4):
+            for position, rows in block_rows(refs, counts, BLOCK, first + 4 * depth, 4):
+                x_ref[solve * 4 + depth, position * 4 : position * 4 + 4, :] = rows
+        frames.append([[x_ref[solve * 4 + depth] for depth in range(4)]])
+        own.append([(dense_ref if solve == 0 else forcing_ref)[0:ROWS, :]])
     for step in range(ITERS):
-        x = frames[-1]
-        met = gather_lines(p, x[0])
-        facing = take(met[0:lines], facing_at)
-        line_ref[step] = facing[0:8]
-        mine = own[-1]
-        flow = (along * ahead(mine, 1) + behind(along * mine, 1)) + (
-            across * ahead(mine, SIDE) + behind(across * mine, SIDE)
-        )
-        image = diagonal * mine - flow - scatter_lines(masks, seam * facing[0:8])
-        image = jnp.where(inside, scale * image - 2.0 * mine, 0.0)
-        own.append(0.5 * image if step == 0 else image - own[-2])
-        following = []
-        for depth in range(ITERS - 1 - step):
-            low, high = ends(
-                x[depth],
-                met[lines : 2 * lines],
-                met[2 * lines : 3 * lines],
-                low_parity,
-                high_parity,
-                depth,
+        for solve in range(2):
+            x = frames[solve][-1]
+            met = gather_lines(p, x[0])
+            facing = take(met[0:lines], facing_at)
+            if solve == 0:
+                line_ref[step] = facing[0:8]
+            mine = own[solve][-1]
+            flow = (along * ahead(mine, 1) + behind(along * mine, 1)) + (
+                across * ahead(mine, SIDE) + behind(across * mine, SIDE)
             )
-            before = facing if depth == 0 else x[depth - 1]
-            flow = (frame_ref[depth, 1] * before + frame_ref[depth, 2] * x[depth + 1]) + (
-                frame_ref[depth, 3] * low + frame_ref[depth, 4] * high
-            )
-            image = scale * (frame_ref[depth, 0] * x[depth] - flow) - 2.0 * x[depth]
-            following.append(0.5 * image if step == 0 else image - frames[-2][depth])
-        frames.append(following)
-        if step < ITERS - 1:
-            v_ref[step] = own[-1]
-    at = 0
-    for first in range(ITERS + 1):
-        for second in range(first + 1):
-            gram_ref[at : at + 1, :] = jnp.sum(own[first] * own[second], axis=0, keepdims=True)
-            at += 1
-    gram_ref[15:16, :] = jnp.zeros((1, LANES), F32)
+            image = diagonal * mine - flow - scatter_lines(masks, seam * facing[0:8])
+            image = jnp.where(inside, scale * image - 2.0 * mine, 0.0)
+            own[solve].append(0.5 * image if step == 0 else image - own[solve][-2])
+            following = []
+            for depth in range(ITERS - 1 - step):
+                low, high = ends(
+                    x[depth],
+                    met[lines : 2 * lines],
+                    met[2 * lines : 3 * lines],
+                    low_parity,
+                    high_parity,
+                    depth,
+                )
+                before = facing if depth == 0 else x[depth - 1]
+                flow = (frame_ref[depth, 1] * before + frame_ref[depth, 2] * x[depth + 1]) + (
+                    frame_ref[depth, 3] * low + frame_ref[depth, 4] * high
+                )
+                image = scale * (frame_ref[depth, 0] * x[depth] - flow) - 2.0 * x[depth]
+                following.append(0.5 * image if step == 0 else image - frames[solve][-2][depth])
+            frames[solve].append(following)
+            if step < ITERS - 1:
+                (vb_ref if solve == 0 else va_ref)[step] = own[solve][-1]
+    for solve in range(2):
+        at = 16 * solve
+        for first in range(ITERS + 1):
+            for second in range(first + 1):
+                gram_ref[at : at + 1, :] = jnp.sum(own[solve][first] * own[solve][second], axis=0, keepdims=True)
+                at += 1
+        gram_ref[at : at + 1, :] = jnp.zeros((1, LANES), F32)
 
 
 def image_of(p):
@@ -504,13 +493,15 @@
     return total
 
 
-def coefficients(refs, sum_ref):
+def total_gram(refs, sum_ref):
     total = refs[0][...]
     for ref in refs[1:]:
         total = total + ref[...]
-    sum_ref[...] = jnp.broadcast_to(jnp.sum(total, axis=1, keepdims=True), (16, LANES))
+    sum_ref[...] = jnp.broadcast_to(jnp.sum(total, axis=1, keepdims=True), sum_ref.shape)
+
+
+def coefficients(sum_ref, at):
     gram = []
-    at = 0
     for first in range(ITERS + 1):
         gram.append([sum_ref[at + second : at + second + 1, :] for second in range(first + 1)])
         at += first + 1
@@ -533,6 +524,12 @@
     return x
 
 
+def store_rows(ref, rows):
+    last = CELLS // LANES
+    ref[:, 0 : last * LANES] = rows[0:last].reshape(1, last * LANES)
+    ref[:, last * LANES : CELLS] = rows[last : last + 1, 0 : CELLS - last * LANES]
+
+
 def combine(x, b_ref, v_ref):
     out = x[0] * b_ref[0:ROWS, :]
     for number in range(1, ITERS):
@@ -543,17 +540,16 @@
 def gradient_kernel(shifts, tiles, levels, grams, me_ref, adj_ref, flag_ref, *rest):
     gram_refs = rest[:grams]
     rest = rest[grams:]
-    dense_ref, v_ref, line_ref, blk_ref, reach_ref, a_ref, q_ref, aq_ref = rest[:8]
-    refs = rest[8 : 8 + len(shifts)]
-    out_ref, sum_ref, w_ref, h_ref = rest[8 + len(shifts) :]
+    dense_ref, forcing_ref, va_ref, v_ref, line_ref, blk_ref, reach_ref, a_ref, q_ref, aq_ref = rest[:10]
+    refs = rest[10 : 10 + len(shifts)]
+    height_ref, out_ref, gram_ref, sum_ref, w_ref, h_ref = rest[10 + len(shifts) :]
     me = me_ref[0]
-    x = coefficients(gram_refs, sum_ref)
+    total_gram(gram_refs, gram_ref)
+    store_rows(height_ref, combine(coefficients(gram_ref, 16), forcing_ref, va_ref))
+    x = coefficients(gram_ref, 0)
     level_scale = 1.0 / math.sqrt(levels)
     adjoint = combine(x, dense_ref, v_ref) * level_scale
-    own_line = x[0] * blk_ref[0:8, :]
     met_line = x[0] * line_ref[0]
-    w_ref[4, 0:ROWS // 2, :] = jnp.zeros((ROWS // 2, LANES), F32)
-    own_sides = []
     depth = dense_ref[2 * ROWS : 3 * ROWS, :]
     along, across = interior_reach(depth)
     sum_ref[0:8, :] = met_line + x[1] * line_ref[1] + x[2] * line_ref[2] + x[3] * line_ref[3]
@@ -594,25 +590,10 @@
         spread = spread + scatter_rows(
             masks, w_ref[0, here, :], w_ref[1, here, :], w_ref[2, here, :], w_ref[3, here, :]
         )
-        h_ref[at, :] = h + SPREAD * spread
+        store_rows(out_ref.at[number], h + SPREAD * spread)
         return carry
 
-    lax.fori_loop(0, levels, per_level, 0)
-    for first in range(0, levels, 8):
-        size = min(8, levels - first)
-        for l in range(ROWS):
-            width = min(LANES, CELLS - l * LANES)
-            x_tile = h_ref[pl.ds(first * ROWS + l, size, stride=ROWS), :]
-            out_ref[0, first : first + size, l * LANES : l * LANES + width] = x_tile[:, 0:width]
-
-
-def height_kernel(grams, *rest):
-    gram_refs = rest[:grams]
-    b_ref, v_ref, out_ref, sum_ref, x_ref = rest[grams:]
-    x_ref[...] = combine(coefficients(gram_refs, sum_ref), b_ref, v_ref)
-    for l in range(ROWS):
-        width = min(LANES, CELLS - l * LANES)
-        out_ref[:, l * LANES : l * LANES + width] = x_ref[l : l + 1, 0:width]
+    lax.fori_loop(0, levels, per_level, 0, unroll=2)
 
 
 def rounds(tiles):
@@ -685,86 +666,88 @@
             out.append(lax.ppermute(x, "tile", pairs))
         return out
 
-    strips, block, dense = call(
-        edges_kernel,
-        (shape(4, 32, LANES), shape(BLOCK, LANES), shape(3 * ROWS, LANES)),
-        [pltpu.VMEM((2, 32, LANES), F32)],
+    def by_level(x):
+        return jnp.transpose(x, (1, 0, 2))
+
+    big = pltpu.VMEM((levels * ROWS, LANES), F32)
+    solved, weight, forcing_inside, strips, edge_lines, block, dense = call(
+        functools.partial(columns_kernel, levels),
+        (
+            shape(levels * ROWS, LANES),
+            shape(levels * ROWS, LANES),
+            shape(ROWS, LANES),
+            shape(4, 32, LANES),
+            shape(8, 32, LANES),
+            shape(72, LANES),
+            shape(3 * ROWS, LANES),
+        ),
+        [big, pltpu.VMEM((12, 32, LANES), F32)],
         (adjacent, flags),
-        (thermal, depth, main_entry, elevation),
-        "edges",
-    )
-    strips_met = to_neighbours(strips)
-    blocks, counts = gather_tiles(block, tiles)
-    big = pltpu.VMEM((levels * ROWS, LANES), F32)
-    solved, weight, forcing_inside, edge_lines = call(
-        functools.partial(columns_kernel, levels),
-        (shape(levels * ROWS, LANES), shape(levels * ROWS, LANES), shape(ROWS, LANES), shape(8, 32, LANES)),
-        [big, big, big, pltpu.VMEM((8, 32, LANES), F32)],
-        (),
-        (stirring, sensitivity, thermal, dense),
+        (by_level(stirring), by_level(sensitivity), by_level(thermal), depth, main_entry, elevation),
         "columns",
         2e7,
         8e6,
     )
-    edge_lines_met = to_neighbours(edge_lines)
-    forcing, forcing_frames, reach = call(
+    strips_met = to_neighbours(strips)
+    forcing, frames, reach = call(
         functools.partial(forcing_kernel, shifts, tiles, levels),
-        (shape(ROWS, LANES), shape(16, LANES), shape(8, LANES)),
+        (shape(ROWS, LANES), shape(BLOCK, LANES), shape(8, LANES)),
         [pltpu.VMEM((8, LANES), F32), pltpu.VMEM((8, LANES), F32)],
         (me, adjacent, flags),
-        (forcing_inside, strips, edge_lines, *strips_met),
+        (forcing_inside, strips, edge_lines, block, *strips_met),
         "forcing",
     )
-    forcing_blocks, _ = gather_tiles(forcing_frames, tiles)
+    blocks, counts = gather_tiles(frames, tiles)
+    edge_lines_met = to_neighbours(edge_lines)
     lines = 4 * tiles
     frame = pltpu.VMEM((4, lines, LANES), F32)
-    prepared = call(
-        functools.partial(prepare_kernel, counts, lines),
+    basis = shape(ITERS - 1, ROWS, LANES)
+    basis_a, basis_b, lines_b, gram = call(
+        functools.partial(krylov_kernel, counts, lines),
+        (basis, basis, shape(ITERS, 8, LANES), shape(32, LANES)),
+        [
+            pltpu.VMEM((3 * lines, lines), jnp.bfloat16),
+            pltpu.VMEM((3 * lines, LANES), I32),
+            pltpu.VMEM((3, 5, lines, LANES), F32),
+            pltpu.VMEM((6, lines, LANES), F32),
+            frame,
+            frame,
+            pltpu.VMEM((8, lines, LANES), F32),
+        ],
+        (me,),
+        (dense, forcing, *blocks),
+        "krylov",
+    )
+    grams = sum_tiles(gram, tiles)
+    height, gradient = call(
+        functools.partial(gradient_kernel, shifts, tiles, levels, len(grams)),
+        (jax.ShapeDtypeStruct(elevation.shape, F32), shape(levels, 1, CELLS)),
+        [
+            pltpu.VMEM((32, LANES), F32),
+            pltpu.VMEM((16, LANES), F32),
+            pltpu.VMEM((5, 32, LANES), F32),
+            pltpu.VMEM((ROWS, LANES), F32),
+        ],
+        (me, adjacent, flags),
         (
-            jax.ShapeDtypeStruct((3 * lines, lines), jnp.bfloat16),
-            jax.ShapeDtypeStruct((3 * lines, LANES), I32),
-            shape(3, 5, lines, LANES),
-            shape(3, ROWS, LANES),
-            shape(8, LANES),
+            *grams,
+            dense,
+            forcing,
+            basis_a,
+            basis_b,
+            lines_b,
+            block,
+            reach,
+            solved,
+            weight,
+            edge_lines,
+            *edge_lines_met,
         ),
-        [pltpu.VMEM((6, lines, LANES), F32), frame, frame],
-        (me,),
-        (dense, *blocks),
-        "prepare",
-    )
-
-    def krylov(rhs, rhs_blocks, rows, name):
-        return call(
-            functools.partial(krylov_kernel, counts, rows, lines),
-            (shape(ITERS - 1, ROWS, LANES), shape(ITERS, 8, LANES), shape(16, LANES)),
-            [frame],
-            (),
-            (rhs, *prepared, *rhs_blocks),
-            name,
-        )
-
-    basis_b, lines_b, gram_b = krylov(dense, blocks, BLOCK, "krylov_adjoint")
-    grams_b = sum_tiles(gram_b, tiles)
-    basis_a, _, gram_a = krylov(forcing, forcing_blocks, 16, "krylov_forward")
-    grams_a = sum_tiles(gram_a, tiles)
-    gradient = call(
-        functools.partial(gradient_kernel, shifts, tiles, levels, len(grams_b)),
-        jax.ShapeDtypeStruct(thermal.shape, F32),
-        [pltpu.VMEM((16, LANES), F32), pltpu.VMEM((5, 32, LANES), F32), big],
-        (me, adjacent, flags),
-        (*grams_b, dense, basis_b, lines_b, block, reach, solved, weight, edge_lines, *edge_lines_met),
         "gradient",
         1e7,
         4e6,
     )
-    height = call(
-        functools.partial(height_kernel, len(grams_a)),
-        jax.ShapeDtypeStruct(elevation.shape, F32),
-        [pltpu.VMEM((16, LANES), F32), pltpu.VMEM((ROWS, LANES), F32)],
-        (),
-        (*grams_a, forcing, basis_a),
-        "height",
-    )
+    gradient = by_level(gradient)
     return height, gradient
 
 

time: 81.2 us -> 74.9 us (0.922)
  starting transfers between devices: 45.1 us -> 27.4 us
  waiting for transfers between devices: 8.35 us -> 23.8 us
  Pallas kernels: 21 us -> 15.8 us
  local copies, waits for them, and re-layouts: 5.58 us -> 6.55 us
    ppermute x24 -> x12, waiting for transfers between devices: 6.22 us -> 22.6 us  [swap(): return lax.ppermute(x, 'tile', [(t, t ^ offset) for t in range(tiles)])]
    ppermute x24 -> x12, starting transfers between devices: 29.6 us -> 14.7 us  [swap(): return lax.ppermute(x, 'tile', [(t, t ^ offset) for t in range(tiles)])]
    pallas_call x8 -> x4, Pallas kernels: 21 us -> 15.8 us  [call(): pl.pallas_call(kernel, out_shape=outs, in_specs=[smem] * len(scalars) + [...]
    ppermute x6, starting transfers between devices: 15.6 us -> 12.7 us  [to_neighbours(): out.append(lax.ppermute(x, 'tile', pairs))]
    unnamed x24 -> x19, local copies, waits for them, and re-layouts: 5.57 us -> 6.54 us
    ppermute x6, waiting for transfers between devices: 2.13 us -> 1.27 us  [to_neighbours(): out.append(lax.ppermute(x, 'tile', pairs))]
  transfers between devices with their start and end apart: 30 -> 18, of which waited for: 6 -> 9; matrix products, arithmetic and copies ran while one was open for 4% -> 0% of each run, Pallas kernels for 24% -> 0%
where the time goes in v2:
time: 74.9 us; the launch traced here: 74.4 us
  starting transfers between devices  27.4 us (37%)
  waiting for transfers between devices  23.8 us (32%)
  Pallas kernels  15.8 us (21%)
  local copies, waits for them, and re-layouts  6.55 us (9%)
  between operations  0.78 us (1%)
    ppermute x12, waiting for transfers between devices, swap(): return lax.ppermute(x, 'tile', [(t, t ^ offset) for t in range(tiles)])  22.6 us
    pallas_call x4, Pallas kernels, call(): pl.pallas_call(kernel, out_shape=outs, in_specs=[smem] * len(scalars) + [...  15.8 us
    ppermute x12, starting transfers between devices, swap(): return lax.ppermute(x, 'tile', [(t, t ^ offset) for t in range(tiles)])  14.7 us
    ppermute x6, starting transfers between devices, to_neighbours(): out.append(lax.ppermute(x, 'tile', pairs))  12.7 us
    unnamed x19, local copies, waits for them, and re-layouts  6.54 us
  transfers between devices with their start and end apart: 18, of which 9 were waited for; matrix products, arithmetic and copies ran while one was open for 0% of the time, Pallas kernels for 0%

profile of v2, /device:TPU:0, one launch (start us, length us, event | category | flops | bytes accessed | tf_op | source)
XLA Modules:
  0.0 74.4 jit_solution(17627715332104098258)
XLA Ops:
  0.7 0.6 copy-done.6
  1.3 0.0 copy-done.7
  1.3 1.2 %copy-done = f32[1,30,8100]{2,0,1:T(1,128)S(1)} copy-done((f32[1,30,8100]{2,0,1:T(1,128)S(1)}, f32[1,30,8100]{2,0,1:T(1,128)}, u32[]{:S(2)}) %copy-start) | copy-done | bytes 972024
  2.5 1.2 %copy-done.1 = f32[1,30,8100]{2,0,1:T(1,128)S(1)} copy-done((f32[1,30,8100]{2,0,1:T(1,128)S(1)}, f32[1,30,8100]{2,0,1:T(1,128)}, u32[]{:S(2)}) %copy-start.1) | copy-done | bytes 972024
  3.7 1.2 %copy-done.2 = f32[1,30,8100]{2,0,1:T(1,128)S(1)} copy-done((f32[1,30,8100]{2,0,1:T(1,128)S(1)}, f32[1,30,8100]{2,0,1:T(1,128)}, u32[]{:S(2)}) %copy-start.2) | copy-done | bytes 972024
  4.9 0.8 %copy-done.3 = s32[1,8100]{1,0:T(1,128)S(1)} copy-done((s32[1,8100]{1,0:T(1,128)S(1)}, s32[1,8100]{1,0:T(1,128)}, u32[]{:S(2)}) %copy-start.3) | copy-done | bytes 32424
  5.7 0.8 %copy-done.4 = f32[1,8100]{1,0:T(1,128)S(1)} copy-done((f32[1,8100]{1,0:T(1,128)S(1)}, f32[1,8100]{1,0:T(1,128)}, u32[]{:S(2)}) %copy-start.4) | copy-done | bytes 32424
  6.4 0.8 %copy-done.5 = f32[1,8100]{1,0:T(1,128)S(1)} copy-done((f32[1,8100]{1,0:T(1,128)S(1)}, f32[1,8100]{1,0:T(1,128)}, u32[]{:S(2)}) %copy-start.5) | copy-done | bytes 32424
  7.2 7.9 %columns.1 = (f32[1920,128]{1,0:T(8,128)S(1)}, f32[1920,128]{1,0:T(8,128)S(1)}, f32[64,128]{1,0:T(8,128)S(1)}, f32[4,32,128]{2,1,0:T(8,128)S(1)}, f32[8,32,128]{...) custom-call(s32[1,4]{1,0:T(1,128)S(1)} %copy-done.6, s32[1,4]{1,0:T(1,128)S(1)} %copy-done.7, ...), custom_call_target="tpu_custom_call" | custom-call | flops 20000000 | bytes 8000000 | tf_op jit(solution)/shard_map/columns/pallas_call | solution.py:643
  15.0 4.1 %collective-permute-start.2 = (f32[4,32,128]{2,1,0:T(8,128)S(1)}, f32[4,32,128]{2,1,0:T(8,128)S(1)}, u32[]{:S(2)}, u32[]{:S(2)}) collective-permute-start(f32[4,32,128]{2,1,0:T(8,128)S(1)} %get-tuple-element.20.ts_ref), channel_id=1, source_target_pairs={{0,8},{1,9},{2,10},{3,11},{4,12},{5,13},{6,14},{7,15},{8,0},{9,1},... | collective-permute-start | bytes 196616 | tf_op jit(solution)/shard_map/ppermute | solution.py:666
  19.2 1.3 %collective-permute-start.1 = (f32[4,32,128]{2,1,0:T(8,128)S(1)}, f32[4,32,128]{2,1,0:T(8,128)S(1)}, u32[]{:S(2)}, u32[]{:S(2)}) collective-permute-start(f32[4,32,128]{2,1,0:T(8,128)S(1)} %get-tuple-element.20.ts_ref), channel_id=1, source_target_pairs={{1,0},{2,1},{3,2},{4,3},{5,4},{6,5},{7,6},{8,7},{9,8},{10,9},{11,1... | collective-permute-start | bytes 196616 | tf_op jit(solution)/shard_map/ppermute | solution.py:666
  20.4 3.0 %collective-permute-start = (f32[4,32,128]{2,1,0:T(8,128)S(1)}, f32[4,32,128]{2,1,0:T(8,128)S(1)}, u32[]{:S(2)}, u32[]{:S(2)}) collective-permute-start(f32[4,32,128]{2,1,0:T(8,128)S(1)} %get-tuple-element.20.ts_ref), channel_id=1, source_target_pairs={{0,1},{1,2},{2,3},{3,4},{4,5},{5,6},{6,7},{7,8},{8,9},{9,10},{10,1... | collective-permute-start | bytes 196616 | tf_op jit(solution)/shard_map/ppermute | solution.py:666
  23.5 0.0 collective-permute-done.2.rest_2_
  23.5 0.0 collective-permute-done.1.rest_1_
  23.5 0.9 %collective-permute-done.rest_0_ = f32[4,32,128]{2,1,0:T(8,128)S(1)} collective-permute-done((f32[4,32,128]{2,1,0:T(8,128)S(1)}, f32[4,32,128]{2,1,0:T(8,128)S(1)}, u32[]{:S(2)}, u32[]{:S(2)}) %collective-permute-start) | collective-permute-done | bytes 65568 | tf_op jit(solution)/shard_map/ppermute | solution.py:666
  24.4 0.9 %forcing.1 = (f32[64,128]{1,0:T(8,128)S(1)}, f32[88,128]{1,0:T(8,128)S(1)}, f32[8,128]{1,0:T(8,128)S(1)}) custom-call(s32[1]{0:T(128)} %bitcast.me_ref, s32[1,4]{1,0:T(1,128)S(1)} %copy-done.6, s32[1,4]{1,0:T(1,128)S(1)} %copy-done.7, f32[64,128]{1,0:T(8,128)S(1)} %get-tuple-element.19.f_ref, f32[4,32,128]{2,1,0:T(8,128)S(1)} %get-tuple-element.20.ts_ref, ...), custom_call_target="tpu_custom_call" | custom-call | flops 1000000 | bytes 1000000 | tf_op jit(solution)/shard_map/forcing/pallas_call | solution.py:643
  25.2 3.3 %collective-permute-start.5 = (f32[88,128]{1,0:T(8,128)S(1)}, f32[88,128]{1,0:T(8,128)S(1)}, u32[]{:S(2)}, u32[]{:S(2)}) collective-permute-start(f32[88,128]{1,0:T(8,128)S(1)} %get-tuple-element.24.rest_0_), channel_id=1, source_target_pairs={{0,3},{1,2},{2,1},{3,0},{4,7},{5,6},{6,5},{7,4},{8,11},{9,10},{10,... | collective-permute-start | bytes 135176 | tf_op jit(solution)/shard_map/ppermute | solution.py:610
  28.5 0.6 collective-permute-start.4
  29.2 0.0 collective-permute-start.3
  29.2 1.2 %collective-permute-done.3.rest_1_ = f32[88,128]{1,0:T(8,128)S(1)} collective-permute-done((f32[88,128]{1,0:T(8,128)S(1)}, f32[88,128]{1,0:T(8,128)S(1)}, u32[]{:S(2)}, u32[]{:S(2)}) %collective-permute-start.3) | collective-permute-done | bytes 45088 | tf_op jit(solution)/shard_map/ppermute | solution.py:610
  30.4 2.4 %collective-permute-done.4.rest_2_ = f32[88,128]{1,0:T(8,128)S(1)} collective-permute-done((f32[88,128]{1,0:T(8,128)S(1)}, f32[88,128]{1,0:T(8,128)S(1)}, u32[]{:S(2)}, u32[]{:S(2)}) %collective-permute-start.4) | collective-permute-done | bytes 45088 | tf_op jit(solution)/shard_map/ppermute | solution.py:610
  32.8 0.0 collective-permute-done.5.rest_3_
  32.8 2.1 %collective-permute-start.8 = (f32[352,128]{1,0:T(8,128)S(1)}, f32[352,128]{1,0:T(8,128)S(1)}, u32[]{:S(2)}, u32[]{:S(2)}) collective-permute-start(f32[352,128]{1,0:T(8,128)S(1)} %constant_dynamic-update-slice_fusion), channel_id=1, source_target_pairs={{0,12},{1,13},{2,14},{3,15},{4,8},{5,9},{6,10},{7,11},{8,4},{9,5},... | collective-permute-start | bytes 540680 | tf_op jit(solution)/shard_map/ppermute | solution.py:610
  34.9 1.7 %collective-permute-start.7 = (f32[352,128]{1,0:T(8,128)S(1)}, f32[352,128]{1,0:T(8,128)S(1)}, u32[]{:S(2)}, u32[]{:S(2)}) collective-permute-start(f32[352,128]{1,0:T(8,128)S(1)} %constant_dynamic-update-slice_fusion), channel_id=1, source_target_pairs={{0,8},{1,9},{2,10},{3,11},{4,12},{5,13},{6,14},{7,15},{8,0},{9,1},... | collective-permute-start | bytes 540680 | tf_op jit(solution)/shard_map/ppermute | solution.py:610
  36.6 0.7 collective-permute-start.6
  37.3 4.9 %collective-permute-done.8.rest_6_ = f32[352,128]{1,0:T(8,128)S(1)} collective-permute-done((f32[352,128]{1,0:T(8,128)S(1)}, f32[352,128]{1,0:T(8,128)S(1)}, u32[]{:S(2)}, u32[]{:S(2)}) %collective-permute-start.8) | collective-permute-done | bytes 180256 | tf_op jit(solution)/shard_map/ppermute | solution.py:610
  42.2 10.3 %collective-permute-done.7.rest_5_ = f32[352,128]{1,0:T(8,128)S(1)} collective-permute-done((f32[352,128]{1,0:T(8,128)S(1)}, f32[352,128]{1,0:T(8,128)S(1)}, u32[]{:S(2)}, u32[]{:S(2)}) %collective-permute-start.7) | collective-permute-done | bytes 180256 | tf_op jit(solution)/shard_map/ppermute | solution.py:610
  52.5 0.0 collective-permute-done.6.rest_4_
  52.5 2.2 %krylov.1 = (f32[3,64,128]{2,1,0:T(8,128)S(1)}, f32[3,64,128]{2,1,0:T(8,128)S(1)}, f32[4,8,128]{2,1,0:T(8,128)S(1)}, f32[32,128]{1,0:T(8,128)S(1)}) custom-call(s32[1]{0:T(128)} %bitcast.me_ref, f32[192,128]{1,0:T(8,128)S(1)} %get-tuple-element.18.dense_ref.rest_4_, f32[64,128]{1,0:T(8,128)S(1)} %get-tuple-element.23.forcing_ref.rest_5_, ...), custom_call_target="tpu_custom_call" | custom-call | flops 1000000 | bytes 1000000 | tf_op jit(solution)/shard_map/krylov/pallas_call | solution.py:643
  54.7 0.1 collective-permute-start.11
  54.8 1.6 %collective-permute-start.10 = (f32[32,128]{1,0:T(8,128)S(1)}, f32[32,128]{1,0:T(8,128)S(1)}, u32[]{:S(2)}, u32[]{:S(2)}) collective-permute-start(f32[32,128]{1,0:T(8,128)S(1)} %get-tuple-element.25), channel_id=1, source_target_pairs={{0,2},{1,3},{2,0},{3,1},{4,6},{5,7},{6,4},{7,5},{8,10},{9,11},{10,... | collective-permute-start | bytes 49160 | tf_op jit(solution)/shard_map/ppermute | solution.py:610
  56.5 0.2 collective-permute-start.9
  56.7 0.0 collective-permute-start.17
  56.7 1.3 %collective-permute-start.16 = (f32[8,32,128]{2,1,0:T(8,128)S(1)}, f32[8,32,128]{2,1,0:T(8,128)S(1)}, u32[]{:S(2)}, u32[]{:S(2)}) collective-permute-start(f32[8,32,128]{2,1,0:T(8,128)S(1)} %get-tuple-element.21.aq_ref.rest_13_), channel_id=1, source_target_pairs={{1,0},{2,1},{3,2},{4,3},{5,4},{6,5},{7,6},{8,7},{9,8},{10,9},{11,1... | collective-permute-start | bytes 393224 | tf_op jit(solution)/shard_map/ppermute | solution.py:666
  58.0 0.0 collective-permute-done.11
  58.0 3.0 %collective-permute-start.15 = (f32[8,32,128]{2,1,0:T(8,128)S(1)}, f32[8,32,128]{2,1,0:T(8,128)S(1)}, u32[]{:S(2)}, u32[]{:S(2)}) collective-permute-start(f32[8,32,128]{2,1,0:T(8,128)S(1)} %get-tuple-element.21.aq_ref.rest_13_), channel_id=1, source_target_pairs={{0,1},{1,2},{2,3},{3,4},{4,5},{5,6},{6,7},{7,8},{8,9},{9,10},{10,1... | collective-permute-start | bytes 393224 | tf_op jit(solution)/shard_map/ppermute | solution.py:666
  61.0 0.0 collective-permute-done.10
  61.0 0.0 collective-permute-done.9
  61.1 3.5 %collective-permute-start.14 = (f32[32,128]{1,0:T(8,128)S(1)}, f32[32,128]{1,0:T(8,128)S(1)}, u32[]{:S(2)}, u32[]{:S(2)}) collective-permute-start(f32[32,128]{1,0:T(8,128)S(1)} %add_add_fusion.rest_0_), channel_id=1, source_target_pairs={{0,12},{1,13},{2,14},{3,15},{4,8},{5,9},{6,10},{7,11},{8,4},{9,5},... | collective-permute-start | bytes 49160 | tf_op jit(solution)/shard_map/ppermute | solution.py:610
  64.5 0.8 %collective-permute-start.13 = (f32[32,128]{1,0:T(8,128)S(1)}, f32[32,128]{1,0:T(8,128)S(1)}, u32[]{:S(2)}, u32[]{:S(2)}) collective-permute-start(f32[32,128]{1,0:T(8,128)S(1)} %add_add_fusion.rest_0_), channel_id=1, source_target_pairs={{0,8},{1,9},{2,10},{3,11},{4,12},{5,13},{6,14},{7,15},{8,0},{9,1},... | collective-permute-start | bytes 49160 | tf_op jit(solution)/shard_map/ppermute | solution.py:610
  65.4 0.4 collective-permute-done.17.rest_16_
  65.8 0.0 collective-permute-start.12
  65.8 0.0 collective-permute-done.16.rest_15_
  65.8 0.0 collective-permute-done.15.rest_14_
  65.8 1.0 %collective-permute-done.14.rest_3_ = f32[32,128]{1,0:T(8,128)S(1)} collective-permute-done((f32[32,128]{1,0:T(8,128)S(1)}, f32[32,128]{1,0:T(8,128)S(1)}, u32[]{:S(2)}, u32[]{:S(2)}) %collective-permute-start.14) | collective-permute-done | bytes 16416 | tf_op jit(solution)/shard_map/ppermute | solution.py:610
  66.8 2.6 %collective-permute-done.13.rest_2_ = f32[32,128]{1,0:T(8,128)S(1)} collective-permute-done((f32[32,128]{1,0:T(8,128)S(1)}, f32[32,128]{1,0:T(8,128)S(1)}, u32[]{:S(2)}, u32[]{:S(2)}) %collective-permute-start.13) | collective-permute-done | bytes 16416 | tf_op jit(solution)/shard_map/ppermute | solution.py:610
  69.3 0.2 collective-permute-done.12.rest_1_
  69.5 4.9 %gradient.1 = (f32[1,8100]{1,0:T(1,128)}, f32[30,1,8100]{2,1,0:T(1,128)}) custom-call(s32[1]{0:T(128)} %bitcast.me_ref, s32[1,4]{1,0:T(1,128)S(1)} %copy-done.6, s32[1,4]{1,0:T(1,128)S(1)} %copy-done.7, f32[32,128]{1,0:T(8,128)S(1)} %add_add_fusion.rest_0_, f32[32,128]{1,0:T(8,128)S(1)} %collective-permute-done.12.rest_1_, ...), custom_call_target="tpu_custom_call" | custom-call | flops 10000000 | bytes 4000000 | tf_op jit(solution)/shard_map/gradient/pallas_call | solution.py:643
  (13 shorter events, 0.0 us)
Async XLA Ops:
  0.6 0.7 copy-start.6
  0.6 0.7 copy-start.7
  1.3 1.2 %copy-start = (f32[1,30,8100]{2,0,1:T(1,128)S(1)}, f32[1,30,8100]{2,0,1:T(1,128)}, u32[]{:S(2)}) copy-start(f32[1,30,8100]{2,0,1:T(1,128)} %param.9) | copy-start | bytes 2916004
  2.5 1.2 %copy-start.1 = (f32[1,30,8100]{2,0,1:T(1,128)S(1)}, f32[1,30,8100]{2,0,1:T(1,128)}, u32[]{:S(2)}) copy-start(f32[1,30,8100]{2,0,1:T(1,128)} %param.14) | copy-start | bytes 2916004
  3.7 1.2 %copy-start.2 = (f32[1,30,8100]{2,0,1:T(1,128)S(1)}, f32[1,30,8100]{2,0,1:T(1,128)}, u32[]{:S(2)}) copy-start(f32[1,30,8100]{2,0,1:T(1,128)} %param.8) | copy-start | bytes 2916004
  4.9 0.8 %copy-start.3 = (s32[1,8100]{1,0:T(1,128)S(1)}, s32[1,8100]{1,0:T(1,128)}, u32[]{:S(2)}) copy-start(s32[1,8100]{1,0:T(1,128)} %depth_ref.1) | copy-start | bytes 97204
  5.7 0.8 %copy-start.4 = (f32[1,8100]{1,0:T(1,128)S(1)}, f32[1,8100]{1,0:T(1,128)}, u32[]{:S(2)}) copy-start(f32[1,8100]{1,0:T(1,128)} %d_ref.1) | copy-start | bytes 97204
  6.4 0.8 %copy-start.5 = (f32[1,8100]{1,0:T(1,128)S(1)}, f32[1,8100]{1,0:T(1,128)}, u32[]{:S(2)}) copy-start(f32[1,8100]{1,0:T(1,128)} %b_ref.1) | copy-start | bytes 97204
  15.0 8.4 %collective-permute-start.2 = (f32[4,32,128]{2,1,0:T(8,128)S(1)}, f32[4,32,128]{2,1,0:T(8,128)S(1)}, u32[]{:S(2)}, u32[]{:S(2)}) collective-permute-start(f32[4,32,128]{2,1,0:T(8,128)S(1)} %get-tuple-element.20.ts_ref), channel_id=1, source_target_pairs={{0,8},{1,9},{2,10},{3,11},{4,12},{5,13},{6,14},{7,15},{8,0},{9,1},... | collective-permute-start | bytes 196616 | tf_op jit(solution)/shard_map/ppermute | solution.py:666
  19.2 4.3 %collective-permute-start.1 = (f32[4,32,128]{2,1,0:T(8,128)S(1)}, f32[4,32,128]{2,1,0:T(8,128)S(1)}, u32[]{:S(2)}, u32[]{:S(2)}) collective-permute-start(f32[4,32,128]{2,1,0:T(8,128)S(1)} %get-tuple-element.20.ts_ref), channel_id=1, source_target_pairs={{1,0},{2,1},{3,2},{4,3},{5,4},{6,5},{7,6},{8,7},{9,8},{10,9},{11,1... | collective-permute-start | bytes 196616 | tf_op jit(solution)/shard_map/ppermute | solution.py:666
  20.4 3.9 %collective-permute-start = (f32[4,32,128]{2,1,0:T(8,128)S(1)}, f32[4,32,128]{2,1,0:T(8,128)S(1)}, u32[]{:S(2)}, u32[]{:S(2)}) collective-permute-start(f32[4,32,128]{2,1,0:T(8,128)S(1)} %get-tuple-element.20.ts_ref), channel_id=1, source_target_pairs={{0,1},{1,2},{2,3},{3,4},{4,5},{5,6},{6,7},{7,8},{8,9},{9,10},{10,1... | collective-permute-start | bytes 196616 | tf_op jit(solution)/shard_map/ppermute | solution.py:666
  25.2 7.6 %collective-permute-start.5 = (f32[88,128]{1,0:T(8,128)S(1)}, f32[88,128]{1,0:T(8,128)S(1)}, u32[]{:S(2)}, u32[]{:S(2)}) collective-permute-start(f32[88,128]{1,0:T(8,128)S(1)} %get-tuple-element.24.rest_0_), channel_id=1, source_target_pairs={{0,3},{1,2},{2,1},{3,0},{4,7},{5,6},{6,5},{7,4},{8,11},{9,10},{10,... | collective-permute-start | bytes 135176 | tf_op jit(solution)/shard_map/ppermute | solution.py:610
  28.5 4.2 %collective-permute-start.4 = (f32[88,128]{1,0:T(8,128)S(1)}, f32[88,128]{1,0:T(8,128)S(1)}, u32[]{:S(2)}, u32[]{:S(2)}) collective-permute-start(f32[88,128]{1,0:T(8,128)S(1)} %get-tuple-element.24.rest_0_), channel_id=1, source_target_pairs={{0,2},{1,3},{2,0},{3,1},{4,6},{5,7},{6,4},{7,5},{8,10},{9,11},{10,... | collective-permute-start | bytes 135176 | tf_op jit(solution)/shard_map/ppermute | solution.py:610
  29.2 1.2 %collective-permute-start.3 = (f32[88,128]{1,0:T(8,128)S(1)}, f32[88,128]{1,0:T(8,128)S(1)}, u32[]{:S(2)}, u32[]{:S(2)}) collective-permute-start(f32[88,128]{1,0:T(8,128)S(1)} %get-tuple-element.24.rest_0_), channel_id=1, source_target_pairs={{0,1},{1,0},{2,3},{3,2},{4,5},{5,4},{6,7},{7,6},{8,9},{9,8},{10,11... | collective-permute-start | bytes 135176 | tf_op jit(solution)/shard_map/ppermute | solution.py:610
  32.8 9.4 %collective-permute-start.8 = (f32[352,128]{1,0:T(8,128)S(1)}, f32[352,128]{1,0:T(8,128)S(1)}, u32[]{:S(2)}, u32[]{:S(2)}) collective-permute-start(f32[352,128]{1,0:T(8,128)S(1)} %constant_dynamic-update-slice_fusion), channel_id=1, source_target_pairs={{0,12},{1,13},{2,14},{3,15},{4,8},{5,9},{6,10},{7,11},{8,4},{9,5},... | collective-permute-start | bytes 540680 | tf_op jit(solution)/shard_map/ppermute | solution.py:610
  34.9 17.6 %collective-permute-start.7 = (f32[352,128]{1,0:T(8,128)S(1)}, f32[352,128]{1,0:T(8,128)S(1)}, u32[]{:S(2)}, u32[]{:S(2)}) collective-permute-start(f32[352,128]{1,0:T(8,128)S(1)} %constant_dynamic-update-slice_fusion), channel_id=1, source_target_pairs={{0,8},{1,9},{2,10},{3,11},{4,12},{5,13},{6,14},{7,15},{8,0},{9,1},... | collective-permute-start | bytes 540680 | tf_op jit(solution)/shard_map/ppermute | solution.py:610
  36.6 15.9 %collective-permute-start.6 = (f32[352,128]{1,0:T(8,128)S(1)}, f32[352,128]{1,0:T(8,128)S(1)}, u32[]{:S(2)}, u32[]{:S(2)}) collective-permute-start(f32[352,128]{1,0:T(8,128)S(1)} %constant_dynamic-update-slice_fusion), channel_id=1, source_target_pairs={{0,4},{1,5},{2,6},{3,7},{4,0},{5,1},{6,2},{7,3},{8,12},{9,13},{10,... | collective-permute-start | bytes 540680 | tf_op jit(solution)/shard_map/ppermute | solution.py:610
  54.7 3.2 %collective-permute-start.11 = (f32[32,128]{1,0:T(8,128)S(1)}, f32[32,128]{1,0:T(8,128)S(1)}, u32[]{:S(2)}, u32[]{:S(2)}) collective-permute-start(f32[32,128]{1,0:T(8,128)S(1)} %get-tuple-element.25), channel_id=1, source_target_pairs={{0,3},{1,2},{2,1},{3,0},{4,7},{5,6},{6,5},{7,4},{8,11},{9,10},{10,... | collective-permute-start | bytes 49160 | tf_op jit(solution)/shard_map/ppermute | solution.py:610
  54.8 6.2 %collective-permute-start.10 = (f32[32,128]{1,0:T(8,128)S(1)}, f32[32,128]{1,0:T(8,128)S(1)}, u32[]{:S(2)}, u32[]{:S(2)}) collective-permute-start(f32[32,128]{1,0:T(8,128)S(1)} %get-tuple-element.25), channel_id=1, source_target_pairs={{0,2},{1,3},{2,0},{3,1},{4,6},{5,7},{6,4},{7,5},{8,10},{9,11},{10,... | collective-permute-start | bytes 49160 | tf_op jit(solution)/shard_map/ppermute | solution.py:610
  56.5 4.6 %collective-permute-start.9 = (f32[32,128]{1,0:T(8,128)S(1)}, f32[32,128]{1,0:T(8,128)S(1)}, u32[]{:S(2)}, u32[]{:S(2)}) collective-permute-start(f32[32,128]{1,0:T(8,128)S(1)} %get-tuple-element.25), channel_id=1, source_target_pairs={{0,1},{1,0},{2,3},{3,2},{4,5},{5,4},{6,7},{7,6},{8,9},{9,8},{10,11... | collective-permute-start | bytes 49160 | tf_op jit(solution)/shard_map/ppermute | solution.py:610
  56.7 9.1 %collective-permute-start.17 = (f32[8,32,128]{2,1,0:T(8,128)S(1)}, f32[8,32,128]{2,1,0:T(8,128)S(1)}, u32[]{:S(2)}, u32[]{:S(2)}) collective-permute-start(f32[8,32,128]{2,1,0:T(8,128)S(1)} %get-tuple-element.21.aq_ref.rest_13_), channel_id=1, source_target_pairs={{0,8},{1,9},{2,10},{3,11},{4,12},{5,13},{6,14},{7,15},{8,0},{9,1},... | collective-permute-start | bytes 393224 | tf_op jit(solution)/shard_map/ppermute | solution.py:666
  56.7 9.1 %collective-permute-start.16 = (f32[8,32,128]{2,1,0:T(8,128)S(1)}, f32[8,32,128]{2,1,0:T(8,128)S(1)}, u32[]{:S(2)}, u32[]{:S(2)}) collective-permute-start(f32[8,32,128]{2,1,0:T(8,128)S(1)} %get-tuple-element.21.aq_ref.rest_13_), channel_id=1, source_target_pairs={{1,0},{2,1},{3,2},{4,3},{5,4},{6,5},{7,6},{8,7},{9,8},{10,9},{11,1... | collective-permute-start | bytes 393224 | tf_op jit(solution)/shard_map/ppermute | solution.py:666
  58.0 7.8 %collective-permute-start.15 = (f32[8,32,128]{2,1,0:T(8,128)S(1)}, f32[8,32,128]{2,1,0:T(8,128)S(1)}, u32[]{:S(2)}, u32[]{:S(2)}) collective-permute-start(f32[8,32,128]{2,1,0:T(8,128)S(1)} %get-tuple-element.21.aq_ref.rest_13_), channel_id=1, source_target_pairs={{0,1},{1,2},{2,3},{3,4},{4,5},{5,6},{6,7},{7,8},{8,9},{9,10},{10,1... | collective-permute-start | bytes 393224 | tf_op jit(solution)/shard_map/ppermute | solution.py:666
  61.1 5.7 %collective-permute-start.14 = (f32[32,128]{1,0:T(8,128)S(1)}, f32[32,128]{1,0:T(8,128)S(1)}, u32[]{:S(2)}, u32[]{:S(2)}) collective-permute-start(f32[32,128]{1,0:T(8,128)S(1)} %add_add_fusion.rest_0_), channel_id=1, source_target_pairs={{0,12},{1,13},{2,14},{3,15},{4,8},{5,9},{6,10},{7,11},{8,4},{9,5},... | collective-permute-start | bytes 49160 | tf_op jit(solution)/shard_map/ppermute | solution.py:610
  64.5 4.8 %collective-permute-start.13 = (f32[32,128]{1,0:T(8,128)S(1)}, f32[32,128]{1,0:T(8,128)S(1)}, u32[]{:S(2)}, u32[]{:S(2)}) collective-permute-start(f32[32,128]{1,0:T(8,128)S(1)} %add_add_fusion.rest_0_), channel_id=1, source_target_pairs={{0,8},{1,9},{2,10},{3,11},{4,12},{5,13},{6,14},{7,15},{8,0},{9,1},... | collective-permute-start | bytes 49160 | tf_op jit(solution)/shard_map/ppermute | solution.py:610
  65.8 3.8 %collective-permute-start.12 = (f32[32,128]{1,0:T(8,128)S(1)}, f32[32,128]{1,0:T(8,128)S(1)}, u32[]{:S(2)}, u32[]{:S(2)}) collective-permute-start(f32[32,128]{1,0:T(8,128)S(1)} %add_add_fusion.rest_0_), channel_id=1, source_target_pairs={{0,4},{1,5},{2,6},{3,7},{4,0},{5,1},{6,2},{7,3},{8,12},{9,13},{10,... | collective-permute-start | bytes 49160 | tf_op jit(solution)/shard_map/ppermute | solution.py:610

commit v3 on v2

--- a/solution.py
+++ b/solution.py
@@ -16,7 +16,7 @@
 ROW_TILES = 8
 SPREAD = 0.2
 CENTRE = 4.1
-BLOCK = 88
+BLOCK = 68
 F32 = jnp.float32
 I32 = jnp.int32
 
@@ -121,28 +121,25 @@
     return jnp.where(lane < LANES - off, top, low)
 
 
-def write_frames(field_ref, base, out_ref, first_row, za_ref, zb_ref):
+def write_frames(field_ref, base, out_ref, first_row, za_ref, zb_ref, depths):
     field = field_ref[base : base + ROWS, :]
     row, lane, cell, i, j = grid_iotas()
-    zero = jnp.zeros_like(field)
-    for depth in range(4):
-        column = (j == depth) | (j == SIDE - 1 - depth)
-        za = jnp.where(column & (i < 64), field, zero)
-        zb = jnp.where(column & (i >= 64), field, zero)
-        za_ref[depth : depth + 1, :] = jnp.sum(za, axis=0, keepdims=True)
-        zb_ref[depth : depth + 1, :] = jnp.sum(zb, axis=0, keepdims=True)
-        out_ref[first_row + depth * 4 : first_row + depth * 4 + 1, :] = row_line(
-            field_ref, base, depth * SIDE
+    za_ref[0:8, :] = jnp.zeros((8, LANES), F32)
+    zb_ref[0:8, :] = jnp.zeros((8, LANES), F32)
+    for depth in range(depths):
+        column = ((j == depth) | (j == SIDE - 1 - depth)) & (i < SIDE)
+        za_ref[depth : depth + 1, :] = jnp.sum(
+            jnp.where(column & (i < 64), field, 0.0)[0:48], axis=0, keepdims=True
         )
-        out_ref[first_row + depth * 4 + 1 : first_row + depth * 4 + 2, :] = row_line(
-            field_ref, base, (SIDE - 1 - depth) * SIDE
+        zb_ref[depth : depth + 1, :] = jnp.sum(
+            jnp.where(column & (i >= 64), field, 0.0)[40:ROWS], axis=0, keepdims=True
         )
-    for depth in range(4, 8):
-        za_ref[depth : depth + 1, :] = jnp.zeros((1, LANES), F32)
-        zb_ref[depth : depth + 1, :] = jnp.zeros((1, LANES), F32)
+        at = first_row + depth * 4
+        out_ref[at : at + 1, :] = row_line(field_ref, base, depth * SIDE)
+        out_ref[at + 1 : at + 2, :] = row_line(field_ref, base, (SIDE - 1 - depth) * SIDE)
     depth_row = lax.broadcasted_iota(I32, (8, LANES), 0) & 3
     side2, side3 = lines_23(za_ref[0:8, :], zb_ref[0:8, :], depth_row)
-    for depth in range(4):
+    for depth in range(depths):
         at = first_row + depth * 4
         out_ref[at + 2 : at + 3, :] = side2[depth : depth + 1]
         out_ref[at + 3 : at + 4, :] = side3[depth : depth + 1]
@@ -191,38 +188,42 @@
     return (flux1 - behind(flux1, 1)) + (flux2 - behind(flux2, SIDE))
 
 
-def columns_kernel(
-    levels,
-    adj_ref,
-    flag_ref,
-    k_ref,
-    s_ref,
-    t_ref,
-    depth_ref,
-    d_ref,
-    b_ref,
-    a_ref,
-    q_ref,
-    f_ref,
-    ts_ref,
-    aq_ref,
-    blk_ref,
-    dense_ref,
-    g_ref,
-    z_ref,
-):
+def depths_kernel(depth_ref, out_ref, dense_ref, z_ref):
+    row, lane, cell, i, j = grid_iotas()
+    dense_ref[...] = jnp.where(cell < CELLS, surface_rows(depth_ref).astype(F32), 0.0)
+    write_frames(dense_ref, 0, out_ref, 0, z_ref.at[0], z_ref.at[1], 1)
+    out_ref[4:8, :] = jnp.zeros((4, LANES), F32)
+
+
+def columns_kernel(shifts, tiles, levels, me_ref, adj_ref, flag_ref, own_ref, *rest):
+    met_refs = rest[: len(shifts)]
+    k_hbm, s_hbm, t_hbm, depth_hbm, d_hbm, b_hbm = rest[len(shifts) : len(shifts) + 6]
+    a_ref, q_ref, as_ref, blk_ref, dense_ref, reach_ref = rest[len(shifts) + 6 : len(shifts) + 12]
+    k_ref, s_ref, t_ref, depth_ref, d_ref, b_ref, g_ref, z_ref, ts_ref, sems = rest[len(shifts) + 12 :]
+    parts = 3
+    third = levels // parts
+    surface = [
+        pltpu.make_async_copy(source, target, sems.at[number])
+        for number, (source, target) in enumerate(((depth_hbm, depth_ref), (b_hbm, b_ref), (d_hbm, d_ref)))
+    ]
+    for copy in surface:
+        copy.start()
+    columns = []
+    for part in range(parts):
+        at = pl.ds(part * third, third if part < parts - 1 else levels - part * third)
+        for number, (source, target) in enumerate(((k_hbm, k_ref), (s_hbm, s_ref))):
+            columns.append(pltpu.make_async_copy(source.at[at], target.at[at], sems.at[3 + 2 * part + number]))
+            columns[-1].start()
+    tracer = pltpu.make_async_copy(t_hbm, t_ref, sems.at[3 + 2 * parts])
+    tracer.start()
+    me = me_ref[0]
     row, lane, cell, i, j = grid_iotas()
     inside = cell < CELLS
-    for number, ref in enumerate((b_ref, d_ref, depth_ref)):
-        rows = slice(number * ROWS, (number + 1) * ROWS)
+    for number, ref in enumerate((depth_ref, b_ref, d_ref)):
+        surface[number].wait()
+        place = (2, 0, 1)[number]
+        rows = slice(place * ROWS, (place + 1) * ROWS)
         dense_ref[rows, :] = jnp.where(inside, surface_rows(ref).astype(F32), 0.0)
-        write_frames(dense_ref, number * ROWS, blk_ref, number * 16, z_ref.at[0], z_ref.at[1])
-    at = 48
-    for sides in ((0, 1, 2, 3), (2, 2, 0, 0), (3, 3, 1, 1)):
-        for ref in (adj_ref, flag_ref):
-            for side in sides:
-                blk_ref[at : at + 1, :] = jnp.full((1, LANES), ref[0, side], I32).astype(F32)
-                at += 1
     depth = dense_ref[2 * ROWS : 3 * ROWS, :]
     along, across = interior_reach(depth)
     zero = jnp.zeros((ROWS, LANES), F32)
@@ -243,14 +244,21 @@
         q_ref[at, :] = vq
         return r, upper * ratio, va, vq
 
-    lax.fori_loop(0, levels, down, (zero, zero, zero, zero), unroll=2)
+    carry = (zero, zero, zero, zero)
+    for part in range(parts):
+        columns[2 * part].wait()
+        columns[2 * part + 1].wait()
+        last = (part + 1) * third if part < parts - 1 else levels
+        carry = lax.fori_loop(part * third, last, down, carry, unroll=2)
+    tracer.wait()
     column = ((j == 0) | (j == SIDE - 1)) & (i < SIDE)
     first = (column & (i < 64))[0:48]
     second = (column & (i >= 64))[40:ROWS]
 
     def up(step, carry):
-        xa, xq, total = carry
+        xa, xq, total, flux1, flux2 = carry
         level = levels - 1 - step
+        here = level.astype(F32)
         at = pl.ds(pl.multiple_of(level * ROWS, ROWS), ROWS)
         ratio = g_ref[at, :]
         xa = a_ref[at, :] + ratio * xa
@@ -258,42 +266,67 @@
         a_ref[at, :] = xa
         q_ref[at, :] = xq
         t = level_rows(t_ref, level)
-        here = pl.ds(level, 1)
-        for number, x in enumerate((t, xa, xq)):
+        line = pl.ds(level, 1)
+        for number, (x, out) in enumerate(((t, ts_ref), (xa, as_ref))):
             base = number * 4
-            z_ref[base, here, :] = jnp.sum(jnp.where(first, x[0:48], 0.0), axis=0, keepdims=True)
-            z_ref[base + 1, here, :] = jnp.sum(jnp.where(second, x[40:ROWS], 0.0), axis=0, keepdims=True)
-            out, side0 = (ts_ref, 0) if number == 0 else (aq_ref, (number - 1) * 4)
-            out[side0, here, :] = x[0:1]
-            z_ref[base + 2, here, :] = x[ROWS - 2 : ROWS - 1]
-            z_ref[base + 3, here, :] = x[ROWS - 1 : ROWS]
-        mixed_h = t + SPREAD * interior_spread(t, along, across, level.astype(F32))
-        return xa, xq, total + xq * mixed_h
-
-    xa, xq, total = lax.fori_loop(0, levels, up, (zero, zero, zero), unroll=2)
-    f_ref[...] = jnp.where(inside, total, zero)
+            z_ref[base, line, :] = jnp.sum(jnp.where(first, x[0:48], 0.0), axis=0, keepdims=True)
+            z_ref[base + 1, line, :] = jnp.sum(jnp.where(second, x[40:ROWS], 0.0), axis=0, keepdims=True)
+            out[0, line, :] = x[0:1]
+            z_ref[base + 2, line, :] = x[ROWS - 2 : ROWS - 1]
+            z_ref[base + 3, line, :] = x[ROWS - 1 : ROWS]
+        flux1 = flux1 + jnp.where(along > here, xq * (ahead(t, 1) - t), zero)
+        flux2 = flux2 + jnp.where(across > here, xq * (ahead(t, SIDE) - t), zero)
+        return xa, xq, total + xq * t, flux1, flux2
+
+    xa, xq, total, flux1, flux2 = lax.fori_loop(0, levels, up, (zero,) * 5, unroll=2)
+    level_scale = 1.0 / math.sqrt(levels)
+    spread = (flux1 - behind(flux1, 1)) + (flux2 - behind(flux2, SIDE))
+    dense_ref[3 * ROWS : 4 * ROWS, :] = jnp.where(inside, (total + SPREAD * spread) * level_scale, zero)
     spare = z_ref.shape[1] - levels
-    for number in range(3):
+    for number, out in enumerate((ts_ref, as_ref)):
         base = number * 4
-        out, at = (ts_ref, 0) if number == 0 else (aq_ref, (number - 1) * 4)
         for part in range(4):
             z_ref[base + part, levels:, :] = jnp.zeros((spare, LANES), F32)
-        out[at, levels:, :] = jnp.zeros((spare, LANES), F32)
+        out[0, levels:, :] = jnp.zeros((spare, LANES), F32)
         side2, side3 = lines_23(z_ref[base], z_ref[base + 1], 0)
-        out[at + 2] = side2
-        out[at + 3] = side3
+        out[2] = side2
+        out[3] = side3
         low, high = z_ref[base + 2], z_ref[base + 3]
         wide = lax.broadcasted_iota(I32, low.shape, 1)
-        out[at + 1] = jnp.where(wide < 54, pltpu.roll(low, 54, 1), pltpu.roll(high, 54, 1))
+        out[1] = jnp.where(wide < 54, pltpu.roll(low, 54, 1), pltpu.roll(high, 54, 1))
+    level = lax.broadcasted_iota(I32, (32, LANES), 0).astype(F32)
+    reach_ref[4:8, :] = jnp.zeros((4, LANES), F32)
     for side in range(4):
-        ts_ref[side, levels : levels + 1, :] = blk_ref[32 + side : 33 + side, :]
-
-
-def pick(refs, shifts, tiles, me, neighbour, first, side_met):
-    value = refs[0][first + side_met]
+        neighbour = adj_ref[0, side]
+        flag = flag_ref[0, side]
+        met = met_refs[0][pl.ds(flag >> 1, 1), :]
+        for number in range(1, len(shifts)):
+            hit = neighbour == lax.rem(me + tiles - shifts[number], tiles)
+            met = jnp.where(hit, met_refs[number][pl.ds(flag >> 1, 1), :], met)
+        met = take(jnp.broadcast_to(met, (8, LANES)), seam_index(flag))[0:1]
+        reach = jnp.where(neighbour >= 0, jnp.minimum(met, own_ref[side : side + 1, :]), 0.0)
+        reach_ref[side : side + 1, :] = reach
+        shared = jnp.sum(jnp.where(reach > level, ts_ref[side], 0.0), axis=0, keepdims=True)
+        blk_ref[60 + side : 61 + side, :] = (SPREAD * level_scale) * shared
+        table = jnp.zeros((1, LANES), F32)
+        where = lax.broadcasted_iota(I32, (1, LANES), 1)
+        for number, of in enumerate((side, 2 if side < 2 else 0, 3 if side < 2 else 1)):
+            table = jnp.where(where == 2 * number, adj_ref[0, of].astype(F32), table)
+            table = jnp.where(where == 2 * number + 1, flag_ref[0, of].astype(F32), table)
+        blk_ref[64 + side : 65 + side, :] = table
+    g_ref[0:ROWS, :] = jnp.minimum(depth, 1.0)
+    za_ref, zb_ref = z_ref.at[0], z_ref.at[1]
+    write_frames(dense_ref, 0, blk_ref, 0, za_ref, zb_ref, 4)
+    write_frames(dense_ref, 3 * ROWS, blk_ref, 16, za_ref, zb_ref, 4)
+    write_frames(g_ref, 0, blk_ref, 32, za_ref, zb_ref, 4)
+    write_frames(dense_ref, ROWS, blk_ref, 48, za_ref, zb_ref, 3)
+
+
+def pick(refs, shifts, tiles, me, neighbour, side_met):
+    value = refs[0][side_met]
     for number in range(1, len(shifts)):
         hit = neighbour == lax.rem(me + tiles - shifts[number], tiles)
-        value = jnp.where(hit, refs[number][first + side_met], value)
+        value = jnp.where(hit, refs[number][side_met], value)
     return value
 
 
@@ -302,36 +335,11 @@
     return jnp.where((flag & 1) == 1, SIDE - 1 - lane, lane) & 127
 
 
-def forcing_kernel(shifts, tiles, levels, me_ref, adj_ref, flag_ref, f_ref, ts_ref, aq_ref, blk_ref, *rest):
-    refs = rest[: len(shifts)]
-    out_ref, frame_ref, reach_ref, za_ref, zb_ref = rest[len(shifts) :]
-    me = me_ref[0]
-    level = lax.broadcasted_iota(I32, (32, LANES), 0).astype(F32)
-    lines = []
-    for side in range(4):
-        neighbour = adj_ref[0, side]
-        flag = flag_ref[0, side]
-        other = take(pick(refs, shifts, tiles, me, neighbour, 0, flag >> 1), seam_index(flag))
-        own = ts_ref[side]
-        reach = jnp.minimum(other[levels : levels + 1], own[levels : levels + 1])
-        reach = jnp.where(neighbour >= 0, reach, 0.0)
-        reach_ref[side : side + 1, :] = reach
-        flux = jnp.where(reach > level, other - own, 0.0)
-        lines.append(jnp.sum(aq_ref[4 + side] * flux, axis=0, keepdims=True))
-    reach_ref[4:8, :] = jnp.zeros((4, LANES), F32)
-    seams = scatter_lines(scatter_masks(), jnp.concatenate(lines + lines, axis=0))
-    out_ref[...] = (f_ref[...] + SPREAD * seams) * (1.0 / math.sqrt(levels))
-    frame_ref[0:72, :] = blk_ref[...]
-    write_frames(out_ref, 0, frame_ref, 72, za_ref, zb_ref)
-
-
-def block_rows(refs, counts, block, first, size):
-    position = 0
-    for ref, count in zip(refs, counts):
-        for number in range(count):
-            at = number * block + first
+def block_rows(refs, places, first, size):
+    for ref, held in zip(refs, places):
+        for number, position in enumerate(held):
+            at = number * BLOCK + first
             yield position, ref[at : at + size, :]
-            position += 1
 
 
 def gather_lines(p, lines):
@@ -354,44 +362,55 @@
     )
 
 
-def krylov_kernel(counts, lines, me_ref, dense_ref, forcing_ref, *rest):
-    refs = rest[: len(counts)]
-    va_ref, vb_ref, line_ref, gram_ref = rest[len(counts) : len(counts) + 4]
-    p_ref, index_ref, frame_ref, work_ref, depth_ref, d_ref, x_ref = rest[len(counts) + 4 :]
+def krylov_kernel(places, lines, me_ref, dense_ref, *rest):
+    refs = rest[: len(places)]
+    va_ref, vb_ref, line_ref, gram_ref = rest[len(places) : len(places) + 4]
+    p_ref, index_ref, frame_ref, work_ref, wet_ref, d_ref, x_ref = rest[len(places) + 4 :]
     me = me_ref[0]
-    for number in range(6):
-        for position, rows in block_rows(refs, counts, BLOCK, 48 + 4 * number, 4):
-            work_ref[number, position * 4 : position * 4 + 4, :] = rows
+
+    def collect(out, first):
+        for position, rows in block_rows(refs, places, first, 4):
+            out[position * 4 : position * 4 + 4, :] = rows
+
+    collect(work_ref.at[0], 60)
+    collect(work_ref.at[1], 64)
     for depth in range(4):
-        for position, rows in block_rows(refs, counts, BLOCK, 16 + 4 * depth, 4):
-            d_ref[depth, position * 4 : position * 4 + 4, :] = rows
-        for position, rows in block_rows(refs, counts, BLOCK, 32 + 4 * depth, 4):
-            depth_ref[depth, position * 4 : position * 4 + 4, :] = rows
+        collect(x_ref.at[depth], 4 * depth)
+        collect(x_ref.at[4 + depth], 16 + 4 * depth)
+        collect(wet_ref.at[depth], 32 + 4 * depth)
+        if depth < 3:
+            collect(d_ref.at[depth], 48 + 4 * depth)
     lane = lax.broadcasted_iota(I32, (lines, LANES), 1)
-    odd = lax.broadcasted_iota(I32, (lines, LANES), 0) & 1
+    line = lax.broadcasted_iota(I32, (lines, LANES), 0)
+    odd = line & 1
     column = lax.broadcasted_iota(I32, (lines, lines), 1)
+    line_of = lax.broadcasted_iota(I32, (lines, lines), 0)
     for number in range(3):
-        tile = work_ref[2 * number, :, 0:1].astype(I32)
-        flag = work_ref[2 * number + 1, :, 0:1].astype(I32)
+        tile = work_ref[1, :, 2 * number : 2 * number + 1].astype(I32)
+        flag = work_ref[1, :, 2 * number + 1 : 2 * number + 2].astype(I32)
         at = jnp.where(tile >= 0, 4 * (tile ^ me) + (flag >> 1), -1)
         p = jnp.where(jnp.broadcast_to(at, (lines, lines)) == column, 1.0, 0.0)
         p_ref[number * lines : (number + 1) * lines, :] = p.astype(jnp.bfloat16)
-        parity = work_ref[2 * number + 1].astype(I32) & 1
+        parity = jnp.broadcast_to(flag & 1, (lines, LANES))
         if number == 0:
             index_ref[0:lines, :] = jnp.where(parity == 1, SIDE - 1 - lane, lane) & 127
         else:
             index_ref[number * lines : (number + 1) * lines, :] = parity ^ odd
-    wet = [jnp.where(depth_ref[depth] > 0.0, 1.0, 0.0) for depth in range(4)]
-    met = gather_lines(p_ref[...], wet[0])
-    facing = take(met[0:lines], index_ref[0:lines, :])
+    first_half = (line_of & 2) == 0
+    for number in range(2):
+        at = (line_of & -4) + jnp.where(first_half, 2, 0) + number
+        p = jnp.where(at == column, 1.0, 0.0)
+        p_ref[(3 + number) * lines : (4 + number) * lines, :] = p.astype(jnp.bfloat16)
+    p = p_ref[0 : 3 * lines, :]
+    facing_at = index_ref[0:lines, :]
+    low_parity = index_ref[lines : 2 * lines, :]
+    high_parity = index_ref[2 * lines : 3 * lines, :]
+    wet = [wet_ref[depth] for depth in range(4)]
+    met = gather_lines(p, wet[0])
+    facing = take(met[0:lines], facing_at)
     for depth in range(3):
         low, high = ends(
-            wet[depth],
-            met[lines : 2 * lines],
-            met[2 * lines : 3 * lines],
-            index_ref[lines : 2 * lines, :],
-            index_ref[2 * lines : 3 * lines, :],
-            depth,
+            wet[depth], met[lines : 2 * lines], met[2 * lines : 3 * lines], low_parity, high_parity, depth
         )
         masks = [
             wet[depth] * (facing if depth == 0 else wet[depth - 1]),
@@ -404,26 +423,30 @@
             frame_ref[depth, 1 + number] = masks[number]
         if depth == 0:
             seam = masks[0][0:8]
+    shared = work_ref[0]
+    gain = take(gather_lines(p_ref[0:lines, :], shared), facing_at) - shared
+    moved = gather_lines(p_ref[3 * lines : 5 * lines, :], gain)
+    zero_line = jnp.zeros((lines, LANES), F32)
+    for depth in range(4):
+        end = jnp.where(odd == 1, SIDE - 1 - depth, depth)
+        extra = jnp.where(lane == 0, take(moved[0:lines], end), zero_line)
+        extra = extra + jnp.where(lane == SIDE - 1, take(moved[lines : 2 * lines], end), zero_line)
+        if depth == 0:
+            extra = extra + gain
+        x_ref[4 + depth] = x_ref[4 + depth] + extra
     surface = jnp.minimum(dense_ref[2 * ROWS : 3 * ROWS, :], 1.0)
     along, across = interior_reach(surface)
     degree = (along + behind(along, 1)) + (across + behind(across, SIDE))
     masks = scatter_masks()
     diagonal = dense_ref[ROWS : 2 * ROWS, :] + (degree + scatter_lines(masks, seam))
-    p = p_ref[...]
-    facing_at = index_ref[0:lines, :]
-    low_parity = index_ref[lines : 2 * lines, :]
-    high_parity = index_ref[2 * lines : 3 * lines, :]
     scale = 2.0 / CENTRE
     row, lane, cell, i, j = grid_iotas()
     inside = cell < CELLS
-    frames = []
-    own = []
-    for solve, first in enumerate((0, 72)):
-        for depth in range(4):
-            for position, rows in block_rows(refs, counts, BLOCK, first + 4 * depth, 4):
-                x_ref[solve * 4 + depth, position * 4 : position * 4 + 4, :] = rows
-        frames.append([[x_ref[solve * 4 + depth] for depth in range(4)]])
-        own.append([(dense_ref if solve == 0 else forcing_ref)[0:ROWS, :]])
+    forcing = dense_ref[3 * ROWS : 4 * ROWS, :] + scatter_lines(masks, gain[0:8])
+    va_ref[0] = forcing
+    vb_ref[0] = dense_ref[0:ROWS, :]
+    frames = [[[x_ref[4 * solve + depth] for depth in range(4)]] for solve in range(2)]
+    own = [[dense_ref[0:ROWS, :]], [forcing]]
     for step in range(ITERS):
         for solve in range(2):
             x = frames[solve][-1]
@@ -456,7 +479,7 @@
                 following.append(0.5 * image if step == 0 else image - frames[solve][-2][depth])
             frames[solve].append(following)
             if step < ITERS - 1:
-                (vb_ref if solve == 0 else va_ref)[step] = own[solve][-1]
+                (vb_ref if solve == 0 else va_ref)[step + 1] = own[solve][-1]
     for solve in range(2):
         at = 16 * solve
         for first in range(ITERS + 1):
@@ -530,25 +553,25 @@
     ref[:, last * LANES : CELLS] = rows[last : last + 1, 0 : CELLS - last * LANES]
 
 
-def combine(x, b_ref, v_ref):
-    out = x[0] * b_ref[0:ROWS, :]
+def combine(x, v_ref):
+    out = x[0] * v_ref[0]
     for number in range(1, ITERS):
-        out = out + x[number] * v_ref[number - 1]
+        out = out + x[number] * v_ref[number]
     return out
 
 
 def gradient_kernel(shifts, tiles, levels, grams, me_ref, adj_ref, flag_ref, *rest):
     gram_refs = rest[:grams]
     rest = rest[grams:]
-    dense_ref, forcing_ref, va_ref, v_ref, line_ref, blk_ref, reach_ref, a_ref, q_ref, aq_ref = rest[:10]
-    refs = rest[10 : 10 + len(shifts)]
-    height_ref, out_ref, gram_ref, sum_ref, w_ref, h_ref = rest[10 + len(shifts) :]
+    dense_ref, va_ref, v_ref, line_ref, reach_ref, a_ref, q_ref, as_ref = rest[:8]
+    refs = rest[8 : 8 + len(shifts)]
+    height_ref, out_ref, gram_ref, sum_ref, w_ref, h_ref = rest[8 + len(shifts) :]
     me = me_ref[0]
     total_gram(gram_refs, gram_ref)
-    store_rows(height_ref, combine(coefficients(gram_ref, 16), forcing_ref, va_ref))
+    store_rows(height_ref, combine(coefficients(gram_ref, 16), va_ref))
     x = coefficients(gram_ref, 0)
     level_scale = 1.0 / math.sqrt(levels)
-    adjoint = combine(x, dense_ref, v_ref) * level_scale
+    adjoint = combine(x, v_ref) * level_scale
     met_line = x[0] * line_ref[0]
     depth = dense_ref[2 * ROWS : 3 * ROWS, :]
     along, across = interior_reach(depth)
@@ -570,10 +593,9 @@
         neighbour = adj_ref[0, side]
         flag = flag_ref[0, side]
         index = seam_index(flag)
-        a_other = take(pick(refs, shifts, tiles, me, neighbour, 0, flag >> 1), index)
-        q_other = take(pick(refs, shifts, tiles, me, neighbour, 4, flag >> 1), index)
-        other = a_other + (sum_ref[side : side + 1, :] * level_scale) * q_other
-        own = aq_ref[side] + w_ref[4, 8 + side : 9 + side, :] * aq_ref[4 + side]
+        other = take(pick(refs, shifts, tiles, me, neighbour, flag >> 1), index)
+        other = other + sum_ref[side : side + 1, :] * level_scale
+        own = as_ref[side] + w_ref[4, 8 + side : 9 + side, :]
         fluxes.append(jnp.where(reach_ref[side : side + 1, :] > level, other - own, 0.0))
     wa, wb, w1 = spread_lines(fluxes[2], fluxes[3], fluxes[1])
     w_ref[0] = wa
@@ -598,11 +620,11 @@
 
 def rounds(tiles):
     out = []
-    stride = 1
-    while stride < tiles:
-        radix = 4 if (tiles // stride) % 4 == 0 else 2
+    stride = tiles
+    while stride > 1:
+        radix = 4 if stride >= 16 else 2
+        stride //= radix
         out.append((stride, radix))
-        stride *= radix
     return out
 
 
@@ -612,13 +634,14 @@
 
 def gather_tiles(block, tiles):
     held = [block]
-    counts = [1]
+    places = [(0,)]
     for stride, radix in rounds(tiles):
         whole = held[0] if len(held) == 1 else jnp.concatenate(held, axis=0)
+        covered = tuple(n for place in places for n in place)
         for number in range(1, radix):
             held.append(swap(whole, tiles, number * stride))
-            counts.append(stride)
-    return held, tuple(counts)
+            places.append(tuple(n ^ (number * stride) for n in covered))
+    return held, tuple(places)
 
 
 def sum_tiles(block, tiles):
@@ -639,17 +662,19 @@
     def shape(*dims):
         return jax.ShapeDtypeStruct(dims, F32)
 
-    def call(kernel, outs, scratch, scalars, arrays, name, flops=1e6, traffic=1e6):
+    hbm = pl.BlockSpec(memory_space=pltpu.HBM)
+
+    def call(kernel, outs, scratch, scalars, arrays, name, flops=1e6, traffic=1e6, far=()):
         return pl.pallas_call(
             kernel,
             out_shape=outs,
-            in_specs=[smem] * len(scalars) + [vmem] * len(arrays),
+            in_specs=[smem] * len(scalars) + [vmem] * len(arrays) + [hbm] * len(far),
             out_specs=jax.tree.map(lambda _: vmem, outs),
             scratch_shapes=scratch,
             compiler_params=params,
             cost_estimate=pl.CostEstimate(flops=int(flops), bytes_accessed=int(traffic), transcendentals=0),
             name=name,
-        )(*scalars, *arrays)
+        )(*scalars, *arrays, *far)
 
     offsets = []
     for offset in (1, -1, ROW_TILES, -ROW_TILES, tiles // 2):
@@ -669,53 +694,64 @@
     def by_level(x):
         return jnp.transpose(x, (1, 0, 2))
 
-    big = pltpu.VMEM((levels * ROWS, LANES), F32)
-    solved, weight, forcing_inside, strips, edge_lines, block, dense = call(
-        functools.partial(columns_kernel, levels),
+    own_depths = call(
+        depths_kernel,
+        shape(8, LANES),
+        [pltpu.VMEM((ROWS, LANES), F32), pltpu.VMEM((2, 8, LANES), F32)],
+        (),
+        (depth,),
+        "depths",
+    )
+    depths_met = to_neighbours(own_depths)
+    far = pltpu.VMEM((levels, 1, CELLS), F32)
+    solved, weight, strips, block, dense, reach = call(
+        functools.partial(columns_kernel, shifts, tiles, levels),
         (
             shape(levels * ROWS, LANES),
             shape(levels * ROWS, LANES),
-            shape(ROWS, LANES),
             shape(4, 32, LANES),
-            shape(8, 32, LANES),
-            shape(72, LANES),
-            shape(3 * ROWS, LANES),
+            shape(BLOCK, LANES),
+            shape(4 * ROWS, LANES),
+            shape(8, LANES),
         ),
-        [big, pltpu.VMEM((12, 32, LANES), F32)],
-        (adjacent, flags),
-        (by_level(stirring), by_level(sensitivity), by_level(thermal), depth, main_entry, elevation),
+        [
+            far,
+            far,
+            far,
+            pltpu.VMEM((1, CELLS), I32),
+            pltpu.VMEM((1, CELLS), F32),
+            pltpu.VMEM((1, CELLS), F32),
+            pltpu.VMEM((levels * ROWS, LANES), F32),
+            pltpu.VMEM((8, 32, LANES), F32),
+            pltpu.VMEM((4, 32, LANES), F32),
+            pltpu.SemaphoreType.DMA((10,)),
+        ],
+        (me, adjacent, flags),
+        (own_depths, *depths_met),
         "columns",
         2e7,
         8e6,
-    )
+        (by_level(stirring), by_level(sensitivity), by_level(thermal), depth, main_entry, elevation),
+    )
+    blocks, places = gather_tiles(block, tiles)
     strips_met = to_neighbours(strips)
-    forcing, frames, reach = call(
-        functools.partial(forcing_kernel, shifts, tiles, levels),
-        (shape(ROWS, LANES), shape(BLOCK, LANES), shape(8, LANES)),
-        [pltpu.VMEM((8, LANES), F32), pltpu.VMEM((8, LANES), F32)],
-        (me, adjacent, flags),
-        (forcing_inside, strips, edge_lines, block, *strips_met),
-        "forcing",
-    )
-    blocks, counts = gather_tiles(frames, tiles)
-    edge_lines_met = to_neighbours(edge_lines)
     lines = 4 * tiles
     frame = pltpu.VMEM((4, lines, LANES), F32)
-    basis = shape(ITERS - 1, ROWS, LANES)
+    basis = shape(ITERS, ROWS, LANES)
     basis_a, basis_b, lines_b, gram = call(
-        functools.partial(krylov_kernel, counts, lines),
+        functools.partial(krylov_kernel, places, lines),
         (basis, basis, shape(ITERS, 8, LANES), shape(32, LANES)),
         [
-            pltpu.VMEM((3 * lines, lines), jnp.bfloat16),
+            pltpu.VMEM((5 * lines, lines), jnp.bfloat16),
             pltpu.VMEM((3 * lines, LANES), I32),
             pltpu.VMEM((3, 5, lines, LANES), F32),
-            pltpu.VMEM((6, lines, LANES), F32),
+            pltpu.VMEM((2, lines, LANES), F32),
             frame,
             frame,
             pltpu.VMEM((8, lines, LANES), F32),
         ],
         (me,),
-        (dense, forcing, *blocks),
+        (dense, *blocks),
         "krylov",
     )
     grams = sum_tiles(gram, tiles)
@@ -732,16 +768,14 @@
         (
             *grams,
             dense,
-            forcing,
             basis_a,
             basis_b,
             lines_b,
-            block,
             reach,
             solved,
             weight,
-            edge_lines,
-            *edge_lines_met,
+            strips,
+            *strips_met,
         ),
         "gradient",
         1e7,

time: 74.9 us -> 64.9 us (0.87)
  waiting for transfers between devices: 23.8 us -> 15.4 us
  starting transfers between devices: 27.4 us -> 25.5 us
    ppermute x12 -> x10, waiting for transfers between devices: 22.6 us -> 14.6 us  [swap(): return lax.ppermute(x, 'tile', [(t, t ^ offset) for t in range(tiles)])]
    ppermute x12 -> x10, starting transfers between devices: 14.7 us -> 11.8 us  [swap(): return lax.ppermute(x, 'tile', [(t, t ^ offset) for t in range(tiles)])]
    ppermute x6, starting transfers between devices: 12.7 us -> 13.7 us  [to_neighbours(): out.append(lax.ppermute(x, 'tile', pairs))]
    unnamed x19 -> x18, local copies, waits for them, and re-layouts: 6.54 us -> 6.54 us
  transfers between devices with their start and end apart: 18 -> 16, of which waited for: 9 -> 8; matrix products, arithmetic and copies ran while one was open for 0% -> 0% of each run, Pallas kernels for 0% -> 0%
where the time goes in v3:
time: 64.9 us; the launch traced here: 64.4 us
  starting transfers between devices  25.5 us (39%)
  Pallas kernels  15.9 us (24%)
  waiting for transfers between devices  15.4 us (24%)
  local copies, waits for them, and re-layouts  6.85 us (11%)
  between operations  0.78 us (1%)
    pallas_call x4, Pallas kernels, call(): pl.pallas_call(kernel, out_shape=outs, in_specs=[smem] * len(scalars) + [...  15.9 us
    ppermute x10, waiting for transfers between devices, swap(): return lax.ppermute(x, 'tile', [(t, t ^ offset) for t in range(tiles)])  14.6 us
    ppermute x6, starting transfers between devices, to_neighbours(): out.append(lax.ppermute(x, 'tile', pairs))  13.7 us
    ppermute x10, starting transfers between devices, swap(): return lax.ppermute(x, 'tile', [(t, t ^ offset) for t in range(tiles)])  11.8 us
    unnamed x18, local copies, waits for them, and re-layouts  6.54 us
  transfers between devices with their start and end apart: 16, of which 8 were waited for; matrix products, arithmetic and copies ran while one was open for 0% of the time, Pallas kernels for 0%

profile of v3, /device:TPU:0, one launch (start us, length us, event | category | flops | bytes accessed | tf_op | source)
XLA Modules:
  0.0 64.4 jit_solution(6988476164115814644)
XLA Ops:
  0.6 0.0 copy-start.3
  0.6 0.7 %copy-done.3 = s32[1,8100]{1,0:T(1,128)S(1)} copy-done((s32[1,8100]{1,0:T(1,128)S(1)}, s32[1,8100]{1,0:T(1,128)}, u32[]{:S(2)}) %copy-start.3) | copy-done | bytes 32424
  1.4 0.0 copy-start.4
  1.4 0.2 depths.1.own_ref
  1.6 4.0 %collective-permute-start.2 = (f32[8,128]{1,0:T(8,128)S(1)}, f32[8,128]{1,0:T(8,128)S(1)}, u32[]{:S(2)}, u32[]{:S(2)}) collective-permute-start(f32[8,128]{1,0:T(8,128)S(1)} %depths.1.own_ref), channel_id=1, source_target_pairs={{0,8},{1,9},{2,10},{3,11},{4,12},{5,13},{6,14},{7,15},{8,0},{9,1},... | collective-permute-start | bytes 12296 | tf_op jit(solution)/shard_map/ppermute | solution.py:691
  5.7 1.3 %collective-permute-start.1 = (f32[8,128]{1,0:T(8,128)S(1)}, f32[8,128]{1,0:T(8,128)S(1)}, u32[]{:S(2)}, u32[]{:S(2)}) collective-permute-start(f32[8,128]{1,0:T(8,128)S(1)} %depths.1.own_ref), channel_id=1, source_target_pairs={{1,0},{2,1},{3,2},{4,3},{5,4},{6,5},{7,6},{8,7},{9,8},{10,9},{11,1... | collective-permute-start | bytes 12296 | tf_op jit(solution)/shard_map/ppermute | solution.py:691
  6.9 3.0 %collective-permute-start = (f32[8,128]{1,0:T(8,128)S(1)}, f32[8,128]{1,0:T(8,128)S(1)}, u32[]{:S(2)}, u32[]{:S(2)}) collective-permute-start(f32[8,128]{1,0:T(8,128)S(1)} %depths.1.own_ref), channel_id=1, source_target_pairs={{0,1},{1,2},{2,3},{3,4},{4,5},{5,6},{6,7},{7,8},{8,9},{9,10},{10,1... | collective-permute-start | bytes 12296 | tf_op jit(solution)/shard_map/ppermute | solution.py:691
  10.0 0.0 collective-permute-done.2.rest_2_
  10.0 0.0 collective-permute-done.1.rest_1_
  10.0 0.8 %collective-permute-done.rest_0_ = f32[8,128]{1,0:T(8,128)S(1)} collective-permute-done((f32[8,128]{1,0:T(8,128)S(1)}, f32[8,128]{1,0:T(8,128)S(1)}, u32[]{:S(2)}, u32[]{:S(2)}) %collective-permute-start) | collective-permute-done | bytes 4128 | tf_op jit(solution)/shard_map/ppermute | solution.py:691
  10.8 0.0 copy-done.4
  10.8 0.6 %copy-done.7 = s32[1,4]{1,0:T(1,128)S(1)} copy-done((s32[1,4]{1,0:T(1,128)S(1)}, s32[1,4]{1,0:T(1,128)}, u32[]{:S(2)}) %copy-start.7) | copy-done | bytes 40
  11.4 0.0 copy-done.8
  11.5 1.2 %copy-done = f32[1,30,8100]{2,0,1:T(1,128)S(1)} copy-done((f32[1,30,8100]{2,0,1:T(1,128)S(1)}, f32[1,30,8100]{2,0,1:T(1,128)}, u32[]{:S(2)}) %copy-start) | copy-done | bytes 972024
  12.7 1.2 %copy-done.1 = f32[1,30,8100]{2,0,1:T(1,128)S(1)} copy-done((f32[1,30,8100]{2,0,1:T(1,128)S(1)}, f32[1,30,8100]{2,0,1:T(1,128)}, u32[]{:S(2)}) %copy-start.1) | copy-done | bytes 972024
  13.9 1.2 %copy-done.2 = f32[1,30,8100]{2,0,1:T(1,128)S(1)} copy-done((f32[1,30,8100]{2,0,1:T(1,128)S(1)}, f32[1,30,8100]{2,0,1:T(1,128)}, u32[]{:S(2)}) %copy-start.2) | copy-done | bytes 972024
  15.1 0.8 %copy-done.5 = f32[1,8100]{1,0:T(1,128)S(1)} copy-done((f32[1,8100]{1,0:T(1,128)S(1)}, f32[1,8100]{1,0:T(1,128)}, u32[]{:S(2)}) %copy-start.5) | copy-done | bytes 32424
  15.8 0.8 %copy-done.6 = f32[1,8100]{1,0:T(1,128)S(1)} copy-done((f32[1,8100]{1,0:T(1,128)S(1)}, f32[1,8100]{1,0:T(1,128)}, u32[]{:S(2)}) %copy-start.6) | copy-done | bytes 32424
  16.6 8.2 %columns.1 = (f32[1920,128]{1,0:T(8,128)S(1)}, f32[1920,128]{1,0:T(8,128)S(1)}, f32[4,32,128]{2,1,0:T(8,128)S(1)}, f32[68,128]{1,0:T(8,128)S(1)}, f32[256,128]{1,0:T(8,128)S(1)}, /*index=5*/f32[8,128]{1,0:T(8,128)S(1)}) custom-call(s32[1]{0:T(128)} %bitcast.me_ref, s32[1,4]{1,0:T(1,128)S(1)} %copy-done.7, s32[1,4]{1,0:T(1,128)S(1)} %copy-done.8, ...), custom_call_target="tpu_custom_call" | custom-call | flops 20000000 | bytes 8000000 | tf_op jit(solution)/shard_map/columns/pallas_call | solution.py:668
  24.8 4.6 %collective-permute-start.5 = (f32[68,128]{1,0:T(8,128)S(1)}, f32[68,128]{1,0:T(8,128)S(1)}, u32[]{:S(2)}, u32[]{:S(2)}) collective-permute-start(f32[68,128]{1,0:T(8,128)S(1)} %get-tuple-element.15.rest_0_), channel_id=1, source_target_pairs={{0,12},{1,13},{2,14},{3,15},{4,8},{5,9},{6,10},{7,11},{8,4},{9,5},... | collective-permute-start | bytes 104456 | tf_op jit(solution)/shard_map/ppermute | solution.py:632
  29.4 1.7 %collective-permute-start.4 = (f32[68,128]{1,0:T(8,128)S(1)}, f32[68,128]{1,0:T(8,128)S(1)}, u32[]{:S(2)}, u32[]{:S(2)}) collective-permute-start(f32[68,128]{1,0:T(8,128)S(1)} %get-tuple-element.15.rest_0_), channel_id=1, source_target_pairs={{0,8},{1,9},{2,10},{3,11},{4,12},{5,13},{6,14},{7,15},{8,0},{9,1},... | collective-permute-start | bytes 104456 | tf_op jit(solution)/shard_map/ppermute | solution.py:632
  31.0 0.1 collective-permute-start.3
  31.2 0.4 collective-permute-done.5.rest_3_
  31.5 2.7 %collective-permute-done.4.rest_2_ = f32[68,128]{1,0:T(8,128)S(1)} collective-permute-done((f32[68,128]{1,0:T(8,128)S(1)}, f32[68,128]{1,0:T(8,128)S(1)}, u32[]{:S(2)}, u32[]{:S(2)}) %collective-permute-start.4) | collective-permute-done | bytes 34848 | tf_op jit(solution)/shard_map/ppermute | solution.py:632
  34.2 0.8 %collective-permute-done.3.rest_1_ = f32[68,128]{1,0:T(8,128)S(1)} collective-permute-done((f32[68,128]{1,0:T(8,128)S(1)}, f32[68,128]{1,0:T(8,128)S(1)}, u32[]{:S(2)}, u32[]{:S(2)}) %collective-permute-start.3) | collective-permute-done | bytes 34848 | tf_op jit(solution)/shard_map/ppermute | solution.py:632
  35.0 0.2 collective-permute-start.6
  35.2 4.9 %collective-permute-done.6.rest_4_ = f32[272,128]{1,0:T(8,128)S(1)} collective-permute-done((f32[272,128]{1,0:T(8,128)S(1)}, f32[272,128]{1,0:T(8,128)S(1)}, u32[]{:S(2)}, u32[]{:S(2)}) %collective-permute-start.6) | collective-permute-done | bytes 139296 | tf_op jit(solution)/shard_map/ppermute | solution.py:632
  40.1 0.3 concatenate.7
  40.5 0.1 collective-permute-start.7
  40.5 1.5 %collective-permute-done.7.rest_5_ = f32[544,128]{1,0:T(8,128)S(1)} collective-permute-done((f32[544,128]{1,0:T(8,128)S(1)}, f32[544,128]{1,0:T(8,128)S(1)}, u32[]{:S(2)}, u32[]{:S(2)}) %collective-permute-start.7) | collective-permute-done | bytes 278560 | tf_op jit(solution)/shard_map/ppermute | solution.py:632
  42.1 2.6 %krylov.1 = (f32[4,64,128]{2,1,0:T(8,128)S(1)}, f32[4,64,128]{2,1,0:T(8,128)S(1)}, f32[4,8,128]{2,1,0:T(8,128)S(1)}, f32[32,128]{1,0:T(8,128)S(1)}) custom-call(s32[1]{0:T(128)} %bitcast.me_ref, f32[256,128]{1,0:T(8,128)S(1)} %get-tuple-element.14.dense_ref.rest_2_, f32[68,128]{1,0:T(8,128)S(1)} %get-tuple-element.15.rest_0_, ...), custom_call_target="tpu_custom_call" | custom-call | flops 1000000 | bytes 1000000 | tf_op jit(solution)/shard_map/krylov/pallas_call | solution.py:668
  44.7 2.5 %collective-permute-start.10 = (f32[32,128]{1,0:T(8,128)S(1)}, f32[32,128]{1,0:T(8,128)S(1)}, u32[]{:S(2)}, u32[]{:S(2)}) collective-permute-start(f32[32,128]{1,0:T(8,128)S(1)} %get-tuple-element.16), channel_id=1, source_target_pairs={{0,12},{1,13},{2,14},{3,15},{4,8},{5,9},{6,10},{7,11},{8,4},{9,5},... | collective-permute-start | bytes 49160 | tf_op jit(solution)/shard_map/ppermute | solution.py:632
  47.2 0.0 collective-permute-start.9
  47.2 1.9 %collective-permute-start.8 = (f32[32,128]{1,0:T(8,128)S(1)}, f32[32,128]{1,0:T(8,128)S(1)}, u32[]{:S(2)}, u32[]{:S(2)}) collective-permute-start(f32[32,128]{1,0:T(8,128)S(1)} %get-tuple-element.16), channel_id=1, source_target_pairs={{0,4},{1,5},{2,6},{3,7},{4,0},{5,1},{6,2},{7,3},{8,12},{9,13},{10,... | collective-permute-start | bytes 49160 | tf_op jit(solution)/shard_map/ppermute | solution.py:632
  49.1 1.0 %collective-permute-start.15 = (f32[4,32,128]{2,1,0:T(8,128)S(1)}, f32[4,32,128]{2,1,0:T(8,128)S(1)}, u32[]{:S(2)}, u32[]{:S(2)}) collective-permute-start(f32[4,32,128]{2,1,0:T(8,128)S(1)} %get-tuple-element.23.rest_9_), channel_id=1, source_target_pairs={{0,8},{1,9},{2,10},{3,11},{4,12},{5,13},{6,14},{7,15},{8,0},{9,1},... | collective-permute-start | bytes 196616 | tf_op jit(solution)/shard_map/ppermute | solution.py:691
  50.2 1.3 %collective-permute-start.14 = (f32[4,32,128]{2,1,0:T(8,128)S(1)}, f32[4,32,128]{2,1,0:T(8,128)S(1)}, u32[]{:S(2)}, u32[]{:S(2)}) collective-permute-start(f32[4,32,128]{2,1,0:T(8,128)S(1)} %get-tuple-element.23.rest_9_), channel_id=1, source_target_pairs={{1,0},{2,1},{3,2},{4,3},{5,4},{6,5},{7,6},{8,7},{9,8},{10,9},{11,1... | collective-permute-start | bytes 196616 | tf_op jit(solution)/shard_map/ppermute | solution.py:691
  51.4 0.0 collective-permute-done.10
  51.5 3.0 %collective-permute-start.13 = (f32[4,32,128]{2,1,0:T(8,128)S(1)}, f32[4,32,128]{2,1,0:T(8,128)S(1)}, u32[]{:S(2)}, u32[]{:S(2)}) collective-permute-start(f32[4,32,128]{2,1,0:T(8,128)S(1)} %get-tuple-element.23.rest_9_), channel_id=1, source_target_pairs={{0,1},{1,2},{2,3},{3,4},{4,5},{5,6},{6,7},{7,8},{8,9},{9,10},{10,1... | collective-permute-start | bytes 196616 | tf_op jit(solution)/shard_map/ppermute | solution.py:691
  54.5 0.0 collective-permute-done.9
  54.5 0.0 collective-permute-done.8
  54.5 0.5 collective-permute-start.11
  55.0 3.3 %collective-permute-done.11 = f32[32,128]{1,0:T(8,128)S(1)} collective-permute-done((f32[32,128]{1,0:T(8,128)S(1)}, f32[32,128]{1,0:T(8,128)S(1)}, u32[]{:S(2)}, u32[]{:S(2)}) %collective-permute-start.11) | collective-permute-done | bytes 16416 | tf_op jit(solution)/shard_map/ppermute | solution.py:632
  58.3 0.2 collective-permute-start.12
  58.6 0.0 collective-permute-done.15.rest_12_
  58.6 0.0 collective-permute-done.14.rest_11_
  58.6 0.0 collective-permute-done.13.rest_10_
  58.6 1.0 %collective-permute-done.12.rest_1_ = f32[32,128]{1,0:T(8,128)S(1)} collective-permute-done((f32[32,128]{1,0:T(8,128)S(1)}, f32[32,128]{1,0:T(8,128)S(1)}, u32[]{:S(2)}, u32[]{:S(2)}) %collective-permute-start.12) | collective-permute-done | bytes 16416 | tf_op jit(solution)/shard_map/ppermute | solution.py:632
  59.5 4.8 %gradient.1 = (f32[1,8100]{1,0:T(1,128)}, f32[30,1,8100]{2,1,0:T(1,128)}) custom-call(s32[1]{0:T(128)} %bitcast.me_ref, s32[1,4]{1,0:T(1,128)S(1)} %copy-done.7, s32[1,4]{1,0:T(1,128)S(1)} %copy-done.8, f32[32,128]{1,0:T(8,128)S(1)} %add.15.rest_0_, f32[32,128]{1,0:T(8,128)S(1)} %collective-permute-done.12.rest_1_, ...), custom_call_target="tpu_custom_call" | custom-call | flops 10000000 | bytes 4000000 | tf_op jit(solution)/shard_map/gradient/pallas_call | solution.py:668
  (10 shorter events, 0.0 us)
Async XLA Ops:
  0.6 0.8 %copy-start.3 = (s32[1,8100]{1,0:T(1,128)S(1)}, s32[1,8100]{1,0:T(1,128)}, u32[]{:S(2)}) copy-start(s32[1,8100]{1,0:T(1,128)} %rest_6_.1) | copy-start | bytes 97204
  1.4 9.4 %copy-start.4 = (s32[1,8100]{1,0:T(1,128)S(1)}, s32[1,8100]{1,0:T(1,128)}, u32[]{:S(2)}) copy-start(s32[1,8100]{1,0:T(1,128)} %rest_6_.1) | copy-start | bytes 97204
  1.6 8.4 %collective-permute-start.2 = (f32[8,128]{1,0:T(8,128)S(1)}, f32[8,128]{1,0:T(8,128)S(1)}, u32[]{:S(2)}, u32[]{:S(2)}) collective-permute-start(f32[8,128]{1,0:T(8,128)S(1)} %depths.1.own_ref), channel_id=1, source_target_pairs={{0,8},{1,9},{2,10},{3,11},{4,12},{5,13},{6,14},{7,15},{8,0},{9,1},... | collective-permute-start | bytes 12296 | tf_op jit(solution)/shard_map/ppermute | solution.py:691
  5.7 4.3 %collective-permute-start.1 = (f32[8,128]{1,0:T(8,128)S(1)}, f32[8,128]{1,0:T(8,128)S(1)}, u32[]{:S(2)}, u32[]{:S(2)}) collective-permute-start(f32[8,128]{1,0:T(8,128)S(1)} %depths.1.own_ref), channel_id=1, source_target_pairs={{1,0},{2,1},{3,2},{4,3},{5,4},{6,5},{7,6},{8,7},{9,8},{10,9},{11,1... | collective-permute-start | bytes 12296 | tf_op jit(solution)/shard_map/ppermute | solution.py:691
  6.9 3.8 %collective-permute-start = (f32[8,128]{1,0:T(8,128)S(1)}, f32[8,128]{1,0:T(8,128)S(1)}, u32[]{:S(2)}, u32[]{:S(2)}) collective-permute-start(f32[8,128]{1,0:T(8,128)S(1)} %depths.1.own_ref), channel_id=1, source_target_pairs={{0,1},{1,2},{2,3},{3,4},{4,5},{5,6},{6,7},{7,8},{8,9},{9,10},{10,1... | collective-permute-start | bytes 12296 | tf_op jit(solution)/shard_map/ppermute | solution.py:691
  10.8 0.7 %copy-start.7 = (s32[1,4]{1,0:T(1,128)S(1)}, s32[1,4]{1,0:T(1,128)}, u32[]{:S(2)}) copy-start(s32[1,4]{1,0:T(1,128)} %adj_ref.3) | copy-start | bytes 52
  10.8 0.7 %copy-start.8 = (s32[1,4]{1,0:T(1,128)S(1)}, s32[1,4]{1,0:T(1,128)}, u32[]{:S(2)}) copy-start(s32[1,4]{1,0:T(1,128)} %flag_ref.3) | copy-start | bytes 52
  11.5 1.2 %copy-start = (f32[1,30,8100]{2,0,1:T(1,128)S(1)}, f32[1,30,8100]{2,0,1:T(1,128)}, u32[]{:S(2)}) copy-start(f32[1,30,8100]{2,0,1:T(1,128)} %param.9) | copy-start | bytes 2916004
  12.7 1.2 %copy-start.1 = (f32[1,30,8100]{2,0,1:T(1,128)S(1)}, f32[1,30,8100]{2,0,1:T(1,128)}, u32[]{:S(2)}) copy-start(f32[1,30,8100]{2,0,1:T(1,128)} %param.14) | copy-start | bytes 2916004
  13.9 1.2 %copy-start.2 = (f32[1,30,8100]{2,0,1:T(1,128)S(1)}, f32[1,30,8100]{2,0,1:T(1,128)}, u32[]{:S(2)}) copy-start(f32[1,30,8100]{2,0,1:T(1,128)} %param.8) | copy-start | bytes 2916004
  15.1 0.8 %copy-start.5 = (f32[1,8100]{1,0:T(1,128)S(1)}, f32[1,8100]{1,0:T(1,128)}, u32[]{:S(2)}) copy-start(f32[1,8100]{1,0:T(1,128)} %rest_7_.1) | copy-start | bytes 97204
  15.8 0.8 %copy-start.6 = (f32[1,8100]{1,0:T(1,128)S(1)}, f32[1,8100]{1,0:T(1,128)}, u32[]{:S(2)}) copy-start(f32[1,8100]{1,0:T(1,128)} %rest_8_.1) | copy-start | bytes 97204
  24.8 6.8 %collective-permute-start.5 = (f32[68,128]{1,0:T(8,128)S(1)}, f32[68,128]{1,0:T(8,128)S(1)}, u32[]{:S(2)}, u32[]{:S(2)}) collective-permute-start(f32[68,128]{1,0:T(8,128)S(1)} %get-tuple-element.15.rest_0_), channel_id=1, source_target_pairs={{0,12},{1,13},{2,14},{3,15},{4,8},{5,9},{6,10},{7,11},{8,4},{9,5},... | collective-permute-start | bytes 104456 | tf_op jit(solution)/shard_map/ppermute | solution.py:632
  29.4 4.9 %collective-permute-start.4 = (f32[68,128]{1,0:T(8,128)S(1)}, f32[68,128]{1,0:T(8,128)S(1)}, u32[]{:S(2)}, u32[]{:S(2)}) collective-permute-start(f32[68,128]{1,0:T(8,128)S(1)} %get-tuple-element.15.rest_0_), channel_id=1, source_target_pairs={{0,8},{1,9},{2,10},{3,11},{4,12},{5,13},{6,14},{7,15},{8,0},{9,1},... | collective-permute-start | bytes 104456 | tf_op jit(solution)/shard_map/ppermute | solution.py:632
  31.0 4.0 %collective-permute-start.3 = (f32[68,128]{1,0:T(8,128)S(1)}, f32[68,128]{1,0:T(8,128)S(1)}, u32[]{:S(2)}, u32[]{:S(2)}) collective-permute-start(f32[68,128]{1,0:T(8,128)S(1)} %get-tuple-element.15.rest_0_), channel_id=1, source_target_pairs={{0,4},{1,5},{2,6},{3,7},{4,0},{5,1},{6,2},{7,3},{8,12},{9,13},{10,... | collective-permute-start | bytes 104456 | tf_op jit(solution)/shard_map/ppermute | solution.py:632
  35.0 5.1 %collective-permute-start.6 = (f32[272,128]{1,0:T(8,128)S(1)}, f32[272,128]{1,0:T(8,128)S(1)}, u32[]{:S(2)}, u32[]{:S(2)}) collective-permute-start(f32[272,128]{1,0:T(8,128)S(1)} %pad_maximum_fusion), channel_id=1, source_target_pairs={{0,2},{1,3},{2,0},{3,1},{4,6},{5,7},{6,4},{7,5},{8,10},{9,11},{10,... | collective-permute-start | bytes 417800 | tf_op jit(solution)/shard_map/ppermute | solution.py:632
  40.5 1.6 %collective-permute-start.7 = (f32[544,128]{1,0:T(8,128)S(1)}, f32[544,128]{1,0:T(8,128)S(1)}, u32[]{:S(2)}, u32[]{:S(2)}) collective-permute-start(f32[544,128]{1,0:T(8,128)S(1)} %concatenate.7), channel_id=1, source_target_pairs={{0,1},{1,0},{2,3},{3,2},{4,5},{5,4},{6,7},{7,6},{8,9},{9,8},{10,11... | collective-permute-start | bytes 835592 | tf_op jit(solution)/shard_map/ppermute | solution.py:632
  44.7 6.8 %collective-permute-start.10 = (f32[32,128]{1,0:T(8,128)S(1)}, f32[32,128]{1,0:T(8,128)S(1)}, u32[]{:S(2)}, u32[]{:S(2)}) collective-permute-start(f32[32,128]{1,0:T(8,128)S(1)} %get-tuple-element.16), channel_id=1, source_target_pairs={{0,12},{1,13},{2,14},{3,15},{4,8},{5,9},{6,10},{7,11},{8,4},{9,5},... | collective-permute-start | bytes 49160 | tf_op jit(solution)/shard_map/ppermute | solution.py:632
  47.2 7.3 %collective-permute-start.9 = (f32[32,128]{1,0:T(8,128)S(1)}, f32[32,128]{1,0:T(8,128)S(1)}, u32[]{:S(2)}, u32[]{:S(2)}) collective-permute-start(f32[32,128]{1,0:T(8,128)S(1)} %get-tuple-element.16), channel_id=1, source_target_pairs={{0,8},{1,9},{2,10},{3,11},{4,12},{5,13},{6,14},{7,15},{8,0},{9,1},... | collective-permute-start | bytes 49160 | tf_op jit(solution)/shard_map/ppermute | solution.py:632
  47.2 7.3 %collective-permute-start.8 = (f32[32,128]{1,0:T(8,128)S(1)}, f32[32,128]{1,0:T(8,128)S(1)}, u32[]{:S(2)}, u32[]{:S(2)}) collective-permute-start(f32[32,128]{1,0:T(8,128)S(1)} %get-tuple-element.16), channel_id=1, source_target_pairs={{0,4},{1,5},{2,6},{3,7},{4,0},{5,1},{6,2},{7,3},{8,12},{9,13},{10,... | collective-permute-start | bytes 49160 | tf_op jit(solution)/shard_map/ppermute | solution.py:632
  49.1 9.4 %collective-permute-start.15 = (f32[4,32,128]{2,1,0:T(8,128)S(1)}, f32[4,32,128]{2,1,0:T(8,128)S(1)}, u32[]{:S(2)}, u32[]{:S(2)}) collective-permute-start(f32[4,32,128]{2,1,0:T(8,128)S(1)} %get-tuple-element.23.rest_9_), channel_id=1, source_target_pairs={{0,8},{1,9},{2,10},{3,11},{4,12},{5,13},{6,14},{7,15},{8,0},{9,1},... | collective-permute-start | bytes 196616 | tf_op jit(solution)/shard_map/ppermute | solution.py:691
  50.2 8.4 %collective-permute-start.14 = (f32[4,32,128]{2,1,0:T(8,128)S(1)}, f32[4,32,128]{2,1,0:T(8,128)S(1)}, u32[]{:S(2)}, u32[]{:S(2)}) collective-permute-start(f32[4,32,128]{2,1,0:T(8,128)S(1)} %get-tuple-element.23.rest_9_), channel_id=1, source_target_pairs={{1,0},{2,1},{3,2},{4,3},{5,4},{6,5},{7,6},{8,7},{9,8},{10,9},{11,1... | collective-permute-start | bytes 196616 | tf_op jit(solution)/shard_map/ppermute | solution.py:691
  51.5 7.1 %collective-permute-start.13 = (f32[4,32,128]{2,1,0:T(8,128)S(1)}, f32[4,32,128]{2,1,0:T(8,128)S(1)}, u32[]{:S(2)}, u32[]{:S(2)}) collective-permute-start(f32[4,32,128]{2,1,0:T(8,128)S(1)} %get-tuple-element.23.rest_9_), channel_id=1, source_target_pairs={{0,1},{1,2},{2,3},{3,4},{4,5},{5,6},{6,7},{7,8},{8,9},{9,10},{10,1... | collective-permute-start | bytes 196616 | tf_op jit(solution)/shard_map/ppermute | solution.py:691
  54.5 3.8 %collective-permute-start.11 = (f32[32,128]{1,0:T(8,128)S(1)}, f32[32,128]{1,0:T(8,128)S(1)}, u32[]{:S(2)}, u32[]{:S(2)}) collective-permute-start(f32[32,128]{1,0:T(8,128)S(1)} %add_add_fusion), channel_id=1, source_target_pairs={{0,2},{1,3},{2,0},{3,1},{4,6},{5,7},{6,4},{7,5},{8,10},{9,11},{10,... | collective-permute-start | bytes 49160 | tf_op jit(solution)/shard_map/ppermute | solution.py:632
  58.3 1.2 %collective-permute-start.12 = (f32[32,128]{1,0:T(8,128)S(1)}, f32[32,128]{1,0:T(8,128)S(1)}, u32[]{:S(2)}, u32[]{:S(2)}) collective-permute-start(f32[32,128]{1,0:T(8,128)S(1)} %add.15.rest_0_), channel_id=1, source_target_pairs={{0,1},{1,0},{2,3},{3,2},{4,5},{5,4},{6,7},{7,6},{8,9},{9,8},{10,11... | collective-permute-start | bytes 49160 | tf_op jit(solution)/shard_map/ppermute | solution.py:632

commit v4 on v3

--- a/solution.py
+++ b/solution.py
@@ -622,9 +622,8 @@
     out = []
     stride = tiles
     while stride > 1:
-        radix = 4 if stride >= 16 else 2
-        stride //= radix
-        out.append((stride, radix))
+        stride //= 2
+        out.append((stride, 2))
     return out
 
 
@@ -657,21 +656,20 @@
     me = lax.axis_index("tile").astype(I32).reshape(1)
     smem = pl.BlockSpec(memory_space=pltpu.SMEM)
     vmem = pl.BlockSpec(memory_space=pltpu.VMEM)
-    params = pltpu.CompilerParams(vmem_limit_bytes=48 * 1024 * 1024)
 
     def shape(*dims):
         return jax.ShapeDtypeStruct(dims, F32)
 
     hbm = pl.BlockSpec(memory_space=pltpu.HBM)
 
-    def call(kernel, outs, scratch, scalars, arrays, name, flops=1e6, traffic=1e6, far=()):
+    def call(kernel, outs, scratch, scalars, arrays, name, flops=1e6, traffic=1e6, far=(), grant=48):
         return pl.pallas_call(
             kernel,
             out_shape=outs,
             in_specs=[smem] * len(scalars) + [vmem] * len(arrays) + [hbm] * len(far),
             out_specs=jax.tree.map(lambda _: vmem, outs),
             scratch_shapes=scratch,
-            compiler_params=params,
+            compiler_params=pltpu.CompilerParams(vmem_limit_bytes=grant * 1024 * 1024),
             cost_estimate=pl.CostEstimate(flops=int(flops), bytes_accessed=int(traffic), transcendentals=0),
             name=name,
         )(*scalars, *arrays, *far)
@@ -731,7 +729,8 @@
         "columns",
         2e7,
         8e6,
-        (by_level(stirring), by_level(sensitivity), by_level(thermal), depth, main_entry, elevation),
+        tuple(pltpu.with_memory_space_constraint(v, pltpu.HBM) for v in (by_level(stirring), by_level(sensitivity), by_level(thermal), depth, main_entry, elevation)),
+        48,
     )
     blocks, places = gather_tiles(block, tiles)
     strips_met = to_neighbours(strips)

time: 64.9 us -> 62.7 us (0.966)
  local copies, waits for them, and re-layouts: 6.85 us -> 1.42 us
  starting transfers between devices: 25.5 us -> 27.4 us
  waiting for transfers between devices: 15.4 us -> 17.1 us
    unnamed x18 -> x6, local copies, waits for them, and re-layouts: 6.54 us -> 1.42 us
    ppermute x10 -> x8, starting transfers between devices: 11.8 us -> 14.7 us  [swap(): return lax.ppermute(x, 'tile', [(t, t ^ offset) for t in range(tiles)])]
    ppermute x10 -> x8, waiting for transfers between devices: 14.6 us -> 16.3 us  [swap(): return lax.ppermute(x, 'tile', [(t, t ^ offset) for t in range(tiles)])]
    ppermute x6, starting transfers between devices: 13.7 us -> 12.7 us  [to_neighbours(): out.append(lax.ppermute(x, 'tile', pairs))]
  transfers between devices with their start and end apart: 16 -> 14, of which waited for: 8 -> 8; matrix products, arithmetic and copies ran while one was open for 0% -> 0% of each run, Pallas kernels for 0% -> 0%
where the time goes in v4:
time: 62.7 us; the launch traced here: 62.4 us
  starting transfers between devices  27.4 us (44%)
  waiting for transfers between devices  17.1 us (27%)
  Pallas kernels  15.6 us (25%)
  local copies, waits for them, and re-layouts  1.42 us (2%)
  between operations  0.78 us (1%)
    ppermute x8, waiting for transfers between devices, swap(): return lax.ppermute(x, 'tile', [(t, t ^ offset) for t in range(tiles)])  16.3 us
    pallas_call x4, Pallas kernels, call(): pl.pallas_call(kernel, out_shape=outs, in_specs=[smem] * len(scalars) + [...  15.6 us
    ppermute x8, starting transfers between devices, swap(): return lax.ppermute(x, 'tile', [(t, t ^ offset) for t in range(tiles)])  14.7 us
    ppermute x6, starting transfers between devices, to_neighbours(): out.append(lax.ppermute(x, 'tile', pairs))  12.7 us
    unnamed x6, local copies, waits for them, and re-layouts  1.42 us
  transfers between devices with their start and end apart: 14, of which 8 were waited for; matrix products, arithmetic and copies ran while one was open for 0% of the time, Pallas kernels for 0%

profile of v4, /device:TPU:0, one launch (start us, length us, event | category | flops | bytes accessed | tf_op | source)
XLA Modules:
  0.0 62.4 jit_solution(5464836588915601141)
XLA Ops:
  0.6 0.0 copy-start
  0.6 0.7 %copy-done = s32[1,8100]{1,0:T(1,128)S(1)} copy-done((s32[1,8100]{1,0:T(1,128)S(1)}, s32[1,8100]{1,0:T(1,128)}, u32[]{:S(2)}) %copy-start) | copy-done | bytes 32424
  1.4 0.2 depths.1.own_ref
  1.6 4.0 %collective-permute-start.2 = (f32[8,128]{1,0:T(8,128)S(1)}, f32[8,128]{1,0:T(8,128)S(1)}, u32[]{:S(2)}, u32[]{:S(2)}) collective-permute-start(f32[8,128]{1,0:T(8,128)S(1)} %depths.1.own_ref), channel_id=1, source_target_pairs={{0,8},{1,9},{2,10},{3,11},{4,12},{5,13},{6,14},{7,15},{8,0},{9,1},... | collective-permute-start | bytes 12296 | tf_op jit(solution)/shard_map/ppermute | solution.py:689
  5.7 1.3 %collective-permute-start.1 = (f32[8,128]{1,0:T(8,128)S(1)}, f32[8,128]{1,0:T(8,128)S(1)}, u32[]{:S(2)}, u32[]{:S(2)}) collective-permute-start(f32[8,128]{1,0:T(8,128)S(1)} %depths.1.own_ref), channel_id=1, source_target_pairs={{1,0},{2,1},{3,2},{4,3},{5,4},{6,5},{7,6},{8,7},{9,8},{10,9},{11,1... | collective-permute-start | bytes 12296 | tf_op jit(solution)/shard_map/ppermute | solution.py:689
  6.9 3.0 %collective-permute-start = (f32[8,128]{1,0:T(8,128)S(1)}, f32[8,128]{1,0:T(8,128)S(1)}, u32[]{:S(2)}, u32[]{:S(2)}) collective-permute-start(f32[8,128]{1,0:T(8,128)S(1)} %depths.1.own_ref), channel_id=1, source_target_pairs={{0,1},{1,2},{2,3},{3,4},{4,5},{5,6},{6,7},{7,8},{8,9},{9,10},{10,1... | collective-permute-start | bytes 12296 | tf_op jit(solution)/shard_map/ppermute | solution.py:689
  10.0 0.0 collective-permute-done.2.rest_2_
  10.0 0.0 collective-permute-done.1.rest_1_
  10.0 0.8 %collective-permute-done.rest_0_ = f32[8,128]{1,0:T(8,128)S(1)} collective-permute-done((f32[8,128]{1,0:T(8,128)S(1)}, f32[8,128]{1,0:T(8,128)S(1)}, u32[]{:S(2)}, u32[]{:S(2)}) %collective-permute-start) | collective-permute-done | bytes 4128 | tf_op jit(solution)/shard_map/ppermute | solution.py:689
  10.8 0.0 copy-start.1
  10.8 0.0 copy-start.2
  10.8 0.7 %copy-done.1 = s32[1,4]{1,0:T(1,128)S(1)} copy-done((s32[1,4]{1,0:T(1,128)S(1)}, s32[1,4]{1,0:T(1,128)}, u32[]{:S(2)}) %copy-start.1) | copy-done | bytes 40
  11.4 0.0 copy-done.2
  11.5 7.9 %columns.1 = (f32[1920,128]{1,0:T(8,128)S(1)}, f32[1920,128]{1,0:T(8,128)S(1)}, f32[4,32,128]{2,1,0:T(8,128)S(1)}, f32[68,128]{1,0:T(8,128)S(1)}, f32[256,128]{1,0:T(8,128)S(1)}, /*index=5*/f32[8,128]{1,0:T(8,128)S(1)}) custom-call(s32[1]{0:T(128)} %bitcast.me_ref, s32[1,4]{1,0:T(1,128)S(1)} %copy-done.1, s32[1,4]{1,0:T(1,128)S(1)} %copy-done.2, ...), custom_call_target="tpu_custom_call" | custom-call | flops 20000000 | bytes 8000000 | tf_op jit(solution)/shard_map/columns/pallas_call | solution.py:666
  19.4 5.8 %collective-permute-start.3 = (f32[68,128]{1,0:T(8,128)S(1)}, f32[68,128]{1,0:T(8,128)S(1)}, u32[]{:S(2)}, u32[]{:S(2)}) collective-permute-start(f32[68,128]{1,0:T(8,128)S(1)} %get-tuple-element.15.rest_0_), channel_id=1, source_target_pairs={{0,8},{1,9},{2,10},{3,11},{4,12},{5,13},{6,14},{7,15},{8,0},{9,1},... | collective-permute-start | bytes 104456 | tf_op jit(solution)/shard_map/ppermute | solution.py:631
  25.2 2.0 %collective-permute-done.3.rest_1_ = f32[68,128]{1,0:T(8,128)S(1)} collective-permute-done((f32[68,128]{1,0:T(8,128)S(1)}, f32[68,128]{1,0:T(8,128)S(1)}, u32[]{:S(2)}, u32[]{:S(2)}) %collective-permute-start.3) | collective-permute-done | bytes 34848 | tf_op jit(solution)/shard_map/ppermute | solution.py:631
  27.1 2.2 %collective-permute-start.4 = (f32[136,128]{1,0:T(8,128)S(1)}, f32[136,128]{1,0:T(8,128)S(1)}, u32[]{:S(2)}, u32[]{:S(2)}) collective-permute-start(f32[136,128]{1,0:T(8,128)S(1)} %pad_maximum_fusion.2), channel_id=1, source_target_pairs={{0,4},{1,5},{2,6},{3,7},{4,0},{5,1},{6,2},{7,3},{8,12},{9,13},{10,... | collective-permute-start | bytes 208904 | tf_op jit(solution)/shard_map/ppermute | solution.py:631
  29.3 2.3 %collective-permute-done.4.rest_2_ = f32[136,128]{1,0:T(8,128)S(1)} collective-permute-done((f32[136,128]{1,0:T(8,128)S(1)}, f32[136,128]{1,0:T(8,128)S(1)}, u32[]{:S(2)}, u32[]{:S(2)}) %collective-permute-start.4) | collective-permute-done | bytes 69664 | tf_op jit(solution)/shard_map/ppermute | solution.py:631
  31.6 0.7 %collective-permute-start.5 = (f32[272,128]{1,0:T(8,128)S(1)}, f32[272,128]{1,0:T(8,128)S(1)}, u32[]{:S(2)}, u32[]{:S(2)}) collective-permute-start(f32[272,128]{1,0:T(8,128)S(1)} %pad_maximum_fusion.1), channel_id=1, source_target_pairs={{0,2},{1,3},{2,0},{3,1},{4,6},{5,7},{6,4},{7,5},{8,10},{9,11},{10,... | collective-permute-start | bytes 417800 | tf_op jit(solution)/shard_map/ppermute | solution.py:631
  32.3 4.4 %collective-permute-done.5.rest_3_ = f32[272,128]{1,0:T(8,128)S(1)} collective-permute-done((f32[272,128]{1,0:T(8,128)S(1)}, f32[272,128]{1,0:T(8,128)S(1)}, u32[]{:S(2)}, u32[]{:S(2)}) %collective-permute-start.5) | collective-permute-done | bytes 139296 | tf_op jit(solution)/shard_map/ppermute | solution.py:631
  36.8 0.1 collective-permute-start.6
  36.8 1.5 %collective-permute-done.6.rest_4_ = f32[544,128]{1,0:T(8,128)S(1)} collective-permute-done((f32[544,128]{1,0:T(8,128)S(1)}, f32[544,128]{1,0:T(8,128)S(1)}, u32[]{:S(2)}, u32[]{:S(2)}) %collective-permute-start.6) | collective-permute-done | bytes 278560 | tf_op jit(solution)/shard_map/ppermute | solution.py:631
  38.4 2.6 %krylov.1 = (f32[4,64,128]{2,1,0:T(8,128)S(1)}, f32[4,64,128]{2,1,0:T(8,128)S(1)}, f32[4,8,128]{2,1,0:T(8,128)S(1)}, f32[32,128]{1,0:T(8,128)S(1)}) custom-call(s32[1]{0:T(128)} %bitcast.me_ref, f32[256,128]{1,0:T(8,128)S(1)} %get-tuple-element.14.dense_ref.rest_2_, f32[68,128]{1,0:T(8,128)S(1)} %get-tuple-element.15.rest_0_, ...), custom_call_target="tpu_custom_call" | custom-call | flops 1000000 | bytes 1000000 | tf_op jit(solution)/shard_map/krylov/pallas_call | solution.py:666
  41.0 3.3 %collective-permute-start.7 = (f32[32,128]{1,0:T(8,128)S(1)}, f32[32,128]{1,0:T(8,128)S(1)}, u32[]{:S(2)}, u32[]{:S(2)}) collective-permute-start(f32[32,128]{1,0:T(8,128)S(1)} %get-tuple-element.16), channel_id=1, source_target_pairs={{0,8},{1,9},{2,10},{3,11},{4,12},{5,13},{6,14},{7,15},{8,0},{9,1},... | collective-permute-start | bytes 49160 | tf_op jit(solution)/shard_map/ppermute | solution.py:631
  44.3 0.1 collective-permute-start.13
  44.4 1.3 %collective-permute-start.12 = (f32[4,32,128]{2,1,0:T(8,128)S(1)}, f32[4,32,128]{2,1,0:T(8,128)S(1)}, u32[]{:S(2)}, u32[]{:S(2)}) collective-permute-start(f32[4,32,128]{2,1,0:T(8,128)S(1)} %get-tuple-element.23.rest_9_), channel_id=1, source_target_pairs={{1,0},{2,1},{3,2},{4,3},{5,4},{6,5},{7,6},{8,7},{9,8},{10,9},{11,1... | collective-permute-start | bytes 196616 | tf_op jit(solution)/shard_map/ppermute | solution.py:689
  45.6 3.0 %collective-permute-start.11 = (f32[4,32,128]{2,1,0:T(8,128)S(1)}, f32[4,32,128]{2,1,0:T(8,128)S(1)}, u32[]{:S(2)}, u32[]{:S(2)}) collective-permute-start(f32[4,32,128]{2,1,0:T(8,128)S(1)} %get-tuple-element.23.rest_9_), channel_id=1, source_target_pairs={{0,1},{1,2},{2,3},{3,4},{4,5},{5,6},{6,7},{7,8},{8,9},{9,10},{10,1... | collective-permute-start | bytes 196616 | tf_op jit(solution)/shard_map/ppermute | solution.py:689
  48.7 0.0 collective-permute-done.7
  48.7 1.7 %collective-permute-start.8 = (f32[32,128]{1,0:T(8,128)S(1)}, f32[32,128]{1,0:T(8,128)S(1)}, u32[]{:S(2)}, u32[]{:S(2)}) collective-permute-start(f32[32,128]{1,0:T(8,128)S(1)} %add.9), channel_id=1, source_target_pairs={{0,4},{1,5},{2,6},{3,7},{4,0},{5,1},{6,2},{7,3},{8,12},{9,13},{10,... | collective-permute-start | bytes 49160 | tf_op jit(solution)/shard_map/ppermute | solution.py:631
  50.4 2.1 %collective-permute-done.8 = f32[32,128]{1,0:T(8,128)S(1)} collective-permute-done((f32[32,128]{1,0:T(8,128)S(1)}, f32[32,128]{1,0:T(8,128)S(1)}, u32[]{:S(2)}, u32[]{:S(2)}) %collective-permute-start.8) | collective-permute-done | bytes 16416 | tf_op jit(solution)/shard_map/ppermute | solution.py:631
  52.6 0.9 %collective-permute-start.9 = (f32[32,128]{1,0:T(8,128)S(1)}, f32[32,128]{1,0:T(8,128)S(1)}, u32[]{:S(2)}, u32[]{:S(2)}) collective-permute-start(f32[32,128]{1,0:T(8,128)S(1)} %add.10), channel_id=1, source_target_pairs={{0,2},{1,3},{2,0},{3,1},{4,6},{5,7},{6,4},{7,5},{8,10},{9,11},{10,... | collective-permute-start | bytes 49160 | tf_op jit(solution)/shard_map/ppermute | solution.py:631
  53.5 2.8 %collective-permute-done.9 = f32[32,128]{1,0:T(8,128)S(1)} collective-permute-done((f32[32,128]{1,0:T(8,128)S(1)}, f32[32,128]{1,0:T(8,128)S(1)}, u32[]{:S(2)}, u32[]{:S(2)}) %collective-permute-start.9) | collective-permute-done | bytes 16416 | tf_op jit(solution)/shard_map/ppermute | solution.py:631
  56.3 0.0 collective-permute-start.10
  56.3 0.0 collective-permute-done.13.rest_12_
  56.3 0.0 collective-permute-done.12.rest_11_
  56.3 0.0 collective-permute-done.11.rest_10_
  56.3 1.1 %collective-permute-done.10.rest_1_ = f32[32,128]{1,0:T(8,128)S(1)} collective-permute-done((f32[32,128]{1,0:T(8,128)S(1)}, f32[32,128]{1,0:T(8,128)S(1)}, u32[]{:S(2)}, u32[]{:S(2)}) %collective-permute-start.10) | collective-permute-done | bytes 16416 | tf_op jit(solution)/shard_map/ppermute | solution.py:631
  57.5 4.9 %gradient.1 = (f32[1,8100]{1,0:T(1,128)}, f32[30,1,8100]{2,1,0:T(1,128)}) custom-call(s32[1]{0:T(128)} %bitcast.me_ref, s32[1,4]{1,0:T(1,128)S(1)} %copy-done.1, s32[1,4]{1,0:T(1,128)S(1)} %copy-done.2, f32[32,128]{1,0:T(8,128)S(1)} %add.11.rest_0_, f32[32,128]{1,0:T(8,128)S(1)} %collective-permute-done.10.rest_1_, ...), custom_call_target="tpu_custom_call" | custom-call | flops 10000000 | bytes 4000000 | tf_op jit(solution)/shard_map/gradient/pallas_call | solution.py:666
  (6 shorter events, 0.1 us)
Async XLA Ops:
  0.6 0.8 %copy-start = (s32[1,8100]{1,0:T(1,128)S(1)}, s32[1,8100]{1,0:T(1,128)}, u32[]{:S(2)}) copy-start(s32[1,8100]{1,0:T(1,128)} %rest_6_.1) | copy-start | bytes 97204
  1.6 8.4 %collective-permute-start.2 = (f32[8,128]{1,0:T(8,128)S(1)}, f32[8,128]{1,0:T(8,128)S(1)}, u32[]{:S(2)}, u32[]{:S(2)}) collective-permute-start(f32[8,128]{1,0:T(8,128)S(1)} %depths.1.own_ref), channel_id=1, source_target_pairs={{0,8},{1,9},{2,10},{3,11},{4,12},{5,13},{6,14},{7,15},{8,0},{9,1},... | collective-permute-start | bytes 12296 | tf_op jit(solution)/shard_map/ppermute | solution.py:689
  5.7 4.3 %collective-permute-start.1 = (f32[8,128]{1,0:T(8,128)S(1)}, f32[8,128]{1,0:T(8,128)S(1)}, u32[]{:S(2)}, u32[]{:S(2)}) collective-permute-start(f32[8,128]{1,0:T(8,128)S(1)} %depths.1.own_ref), channel_id=1, source_target_pairs={{1,0},{2,1},{3,2},{4,3},{5,4},{6,5},{7,6},{8,7},{9,8},{10,9},{11,1... | collective-permute-start | bytes 12296 | tf_op jit(solution)/shard_map/ppermute | solution.py:689
  6.9 3.8 %collective-permute-start = (f32[8,128]{1,0:T(8,128)S(1)}, f32[8,128]{1,0:T(8,128)S(1)}, u32[]{:S(2)}, u32[]{:S(2)}) collective-permute-start(f32[8,128]{1,0:T(8,128)S(1)} %depths.1.own_ref), channel_id=1, source_target_pairs={{0,1},{1,2},{2,3},{3,4},{4,5},{5,6},{6,7},{7,8},{8,9},{9,10},{10,1... | collective-permute-start | bytes 12296 | tf_op jit(solution)/shard_map/ppermute | solution.py:689
  10.8 0.7 %copy-start.1 = (s32[1,4]{1,0:T(1,128)S(1)}, s32[1,4]{1,0:T(1,128)}, u32[]{:S(2)}) copy-start(s32[1,4]{1,0:T(1,128)} %adj_ref.3) | copy-start | bytes 52
  10.8 0.7 %copy-start.2 = (s32[1,4]{1,0:T(1,128)S(1)}, s32[1,4]{1,0:T(1,128)}, u32[]{:S(2)}) copy-start(s32[1,4]{1,0:T(1,128)} %flag_ref.3) | copy-start | bytes 52
  19.4 7.8 %collective-permute-start.3 = (f32[68,128]{1,0:T(8,128)S(1)}, f32[68,128]{1,0:T(8,128)S(1)}, u32[]{:S(2)}, u32[]{:S(2)}) collective-permute-start(f32[68,128]{1,0:T(8,128)S(1)} %get-tuple-element.15.rest_0_), channel_id=1, source_target_pairs={{0,8},{1,9},{2,10},{3,11},{4,12},{5,13},{6,14},{7,15},{8,0},{9,1},... | collective-permute-start | bytes 104456 | tf_op jit(solution)/shard_map/ppermute | solution.py:631
  27.1 4.5 %collective-permute-start.4 = (f32[136,128]{1,0:T(8,128)S(1)}, f32[136,128]{1,0:T(8,128)S(1)}, u32[]{:S(2)}, u32[]{:S(2)}) collective-permute-start(f32[136,128]{1,0:T(8,128)S(1)} %pad_maximum_fusion.2), channel_id=1, source_target_pairs={{0,4},{1,5},{2,6},{3,7},{4,0},{5,1},{6,2},{7,3},{8,12},{9,13},{10,... | collective-permute-start | bytes 208904 | tf_op jit(solution)/shard_map/ppermute | solution.py:631
  31.6 5.1 %collective-permute-start.5 = (f32[272,128]{1,0:T(8,128)S(1)}, f32[272,128]{1,0:T(8,128)S(1)}, u32[]{:S(2)}, u32[]{:S(2)}) collective-permute-start(f32[272,128]{1,0:T(8,128)S(1)} %pad_maximum_fusion.1), channel_id=1, source_target_pairs={{0,2},{1,3},{2,0},{3,1},{4,6},{5,7},{6,4},{7,5},{8,10},{9,11},{10,... | collective-permute-start | bytes 417800 | tf_op jit(solution)/shard_map/ppermute | solution.py:631
  36.8 1.6 %collective-permute-start.6 = (f32[544,128]{1,0:T(8,128)S(1)}, f32[544,128]{1,0:T(8,128)S(1)}, u32[]{:S(2)}, u32[]{:S(2)}) collective-permute-start(f32[544,128]{1,0:T(8,128)S(1)} %pad_maximum_fusion), channel_id=1, source_target_pairs={{0,1},{1,0},{2,3},{3,2},{4,5},{5,4},{6,7},{7,6},{8,9},{9,8},{10,11... | collective-permute-start | bytes 835592 | tf_op jit(solution)/shard_map/ppermute | solution.py:631
  41.0 7.7 %collective-permute-start.7 = (f32[32,128]{1,0:T(8,128)S(1)}, f32[32,128]{1,0:T(8,128)S(1)}, u32[]{:S(2)}, u32[]{:S(2)}) collective-permute-start(f32[32,128]{1,0:T(8,128)S(1)} %get-tuple-element.16), channel_id=1, source_target_pairs={{0,8},{1,9},{2,10},{3,11},{4,12},{5,13},{6,14},{7,15},{8,0},{9,1},... | collective-permute-start | bytes 49160 | tf_op jit(solution)/shard_map/ppermute | solution.py:631
  44.3 12.0 %collective-permute-start.13 = (f32[4,32,128]{2,1,0:T(8,128)S(1)}, f32[4,32,128]{2,1,0:T(8,128)S(1)}, u32[]{:S(2)}, u32[]{:S(2)}) collective-permute-start(f32[4,32,128]{2,1,0:T(8,128)S(1)} %get-tuple-element.23.rest_9_), channel_id=1, source_target_pairs={{0,8},{1,9},{2,10},{3,11},{4,12},{5,13},{6,14},{7,15},{8,0},{9,1},... | collective-permute-start | bytes 196616 | tf_op jit(solution)/shard_map/ppermute | solution.py:689
  44.4 12.0 %collective-permute-start.12 = (f32[4,32,128]{2,1,0:T(8,128)S(1)}, f32[4,32,128]{2,1,0:T(8,128)S(1)}, u32[]{:S(2)}, u32[]{:S(2)}) collective-permute-start(f32[4,32,128]{2,1,0:T(8,128)S(1)} %get-tuple-element.23.rest_9_), channel_id=1, source_target_pairs={{1,0},{2,1},{3,2},{4,3},{5,4},{6,5},{7,6},{8,7},{9,8},{10,9},{11,1... | collective-permute-start | bytes 196616 | tf_op jit(solution)/shard_map/ppermute | solution.py:689
  45.6 10.7 %collective-permute-start.11 = (f32[4,32,128]{2,1,0:T(8,128)S(1)}, f32[4,32,128]{2,1,0:T(8,128)S(1)}, u32[]{:S(2)}, u32[]{:S(2)}) collective-permute-start(f32[4,32,128]{2,1,0:T(8,128)S(1)} %get-tuple-element.23.rest_9_), channel_id=1, source_target_pairs={{0,1},{1,2},{2,3},{3,4},{4,5},{5,6},{6,7},{7,8},{8,9},{9,10},{10,1... | collective-permute-start | bytes 196616 | tf_op jit(solution)/shard_map/ppermute | solution.py:689
  48.7 3.9 %collective-permute-start.8 = (f32[32,128]{1,0:T(8,128)S(1)}, f32[32,128]{1,0:T(8,128)S(1)}, u32[]{:S(2)}, u32[]{:S(2)}) collective-permute-start(f32[32,128]{1,0:T(8,128)S(1)} %add.9), channel_id=1, source_target_pairs={{0,4},{1,5},{2,6},{3,7},{4,0},{5,1},{6,2},{7,3},{8,12},{9,13},{10,... | collective-permute-start | bytes 49160 | tf_op jit(solution)/shard_map/ppermute | solution.py:631
  52.6 3.7 %collective-permute-start.9 = (f32[32,128]{1,0:T(8,128)S(1)}, f32[32,128]{1,0:T(8,128)S(1)}, u32[]{:S(2)}, u32[]{:S(2)}) collective-permute-start(f32[32,128]{1,0:T(8,128)S(1)} %add.10), channel_id=1, source_target_pairs={{0,2},{1,3},{2,0},{3,1},{4,6},{5,7},{6,4},{7,5},{8,10},{9,11},{10,... | collective-permute-start | bytes 49160 | tf_op jit(solution)/shard_map/ppermute | solution.py:631
  56.3 1.2 %collective-permute-start.10 = (f32[32,128]{1,0:T(8,128)S(1)}, f32[32,128]{1,0:T(8,128)S(1)}, u32[]{:S(2)}, u32[]{:S(2)}) collective-permute-start(f32[32,128]{1,0:T(8,128)S(1)} %add.11.rest_0_), channel_id=1, source_target_pairs={{0,1},{1,0},{2,3},{3,2},{4,5},{5,4},{6,7},{7,6},{8,9},{9,8},{10,11... | collective-permute-start | bytes 49160 | tf_op jit(solution)/shard_map/ppermute | solution.py:631

commit v5 on v4

--- a/solution.py
+++ b/solution.py
@@ -195,11 +195,11 @@
     out_ref[4:8, :] = jnp.zeros((4, LANES), F32)
 
 
-def columns_kernel(shifts, tiles, levels, me_ref, adj_ref, flag_ref, own_ref, *rest):
-    met_refs = rest[: len(shifts)]
-    k_hbm, s_hbm, t_hbm, depth_hbm, d_hbm, b_hbm = rest[len(shifts) : len(shifts) + 6]
-    a_ref, q_ref, as_ref, blk_ref, dense_ref, reach_ref = rest[len(shifts) + 6 : len(shifts) + 12]
-    k_ref, s_ref, t_ref, depth_ref, d_ref, b_ref, g_ref, z_ref, ts_ref, sems = rest[len(shifts) + 12 :]
+def columns_kernel(exchanges, levels, me_ref, adj_ref, flag_ref, own_ref, *rest):
+    met_refs = rest[: len(exchanges)]
+    k_hbm, s_hbm, t_hbm, depth_hbm, d_hbm, b_hbm = rest[len(exchanges) : len(exchanges) + 6]
+    a_ref, q_ref, as_ref, blk_ref, dense_ref, reach_ref = rest[len(exchanges) + 6 : len(exchanges) + 12]
+    k_ref, s_ref, t_ref, depth_ref, d_ref, b_ref, g_ref, z_ref, ts_ref, sems = rest[len(exchanges) + 12 :]
     parts = 3
     third = levels // parts
     surface = [
@@ -299,10 +299,7 @@
     for side in range(4):
         neighbour = adj_ref[0, side]
         flag = flag_ref[0, side]
-        met = met_refs[0][pl.ds(flag >> 1, 1), :]
-        for number in range(1, len(shifts)):
-            hit = neighbour == lax.rem(me + tiles - shifts[number], tiles)
-            met = jnp.where(hit, met_refs[number][pl.ds(flag >> 1, 1), :], met)
+        met = pick(exchanges, me, neighbour, lambda n: met_refs[n][pl.ds(flag >> 1, 1), :])
         met = take(jnp.broadcast_to(met, (8, LANES)), seam_index(flag))[0:1]
         reach = jnp.where(neighbour >= 0, jnp.minimum(met, own_ref[side : side + 1, :]), 0.0)
         reach_ref[side : side + 1, :] = reach
@@ -322,11 +319,17 @@
     write_frames(dense_ref, ROWS, blk_ref, 48, za_ref, zb_ref, 3)
 
 
-def pick(refs, shifts, tiles, me, neighbour, side_met):
-    value = refs[0][side_met]
-    for number in range(1, len(shifts)):
-        hit = neighbour == lax.rem(me + tiles - shifts[number], tiles)
-        value = jnp.where(hit, refs[number][side_met], value)
+def partner(exchange, me):
+    stride, odd = exchange
+    if not odd:
+        return me ^ stride
+    return jnp.where(((me // stride) & 1) == 1, me + stride, me - stride)
+
+
+def pick(exchanges, me, neighbour, lines_of):
+    value = lines_of(0)
+    for number in range(1, len(exchanges)):
+        value = jnp.where(neighbour == partner(exchanges[number], me), lines_of(number), value)
     return value
 
 
@@ -560,12 +563,12 @@
     return out
 
 
-def gradient_kernel(shifts, tiles, levels, grams, me_ref, adj_ref, flag_ref, *rest):
+def gradient_kernel(exchanges, levels, grams, me_ref, adj_ref, flag_ref, *rest):
     gram_refs = rest[:grams]
     rest = rest[grams:]
     dense_ref, va_ref, v_ref, line_ref, reach_ref, a_ref, q_ref, as_ref = rest[:8]
-    refs = rest[8 : 8 + len(shifts)]
-    height_ref, out_ref, gram_ref, sum_ref, w_ref, h_ref = rest[8 + len(shifts) :]
+    refs = rest[8 : 8 + len(exchanges)]
+    height_ref, out_ref, gram_ref, sum_ref, w_ref, h_ref = rest[8 + len(exchanges) :]
     me = me_ref[0]
     total_gram(gram_refs, gram_ref)
     store_rows(height_ref, combine(coefficients(gram_ref, 16), va_ref))
@@ -593,7 +596,7 @@
         neighbour = adj_ref[0, side]
         flag = flag_ref[0, side]
         index = seam_index(flag)
-        other = take(pick(refs, shifts, tiles, me, neighbour, flag >> 1), index)
+        other = take(pick(exchanges, me, neighbour, lambda n: refs[n][flag >> 1]), index)
         other = other + sum_ref[side : side + 1, :] * level_scale
         own = as_ref[side] + w_ref[4, 8 + side : 9 + side, :]
         fluxes.append(jnp.where(reach_ref[side : side + 1, :] > level, other - own, 0.0))
@@ -622,8 +625,9 @@
     out = []
     stride = tiles
     while stride > 1:
-        stride //= 2
-        out.append((stride, 2))
+        radix = 4 if stride >= 16 else 2
+        stride //= radix
+        out.append((stride, radix))
     return out
 
 
@@ -674,18 +678,22 @@
             name=name,
         )(*scalars, *arrays, *far)
 
-    offsets = []
-    for offset in (1, -1, ROW_TILES, -ROW_TILES, tiles // 2):
-        if offset % tiles not in [o % tiles for o in offsets] and offset % tiles:
-            offsets.append(offset)
-    shifts = tuple(offset % tiles for offset in offsets)
+    exchanges = []
+    for stride in (1, ROW_TILES, tiles // 2):
+        if (stride, False) not in exchanges and stride < tiles:
+            exchanges.append((stride, False))
+            if stride < ROW_TILES * 2 and stride * 2 < tiles:
+                exchanges.append((stride, True))
+    exchanges = tuple(exchanges)
 
     def to_neighbours(x):
         out = []
-        for offset in offsets:
-            pairs = [(t, t + offset) for t in range(tiles) if 0 <= t + offset < tiles]
-            if 2 * offset == tiles or 2 * offset == -tiles:
-                pairs = [(t, (t + offset) % tiles) for t in range(tiles)]
+        for stride, odd in exchanges:
+            if odd:
+                pairs = [(t, t + stride if (t // stride) % 2 else t - stride) for t in range(tiles)]
+                pairs = [(t, u) for t, u in pairs if 0 <= u < tiles]
+            else:
+                pairs = [(t, t ^ stride) for t in range(tiles)]
             out.append(lax.ppermute(x, "tile", pairs))
         return out
 
@@ -703,7 +711,7 @@
     depths_met = to_neighbours(own_depths)
     far = pltpu.VMEM((levels, 1, CELLS), F32)
     solved, weight, strips, block, dense, reach = call(
-        functools.partial(columns_kernel, shifts, tiles, levels),
+        functools.partial(columns_kernel, exchanges, levels),
         (
             shape(levels * ROWS, LANES),
             shape(levels * ROWS, LANES),
@@ -729,7 +737,17 @@
         "columns",
         2e7,
         8e6,
-        tuple(pltpu.with_memory_space_constraint(v, pltpu.HBM) for v in (by_level(stirring), by_level(sensitivity), by_level(thermal), depth, main_entry, elevation)),
+        tuple(
+            pltpu.with_memory_space_constraint(x, pltpu.HBM)
+            for x in (
+                by_level(stirring),
+                by_level(sensitivity),
+                by_level(thermal),
+                depth,
+                main_entry,
+                elevation,
+            )
+        ),
         48,
     )
     blocks, places = gather_tiles(block, tiles)
@@ -755,7 +773,7 @@
     )
     grams = sum_tiles(gram, tiles)
     height, gradient = call(
-        functools.partial(gradient_kernel, shifts, tiles, levels, len(grams)),
+        functools.partial(gradient_kernel, exchanges, levels, len(grams)),
         (jax.ShapeDtypeStruct(elevation.shape, F32), shape(levels, 1, CELLS)),
         [
             pltpu.VMEM((32, LANES), F32),

time: 62.7 us -> 54.7 us (0.87)
  starting transfers between devices: 27.4 us -> 22.8 us
  waiting for transfers between devices: 17.1 us -> 13.6 us
    ppermute x8 -> x10, waiting for transfers between devices: 16.3 us -> 12.8 us  [swap(): return lax.ppermute(x, 'tile', [(t, t ^ offset) for t in range(tiles)])]
    ppermute x8 -> x10, starting transfers between devices: 14.7 us -> 12 us  [swap(): return lax.ppermute(x, 'tile', [(t, t ^ offset) for t in range(tiles)])]
    ppermute x6, starting transfers between devices: 12.7 us -> 10.8 us  [to_neighbours(): out.append(lax.ppermute(x, 'tile', pairs))]
  transfers between devices with their start and end apart: 14 -> 16, of which waited for: 8 -> 9; matrix products, arithmetic and copies ran while one was open for 0% -> 0% of each run, Pallas kernels for 0% -> 0%
where the time goes in v5:
time: 54.7 us; the launch traced here: 54.4 us
  starting transfers between devices  22.8 us (42%)
  Pallas kernels  15.6 us (29%)
  waiting for transfers between devices  13.6 us (25%)
  local copies, waits for them, and re-layouts  1.73 us (3%)
  between operations  0.73 us (1%)
    pallas_call x4, Pallas kernels, call(): pl.pallas_call(kernel, out_shape=outs, in_specs=[smem] * len(scalars) + [...  15.6 us
    ppermute x10, waiting for transfers between devices, swap(): return lax.ppermute(x, 'tile', [(t, t ^ offset) for t in range(tiles)])  12.8 us
    ppermute x10, starting transfers between devices, swap(): return lax.ppermute(x, 'tile', [(t, t ^ offset) for t in range(tiles)])  12 us
    ppermute x6, starting transfers between devices, to_neighbours(): out.append(lax.ppermute(x, 'tile', pairs))  10.8 us
    unnamed x6, local copies, waits for them, and re-layouts  1.42 us
  transfers between devices with their start and end apart: 16, of which 9 were waited for; matrix products, arithmetic and copies ran while one was open for 0% of the time, Pallas kernels for 0%

profile of v5, /device:TPU:0, one launch (start us, length us, event | category | flops | bytes accessed | tf_op | source)
XLA Modules:
  0.0 54.4 jit_solution(11752790285314694217)
XLA Ops:
  0.6 0.0 copy-start
  0.6 0.7 %copy-done = s32[1,8100]{1,0:T(1,128)S(1)} copy-done((s32[1,8100]{1,0:T(1,128)S(1)}, s32[1,8100]{1,0:T(1,128)}, u32[]{:S(2)}) %copy-start) | copy-done | bytes 32424
  1.4 0.2 depths.1.own_ref
  1.6 4.0 %collective-permute-start.2 = (f32[8,128]{1,0:T(8,128)S(1)}, f32[8,128]{1,0:T(8,128)S(1)}, u32[]{:S(2)}, u32[]{:S(2)}) collective-permute-start(f32[8,128]{1,0:T(8,128)S(1)} %depths.1.own_ref), channel_id=1, source_target_pairs={{0,8},{1,9},{2,10},{3,11},{4,12},{5,13},{6,14},{7,15},{8,0},{9,1},... | collective-permute-start | bytes 12296 | tf_op jit(solution)/shard_map/ppermute | solution.py:697
  5.7 0.6 %collective-permute-start.1 = (f32[8,128]{1,0:T(8,128)S(1)}, f32[8,128]{1,0:T(8,128)S(1)}, u32[]{:S(2)}, u32[]{:S(2)}) collective-permute-start(f32[8,128]{1,0:T(8,128)S(1)} %depths.1.own_ref), channel_id=1, source_target_pairs={{1,2},{2,1},{3,4},{4,3},{5,6},{6,5},{7,8},{8,7},{9,10},{10,9},{11,... | collective-permute-start | bytes 12296 | tf_op jit(solution)/shard_map/ppermute | solution.py:697
  6.3 2.9 %collective-permute-start = (f32[8,128]{1,0:T(8,128)S(1)}, f32[8,128]{1,0:T(8,128)S(1)}, u32[]{:S(2)}, u32[]{:S(2)}) collective-permute-start(f32[8,128]{1,0:T(8,128)S(1)} %depths.1.own_ref), channel_id=1, source_target_pairs={{0,1},{1,0},{2,3},{3,2},{4,5},{5,4},{6,7},{7,6},{8,9},{9,8},{10,11... | collective-permute-start | bytes 12296 | tf_op jit(solution)/shard_map/ppermute | solution.py:697
  9.3 0.0 collective-permute-done.2.rest_2_
  9.3 0.0 collective-permute-done.1.rest_1_
  9.3 0.8 %collective-permute-done.rest_0_ = f32[8,128]{1,0:T(8,128)S(1)} collective-permute-done((f32[8,128]{1,0:T(8,128)S(1)}, f32[8,128]{1,0:T(8,128)S(1)}, u32[]{:S(2)}, u32[]{:S(2)}) %collective-permute-start) | collective-permute-done | bytes 4128 | tf_op jit(solution)/shard_map/ppermute | solution.py:697
  10.1 0.0 copy-start.1
  10.1 0.0 copy-start.2
  10.1 0.7 %copy-done.1 = s32[1,4]{1,0:T(1,128)S(1)} copy-done((s32[1,4]{1,0:T(1,128)S(1)}, s32[1,4]{1,0:T(1,128)}, u32[]{:S(2)}) %copy-start.1) | copy-done | bytes 40
  10.7 0.0 copy-done.2
  10.8 7.9 %columns.1 = (f32[1920,128]{1,0:T(8,128)S(1)}, f32[1920,128]{1,0:T(8,128)S(1)}, f32[4,32,128]{2,1,0:T(8,128)S(1)}, f32[68,128]{1,0:T(8,128)S(1)}, f32[256,128]{1,0:T(8,128)S(1)}, /*index=5*/f32[8,128]{1,0:T(8,128)S(1)}) custom-call(s32[1]{0:T(128)} %bitcast.me_ref, s32[1,4]{1,0:T(1,128)S(1)} %copy-done.1, s32[1,4]{1,0:T(1,128)S(1)} %copy-done.2, ...), custom_call_target="tpu_custom_call" | custom-call | flops 20000000 | bytes 8000000 | tf_op jit(solution)/shard_map/columns/pallas_call | solution.py:670
  18.6 2.8 %collective-permute-start.5 = (f32[68,128]{1,0:T(8,128)S(1)}, f32[68,128]{1,0:T(8,128)S(1)}, u32[]{:S(2)}, u32[]{:S(2)}) collective-permute-start(f32[68,128]{1,0:T(8,128)S(1)} %get-tuple-element.15.rest_0_), channel_id=1, source_target_pairs={{0,12},{1,13},{2,14},{3,15},{4,8},{5,9},{6,10},{7,11},{8,4},{9,5},... | collective-permute-start | bytes 104456 | tf_op jit(solution)/shard_map/ppermute | solution.py:635
  21.5 1.7 %collective-permute-start.4 = (f32[68,128]{1,0:T(8,128)S(1)}, f32[68,128]{1,0:T(8,128)S(1)}, u32[]{:S(2)}, u32[]{:S(2)}) collective-permute-start(f32[68,128]{1,0:T(8,128)S(1)} %get-tuple-element.15.rest_0_), channel_id=1, source_target_pairs={{0,8},{1,9},{2,10},{3,11},{4,12},{5,13},{6,14},{7,15},{8,0},{9,1},... | collective-permute-start | bytes 104456 | tf_op jit(solution)/shard_map/ppermute | solution.py:635
  23.1 0.0 collective-permute-start.3
  23.1 1.7 %collective-permute-done.5.rest_3_ = f32[68,128]{1,0:T(8,128)S(1)} collective-permute-done((f32[68,128]{1,0:T(8,128)S(1)}, f32[68,128]{1,0:T(8,128)S(1)}, u32[]{:S(2)}, u32[]{:S(2)}) %collective-permute-start.5) | collective-permute-done | bytes 34848 | tf_op jit(solution)/shard_map/ppermute | solution.py:635
  24.8 1.6 %collective-permute-done.4.rest_2_ = f32[68,128]{1,0:T(8,128)S(1)} collective-permute-done((f32[68,128]{1,0:T(8,128)S(1)}, f32[68,128]{1,0:T(8,128)S(1)}, u32[]{:S(2)}, u32[]{:S(2)}) %collective-permute-start.4) | collective-permute-done | bytes 34848 | tf_op jit(solution)/shard_map/ppermute | solution.py:635
  26.4 0.7 %collective-permute-done.3.rest_1_ = f32[68,128]{1,0:T(8,128)S(1)} collective-permute-done((f32[68,128]{1,0:T(8,128)S(1)}, f32[68,128]{1,0:T(8,128)S(1)}, u32[]{:S(2)}, u32[]{:S(2)}) %collective-permute-start.3) | collective-permute-done | bytes 34848 | tf_op jit(solution)/shard_map/ppermute | solution.py:635
  27.1 1.1 %collective-permute-start.6 = (f32[272,128]{1,0:T(8,128)S(1)}, f32[272,128]{1,0:T(8,128)S(1)}, u32[]{:S(2)}, u32[]{:S(2)}) collective-permute-start(f32[272,128]{1,0:T(8,128)S(1)} %pad_maximum_fusion), channel_id=1, source_target_pairs={{0,2},{1,3},{2,0},{3,1},{4,6},{5,7},{6,4},{7,5},{8,10},{9,11},{10,... | collective-permute-start | bytes 417800 | tf_op jit(solution)/shard_map/ppermute | solution.py:635
  28.2 4.0 %collective-permute-done.6.rest_4_ = f32[272,128]{1,0:T(8,128)S(1)} collective-permute-done((f32[272,128]{1,0:T(8,128)S(1)}, f32[272,128]{1,0:T(8,128)S(1)}, u32[]{:S(2)}, u32[]{:S(2)}) %collective-permute-start.6) | collective-permute-done | bytes 139296 | tf_op jit(solution)/shard_map/ppermute | solution.py:635
  32.2 0.3 concatenate.7
  32.6 0.1 collective-permute-start.7
  32.6 1.5 %collective-permute-done.7.rest_5_ = f32[544,128]{1,0:T(8,128)S(1)} collective-permute-done((f32[544,128]{1,0:T(8,128)S(1)}, f32[544,128]{1,0:T(8,128)S(1)}, u32[]{:S(2)}, u32[]{:S(2)}) %collective-permute-start.7) | collective-permute-done | bytes 278560 | tf_op jit(solution)/shard_map/ppermute | solution.py:635
  34.2 2.6 %krylov.1 = (f32[4,64,128]{2,1,0:T(8,128)S(1)}, f32[4,64,128]{2,1,0:T(8,128)S(1)}, f32[4,8,128]{2,1,0:T(8,128)S(1)}, f32[32,128]{1,0:T(8,128)S(1)}) custom-call(s32[1]{0:T(128)} %bitcast.me_ref, f32[256,128]{1,0:T(8,128)S(1)} %get-tuple-element.14.dense_ref.rest_2_, f32[68,128]{1,0:T(8,128)S(1)} %get-tuple-element.15.rest_0_, ...), custom_call_target="tpu_custom_call" | custom-call | flops 1000000 | bytes 1000000 | tf_op jit(solution)/shard_map/krylov/pallas_call | solution.py:670
  36.8 1.1 %collective-permute-start.10 = (f32[32,128]{1,0:T(8,128)S(1)}, f32[32,128]{1,0:T(8,128)S(1)}, u32[]{:S(2)}, u32[]{:S(2)}) collective-permute-start(f32[32,128]{1,0:T(8,128)S(1)} %get-tuple-element.16), channel_id=1, source_target_pairs={{0,12},{1,13},{2,14},{3,15},{4,8},{5,9},{6,10},{7,11},{8,4},{9,5},... | collective-permute-start | bytes 49160 | tf_op jit(solution)/shard_map/ppermute | solution.py:635
  37.9 0.8 %collective-permute-start.9 = (f32[32,128]{1,0:T(8,128)S(1)}, f32[32,128]{1,0:T(8,128)S(1)}, u32[]{:S(2)}, u32[]{:S(2)}) collective-permute-start(f32[32,128]{1,0:T(8,128)S(1)} %get-tuple-element.16), channel_id=1, source_target_pairs={{0,8},{1,9},{2,10},{3,11},{4,12},{5,13},{6,14},{7,15},{8,0},{9,1},... | collective-permute-start | bytes 49160 | tf_op jit(solution)/shard_map/ppermute | solution.py:635
  38.7 2.5 %collective-permute-start.8 = (f32[32,128]{1,0:T(8,128)S(1)}, f32[32,128]{1,0:T(8,128)S(1)}, u32[]{:S(2)}, u32[]{:S(2)}) collective-permute-start(f32[32,128]{1,0:T(8,128)S(1)} %get-tuple-element.16), channel_id=1, source_target_pairs={{0,4},{1,5},{2,6},{3,7},{4,0},{5,1},{6,2},{7,3},{8,12},{9,13},{10,... | collective-permute-start | bytes 49160 | tf_op jit(solution)/shard_map/ppermute | solution.py:635
  41.2 0.3 collective-permute-start.15
  41.6 0.7 %collective-permute-start.14 = (f32[4,32,128]{2,1,0:T(8,128)S(1)}, f32[4,32,128]{2,1,0:T(8,128)S(1)}, u32[]{:S(2)}, u32[]{:S(2)}) collective-permute-start(f32[4,32,128]{2,1,0:T(8,128)S(1)} %get-tuple-element.23.rest_9_), channel_id=1, source_target_pairs={{1,2},{2,1},{3,4},{4,3},{5,6},{6,5},{7,8},{8,7},{9,10},{10,9},{11,... | collective-permute-start | bytes 196616 | tf_op jit(solution)/shard_map/ppermute | solution.py:697
  42.2 0.2 collective-permute-done.10
  42.4 2.2 %collective-permute-start.13 = (f32[4,32,128]{2,1,0:T(8,128)S(1)}, f32[4,32,128]{2,1,0:T(8,128)S(1)}, u32[]{:S(2)}, u32[]{:S(2)}) collective-permute-start(f32[4,32,128]{2,1,0:T(8,128)S(1)} %get-tuple-element.23.rest_9_), channel_id=1, source_target_pairs={{0,1},{1,0},{2,3},{3,2},{4,5},{5,4},{6,7},{7,6},{8,9},{9,8},{10,11... | collective-permute-start | bytes 196616 | tf_op jit(solution)/shard_map/ppermute | solution.py:697
  44.6 0.0 collective-permute-done.9
  44.6 0.0 collective-permute-done.8
  44.6 1.9 %collective-permute-start.11 = (f32[32,128]{1,0:T(8,128)S(1)}, f32[32,128]{1,0:T(8,128)S(1)}, u32[]{:S(2)}, u32[]{:S(2)}) collective-permute-start(f32[32,128]{1,0:T(8,128)S(1)} %add_add_fusion), channel_id=1, source_target_pairs={{0,2},{1,3},{2,0},{3,1},{4,6},{5,7},{6,4},{7,5},{8,10},{9,11},{10,... | collective-permute-start | bytes 49160 | tf_op jit(solution)/shard_map/ppermute | solution.py:635
  46.5 1.9 %collective-permute-done.11 = f32[32,128]{1,0:T(8,128)S(1)} collective-permute-done((f32[32,128]{1,0:T(8,128)S(1)}, f32[32,128]{1,0:T(8,128)S(1)}, u32[]{:S(2)}, u32[]{:S(2)}) %collective-permute-start.11) | collective-permute-done | bytes 16416 | tf_op jit(solution)/shard_map/ppermute | solution.py:635
  48.4 0.0 collective-permute-start.12
  48.4 0.0 collective-permute-done.15.rest_12_
  48.4 0.0 collective-permute-done.14.rest_11_
  48.4 0.0 collective-permute-done.13.rest_10_
  48.4 1.1 %collective-permute-done.12.rest_1_ = f32[32,128]{1,0:T(8,128)S(1)} collective-permute-done((f32[32,128]{1,0:T(8,128)S(1)}, f32[32,128]{1,0:T(8,128)S(1)}, u32[]{:S(2)}, u32[]{:S(2)}) %collective-permute-start.12) | collective-permute-done | bytes 16416 | tf_op jit(solution)/shard_map/ppermute | solution.py:635
  49.6 4.8 %gradient.1 = (f32[1,8100]{1,0:T(1,128)}, f32[30,1,8100]{2,1,0:T(1,128)}) custom-call(s32[1]{0:T(128)} %bitcast.me_ref, s32[1,4]{1,0:T(1,128)S(1)} %copy-done.1, s32[1,4]{1,0:T(1,128)S(1)} %copy-done.2, f32[32,128]{1,0:T(8,128)S(1)} %add.15.rest_0_, f32[32,128]{1,0:T(8,128)S(1)} %collective-permute-done.12.rest_1_, ...), custom_call_target="tpu_custom_call" | custom-call | flops 10000000 | bytes 4000000 | tf_op jit(solution)/shard_map/gradient/pallas_call | solution.py:670
  (3 shorter events, 0.0 us)
Async XLA Ops:
  0.6 0.8 %copy-start = (s32[1,8100]{1,0:T(1,128)S(1)}, s32[1,8100]{1,0:T(1,128)}, u32[]{:S(2)}) copy-start(s32[1,8100]{1,0:T(1,128)} %rest_6_.1) | copy-start | bytes 97204
  1.6 7.7 %collective-permute-start.2 = (f32[8,128]{1,0:T(8,128)S(1)}, f32[8,128]{1,0:T(8,128)S(1)}, u32[]{:S(2)}, u32[]{:S(2)}) collective-permute-start(f32[8,128]{1,0:T(8,128)S(1)} %depths.1.own_ref), channel_id=1, source_target_pairs={{0,8},{1,9},{2,10},{3,11},{4,12},{5,13},{6,14},{7,15},{8,0},{9,1},... | collective-permute-start | bytes 12296 | tf_op jit(solution)/shard_map/ppermute | solution.py:697
  5.7 3.6 %collective-permute-start.1 = (f32[8,128]{1,0:T(8,128)S(1)}, f32[8,128]{1,0:T(8,128)S(1)}, u32[]{:S(2)}, u32[]{:S(2)}) collective-permute-start(f32[8,128]{1,0:T(8,128)S(1)} %depths.1.own_ref), channel_id=1, source_target_pairs={{1,2},{2,1},{3,4},{4,3},{5,6},{6,5},{7,8},{8,7},{9,10},{10,9},{11,... | collective-permute-start | bytes 12296 | tf_op jit(solution)/shard_map/ppermute | solution.py:697
  6.3 3.8 %collective-permute-start = (f32[8,128]{1,0:T(8,128)S(1)}, f32[8,128]{1,0:T(8,128)S(1)}, u32[]{:S(2)}, u32[]{:S(2)}) collective-permute-start(f32[8,128]{1,0:T(8,128)S(1)} %depths.1.own_ref), channel_id=1, source_target_pairs={{0,1},{1,0},{2,3},{3,2},{4,5},{5,4},{6,7},{7,6},{8,9},{9,8},{10,11... | collective-permute-start | bytes 12296 | tf_op jit(solution)/shard_map/ppermute | solution.py:697
  10.1 0.7 %copy-start.1 = (s32[1,4]{1,0:T(1,128)S(1)}, s32[1,4]{1,0:T(1,128)}, u32[]{:S(2)}) copy-start(s32[1,4]{1,0:T(1,128)} %adj_ref.3) | copy-start | bytes 52
  10.1 0.7 %copy-start.2 = (s32[1,4]{1,0:T(1,128)S(1)}, s32[1,4]{1,0:T(1,128)}, u32[]{:S(2)}) copy-start(s32[1,4]{1,0:T(1,128)} %flag_ref.3) | copy-start | bytes 52
  18.6 6.1 %collective-permute-start.5 = (f32[68,128]{1,0:T(8,128)S(1)}, f32[68,128]{1,0:T(8,128)S(1)}, u32[]{:S(2)}, u32[]{:S(2)}) collective-permute-start(f32[68,128]{1,0:T(8,128)S(1)} %get-tuple-element.15.rest_0_), channel_id=1, source_target_pairs={{0,12},{1,13},{2,14},{3,15},{4,8},{5,9},{6,10},{7,11},{8,4},{9,5},... | collective-permute-start | bytes 104456 | tf_op jit(solution)/shard_map/ppermute | solution.py:635
  21.5 5.0 %collective-permute-start.4 = (f32[68,128]{1,0:T(8,128)S(1)}, f32[68,128]{1,0:T(8,128)S(1)}, u32[]{:S(2)}, u32[]{:S(2)}) collective-permute-start(f32[68,128]{1,0:T(8,128)S(1)} %get-tuple-element.15.rest_0_), channel_id=1, source_target_pairs={{0,8},{1,9},{2,10},{3,11},{4,12},{5,13},{6,14},{7,15},{8,0},{9,1},... | collective-permute-start | bytes 104456 | tf_op jit(solution)/shard_map/ppermute | solution.py:635
  23.1 4.0 %collective-permute-start.3 = (f32[68,128]{1,0:T(8,128)S(1)}, f32[68,128]{1,0:T(8,128)S(1)}, u32[]{:S(2)}, u32[]{:S(2)}) collective-permute-start(f32[68,128]{1,0:T(8,128)S(1)} %get-tuple-element.15.rest_0_), channel_id=1, source_target_pairs={{0,4},{1,5},{2,6},{3,7},{4,0},{5,1},{6,2},{7,3},{8,12},{9,13},{10,... | collective-permute-start | bytes 104456 | tf_op jit(solution)/shard_map/ppermute | solution.py:635
  27.1 5.1 %collective-permute-start.6 = (f32[272,128]{1,0:T(8,128)S(1)}, f32[272,128]{1,0:T(8,128)S(1)}, u32[]{:S(2)}, u32[]{:S(2)}) collective-permute-start(f32[272,128]{1,0:T(8,128)S(1)} %pad_maximum_fusion), channel_id=1, source_target_pairs={{0,2},{1,3},{2,0},{3,1},{4,6},{5,7},{6,4},{7,5},{8,10},{9,11},{10,... | collective-permute-start | bytes 417800 | tf_op jit(solution)/shard_map/ppermute | solution.py:635
  32.6 1.6 %collective-permute-start.7 = (f32[544,128]{1,0:T(8,128)S(1)}, f32[544,128]{1,0:T(8,128)S(1)}, u32[]{:S(2)}, u32[]{:S(2)}) collective-permute-start(f32[544,128]{1,0:T(8,128)S(1)} %concatenate.7), channel_id=1, source_target_pairs={{0,1},{1,0},{2,3},{3,2},{4,5},{5,4},{6,7},{7,6},{8,9},{9,8},{10,11... | collective-permute-start | bytes 835592 | tf_op jit(solution)/shard_map/ppermute | solution.py:635
  36.8 5.6 %collective-permute-start.10 = (f32[32,128]{1,0:T(8,128)S(1)}, f32[32,128]{1,0:T(8,128)S(1)}, u32[]{:S(2)}, u32[]{:S(2)}) collective-permute-start(f32[32,128]{1,0:T(8,128)S(1)} %get-tuple-element.16), channel_id=1, source_target_pairs={{0,12},{1,13},{2,14},{3,15},{4,8},{5,9},{6,10},{7,11},{8,4},{9,5},... | collective-permute-start | bytes 49160 | tf_op jit(solution)/shard_map/ppermute | solution.py:635
  37.9 6.7 %collective-permute-start.9 = (f32[32,128]{1,0:T(8,128)S(1)}, f32[32,128]{1,0:T(8,128)S(1)}, u32[]{:S(2)}, u32[]{:S(2)}) collective-permute-start(f32[32,128]{1,0:T(8,128)S(1)} %get-tuple-element.16), channel_id=1, source_target_pairs={{0,8},{1,9},{2,10},{3,11},{4,12},{5,13},{6,14},{7,15},{8,0},{9,1},... | collective-permute-start | bytes 49160 | tf_op jit(solution)/shard_map/ppermute | solution.py:635
  38.7 5.9 %collective-permute-start.8 = (f32[32,128]{1,0:T(8,128)S(1)}, f32[32,128]{1,0:T(8,128)S(1)}, u32[]{:S(2)}, u32[]{:S(2)}) collective-permute-start(f32[32,128]{1,0:T(8,128)S(1)} %get-tuple-element.16), channel_id=1, source_target_pairs={{0,4},{1,5},{2,6},{3,7},{4,0},{5,1},{6,2},{7,3},{8,12},{9,13},{10,... | collective-permute-start | bytes 49160 | tf_op jit(solution)/shard_map/ppermute | solution.py:635
  41.2 7.2 %collective-permute-start.15 = (f32[4,32,128]{2,1,0:T(8,128)S(1)}, f32[4,32,128]{2,1,0:T(8,128)S(1)}, u32[]{:S(2)}, u32[]{:S(2)}) collective-permute-start(f32[4,32,128]{2,1,0:T(8,128)S(1)} %get-tuple-element.23.rest_9_), channel_id=1, source_target_pairs={{0,8},{1,9},{2,10},{3,11},{4,12},{5,13},{6,14},{7,15},{8,0},{9,1},... | collective-permute-start | bytes 196616 | tf_op jit(solution)/shard_map/ppermute | solution.py:697
  41.6 6.8 %collective-permute-start.14 = (f32[4,32,128]{2,1,0:T(8,128)S(1)}, f32[4,32,128]{2,1,0:T(8,128)S(1)}, u32[]{:S(2)}, u32[]{:S(2)}) collective-permute-start(f32[4,32,128]{2,1,0:T(8,128)S(1)} %get-tuple-element.23.rest_9_), channel_id=1, source_target_pairs={{1,2},{2,1},{3,4},{4,3},{5,6},{6,5},{7,8},{8,7},{9,10},{10,9},{11,... | collective-permute-start | bytes 196616 | tf_op jit(solution)/shard_map/ppermute | solution.py:697
  42.4 6.0 %collective-permute-start.13 = (f32[4,32,128]{2,1,0:T(8,128)S(1)}, f32[4,32,128]{2,1,0:T(8,128)S(1)}, u32[]{:S(2)}, u32[]{:S(2)}) collective-permute-start(f32[4,32,128]{2,1,0:T(8,128)S(1)} %get-tuple-element.23.rest_9_), channel_id=1, source_target_pairs={{0,1},{1,0},{2,3},{3,2},{4,5},{5,4},{6,7},{7,6},{8,9},{9,8},{10,11... | collective-permute-start | bytes 196616 | tf_op jit(solution)/shard_map/ppermute | solution.py:697
  44.6 3.8 %collective-permute-start.11 = (f32[32,128]{1,0:T(8,128)S(1)}, f32[32,128]{1,0:T(8,128)S(1)}, u32[]{:S(2)}, u32[]{:S(2)}) collective-permute-start(f32[32,128]{1,0:T(8,128)S(1)} %add_add_fusion), channel_id=1, source_target_pairs={{0,2},{1,3},{2,0},{3,1},{4,6},{5,7},{6,4},{7,5},{8,10},{9,11},{10,... | collective-permute-start | bytes 49160 | tf_op jit(solution)/shard_map/ppermute | solution.py:635
  48.4 1.2 %collective-permute-start.12 = (f32[32,128]{1,0:T(8,128)S(1)}, f32[32,128]{1,0:T(8,128)S(1)}, u32[]{:S(2)}, u32[]{:S(2)}) collective-permute-start(f32[32,128]{1,0:T(8,128)S(1)} %add.15.rest_0_), channel_id=1, source_target_pairs={{0,1},{1,0},{2,3},{3,2},{4,5},{5,4},{6,7},{7,6},{8,9},{9,8},{10,11... | collective-permute-start | bytes 49160 | tf_op jit(solution)/shard_map/ppermute | solution.py:635

commit v6 on v5

--- a/solution.py
+++ b/solution.py
@@ -16,7 +16,7 @@
 ROW_TILES = 8
 SPREAD = 0.2
 CENTRE = 4.1
-BLOCK = 68
+BLOCK = 48
 F32 = jnp.float32
 I32 = jnp.int32
 
@@ -145,6 +145,17 @@
         out_ref[at + 3 : at + 4, :] = side3[depth : depth + 1]
 
 
+def pack_line(rows, spare, depth):
+    lane = lax.broadcasted_iota(I32, rows.shape, 1)
+    return jnp.where(lane < SIDE, rows, pltpu.roll(spare, (SIDE - 38 * depth) % LANES, 1))
+
+
+def unpack_line(first, second, third):
+    lane = lax.broadcasted_iota(I32, first.shape, 1)
+    out = jnp.where(lane < 38, pltpu.roll(first, 38, 1), pltpu.roll(second, 76, 1))
+    return jnp.where(lane < 76, out, pltpu.roll(third, 114, 1))
+
+
 def level_rows(ref, level):
     whole = (CELLS // LANES // 8) * 8
     rows = CELLS // LANES
@@ -188,7 +199,7 @@
     return (flux1 - behind(flux1, 1)) + (flux2 - behind(flux2, SIDE))
 
 
-def depths_kernel(depth_ref, out_ref, dense_ref, z_ref):
+def depths_kernel(adj_ref, flag_ref, depth_ref, out_ref, dense_ref, z_ref):
     row, lane, cell, i, j = grid_iotas()
     dense_ref[...] = jnp.where(cell < CELLS, surface_rows(depth_ref).astype(F32), 0.0)
     write_frames(dense_ref, 0, out_ref, 0, z_ref.at[0], z_ref.at[1], 1)
@@ -199,7 +210,7 @@
     met_refs = rest[: len(exchanges)]
     k_hbm, s_hbm, t_hbm, depth_hbm, d_hbm, b_hbm = rest[len(exchanges) : len(exchanges) + 6]
     a_ref, q_ref, as_ref, blk_ref, dense_ref, reach_ref = rest[len(exchanges) + 6 : len(exchanges) + 12]
-    k_ref, s_ref, t_ref, depth_ref, d_ref, b_ref, g_ref, z_ref, ts_ref, sems = rest[len(exchanges) + 12 :]
+    k_ref, s_ref, t_ref, depth_ref, d_ref, b_ref, g_ref, z_ref, ts_ref, frame_ref, sems = rest[len(exchanges) + 12 :]
     parts = 3
     third = levels // parts
     surface = [
@@ -235,7 +246,9 @@
         r = jnp.where(depth > here + 1.0, level_rows(k_ref, level), zero)
         wet = jnp.where(depth > here, 1.0, zero)
         upper = 1.0 + below
-        inverse = 1.0 / (upper + r)
+        centre = upper + r
+        inverse = pl.reciprocal(centre, approx=True)
+        inverse = inverse * (2.0 - centre * inverse)
         ratio = r * inverse
         va = (level_rows(s_ref, level) + link * va) * inverse
         vq = (wet + link * vq) * inverse
@@ -304,19 +317,27 @@
         reach = jnp.where(neighbour >= 0, jnp.minimum(met, own_ref[side : side + 1, :]), 0.0)
         reach_ref[side : side + 1, :] = reach
         shared = jnp.sum(jnp.where(reach > level, ts_ref[side], 0.0), axis=0, keepdims=True)
-        blk_ref[60 + side : 61 + side, :] = (SPREAD * level_scale) * shared
+        frame_ref[12 + side : 13 + side, :] = (SPREAD * level_scale) * shared
         table = jnp.zeros((1, LANES), F32)
         where = lax.broadcasted_iota(I32, (1, LANES), 1)
         for number, of in enumerate((side, 2 if side < 2 else 0, 3 if side < 2 else 1)):
-            table = jnp.where(where == 2 * number, adj_ref[0, of].astype(F32), table)
-            table = jnp.where(where == 2 * number + 1, flag_ref[0, of].astype(F32), table)
-        blk_ref[64 + side : 65 + side, :] = table
+            table = jnp.where(where == 104 + 2 * number, adj_ref[0, of].astype(F32), table)
+            table = jnp.where(where == 105 + 2 * number, flag_ref[0, of].astype(F32), table)
+        frame_ref[16 + side : 17 + side, :] = table
     g_ref[0:ROWS, :] = jnp.minimum(depth, 1.0)
     za_ref, zb_ref = z_ref.at[0], z_ref.at[1]
-    write_frames(dense_ref, 0, blk_ref, 0, za_ref, zb_ref, 4)
-    write_frames(dense_ref, 3 * ROWS, blk_ref, 16, za_ref, zb_ref, 4)
-    write_frames(g_ref, 0, blk_ref, 32, za_ref, zb_ref, 4)
-    write_frames(dense_ref, ROWS, blk_ref, 48, za_ref, zb_ref, 3)
+    sums = frame_ref[12:16, :]
+    tables = frame_ref[16:20, :]
+    for number, (source, base) in enumerate(((dense_ref, 0), (dense_ref, 3 * ROWS), (g_ref, 0), (dense_ref, ROWS))):
+        depths = 4 if number < 3 else 3
+        write_frames(source, base, frame_ref, 0, za_ref, zb_ref, depths)
+        spare = frame_ref[12:16, :] if number < 3 else sums
+        for depth in range(3):
+            rows = pack_line(frame_ref[4 * depth : 4 * depth + 4, :], spare, depth)
+            if number == 3 and depth == 2:
+                rows = jnp.where(lax.broadcasted_iota(I32, (4, LANES), 1) >= 104, tables, rows)
+            at = 12 * number + 4 * depth
+            blk_ref[at : at + 4, :] = rows
 
 
 def partner(exchange, me):
@@ -368,29 +389,30 @@
 def krylov_kernel(places, lines, me_ref, dense_ref, *rest):
     refs = rest[: len(places)]
     va_ref, vb_ref, line_ref, gram_ref = rest[len(places) : len(places) + 4]
-    p_ref, index_ref, frame_ref, work_ref, wet_ref, d_ref, x_ref = rest[len(places) + 4 :]
+    p_ref, index_ref, frame_ref, wet_ref, d_ref, x_ref = rest[len(places) + 4 :]
     me = me_ref[0]
 
     def collect(out, first):
         for position, rows in block_rows(refs, places, first, 4):
             out[position * 4 : position * 4 + 4, :] = rows
 
-    collect(work_ref.at[0], 60)
-    collect(work_ref.at[1], 64)
-    for depth in range(4):
+    for depth in range(3):
         collect(x_ref.at[depth], 4 * depth)
-        collect(x_ref.at[4 + depth], 16 + 4 * depth)
-        collect(wet_ref.at[depth], 32 + 4 * depth)
-        if depth < 3:
-            collect(d_ref.at[depth], 48 + 4 * depth)
+        collect(x_ref.at[4 + depth], 12 + 4 * depth)
+        collect(wet_ref.at[depth], 24 + 4 * depth)
+        collect(d_ref.at[depth], 36 + 4 * depth)
+    x_ref[3] = unpack_line(x_ref[0], x_ref[1], x_ref[2])
+    x_ref[7] = unpack_line(x_ref[4], x_ref[5], x_ref[6])
+    wet_ref[3] = unpack_line(wet_ref[0], wet_ref[1], wet_ref[2])
+    shared = unpack_line(d_ref[0], d_ref[1], d_ref[2])
     lane = lax.broadcasted_iota(I32, (lines, LANES), 1)
     line = lax.broadcasted_iota(I32, (lines, LANES), 0)
     odd = line & 1
     column = lax.broadcasted_iota(I32, (lines, lines), 1)
     line_of = lax.broadcasted_iota(I32, (lines, lines), 0)
     for number in range(3):
-        tile = work_ref[1, :, 2 * number : 2 * number + 1].astype(I32)
-        flag = work_ref[1, :, 2 * number + 1 : 2 * number + 2].astype(I32)
+        tile = d_ref[2, :, 104 + 2 * number : 105 + 2 * number].astype(I32)
+        flag = d_ref[2, :, 105 + 2 * number : 106 + 2 * number].astype(I32)
         at = jnp.where(tile >= 0, 4 * (tile ^ me) + (flag >> 1), -1)
         p = jnp.where(jnp.broadcast_to(at, (lines, lines)) == column, 1.0, 0.0)
         p_ref[number * lines : (number + 1) * lines, :] = p.astype(jnp.bfloat16)
@@ -426,7 +448,6 @@
             frame_ref[depth, 1 + number] = masks[number]
         if depth == 0:
             seam = masks[0][0:8]
-    shared = work_ref[0]
     gain = take(gather_lines(p_ref[0:lines, :], shared), facing_at) - shared
     moved = gather_lines(p_ref[3 * lines : 5 * lines, :], gain)
     zero_line = jnp.zeros((lines, LANES), F32)
@@ -483,13 +504,13 @@
             frames[solve].append(following)
             if step < ITERS - 1:
                 (vb_ref if solve == 0 else va_ref)[step + 1] = own[solve][-1]
+    gram_ref[30:32, :] = jnp.zeros((2, LANES), F32)
     for solve in range(2):
-        at = 16 * solve
+        at = solve
         for first in range(ITERS + 1):
             for second in range(first + 1):
                 gram_ref[at : at + 1, :] = jnp.sum(own[solve][first] * own[solve][second], axis=0, keepdims=True)
-                at += 1
-        gram_ref[at : at + 1, :] = jnp.zeros((1, LANES), F32)
+                at += 2
 
 
 def image_of(p):
@@ -526,12 +547,13 @@
     sum_ref[...] = jnp.broadcast_to(jnp.sum(total, axis=1, keepdims=True), sum_ref.shape)
 
 
-def coefficients(sum_ref, at):
+def coefficients(sum_ref):
     gram = []
+    at = 0
     for first in range(ITERS + 1):
-        gram.append([sum_ref[at + second : at + second + 1, :] for second in range(first + 1)])
-        at += first + 1
-    one = jnp.ones((1, LANES), F32)
+        gram.append([sum_ref[at + 2 * second : at + 2 * second + 2, :] for second in range(first + 1)])
+        at += 2 * (first + 1)
+    one = jnp.ones((2, LANES), F32)
     x = []
     r = [one]
     p = [one]
@@ -571,8 +593,9 @@
     height_ref, out_ref, gram_ref, sum_ref, w_ref, h_ref = rest[8 + len(exchanges) :]
     me = me_ref[0]
     total_gram(gram_refs, gram_ref)
-    store_rows(height_ref, combine(coefficients(gram_ref, 16), va_ref))
-    x = coefficients(gram_ref, 0)
+    both = coefficients(gram_ref)
+    store_rows(height_ref, combine([x[1:2] for x in both], va_ref))
+    x = [x[0:1] for x in both]
     level_scale = 1.0 / math.sqrt(levels)
     adjoint = combine(x, v_ref) * level_scale
     met_line = x[0] * line_ref[0]
@@ -607,15 +630,38 @@
     w_ref[3] = w1
     masks = scatter_masks()
 
+    along_back, across_back = behind(along, 1), behind(across, SIDE)
+    h_ref[0:ROWS, :] = along
+    h_ref[ROWS : 2 * ROWS, :] = across
+    h_ref[2 * ROWS : 3 * ROWS, :] = along_back
+    h_ref[3 * ROWS : 4 * ROWS, :] = across_back
+    for number, step in enumerate((ahead(adjoint, 1), ahead(adjoint, SIDE), behind(adjoint, 1), behind(adjoint, SIDE))):
+        h_ref[(4 + number) * ROWS : (5 + number) * ROWS, :] = step - adjoint
+
     def per_level(number, carry):
         at = pl.ds(pl.multiple_of(number * ROWS, ROWS), ROWS)
         here = pl.ds(number, 1)
-        h = a_ref[at, :] + adjoint * q_ref[at, :]
-        spread = interior_spread(h, along, across, number.astype(F32))
-        spread = spread + scatter_rows(
+        floor = number.astype(F32)
+        spread = scatter_rows(
             masks, w_ref[0, here, :], w_ref[1, here, :], w_ref[2, here, :], w_ref[3, here, :]
         )
-        store_rows(out_ref.at[number], h + SPREAD * spread)
+        for way in range(4):
+            reach = h_ref[way * ROWS : (way + 1) * ROWS, :]
+            gain = h_ref[(4 + way) * ROWS : (5 + way) * ROWS, :]
+            spread = spread + jnp.where(reach > floor, gain, 0.0)
+        store_rows(out_ref.at[number], a_ref[at, :] + adjoint * q_ref[at, :] + SPREAD * spread)
+        return carry
+
+    lax.fori_loop(0, levels, per_level, 0, unroll=2)
+
+
+def interior_kernel(levels, dense_ref, a_ref, out_ref):
+    along, across = interior_reach(dense_ref[2 * ROWS : 3 * ROWS, :])
+
+    def per_level(number, carry):
+        at = pl.ds(pl.multiple_of(number * ROWS, ROWS), ROWS)
+        a = a_ref[at, :]
+        out_ref[at, :] = a + SPREAD * interior_spread(a, along, across, number.astype(F32))
         return carry
 
     lax.fori_loop(0, levels, per_level, 0, unroll=2)
@@ -635,16 +681,18 @@
     return lax.ppermute(x, "tile", [(t, t ^ offset) for t in range(tiles)])
 
 
-def gather_tiles(block, tiles):
+def gather_tiles(block, tiles, beside):
     held = [block]
     places = [(0,)]
     for stride, radix in rounds(tiles):
         whole = held[0] if len(held) == 1 else jnp.concatenate(held, axis=0)
+        if stride == 1:
+            whole, beside = lax.optimization_barrier((whole, beside))
         covered = tuple(n for place in places for n in place)
         for number in range(1, radix):
             held.append(swap(whole, tiles, number * stride))
             places.append(tuple(n ^ (number * stride) for n in covered))
-    return held, tuple(places)
+    return held, tuple(places), beside
 
 
 def sum_tiles(block, tiles):
@@ -704,7 +752,7 @@
         depths_kernel,
         shape(8, LANES),
         [pltpu.VMEM((ROWS, LANES), F32), pltpu.VMEM((2, 8, LANES), F32)],
-        (),
+        (adjacent, flags),
         (depth,),
         "depths",
     )
@@ -730,6 +778,7 @@
             pltpu.VMEM((levels * ROWS, LANES), F32),
             pltpu.VMEM((8, 32, LANES), F32),
             pltpu.VMEM((4, 32, LANES), F32),
+            pltpu.VMEM((24, LANES), F32),
             pltpu.SemaphoreType.DMA((10,)),
         ],
         (me, adjacent, flags),
@@ -750,7 +799,17 @@
         ),
         48,
     )
-    blocks, places = gather_tiles(block, tiles)
+    inside = call(
+        functools.partial(interior_kernel, levels),
+        shape(levels * ROWS, LANES),
+        [],
+        (),
+        (dense, solved),
+        "interior",
+        1e7,
+        4e6,
+    )
+    blocks, places, inside = gather_tiles(block, tiles, inside)
     strips_met = to_neighbours(strips)
     lines = 4 * tiles
     frame = pltpu.VMEM((4, lines, LANES), F32)
@@ -762,7 +821,6 @@
             pltpu.VMEM((5 * lines, lines), jnp.bfloat16),
             pltpu.VMEM((3 * lines, LANES), I32),
             pltpu.VMEM((3, 5, lines, LANES), F32),
-            pltpu.VMEM((2, lines, LANES), F32),
             frame,
             frame,
             pltpu.VMEM((8, lines, LANES), F32),
@@ -779,7 +837,7 @@
             pltpu.VMEM((32, LANES), F32),
             pltpu.VMEM((16, LANES), F32),
             pltpu.VMEM((5, 32, LANES), F32),
-            pltpu.VMEM((ROWS, LANES), F32),
+            pltpu.VMEM((8 * ROWS, LANES), F32),
         ],
         (me, adjacent, flags),
         (
@@ -789,7 +847,7 @@
             basis_b,
             lines_b,
             reach,
-            solved,
+            inside,
             weight,
             strips,
             *strips_met,

time: 54.7 us -> 54.7 us (level)
  waiting for transfers between devices: 13.6 us -> 9.81 us
  Pallas kernels: 15.6 us -> 17.5 us
  local copies, waits for them, and re-layouts: 1.73 us -> 2.75 us
  starting transfers between devices: 22.8 us -> 23.5 us
    ppermute x10, waiting for transfers between devices: 12.8 us -> 8.98 us  [swap(): return lax.ppermute(x, 'tile', [(t, t ^ offset) for t in range(tiles)])]
    pallas_call x4 -> x5, Pallas kernels: 15.6 us -> 17.5 us  [call(): pl.pallas_call(kernel, out_shape=outs, in_specs=[smem] * len(scalars) + [...]
    unnamed x6 -> x14, local copies, waits for them, and re-layouts: 1.42 us -> 2.74 us
    ppermute x10, starting transfers between devices: 12 us -> 12.9 us  [swap(): return lax.ppermute(x, 'tile', [(t, t ^ offset) for t in range(tiles)])]
  transfers between devices with their start and end apart: 16 -> 16, of which waited for: 9 -> 8; matrix products, arithmetic and copies ran while one was open for 0% -> 0% of each run, Pallas kernels for 0% -> 5%
where the time goes in v6:
time: 54.7 us; the launch traced here: 54.4 us
  starting transfers between devices  23.5 us (43%)
  Pallas kernels  17.5 us (32%)
  waiting for transfers between devices  9.81 us (18%)
  local copies, waits for them, and re-layouts  2.75 us (5%)
  between operations  0.75 us (1%)
    pallas_call x5, Pallas kernels, call(): pl.pallas_call(kernel, out_shape=outs, in_specs=[smem] * len(scalars) + [...  17.5 us
    ppermute x10, starting transfers between devices, swap(): return lax.ppermute(x, 'tile', [(t, t ^ offset) for t in range(tiles)])  12.9 us
    ppermute x6, starting transfers between devices, to_neighbours(): out.append(lax.ppermute(x, 'tile', pairs))  10.7 us
    ppermute x10, waiting for transfers between devices, swap(): return lax.ppermute(x, 'tile', [(t, t ^ offset) for t in range(tiles)])  8.98 us
    unnamed x14, local copies, waits for them, and re-layouts  2.74 us
  transfers between devices with their start and end apart: 16, of which 8 were waited for; matrix products, arithmetic and copies ran while one was open for 0% of the time, Pallas kernels for 5%

profile of v6, /device:TPU:0, one launch (start us, length us, event | category | flops | bytes accessed | tf_op | source)
XLA Modules:
  0.0 54.4 jit_solution(58454821122119809)
XLA Ops:
  0.6 0.0 copy-start
  0.6 0.7 %copy-done = s32[1,8100]{1,0:T(1,128)S(1)} copy-done((s32[1,8100]{1,0:T(1,128)S(1)}, s32[1,8100]{1,0:T(1,128)}, u32[]{:S(2)}) %copy-start) | copy-done | bytes 32424
  1.4 0.0 copy-start.1
  1.4 0.7 %copy-done.1 = s32[1,4]{1,0:T(1,128)S(1)} copy-done((s32[1,4]{1,0:T(1,128)S(1)}, s32[1,4]{1,0:T(1,128)}, u32[]{:S(2)}) %copy-start.1) | copy-done | bytes 40
  2.0 0.0 copy-start.3
  2.0 0.7 %copy-done.3 = s32[1,4]{1,0:T(1,128)S(1)} copy-done((s32[1,4]{1,0:T(1,128)S(1)}, s32[1,4]{1,0:T(1,128)}, u32[]{:S(2)}) %copy-start.3) | copy-done | bytes 40
  2.7 0.8 %depths.1.own_ref = f32[8,128]{1,0:T(8,128)S(1)} custom-call(s32[1,4]{1,0:T(1,128)S(1)} %copy-done.1, s32[1,4]{1,0:T(1,128)S(1)} %copy-done.3, s32[1,8100]{1,0:T(1,128)S(1)} %copy-done), custom_call_target="tpu_custom_call" | custom-call | flops 1000000 | bytes 1000000 | tf_op jit(solution)/shard_map/depths/pallas_call | solution.py:718
  3.5 4.0 %collective-permute-start.2 = (f32[8,128]{1,0:T(8,128)S(1)}, f32[8,128]{1,0:T(8,128)S(1)}, u32[]{:S(2)}, u32[]{:S(2)}) collective-permute-start(f32[8,128]{1,0:T(8,128)S(1)} %depths.1.own_ref), channel_id=1, source_target_pairs={{0,8},{1,9},{2,10},{3,11},{4,12},{5,13},{6,14},{7,15},{8,0},{9,1},... | collective-permute-start | bytes 12296 | tf_op jit(solution)/shard_map/ppermute | solution.py:745
  7.5 0.6 %collective-permute-start.1 = (f32[8,128]{1,0:T(8,128)S(1)}, f32[8,128]{1,0:T(8,128)S(1)}, u32[]{:S(2)}, u32[]{:S(2)}) collective-permute-start(f32[8,128]{1,0:T(8,128)S(1)} %depths.1.own_ref), channel_id=1, source_target_pairs={{1,2},{2,1},{3,4},{4,3},{5,6},{6,5},{7,8},{8,7},{9,10},{10,9},{11,... | collective-permute-start | bytes 12296 | tf_op jit(solution)/shard_map/ppermute | solution.py:745
  8.2 2.9 %collective-permute-start = (f32[8,128]{1,0:T(8,128)S(1)}, f32[8,128]{1,0:T(8,128)S(1)}, u32[]{:S(2)}, u32[]{:S(2)}) collective-permute-start(f32[8,128]{1,0:T(8,128)S(1)} %depths.1.own_ref), channel_id=1, source_target_pairs={{0,1},{1,0},{2,3},{3,2},{4,5},{5,4},{6,7},{7,6},{8,9},{9,8},{10,11... | collective-permute-start | bytes 12296 | tf_op jit(solution)/shard_map/ppermute | solution.py:745
  11.1 0.0 collective-permute-done.2.rest_2_
  11.1 0.0 collective-permute-done.1.rest_1_
  11.1 0.8 %collective-permute-done.rest_0_ = f32[8,128]{1,0:T(8,128)S(1)} collective-permute-done((f32[8,128]{1,0:T(8,128)S(1)}, f32[8,128]{1,0:T(8,128)S(1)}, u32[]{:S(2)}, u32[]{:S(2)}) %collective-permute-start) | collective-permute-done | bytes 4128 | tf_op jit(solution)/shard_map/ppermute | solution.py:745
  11.9 0.0 copy-start.2
  11.9 0.0 copy-start.4
  11.9 0.7 %copy-done.2 = s32[1,4]{1,0:T(1,128)S(1)} copy-done((s32[1,4]{1,0:T(1,128)S(1)}, s32[1,4]{1,0:T(1,128)}, u32[]{:S(2)}) %copy-start.2) | copy-done | bytes 40
  12.6 0.0 copy-done.4
  12.6 8.0 %columns.1 = (f32[1920,128]{1,0:T(8,128)S(1)}, f32[1920,128]{1,0:T(8,128)S(1)}, f32[4,32,128]{2,1,0:T(8,128)S(1)}, f32[48,128]{1,0:T(8,128)S(1)}, f32[256,128]{1,0:T(8,128)S(1)}, /*index=5*/f32[8,128]{1,0:T(8,128)S(1)}) custom-call(s32[1]{0:T(128)} %bitcast.me_ref, s32[1,4]{1,0:T(1,128)S(1)} %copy-done.2, s32[1,4]{1,0:T(1,128)S(1)} %copy-done.4, ...), custom_call_target="tpu_custom_call" | custom-call | flops 20000000 | bytes 8000000 | tf_op jit(solution)/shard_map/columns/pallas_call | solution.py:718
  20.7 2.8 %collective-permute-start.5 = (f32[48,128]{1,0:T(8,128)S(1)}, f32[48,128]{1,0:T(8,128)S(1)}, u32[]{:S(2)}, u32[]{:S(2)}) collective-permute-start(f32[48,128]{1,0:T(8,128)S(1)} %get-tuple-element.17.rest_0_), channel_id=1, source_target_pairs={{0,12},{1,13},{2,14},{3,15},{4,8},{5,9},{6,10},{7,11},{8,4},{9,5},... | collective-permute-start | bytes 73736 | tf_op jit(solution)/shard_map/ppermute | solution.py:681
  23.5 1.7 %collective-permute-start.4 = (f32[48,128]{1,0:T(8,128)S(1)}, f32[48,128]{1,0:T(8,128)S(1)}, u32[]{:S(2)}, u32[]{:S(2)}) collective-permute-start(f32[48,128]{1,0:T(8,128)S(1)} %get-tuple-element.17.rest_0_), channel_id=1, source_target_pairs={{0,8},{1,9},{2,10},{3,11},{4,12},{5,13},{6,14},{7,15},{8,0},{9,1},... | collective-permute-start | bytes 73736 | tf_op jit(solution)/shard_map/ppermute | solution.py:681
  25.1 0.0 collective-permute-start.3
  25.2 2.8 %interior.1.rest_7_ = f32[1920,128]{1,0:T(8,128)S(1)} custom-call(f32[256,128]{1,0:T(8,128)S(1)} %get-tuple-element.16.dense_ref.rest_2_, f32[1920,128]{1,0:T(8,128)S(1)} %get-tuple-element.18.a_ref), custom_call_target="tpu_custom_call" | custom-call | flops 10000000 | bytes 4000000 | tf_op jit(solution)/shard_map/interior/pallas_call | solution.py:718
  28.0 0.0 collective-permute-done.5.rest_3_
  28.0 0.2 collective-permute-done.4.rest_2_
  28.2 0.8 %collective-permute-done.3.rest_1_ = f32[48,128]{1,0:T(8,128)S(1)} collective-permute-done((f32[48,128]{1,0:T(8,128)S(1)}, f32[48,128]{1,0:T(8,128)S(1)}, u32[]{:S(2)}, u32[]{:S(2)}) %collective-permute-start.3) | collective-permute-done | bytes 24608 | tf_op jit(solution)/shard_map/ppermute | solution.py:681
  29.0 1.1 %collective-permute-start.6 = (f32[192,128]{1,0:T(8,128)S(1)}, f32[192,128]{1,0:T(8,128)S(1)}, u32[]{:S(2)}, u32[]{:S(2)}) collective-permute-start(f32[192,128]{1,0:T(8,128)S(1)} %pad_maximum_fusion), channel_id=1, source_target_pairs={{0,2},{1,3},{2,0},{3,1},{4,6},{5,7},{6,4},{7,5},{8,10},{9,11},{10,... | collective-permute-start | bytes 294920 | tf_op jit(solution)/shard_map/ppermute | solution.py:681
  30.1 3.6 %collective-permute-done.6.rest_4_ = f32[192,128]{1,0:T(8,128)S(1)} collective-permute-done((f32[192,128]{1,0:T(8,128)S(1)}, f32[192,128]{1,0:T(8,128)S(1)}, u32[]{:S(2)}, u32[]{:S(2)}) %collective-permute-start.6) | collective-permute-done | bytes 98336 | tf_op jit(solution)/shard_map/ppermute | solution.py:681
  33.7 0.1 collective-permute-start.7
  33.8 1.4 %collective-permute-done.7.rest_5_ = f32[384,128]{1,0:T(8,128)S(1)} collective-permute-done((f32[384,128]{1,0:T(8,128)S(1)}, f32[384,128]{1,0:T(8,128)S(1)}, u32[]{:S(2)}, u32[]{:S(2)}) %collective-permute-start.7) | collective-permute-done | bytes 196640 | tf_op jit(solution)/shard_map/ppermute | solution.py:681
  35.2 2.9 %krylov.1 = (f32[4,64,128]{2,1,0:T(8,128)S(1)}, f32[4,64,128]{2,1,0:T(8,128)S(1)}, f32[4,8,128]{2,1,0:T(8,128)S(1)}, f32[32,128]{1,0:T(8,128)S(1)}) custom-call(s32[1]{0:T(128)} %bitcast.me_ref, f32[256,128]{1,0:T(8,128)S(1)} %get-tuple-element.16.dense_ref.rest_2_, f32[48,128]{1,0:T(8,128)S(1)} %get-tuple-element.17.rest_0_, ...), custom_call_target="tpu_custom_call" | custom-call | flops 1000000 | bytes 1000000 | tf_op jit(solution)/shard_map/krylov/pallas_call | solution.py:718
  38.1 1.8 %collective-permute-start.10 = (f32[32,128]{1,0:T(8,128)S(1)}, f32[32,128]{1,0:T(8,128)S(1)}, u32[]{:S(2)}, u32[]{:S(2)}) collective-permute-start(f32[32,128]{1,0:T(8,128)S(1)} %get-tuple-element.20), channel_id=1, source_target_pairs={{0,12},{1,13},{2,14},{3,15},{4,8},{5,9},{6,10},{7,11},{8,4},{9,5},... | collective-permute-start | bytes 49160 | tf_op jit(solution)/shard_map/ppermute | solution.py:681
  39.9 0.8 %collective-permute-start.9 = (f32[32,128]{1,0:T(8,128)S(1)}, f32[32,128]{1,0:T(8,128)S(1)}, u32[]{:S(2)}, u32[]{:S(2)}) collective-permute-start(f32[32,128]{1,0:T(8,128)S(1)} %get-tuple-element.20), channel_id=1, source_target_pairs={{0,8},{1,9},{2,10},{3,11},{4,12},{5,13},{6,14},{7,15},{8,0},{9,1},... | collective-permute-start | bytes 49160 | tf_op jit(solution)/shard_map/ppermute | solution.py:681
  40.7 1.8 %collective-permute-start.8 = (f32[32,128]{1,0:T(8,128)S(1)}, f32[32,128]{1,0:T(8,128)S(1)}, u32[]{:S(2)}, u32[]{:S(2)}) collective-permute-start(f32[32,128]{1,0:T(8,128)S(1)} %get-tuple-element.20), channel_id=1, source_target_pairs={{0,4},{1,5},{2,6},{3,7},{4,0},{5,1},{6,2},{7,3},{8,12},{9,13},{10,... | collective-permute-start | bytes 49160 | tf_op jit(solution)/shard_map/ppermute | solution.py:681
  42.6 0.3 collective-permute-start.15
  42.9 0.7 %collective-permute-start.14 = (f32[4,32,128]{2,1,0:T(8,128)S(1)}, f32[4,32,128]{2,1,0:T(8,128)S(1)}, u32[]{:S(2)}, u32[]{:S(2)}) collective-permute-start(f32[4,32,128]{2,1,0:T(8,128)S(1)} %get-tuple-element.27.rest_9_), channel_id=1, source_target_pairs={{1,2},{2,1},{3,4},{4,3},{5,6},{6,5},{7,8},{8,7},{9,10},{10,9},{11,... | collective-permute-start | bytes 196616 | tf_op jit(solution)/shard_map/ppermute | solution.py:745
  43.6 0.2 collective-permute-done.10
  43.7 2.1 %collective-permute-start.13 = (f32[4,32,128]{2,1,0:T(8,128)S(1)}, f32[4,32,128]{2,1,0:T(8,128)S(1)}, u32[]{:S(2)}, u32[]{:S(2)}) collective-permute-start(f32[4,32,128]{2,1,0:T(8,128)S(1)} %get-tuple-element.27.rest_9_), channel_id=1, source_target_pairs={{0,1},{1,0},{2,3},{3,2},{4,5},{5,4},{6,7},{7,6},{8,9},{9,8},{10,11... | collective-permute-start | bytes 196616 | tf_op jit(solution)/shard_map/ppermute | solution.py:745
  45.8 0.0 collective-permute-done.9
  45.8 0.0 collective-permute-done.8
  45.8 2.7 %collective-permute-start.11 = (f32[32,128]{1,0:T(8,128)S(1)}, f32[32,128]{1,0:T(8,128)S(1)}, u32[]{:S(2)}, u32[]{:S(2)}) collective-permute-start(f32[32,128]{1,0:T(8,128)S(1)} %add_add_fusion), channel_id=1, source_target_pairs={{0,2},{1,3},{2,0},{3,1},{4,6},{5,7},{6,4},{7,5},{8,10},{9,11},{10,... | collective-permute-start | bytes 49160 | tf_op jit(solution)/shard_map/ppermute | solution.py:681
  48.5 1.7 %collective-permute-done.11 = f32[32,128]{1,0:T(8,128)S(1)} collective-permute-done((f32[32,128]{1,0:T(8,128)S(1)}, f32[32,128]{1,0:T(8,128)S(1)}, u32[]{:S(2)}, u32[]{:S(2)}) %collective-permute-start.11) | collective-permute-done | bytes 16416 | tf_op jit(solution)/shard_map/ppermute | solution.py:681
  50.3 0.0 collective-permute-start.12
  50.3 0.0 collective-permute-done.15.rest_12_
  50.3 0.0 collective-permute-done.14.rest_11_
  50.3 0.0 collective-permute-done.13.rest_10_
  50.3 1.1 %collective-permute-done.12.rest_1_ = f32[32,128]{1,0:T(8,128)S(1)} collective-permute-done((f32[32,128]{1,0:T(8,128)S(1)}, f32[32,128]{1,0:T(8,128)S(1)}, u32[]{:S(2)}, u32[]{:S(2)}) %collective-permute-start.12) | collective-permute-done | bytes 16416 | tf_op jit(solution)/shard_map/ppermute | solution.py:681
  51.4 3.0 %gradient.1 = (f32[1,8100]{1,0:T(1,128)}, f32[30,1,8100]{2,1,0:T(1,128)}) custom-call(s32[1]{0:T(128)} %bitcast.me_ref, s32[1,4]{1,0:T(1,128)S(1)} %copy-done.2, s32[1,4]{1,0:T(1,128)S(1)} %copy-done.4, f32[32,128]{1,0:T(8,128)S(1)} %add.15.rest_0_, f32[32,128]{1,0:T(8,128)S(1)} %collective-permute-done.12.rest_1_, ...), custom_call_target="tpu_custom_call" | custom-call | flops 10000000 | bytes 4000000 | tf_op jit(solution)/shard_map/gradient/pallas_call | solution.py:718
  (8 shorter events, 0.0 us)
Async XLA Ops:
  0.6 0.8 %copy-start = (s32[1,8100]{1,0:T(1,128)S(1)}, s32[1,8100]{1,0:T(1,128)}, u32[]{:S(2)}) copy-start(s32[1,8100]{1,0:T(1,128)} %rest_6_.1) | copy-start | bytes 97204
  1.4 0.7 %copy-start.1 = (s32[1,4]{1,0:T(1,128)S(1)}, s32[1,4]{1,0:T(1,128)}, u32[]{:S(2)}) copy-start(s32[1,4]{1,0:T(1,128)} %adj_ref.5) | copy-start | bytes 52
  2.0 0.7 %copy-start.3 = (s32[1,4]{1,0:T(1,128)S(1)}, s32[1,4]{1,0:T(1,128)}, u32[]{:S(2)}) copy-start(s32[1,4]{1,0:T(1,128)} %flag_ref.5) | copy-start | bytes 52
  3.5 7.7 %collective-permute-start.2 = (f32[8,128]{1,0:T(8,128)S(1)}, f32[8,128]{1,0:T(8,128)S(1)}, u32[]{:S(2)}, u32[]{:S(2)}) collective-permute-start(f32[8,128]{1,0:T(8,128)S(1)} %depths.1.own_ref), channel_id=1, source_target_pairs={{0,8},{1,9},{2,10},{3,11},{4,12},{5,13},{6,14},{7,15},{8,0},{9,1},... | collective-permute-start | bytes 12296 | tf_op jit(solution)/shard_map/ppermute | solution.py:745
  7.5 3.6 %collective-permute-start.1 = (f32[8,128]{1,0:T(8,128)S(1)}, f32[8,128]{1,0:T(8,128)S(1)}, u32[]{:S(2)}, u32[]{:S(2)}) collective-permute-start(f32[8,128]{1,0:T(8,128)S(1)} %depths.1.own_ref), channel_id=1, source_target_pairs={{1,2},{2,1},{3,4},{4,3},{5,6},{6,5},{7,8},{8,7},{9,10},{10,9},{11,... | collective-permute-start | bytes 12296 | tf_op jit(solution)/shard_map/ppermute | solution.py:745
  8.2 3.8 %collective-permute-start = (f32[8,128]{1,0:T(8,128)S(1)}, f32[8,128]{1,0:T(8,128)S(1)}, u32[]{:S(2)}, u32[]{:S(2)}) collective-permute-start(f32[8,128]{1,0:T(8,128)S(1)} %depths.1.own_ref), channel_id=1, source_target_pairs={{0,1},{1,0},{2,3},{3,2},{4,5},{5,4},{6,7},{7,6},{8,9},{9,8},{10,11... | collective-permute-start | bytes 12296 | tf_op jit(solution)/shard_map/ppermute | solution.py:745
  11.9 0.7 %copy-start.2 = (s32[1,4]{1,0:T(1,128)S(1)}, s32[1,4]{1,0:T(1,128)}, u32[]{:S(2)}) copy-start(s32[1,4]{1,0:T(1,128)} %adj_ref.5) | copy-start | bytes 52
  11.9 0.7 %copy-start.4 = (s32[1,4]{1,0:T(1,128)S(1)}, s32[1,4]{1,0:T(1,128)}, u32[]{:S(2)}) copy-start(s32[1,4]{1,0:T(1,128)} %flag_ref.5) | copy-start | bytes 52
  20.7 7.4 %collective-permute-start.5 = (f32[48,128]{1,0:T(8,128)S(1)}, f32[48,128]{1,0:T(8,128)S(1)}, u32[]{:S(2)}, u32[]{:S(2)}) collective-permute-start(f32[48,128]{1,0:T(8,128)S(1)} %get-tuple-element.17.rest_0_), channel_id=1, source_target_pairs={{0,12},{1,13},{2,14},{3,15},{4,8},{5,9},{6,10},{7,11},{8,4},{9,5},... | collective-permute-start | bytes 73736 | tf_op jit(solution)/shard_map/ppermute | solution.py:681
  23.5 4.7 %collective-permute-start.4 = (f32[48,128]{1,0:T(8,128)S(1)}, f32[48,128]{1,0:T(8,128)S(1)}, u32[]{:S(2)}, u32[]{:S(2)}) collective-permute-start(f32[48,128]{1,0:T(8,128)S(1)} %get-tuple-element.17.rest_0_), channel_id=1, source_target_pairs={{0,8},{1,9},{2,10},{3,11},{4,12},{5,13},{6,14},{7,15},{8,0},{9,1},... | collective-permute-start | bytes 73736 | tf_op jit(solution)/shard_map/ppermute | solution.py:681
  25.1 3.8 %collective-permute-start.3 = (f32[48,128]{1,0:T(8,128)S(1)}, f32[48,128]{1,0:T(8,128)S(1)}, u32[]{:S(2)}, u32[]{:S(2)}) collective-permute-start(f32[48,128]{1,0:T(8,128)S(1)} %get-tuple-element.17.rest_0_), channel_id=1, source_target_pairs={{0,4},{1,5},{2,6},{3,7},{4,0},{5,1},{6,2},{7,3},{8,12},{9,13},{10,... | collective-permute-start | bytes 73736 | tf_op jit(solution)/shard_map/ppermute | solution.py:681
  29.0 4.7 %collective-permute-start.6 = (f32[192,128]{1,0:T(8,128)S(1)}, f32[192,128]{1,0:T(8,128)S(1)}, u32[]{:S(2)}, u32[]{:S(2)}) collective-permute-start(f32[192,128]{1,0:T(8,128)S(1)} %pad_maximum_fusion), channel_id=1, source_target_pairs={{0,2},{1,3},{2,0},{3,1},{4,6},{5,7},{6,4},{7,5},{8,10},{9,11},{10,... | collective-permute-start | bytes 294920 | tf_op jit(solution)/shard_map/ppermute | solution.py:681
  33.7 1.5 %collective-permute-start.7 = (f32[384,128]{1,0:T(8,128)S(1)}, f32[384,128]{1,0:T(8,128)S(1)}, u32[]{:S(2)}, u32[]{:S(2)}) collective-permute-start(f32[384,128]{1,0:T(8,128)S(1)} %constant_dynamic-update-slice_fusion), channel_id=1, source_target_pairs={{0,1},{1,0},{2,3},{3,2},{4,5},{5,4},{6,7},{7,6},{8,9},{9,8},{10,11... | collective-permute-start | bytes 589832 | tf_op jit(solution)/shard_map/ppermute | solution.py:681
  38.1 5.6 %collective-permute-start.10 = (f32[32,128]{1,0:T(8,128)S(1)}, f32[32,128]{1,0:T(8,128)S(1)}, u32[]{:S(2)}, u32[]{:S(2)}) collective-permute-start(f32[32,128]{1,0:T(8,128)S(1)} %get-tuple-element.20), channel_id=1, source_target_pairs={{0,12},{1,13},{2,14},{3,15},{4,8},{5,9},{6,10},{7,11},{8,4},{9,5},... | collective-permute-start | bytes 49160 | tf_op jit(solution)/shard_map/ppermute | solution.py:681
  39.9 5.8 %collective-permute-start.9 = (f32[32,128]{1,0:T(8,128)S(1)}, f32[32,128]{1,0:T(8,128)S(1)}, u32[]{:S(2)}, u32[]{:S(2)}) collective-permute-start(f32[32,128]{1,0:T(8,128)S(1)} %get-tuple-element.20), channel_id=1, source_target_pairs={{0,8},{1,9},{2,10},{3,11},{4,12},{5,13},{6,14},{7,15},{8,0},{9,1},... | collective-permute-start | bytes 49160 | tf_op jit(solution)/shard_map/ppermute | solution.py:681
  40.7 5.1 %collective-permute-start.8 = (f32[32,128]{1,0:T(8,128)S(1)}, f32[32,128]{1,0:T(8,128)S(1)}, u32[]{:S(2)}, u32[]{:S(2)}) collective-permute-start(f32[32,128]{1,0:T(8,128)S(1)} %get-tuple-element.20), channel_id=1, source_target_pairs={{0,4},{1,5},{2,6},{3,7},{4,0},{5,1},{6,2},{7,3},{8,12},{9,13},{10,... | collective-permute-start | bytes 49160 | tf_op jit(solution)/shard_map/ppermute | solution.py:681
  42.6 7.7 %collective-permute-start.15 = (f32[4,32,128]{2,1,0:T(8,128)S(1)}, f32[4,32,128]{2,1,0:T(8,128)S(1)}, u32[]{:S(2)}, u32[]{:S(2)}) collective-permute-start(f32[4,32,128]{2,1,0:T(8,128)S(1)} %get-tuple-element.27.rest_9_), channel_id=1, source_target_pairs={{0,8},{1,9},{2,10},{3,11},{4,12},{5,13},{6,14},{7,15},{8,0},{9,1},... | collective-permute-start | bytes 196616 | tf_op jit(solution)/shard_map/ppermute | solution.py:745
  42.9 7.4 %collective-permute-start.14 = (f32[4,32,128]{2,1,0:T(8,128)S(1)}, f32[4,32,128]{2,1,0:T(8,128)S(1)}, u32[]{:S(2)}, u32[]{:S(2)}) collective-permute-start(f32[4,32,128]{2,1,0:T(8,128)S(1)} %get-tuple-element.27.rest_9_), channel_id=1, source_target_pairs={{1,2},{2,1},{3,4},{4,3},{5,6},{6,5},{7,8},{8,7},{9,10},{10,9},{11,... | collective-permute-start | bytes 196616 | tf_op jit(solution)/shard_map/ppermute | solution.py:745
  43.7 6.6 %collective-permute-start.13 = (f32[4,32,128]{2,1,0:T(8,128)S(1)}, f32[4,32,128]{2,1,0:T(8,128)S(1)}, u32[]{:S(2)}, u32[]{:S(2)}) collective-permute-start(f32[4,32,128]{2,1,0:T(8,128)S(1)} %get-tuple-element.27.rest_9_), channel_id=1, source_target_pairs={{0,1},{1,0},{2,3},{3,2},{4,5},{5,4},{6,7},{7,6},{8,9},{9,8},{10,11... | collective-permute-start | bytes 196616 | tf_op jit(solution)/shard_map/ppermute | solution.py:745
  45.8 4.5 %collective-permute-start.11 = (f32[32,128]{1,0:T(8,128)S(1)}, f32[32,128]{1,0:T(8,128)S(1)}, u32[]{:S(2)}, u32[]{:S(2)}) collective-permute-start(f32[32,128]{1,0:T(8,128)S(1)} %add_add_fusion), channel_id=1, source_target_pairs={{0,2},{1,3},{2,0},{3,1},{4,6},{5,7},{6,4},{7,5},{8,10},{9,11},{10,... | collective-permute-start | bytes 49160 | tf_op jit(solution)/shard_map/ppermute | solution.py:681
  50.3 1.2 %collective-permute-start.12 = (f32[32,128]{1,0:T(8,128)S(1)}, f32[32,128]{1,0:T(8,128)S(1)}, u32[]{:S(2)}, u32[]{:S(2)}) collective-permute-start(f32[32,128]{1,0:T(8,128)S(1)} %add.15.rest_0_), channel_id=1, source_target_pairs={{0,1},{1,0},{2,3},{3,2},{4,5},{5,4},{6,7},{7,6},{8,9},{9,8},{10,11... | collective-permute-start | bytes 49160 | tf_op jit(solution)/shard_map/ppermute | solution.py:681

commit v7 on v6

--- a/solution.py
+++ b/solution.py
@@ -199,18 +199,18 @@
     return (flux1 - behind(flux1, 1)) + (flux2 - behind(flux2, SIDE))
 
 
-def depths_kernel(adj_ref, flag_ref, depth_ref, out_ref, dense_ref, z_ref):
+def depths_kernel(depth_ref, out_ref, dense_ref, z_ref):
     row, lane, cell, i, j = grid_iotas()
     dense_ref[...] = jnp.where(cell < CELLS, surface_rows(depth_ref).astype(F32), 0.0)
     write_frames(dense_ref, 0, out_ref, 0, z_ref.at[0], z_ref.at[1], 1)
     out_ref[4:8, :] = jnp.zeros((4, LANES), F32)
 
 
-def columns_kernel(exchanges, levels, me_ref, adj_ref, flag_ref, own_ref, *rest):
+def columns_kernel(exchanges, levels, me_ref, own_ref, *rest):
     met_refs = rest[: len(exchanges)]
-    k_hbm, s_hbm, t_hbm, depth_hbm, d_hbm, b_hbm = rest[len(exchanges) : len(exchanges) + 6]
-    a_ref, q_ref, as_ref, blk_ref, dense_ref, reach_ref = rest[len(exchanges) + 6 : len(exchanges) + 12]
-    k_ref, s_ref, t_ref, depth_ref, d_ref, b_ref, g_ref, z_ref, ts_ref, frame_ref, sems = rest[len(exchanges) + 12 :]
+    k_hbm, s_hbm, t_hbm, depth_hbm, d_hbm, b_hbm, adj_hbm, flag_hbm = rest[len(exchanges) : len(exchanges) + 8]
+    a_ref, q_ref, as_ref, blk_ref, dense_ref, reach_ref = rest[len(exchanges) + 8 : len(exchanges) + 14]
+    k_ref, s_ref, t_ref, depth_ref, d_ref, b_ref, g_ref, z_ref, ts_ref, frame_ref, adj_ref, flag_ref, sems = rest[len(exchanges) + 14 :]
     parts = 3
     third = levels // parts
     surface = [
@@ -227,6 +227,12 @@
             columns[-1].start()
     tracer = pltpu.make_async_copy(t_hbm, t_ref, sems.at[3 + 2 * parts])
     tracer.start()
+    tables = [
+        pltpu.make_async_copy(source, target, sems.at[4 + 2 * parts + number])
+        for number, (source, target) in enumerate(((adj_hbm, adj_ref), (flag_hbm, flag_ref)))
+    ]
+    for copy in tables:
+        copy.start()
     me = me_ref[0]
     row, lane, cell, i, j = grid_iotas()
     inside = cell < CELLS
@@ -262,8 +268,10 @@
         columns[2 * part].wait()
         columns[2 * part + 1].wait()
         last = (part + 1) * third if part < parts - 1 else levels
-        carry = lax.fori_loop(part * third, last, down, carry, unroll=2)
+        carry = lax.fori_loop(part * third, last, down, carry, unroll=5)
     tracer.wait()
+    for copy in tables:
+        copy.wait()
     column = ((j == 0) | (j == SIDE - 1)) & (i < SIDE)
     first = (column & (i < 64))[0:48]
     second = (column & (i >= 64))[40:ROWS]
@@ -291,7 +299,7 @@
         flux2 = flux2 + jnp.where(across > here, xq * (ahead(t, SIDE) - t), zero)
         return xa, xq, total + xq * t, flux1, flux2
 
-    xa, xq, total, flux1, flux2 = lax.fori_loop(0, levels, up, (zero,) * 5, unroll=2)
+    xa, xq, total, flux1, flux2 = lax.fori_loop(0, levels, up, (zero,) * 5, unroll=3)
     level_scale = 1.0 / math.sqrt(levels)
     spread = (flux1 - behind(flux1, 1)) + (flux2 - behind(flux2, SIDE))
     dense_ref[3 * ROWS : 4 * ROWS, :] = jnp.where(inside, (total + SPREAD * spread) * level_scale, zero)
@@ -327,7 +335,7 @@
     g_ref[0:ROWS, :] = jnp.minimum(depth, 1.0)
     za_ref, zb_ref = z_ref.at[0], z_ref.at[1]
     sums = frame_ref[12:16, :]
-    tables = frame_ref[16:20, :]
+    seams = frame_ref[16:20, :]
     for number, (source, base) in enumerate(((dense_ref, 0), (dense_ref, 3 * ROWS), (g_ref, 0), (dense_ref, ROWS))):
         depths = 4 if number < 3 else 3
         write_frames(source, base, frame_ref, 0, za_ref, zb_ref, depths)
@@ -335,7 +343,7 @@
         for depth in range(3):
             rows = pack_line(frame_ref[4 * depth : 4 * depth + 4, :], spare, depth)
             if number == 3 and depth == 2:
-                rows = jnp.where(lax.broadcasted_iota(I32, (4, LANES), 1) >= 104, tables, rows)
+                rows = jnp.where(lax.broadcasted_iota(I32, (4, LANES), 1) >= 104, seams, rows)
             at = 12 * number + 4 * depth
             blk_ref[at : at + 4, :] = rows
 
@@ -585,12 +593,19 @@
     return out
 
 
-def gradient_kernel(exchanges, levels, grams, me_ref, adj_ref, flag_ref, *rest):
+def gradient_kernel(exchanges, levels, grams, me_ref, *rest):
     gram_refs = rest[:grams]
     rest = rest[grams:]
     dense_ref, va_ref, v_ref, line_ref, reach_ref, a_ref, q_ref, as_ref = rest[:8]
     refs = rest[8 : 8 + len(exchanges)]
-    height_ref, out_ref, gram_ref, sum_ref, w_ref, h_ref = rest[8 + len(exchanges) :]
+    adj_hbm, flag_hbm, height_ref, out_ref = rest[8 + len(exchanges) : 12 + len(exchanges)]
+    gram_ref, sum_ref, w_ref, h_ref, adj_ref, flag_ref, sems = rest[12 + len(exchanges) :]
+    tables = [
+        pltpu.make_async_copy(source, target, sems.at[number])
+        for number, (source, target) in enumerate(((adj_hbm, adj_ref), (flag_hbm, flag_ref)))
+    ]
+    for copy in tables:
+        copy.start()
     me = me_ref[0]
     total_gram(gram_refs, gram_ref)
     both = coefficients(gram_ref)
@@ -615,6 +630,8 @@
     w_ref[4, 11:12, :] = side3[0:1]
     level = lax.broadcasted_iota(I32, (32, LANES), 0).astype(F32)
     fluxes = []
+    for copy in tables:
+        copy.wait()
     for side in range(4):
         neighbour = adj_ref[0, side]
         flag = flag_ref[0, side]
@@ -752,7 +769,7 @@
         depths_kernel,
         shape(8, LANES),
         [pltpu.VMEM((ROWS, LANES), F32), pltpu.VMEM((2, 8, LANES), F32)],
-        (adjacent, flags),
+        (),
         (depth,),
         "depths",
     )
@@ -779,9 +796,11 @@
             pltpu.VMEM((8, 32, LANES), F32),
             pltpu.VMEM((4, 32, LANES), F32),
             pltpu.VMEM((24, LANES), F32),
-            pltpu.SemaphoreType.DMA((10,)),
+            pltpu.SMEM((1, 4), I32),
+            pltpu.SMEM((1, 4), I32),
+            pltpu.SemaphoreType.DMA((12,)),
         ],
-        (me, adjacent, flags),
+        (me,),
         (own_depths, *depths_met),
         "columns",
         2e7,
@@ -795,6 +814,8 @@
                 depth,
                 main_entry,
                 elevation,
+                adjacent,
+                flags,
             )
         ),
         48,
@@ -838,8 +859,11 @@
             pltpu.VMEM((16, LANES), F32),
             pltpu.VMEM((5, 32, LANES), F32),
             pltpu.VMEM((8 * ROWS, LANES), F32),
+            pltpu.SMEM((1, 4), I32),
+            pltpu.SMEM((1, 4), I32),
+            pltpu.SemaphoreType.DMA((2,)),
         ],
-        (me, adjacent, flags),
+        (me,),
         (
             *grams,
             dense,
@@ -855,6 +879,7 @@
         "gradient",
         1e7,
         4e6,
+        tuple(pltpu.with_memory_space_constraint(x, pltpu.HBM) for x in (adjacent, flags)),
     )
     gradient = by_level(gradient)
     return height, gradient

time: 54.7 us -> 49.8 us (0.910)
  Pallas kernels: 17.5 us -> 14.7 us
  local copies, waits for them, and re-layouts: 2.75 us -> 0.77 us
    pallas_call x5, Pallas kernels: 17.5 us -> 14.7 us  [call(): pl.pallas_call(kernel, out_shape=outs, in_specs=[smem] * len(scalars) + [...]
    unnamed x14 -> x6, local copies, waits for them, and re-layouts: 2.74 us -> 0.77 us
  transfers between devices with their start and end apart: 16 -> 16, of which waited for: 8 -> 8; matrix products, arithmetic and copies ran while one was open for 0% -> 0% of each run, Pallas kernels for 5% -> 6%
where the time goes in v7:
time: 49.8 us; the launch traced here: 49.6 us
  starting transfers between devices  23.6 us (47%)
  Pallas kernels  14.7 us (30%)
  waiting for transfers between devices  9.8 us (20%)
  local copies, waits for them, and re-layouts  0.77 us (2%)
  between operations  0.75 us (2%)
    pallas_call x5, Pallas kernels, call(): pl.pallas_call(kernel, out_shape=outs, in_specs=[smem] * len(scalars) + [...  14.7 us
    ppermute x10, starting transfers between devices, swap(): return lax.ppermute(x, 'tile', [(t, t ^ offset) for t in range(tiles)])  12.9 us
    ppermute x6, starting transfers between devices, to_neighbours(): out.append(lax.ppermute(x, 'tile', pairs))  10.7 us
    ppermute x10, waiting for transfers between devices, swap(): return lax.ppermute(x, 'tile', [(t, t ^ offset) for t in range(tiles)])  8.97 us
  transfers between devices with their start and end apart: 16, of which 8 were waited for; matrix products, arithmetic and copies ran while one was open for 0% of the time, Pallas kernels for 6%

profile of v7, /device:TPU:0, one launch (start us, length us, event | category | flops | bytes accessed | tf_op | source)
XLA Modules:
  0.0 49.6 jit_solution(6621352895499409138)
XLA Ops:
  0.6 0.0 copy-start
  0.6 0.7 %copy-done = s32[1,8100]{1,0:T(1,128)S(1)} copy-done((s32[1,8100]{1,0:T(1,128)S(1)}, s32[1,8100]{1,0:T(1,128)}, u32[]{:S(2)}) %copy-start) | copy-done | bytes 32424
  1.4 0.2 depths.1.own_ref
  1.6 4.0 %collective-permute-start.2 = (f32[8,128]{1,0:T(8,128)S(1)}, f32[8,128]{1,0:T(8,128)S(1)}, u32[]{:S(2)}, u32[]{:S(2)}) collective-permute-start(f32[8,128]{1,0:T(8,128)S(1)} %depths.1.own_ref), channel_id=1, source_target_pairs={{0,8},{1,9},{2,10},{3,11},{4,12},{5,13},{6,14},{7,15},{8,0},{9,1},... | collective-permute-start | bytes 12296 | tf_op jit(solution)/shard_map/ppermute | solution.py:762
  5.7 0.6 %collective-permute-start.1 = (f32[8,128]{1,0:T(8,128)S(1)}, f32[8,128]{1,0:T(8,128)S(1)}, u32[]{:S(2)}, u32[]{:S(2)}) collective-permute-start(f32[8,128]{1,0:T(8,128)S(1)} %depths.1.own_ref), channel_id=1, source_target_pairs={{1,2},{2,1},{3,4},{4,3},{5,6},{6,5},{7,8},{8,7},{9,10},{10,9},{11,... | collective-permute-start | bytes 12296 | tf_op jit(solution)/shard_map/ppermute | solution.py:762
  6.3 2.9 %collective-permute-start = (f32[8,128]{1,0:T(8,128)S(1)}, f32[8,128]{1,0:T(8,128)S(1)}, u32[]{:S(2)}, u32[]{:S(2)}) collective-permute-start(f32[8,128]{1,0:T(8,128)S(1)} %depths.1.own_ref), channel_id=1, source_target_pairs={{0,1},{1,0},{2,3},{3,2},{4,5},{5,4},{6,7},{7,6},{8,9},{9,8},{10,11... | collective-permute-start | bytes 12296 | tf_op jit(solution)/shard_map/ppermute | solution.py:762
  9.3 0.0 collective-permute-done.2.rest_2_
  9.3 0.0 collective-permute-done.1.rest_1_
  9.3 0.8 %collective-permute-done.rest_0_ = f32[8,128]{1,0:T(8,128)S(1)} collective-permute-done((f32[8,128]{1,0:T(8,128)S(1)}, f32[8,128]{1,0:T(8,128)S(1)}, u32[]{:S(2)}, u32[]{:S(2)}) %collective-permute-start) | collective-permute-done | bytes 4128 | tf_op jit(solution)/shard_map/ppermute | solution.py:762
  10.1 5.4 %columns.1 = (f32[1920,128]{1,0:T(8,128)S(1)}, f32[1920,128]{1,0:T(8,128)S(1)}, f32[4,32,128]{2,1,0:T(8,128)S(1)}, f32[48,128]{1,0:T(8,128)S(1)}, f32[256,128]{1,0:T(8,128)S(1)}, /*index=5*/f32[8,128]{1,0:T(8,128)S(1)}) custom-call(s32[1]{0:T(128)} %bitcast.me_ref, f32[8,128]{1,0:T(8,128)S(1)} %depths.1.own_ref, f32[8,128]{1,0:T(8,128)S(1)} %collective-permute-done.rest_0_, ...), custom_call_target="tpu_custom_call" | custom-call | flops 20000000 | bytes 8000000 | tf_op jit(solution)/shard_map/columns/pallas_call | solution.py:735
  15.5 2.8 %collective-permute-start.5 = (f32[48,128]{1,0:T(8,128)S(1)}, f32[48,128]{1,0:T(8,128)S(1)}, u32[]{:S(2)}, u32[]{:S(2)}) collective-permute-start(f32[48,128]{1,0:T(8,128)S(1)} %get-tuple-element.17.rest_0_), channel_id=1, source_target_pairs={{0,12},{1,13},{2,14},{3,15},{4,8},{5,9},{6,10},{7,11},{8,4},{9,5},... | collective-permute-start | bytes 73736 | tf_op jit(solution)/shard_map/ppermute | solution.py:698
  18.3 1.7 %collective-permute-start.4 = (f32[48,128]{1,0:T(8,128)S(1)}, f32[48,128]{1,0:T(8,128)S(1)}, u32[]{:S(2)}, u32[]{:S(2)}) collective-permute-start(f32[48,128]{1,0:T(8,128)S(1)} %get-tuple-element.17.rest_0_), channel_id=1, source_target_pairs={{0,8},{1,9},{2,10},{3,11},{4,12},{5,13},{6,14},{7,15},{8,0},{9,1},... | collective-permute-start | bytes 73736 | tf_op jit(solution)/shard_map/ppermute | solution.py:698
  20.0 0.0 collective-permute-start.3
  20.0 2.8 %interior.1.rest_7_ = f32[1920,128]{1,0:T(8,128)S(1)} custom-call(f32[256,128]{1,0:T(8,128)S(1)} %get-tuple-element.16.dense_ref.rest_2_, f32[1920,128]{1,0:T(8,128)S(1)} %get-tuple-element.18.a_ref), custom_call_target="tpu_custom_call" | custom-call | flops 10000000 | bytes 4000000 | tf_op jit(solution)/shard_map/interior/pallas_call | solution.py:735
  22.8 0.0 collective-permute-done.5.rest_3_
  22.9 0.2 collective-permute-done.4.rest_2_
  23.0 0.8 %collective-permute-done.3.rest_1_ = f32[48,128]{1,0:T(8,128)S(1)} collective-permute-done((f32[48,128]{1,0:T(8,128)S(1)}, f32[48,128]{1,0:T(8,128)S(1)}, u32[]{:S(2)}, u32[]{:S(2)}) %collective-permute-start.3) | collective-permute-done | bytes 24608 | tf_op jit(solution)/shard_map/ppermute | solution.py:698
  23.8 1.1 %collective-permute-start.6 = (f32[192,128]{1,0:T(8,128)S(1)}, f32[192,128]{1,0:T(8,128)S(1)}, u32[]{:S(2)}, u32[]{:S(2)}) collective-permute-start(f32[192,128]{1,0:T(8,128)S(1)} %pad_maximum_fusion), channel_id=1, source_target_pairs={{0,2},{1,3},{2,0},{3,1},{4,6},{5,7},{6,4},{7,5},{8,10},{9,11},{10,... | collective-permute-start | bytes 294920 | tf_op jit(solution)/shard_map/ppermute | solution.py:698
  24.9 3.6 %collective-permute-done.6.rest_4_ = f32[192,128]{1,0:T(8,128)S(1)} collective-permute-done((f32[192,128]{1,0:T(8,128)S(1)}, f32[192,128]{1,0:T(8,128)S(1)}, u32[]{:S(2)}, u32[]{:S(2)}) %collective-permute-start.6) | collective-permute-done | bytes 98336 | tf_op jit(solution)/shard_map/ppermute | solution.py:698
  28.5 0.1 collective-permute-start.7
  28.6 1.4 %collective-permute-done.7.rest_5_ = f32[384,128]{1,0:T(8,128)S(1)} collective-permute-done((f32[384,128]{1,0:T(8,128)S(1)}, f32[384,128]{1,0:T(8,128)S(1)}, u32[]{:S(2)}, u32[]{:S(2)}) %collective-permute-start.7) | collective-permute-done | bytes 196640 | tf_op jit(solution)/shard_map/ppermute | solution.py:698
  30.0 2.9 %krylov.1 = (f32[4,64,128]{2,1,0:T(8,128)S(1)}, f32[4,64,128]{2,1,0:T(8,128)S(1)}, f32[4,8,128]{2,1,0:T(8,128)S(1)}, f32[32,128]{1,0:T(8,128)S(1)}) custom-call(s32[1]{0:T(128)} %bitcast.me_ref, f32[256,128]{1,0:T(8,128)S(1)} %get-tuple-element.16.dense_ref.rest_2_, f32[48,128]{1,0:T(8,128)S(1)} %get-tuple-element.17.rest_0_, ...), custom_call_target="tpu_custom_call" | custom-call | flops 1000000 | bytes 1000000 | tf_op jit(solution)/shard_map/krylov/pallas_call | solution.py:735
  32.9 1.8 %collective-permute-start.10 = (f32[32,128]{1,0:T(8,128)S(1)}, f32[32,128]{1,0:T(8,128)S(1)}, u32[]{:S(2)}, u32[]{:S(2)}) collective-permute-start(f32[32,128]{1,0:T(8,128)S(1)} %get-tuple-element.20), channel_id=1, source_target_pairs={{0,12},{1,13},{2,14},{3,15},{4,8},{5,9},{6,10},{7,11},{8,4},{9,5},... | collective-permute-start | bytes 49160 | tf_op jit(solution)/shard_map/ppermute | solution.py:698
  34.8 0.8 %collective-permute-start.9 = (f32[32,128]{1,0:T(8,128)S(1)}, f32[32,128]{1,0:T(8,128)S(1)}, u32[]{:S(2)}, u32[]{:S(2)}) collective-permute-start(f32[32,128]{1,0:T(8,128)S(1)} %get-tuple-element.20), channel_id=1, source_target_pairs={{0,8},{1,9},{2,10},{3,11},{4,12},{5,13},{6,14},{7,15},{8,0},{9,1},... | collective-permute-start | bytes 49160 | tf_op jit(solution)/shard_map/ppermute | solution.py:698
  35.6 1.8 %collective-permute-start.8 = (f32[32,128]{1,0:T(8,128)S(1)}, f32[32,128]{1,0:T(8,128)S(1)}, u32[]{:S(2)}, u32[]{:S(2)}) collective-permute-start(f32[32,128]{1,0:T(8,128)S(1)} %get-tuple-element.20), channel_id=1, source_target_pairs={{0,4},{1,5},{2,6},{3,7},{4,0},{5,1},{6,2},{7,3},{8,12},{9,13},{10,... | collective-permute-start | bytes 49160 | tf_op jit(solution)/shard_map/ppermute | solution.py:698
  37.4 0.3 collective-permute-start.15
  37.7 0.7 %collective-permute-start.14 = (f32[4,32,128]{2,1,0:T(8,128)S(1)}, f32[4,32,128]{2,1,0:T(8,128)S(1)}, u32[]{:S(2)}, u32[]{:S(2)}) collective-permute-start(f32[4,32,128]{2,1,0:T(8,128)S(1)} %get-tuple-element.27.rest_9_), channel_id=1, source_target_pairs={{1,2},{2,1},{3,4},{4,3},{5,6},{6,5},{7,8},{8,7},{9,10},{10,9},{11,... | collective-permute-start | bytes 196616 | tf_op jit(solution)/shard_map/ppermute | solution.py:762
  38.4 0.2 collective-permute-done.10
  38.6 2.1 %collective-permute-start.13 = (f32[4,32,128]{2,1,0:T(8,128)S(1)}, f32[4,32,128]{2,1,0:T(8,128)S(1)}, u32[]{:S(2)}, u32[]{:S(2)}) collective-permute-start(f32[4,32,128]{2,1,0:T(8,128)S(1)} %get-tuple-element.27.rest_9_), channel_id=1, source_target_pairs={{0,1},{1,0},{2,3},{3,2},{4,5},{5,4},{6,7},{7,6},{8,9},{9,8},{10,11... | collective-permute-start | bytes 196616 | tf_op jit(solution)/shard_map/ppermute | solution.py:762
  40.6 0.0 collective-permute-done.9
  40.6 0.0 collective-permute-done.8
  40.6 2.7 %collective-permute-start.11 = (f32[32,128]{1,0:T(8,128)S(1)}, f32[32,128]{1,0:T(8,128)S(1)}, u32[]{:S(2)}, u32[]{:S(2)}) collective-permute-start(f32[32,128]{1,0:T(8,128)S(1)} %add_add_fusion), channel_id=1, source_target_pairs={{0,2},{1,3},{2,0},{3,1},{4,6},{5,7},{6,4},{7,5},{8,10},{9,11},{10,... | collective-permute-start | bytes 49160 | tf_op jit(solution)/shard_map/ppermute | solution.py:698
  43.4 1.7 %collective-permute-done.11 = f32[32,128]{1,0:T(8,128)S(1)} collective-permute-done((f32[32,128]{1,0:T(8,128)S(1)}, f32[32,128]{1,0:T(8,128)S(1)}, u32[]{:S(2)}, u32[]{:S(2)}) %collective-permute-start.11) | collective-permute-done | bytes 16416 | tf_op jit(solution)/shard_map/ppermute | solution.py:698
  45.1 0.0 collective-permute-start.12
  45.1 0.0 collective-permute-done.15.rest_12_
  45.1 0.0 collective-permute-done.14.rest_11_
  45.1 0.0 collective-permute-done.13.rest_10_
  45.1 1.1 %collective-permute-done.12.rest_1_ = f32[32,128]{1,0:T(8,128)S(1)} collective-permute-done((f32[32,128]{1,0:T(8,128)S(1)}, f32[32,128]{1,0:T(8,128)S(1)}, u32[]{:S(2)}, u32[]{:S(2)}) %collective-permute-start.12) | collective-permute-done | bytes 16416 | tf_op jit(solution)/shard_map/ppermute | solution.py:698
  46.3 3.3 %gradient.1 = (f32[1,8100]{1,0:T(1,128)}, f32[30,1,8100]{2,1,0:T(1,128)}) custom-call(s32[1]{0:T(128)} %bitcast.me_ref, f32[32,128]{1,0:T(8,128)S(1)} %add.15.rest_0_, f32[32,128]{1,0:T(8,128)S(1)} %collective-permute-done.12.rest_1_, f32[256,128]{1,0:T(8,128)S(1)} %get-tuple-element.16.dense_ref.rest_2_, f32[4,64,128]{2,1,0:T(8,128)S(1)} %get-tuple-element.21.rest_3_, ...), custom_call_target="tpu_custom_call" | custom-call | flops 10000000 | bytes 4000000 | tf_op jit(solution)/shard_map/gradient/pallas_call | solution.py:735
  (8 shorter events, 0.0 us)
Async XLA Ops:
  0.6 0.8 %copy-start = (s32[1,8100]{1,0:T(1,128)S(1)}, s32[1,8100]{1,0:T(1,128)}, u32[]{:S(2)}) copy-start(s32[1,8100]{1,0:T(1,128)} %rest_6_.1) | copy-start | bytes 97204
  1.6 7.7 %collective-permute-start.2 = (f32[8,128]{1,0:T(8,128)S(1)}, f32[8,128]{1,0:T(8,128)S(1)}, u32[]{:S(2)}, u32[]{:S(2)}) collective-permute-start(f32[8,128]{1,0:T(8,128)S(1)} %depths.1.own_ref), channel_id=1, source_target_pairs={{0,8},{1,9},{2,10},{3,11},{4,12},{5,13},{6,14},{7,15},{8,0},{9,1},... | collective-permute-start | bytes 12296 | tf_op jit(solution)/shard_map/ppermute | solution.py:762
  5.7 3.6 %collective-permute-start.1 = (f32[8,128]{1,0:T(8,128)S(1)}, f32[8,128]{1,0:T(8,128)S(1)}, u32[]{:S(2)}, u32[]{:S(2)}) collective-permute-start(f32[8,128]{1,0:T(8,128)S(1)} %depths.1.own_ref), channel_id=1, source_target_pairs={{1,2},{2,1},{3,4},{4,3},{5,6},{6,5},{7,8},{8,7},{9,10},{10,9},{11,... | collective-permute-start | bytes 12296 | tf_op jit(solution)/shard_map/ppermute | solution.py:762
  6.3 3.8 %collective-permute-start = (f32[8,128]{1,0:T(8,128)S(1)}, f32[8,128]{1,0:T(8,128)S(1)}, u32[]{:S(2)}, u32[]{:S(2)}) collective-permute-start(f32[8,128]{1,0:T(8,128)S(1)} %depths.1.own_ref), channel_id=1, source_target_pairs={{0,1},{1,0},{2,3},{3,2},{4,5},{5,4},{6,7},{7,6},{8,9},{9,8},{10,11... | collective-permute-start | bytes 12296 | tf_op jit(solution)/shard_map/ppermute | solution.py:762
  15.5 7.4 %collective-permute-start.5 = (f32[48,128]{1,0:T(8,128)S(1)}, f32[48,128]{1,0:T(8,128)S(1)}, u32[]{:S(2)}, u32[]{:S(2)}) collective-permute-start(f32[48,128]{1,0:T(8,128)S(1)} %get-tuple-element.17.rest_0_), channel_id=1, source_target_pairs={{0,12},{1,13},{2,14},{3,15},{4,8},{5,9},{6,10},{7,11},{8,4},{9,5},... | collective-permute-start | bytes 73736 | tf_op jit(solution)/shard_map/ppermute | solution.py:698
  18.3 4.7 %collective-permute-start.4 = (f32[48,128]{1,0:T(8,128)S(1)}, f32[48,128]{1,0:T(8,128)S(1)}, u32[]{:S(2)}, u32[]{:S(2)}) collective-permute-start(f32[48,128]{1,0:T(8,128)S(1)} %get-tuple-element.17.rest_0_), channel_id=1, source_target_pairs={{0,8},{1,9},{2,10},{3,11},{4,12},{5,13},{6,14},{7,15},{8,0},{9,1},... | collective-permute-start | bytes 73736 | tf_op jit(solution)/shard_map/ppermute | solution.py:698
  20.0 3.8 %collective-permute-start.3 = (f32[48,128]{1,0:T(8,128)S(1)}, f32[48,128]{1,0:T(8,128)S(1)}, u32[]{:S(2)}, u32[]{:S(2)}) collective-permute-start(f32[48,128]{1,0:T(8,128)S(1)} %get-tuple-element.17.rest_0_), channel_id=1, source_target_pairs={{0,4},{1,5},{2,6},{3,7},{4,0},{5,1},{6,2},{7,3},{8,12},{9,13},{10,... | collective-permute-start | bytes 73736 | tf_op jit(solution)/shard_map/ppermute | solution.py:698
  23.8 4.7 %collective-permute-start.6 = (f32[192,128]{1,0:T(8,128)S(1)}, f32[192,128]{1,0:T(8,128)S(1)}, u32[]{:S(2)}, u32[]{:S(2)}) collective-permute-start(f32[192,128]{1,0:T(8,128)S(1)} %pad_maximum_fusion), channel_id=1, source_target_pairs={{0,2},{1,3},{2,0},{3,1},{4,6},{5,7},{6,4},{7,5},{8,10},{9,11},{10,... | collective-permute-start | bytes 294920 | tf_op jit(solution)/shard_map/ppermute | solution.py:698
  28.5 1.5 %collective-permute-start.7 = (f32[384,128]{1,0:T(8,128)S(1)}, f32[384,128]{1,0:T(8,128)S(1)}, u32[]{:S(2)}, u32[]{:S(2)}) collective-permute-start(f32[384,128]{1,0:T(8,128)S(1)} %constant_dynamic-update-slice_fusion), channel_id=1, source_target_pairs={{0,1},{1,0},{2,3},{3,2},{4,5},{5,4},{6,7},{7,6},{8,9},{9,8},{10,11... | collective-permute-start | bytes 589832 | tf_op jit(solution)/shard_map/ppermute | solution.py:698
  32.9 5.6 %collective-permute-start.10 = (f32[32,128]{1,0:T(8,128)S(1)}, f32[32,128]{1,0:T(8,128)S(1)}, u32[]{:S(2)}, u32[]{:S(2)}) collective-permute-start(f32[32,128]{1,0:T(8,128)S(1)} %get-tuple-element.20), channel_id=1, source_target_pairs={{0,12},{1,13},{2,14},{3,15},{4,8},{5,9},{6,10},{7,11},{8,4},{9,5},... | collective-permute-start | bytes 49160 | tf_op jit(solution)/shard_map/ppermute | solution.py:698
  34.8 5.8 %collective-permute-start.9 = (f32[32,128]{1,0:T(8,128)S(1)}, f32[32,128]{1,0:T(8,128)S(1)}, u32[]{:S(2)}, u32[]{:S(2)}) collective-permute-start(f32[32,128]{1,0:T(8,128)S(1)} %get-tuple-element.20), channel_id=1, source_target_pairs={{0,8},{1,9},{2,10},{3,11},{4,12},{5,13},{6,14},{7,15},{8,0},{9,1},... | collective-permute-start | bytes 49160 | tf_op jit(solution)/shard_map/ppermute | solution.py:698
  35.6 5.0 %collective-permute-start.8 = (f32[32,128]{1,0:T(8,128)S(1)}, f32[32,128]{1,0:T(8,128)S(1)}, u32[]{:S(2)}, u32[]{:S(2)}) collective-permute-start(f32[32,128]{1,0:T(8,128)S(1)} %get-tuple-element.20), channel_id=1, source_target_pairs={{0,4},{1,5},{2,6},{3,7},{4,0},{5,1},{6,2},{7,3},{8,12},{9,13},{10,... | collective-permute-start | bytes 49160 | tf_op jit(solution)/shard_map/ppermute | solution.py:698
  37.4 7.7 %collective-permute-start.15 = (f32[4,32,128]{2,1,0:T(8,128)S(1)}, f32[4,32,128]{2,1,0:T(8,128)S(1)}, u32[]{:S(2)}, u32[]{:S(2)}) collective-permute-start(f32[4,32,128]{2,1,0:T(8,128)S(1)} %get-tuple-element.27.rest_9_), channel_id=1, source_target_pairs={{0,8},{1,9},{2,10},{3,11},{4,12},{5,13},{6,14},{7,15},{8,0},{9,1},... | collective-permute-start | bytes 196616 | tf_op jit(solution)/shard_map/ppermute | solution.py:762
  37.7 7.4 %collective-permute-start.14 = (f32[4,32,128]{2,1,0:T(8,128)S(1)}, f32[4,32,128]{2,1,0:T(8,128)S(1)}, u32[]{:S(2)}, u32[]{:S(2)}) collective-permute-start(f32[4,32,128]{2,1,0:T(8,128)S(1)} %get-tuple-element.27.rest_9_), channel_id=1, source_target_pairs={{1,2},{2,1},{3,4},{4,3},{5,6},{6,5},{7,8},{8,7},{9,10},{10,9},{11,... | collective-permute-start | bytes 196616 | tf_op jit(solution)/shard_map/ppermute | solution.py:762
  38.6 6.6 %collective-permute-start.13 = (f32[4,32,128]{2,1,0:T(8,128)S(1)}, f32[4,32,128]{2,1,0:T(8,128)S(1)}, u32[]{:S(2)}, u32[]{:S(2)}) collective-permute-start(f32[4,32,128]{2,1,0:T(8,128)S(1)} %get-tuple-element.27.rest_9_), channel_id=1, source_target_pairs={{0,1},{1,0},{2,3},{3,2},{4,5},{5,4},{6,7},{7,6},{8,9},{9,8},{10,11... | collective-permute-start | bytes 196616 | tf_op jit(solution)/shard_map/ppermute | solution.py:762
  40.6 4.5 %collective-permute-start.11 = (f32[32,128]{1,0:T(8,128)S(1)}, f32[32,128]{1,0:T(8,128)S(1)}, u32[]{:S(2)}, u32[]{:S(2)}) collective-permute-start(f32[32,128]{1,0:T(8,128)S(1)} %add_add_fusion), channel_id=1, source_target_pairs={{0,2},{1,3},{2,0},{3,1},{4,6},{5,7},{6,4},{7,5},{8,10},{9,11},{10,... | collective-permute-start | bytes 49160 | tf_op jit(solution)/shard_map/ppermute | solution.py:698
  45.1 1.2 %collective-permute-start.12 = (f32[32,128]{1,0:T(8,128)S(1)}, f32[32,128]{1,0:T(8,128)S(1)}, u32[]{:S(2)}, u32[]{:S(2)}) collective-permute-start(f32[32,128]{1,0:T(8,128)S(1)} %add.15.rest_0_), channel_id=1, source_target_pairs={{0,1},{1,0},{2,3},{3,2},{4,5},{5,4},{6,7},{7,6},{8,9},{9,8},{10,11... | collective-permute-start | bytes 49160 | tf_op jit(solution)/shard_map/ppermute | solution.py:698

commit v8 on v7

--- a/solution.py
+++ b/solution.py
@@ -268,7 +268,7 @@
         columns[2 * part].wait()
         columns[2 * part + 1].wait()
         last = (part + 1) * third if part < parts - 1 else levels
-        carry = lax.fori_loop(part * third, last, down, carry, unroll=5)
+        carry = lax.fori_loop(part * third, last, down, carry, unroll=10)
     tracer.wait()
     for copy in tables:
         copy.wait()
@@ -299,7 +299,7 @@
         flux2 = flux2 + jnp.where(across > here, xq * (ahead(t, SIDE) - t), zero)
         return xa, xq, total + xq * t, flux1, flux2
 
-    xa, xq, total, flux1, flux2 = lax.fori_loop(0, levels, up, (zero,) * 5, unroll=3)
+    xa, xq, total, flux1, flux2 = lax.fori_loop(0, levels, up, (zero,) * 5, unroll=6)
     level_scale = 1.0 / math.sqrt(levels)
     spread = (flux1 - behind(flux1, 1)) + (flux2 - behind(flux2, SIDE))
     dense_ref[3 * ROWS : 4 * ROWS, :] = jnp.where(inside, (total + SPREAD * spread) * level_scale, zero)
@@ -669,7 +669,7 @@
         store_rows(out_ref.at[number], a_ref[at, :] + adjoint * q_ref[at, :] + SPREAD * spread)
         return carry
 
-    lax.fori_loop(0, levels, per_level, 0, unroll=2)
+    lax.fori_loop(0, levels, per_level, 0, unroll=5)
 
 
 def interior_kernel(levels, dense_ref, a_ref, out_ref):
@@ -681,7 +681,7 @@
         out_ref[at, :] = a + SPREAD * interior_spread(a, along, across, number.astype(F32))
         return carry
 
-    lax.fori_loop(0, levels, per_level, 0, unroll=2)
+    lax.fori_loop(0, levels, per_level, 0, unroll=5)
 
 
 def rounds(tiles):

time: 49.8 us -> 48 us (0.964)
  Pallas kernels: 14.7 us -> 12.6 us
  waiting for transfers between devices: 9.8 us -> 11.3 us
  starting transfers between devices: 23.6 us -> 22.3 us
    pallas_call x5, Pallas kernels: 14.7 us -> 12.6 us  [call(): pl.pallas_call(kernel, out_shape=outs, in_specs=[smem] * len(scalars) + [...]
    ppermute x10, waiting for transfers between devices: 8.97 us -> 10.5 us  [swap(): return lax.ppermute(x, 'tile', [(t, t ^ offset) for t in range(tiles)])]
    ppermute x10, starting transfers between devices: 12.9 us -> 11.7 us  [swap(): return lax.ppermute(x, 'tile', [(t, t ^ offset) for t in range(tiles)])]
  transfers between devices with their start and end apart: 16 -> 16, of which waited for: 8 -> 8; matrix products, arithmetic and copies ran while one was open for 0% -> 0% of each run, Pallas kernels for 6% -> 4%
where the time goes in v8:
time: 48 us; the launch traced here: 47.8 us
  starting transfers between devices  22.3 us (46%)
  Pallas kernels  12.6 us (26%)
  waiting for transfers between devices  11.3 us (24%)
  local copies, waits for them, and re-layouts  0.77 us (2%)
  between operations  0.75 us (2%)
    pallas_call x5, Pallas kernels, call(): pl.pallas_call(kernel, out_shape=outs, in_specs=[smem] * len(scalars) + [...  12.6 us
    ppermute x10, starting transfers between devices, swap(): return lax.ppermute(x, 'tile', [(t, t ^ offset) for t in range(tiles)])  11.7 us
    ppermute x6, starting transfers between devices, to_neighbours(): out.append(lax.ppermute(x, 'tile', pairs))  10.7 us
    ppermute x10, waiting for transfers between devices, swap(): return lax.ppermute(x, 'tile', [(t, t ^ offset) for t in range(tiles)])  10.5 us
  transfers between devices with their start and end apart: 16, of which 8 were waited for; matrix products, arithmetic and copies ran while one was open for 0% of the time, Pallas kernels for 4%

profile of v8, /device:TPU:0, one launch (start us, length us, event | category | flops | bytes accessed | tf_op | source)
XLA Modules:
  0.0 47.8 jit_solution(4951097968226117426)
XLA Ops:
  0.6 0.0 copy-start
  0.6 0.7 %copy-done = s32[1,8100]{1,0:T(1,128)S(1)} copy-done((s32[1,8100]{1,0:T(1,128)S(1)}, s32[1,8100]{1,0:T(1,128)}, u32[]{:S(2)}) %copy-start) | copy-done | bytes 32424
  1.4 0.2 depths.1.own_ref
  1.6 4.0 %collective-permute-start.2 = (f32[8,128]{1,0:T(8,128)S(1)}, f32[8,128]{1,0:T(8,128)S(1)}, u32[]{:S(2)}, u32[]{:S(2)}) collective-permute-start(f32[8,128]{1,0:T(8,128)S(1)} %depths.1.own_ref), channel_id=1, source_target_pairs={{0,8},{1,9},{2,10},{3,11},{4,12},{5,13},{6,14},{7,15},{8,0},{9,1},... | collective-permute-start | bytes 12296 | tf_op jit(solution)/shard_map/ppermute | solution.py:762
  5.7 0.6 %collective-permute-start.1 = (f32[8,128]{1,0:T(8,128)S(1)}, f32[8,128]{1,0:T(8,128)S(1)}, u32[]{:S(2)}, u32[]{:S(2)}) collective-permute-start(f32[8,128]{1,0:T(8,128)S(1)} %depths.1.own_ref), channel_id=1, source_target_pairs={{1,2},{2,1},{3,4},{4,3},{5,6},{6,5},{7,8},{8,7},{9,10},{10,9},{11,... | collective-permute-start | bytes 12296 | tf_op jit(solution)/shard_map/ppermute | solution.py:762
  6.3 2.9 %collective-permute-start = (f32[8,128]{1,0:T(8,128)S(1)}, f32[8,128]{1,0:T(8,128)S(1)}, u32[]{:S(2)}, u32[]{:S(2)}) collective-permute-start(f32[8,128]{1,0:T(8,128)S(1)} %depths.1.own_ref), channel_id=1, source_target_pairs={{0,1},{1,0},{2,3},{3,2},{4,5},{5,4},{6,7},{7,6},{8,9},{9,8},{10,11... | collective-permute-start | bytes 12296 | tf_op jit(solution)/shard_map/ppermute | solution.py:762
  9.3 0.0 collective-permute-done.2.rest_2_
  9.3 0.0 collective-permute-done.1.rest_1_
  9.3 0.8 %collective-permute-done.rest_0_ = f32[8,128]{1,0:T(8,128)S(1)} collective-permute-done((f32[8,128]{1,0:T(8,128)S(1)}, f32[8,128]{1,0:T(8,128)S(1)}, u32[]{:S(2)}, u32[]{:S(2)}) %collective-permute-start) | collective-permute-done | bytes 4128 | tf_op jit(solution)/shard_map/ppermute | solution.py:762
  10.1 4.3 %columns.1 = (f32[1920,128]{1,0:T(8,128)S(1)}, f32[1920,128]{1,0:T(8,128)S(1)}, f32[4,32,128]{2,1,0:T(8,128)S(1)}, f32[48,128]{1,0:T(8,128)S(1)}, f32[256,128]{1,0:T(8,128)S(1)}, /*index=5*/f32[8,128]{1,0:T(8,128)S(1)}) custom-call(s32[1]{0:T(128)} %bitcast.me_ref, f32[8,128]{1,0:T(8,128)S(1)} %depths.1.own_ref, f32[8,128]{1,0:T(8,128)S(1)} %collective-permute-done.rest_0_, ...), custom_call_target="tpu_custom_call" | custom-call | flops 20000000 | bytes 8000000 | tf_op jit(solution)/shard_map/columns/pallas_call | solution.py:735
  14.4 2.8 %collective-permute-start.5 = (f32[48,128]{1,0:T(8,128)S(1)}, f32[48,128]{1,0:T(8,128)S(1)}, u32[]{:S(2)}, u32[]{:S(2)}) collective-permute-start(f32[48,128]{1,0:T(8,128)S(1)} %get-tuple-element.17.rest_0_), channel_id=1, source_target_pairs={{0,12},{1,13},{2,14},{3,15},{4,8},{5,9},{6,10},{7,11},{8,4},{9,5},... | collective-permute-start | bytes 73736 | tf_op jit(solution)/shard_map/ppermute | solution.py:698
  17.2 1.7 %collective-permute-start.4 = (f32[48,128]{1,0:T(8,128)S(1)}, f32[48,128]{1,0:T(8,128)S(1)}, u32[]{:S(2)}, u32[]{:S(2)}) collective-permute-start(f32[48,128]{1,0:T(8,128)S(1)} %get-tuple-element.17.rest_0_), channel_id=1, source_target_pairs={{0,8},{1,9},{2,10},{3,11},{4,12},{5,13},{6,14},{7,15},{8,0},{9,1},... | collective-permute-start | bytes 73736 | tf_op jit(solution)/shard_map/ppermute | solution.py:698
  18.9 0.0 collective-permute-start.3
  18.9 1.9 %interior.1.rest_7_ = f32[1920,128]{1,0:T(8,128)S(1)} custom-call(f32[256,128]{1,0:T(8,128)S(1)} %get-tuple-element.16.dense_ref.rest_2_, f32[1920,128]{1,0:T(8,128)S(1)} %get-tuple-element.18.a_ref), custom_call_target="tpu_custom_call" | custom-call | flops 10000000 | bytes 4000000 | tf_op jit(solution)/shard_map/interior/pallas_call | solution.py:735
  20.8 0.0 collective-permute-done.5.rest_3_
  20.8 1.1 %collective-permute-done.4.rest_2_ = f32[48,128]{1,0:T(8,128)S(1)} collective-permute-done((f32[48,128]{1,0:T(8,128)S(1)}, f32[48,128]{1,0:T(8,128)S(1)}, u32[]{:S(2)}, u32[]{:S(2)}) %collective-permute-start.4) | collective-permute-done | bytes 24608 | tf_op jit(solution)/shard_map/ppermute | solution.py:698
  21.9 0.8 %collective-permute-done.3.rest_1_ = f32[48,128]{1,0:T(8,128)S(1)} collective-permute-done((f32[48,128]{1,0:T(8,128)S(1)}, f32[48,128]{1,0:T(8,128)S(1)}, u32[]{:S(2)}, u32[]{:S(2)}) %collective-permute-start.3) | collective-permute-done | bytes 24608 | tf_op jit(solution)/shard_map/ppermute | solution.py:698
  22.7 0.7 %collective-permute-start.6 = (f32[192,128]{1,0:T(8,128)S(1)}, f32[192,128]{1,0:T(8,128)S(1)}, u32[]{:S(2)}, u32[]{:S(2)}) collective-permute-start(f32[192,128]{1,0:T(8,128)S(1)} %pad_maximum_fusion), channel_id=1, source_target_pairs={{0,2},{1,3},{2,0},{3,1},{4,6},{5,7},{6,4},{7,5},{8,10},{9,11},{10,... | collective-permute-start | bytes 294920 | tf_op jit(solution)/shard_map/ppermute | solution.py:698
  23.4 4.0 %collective-permute-done.6.rest_4_ = f32[192,128]{1,0:T(8,128)S(1)} collective-permute-done((f32[192,128]{1,0:T(8,128)S(1)}, f32[192,128]{1,0:T(8,128)S(1)}, u32[]{:S(2)}, u32[]{:S(2)}) %collective-permute-start.6) | collective-permute-done | bytes 98336 | tf_op jit(solution)/shard_map/ppermute | solution.py:698
  27.4 0.1 collective-permute-start.7
  27.5 1.4 %collective-permute-done.7.rest_5_ = f32[384,128]{1,0:T(8,128)S(1)} collective-permute-done((f32[384,128]{1,0:T(8,128)S(1)}, f32[384,128]{1,0:T(8,128)S(1)}, u32[]{:S(2)}, u32[]{:S(2)}) %collective-permute-start.7) | collective-permute-done | bytes 196640 | tf_op jit(solution)/shard_map/ppermute | solution.py:698
  28.9 2.9 %krylov.1 = (f32[4,64,128]{2,1,0:T(8,128)S(1)}, f32[4,64,128]{2,1,0:T(8,128)S(1)}, f32[4,8,128]{2,1,0:T(8,128)S(1)}, f32[32,128]{1,0:T(8,128)S(1)}) custom-call(s32[1]{0:T(128)} %bitcast.me_ref, f32[256,128]{1,0:T(8,128)S(1)} %get-tuple-element.16.dense_ref.rest_2_, f32[48,128]{1,0:T(8,128)S(1)} %get-tuple-element.17.rest_0_, ...), custom_call_target="tpu_custom_call" | custom-call | flops 1000000 | bytes 1000000 | tf_op jit(solution)/shard_map/krylov/pallas_call | solution.py:735
  31.9 1.0 %collective-permute-start.10 = (f32[32,128]{1,0:T(8,128)S(1)}, f32[32,128]{1,0:T(8,128)S(1)}, u32[]{:S(2)}, u32[]{:S(2)}) collective-permute-start(f32[32,128]{1,0:T(8,128)S(1)} %get-tuple-element.20), channel_id=1, source_target_pairs={{0,12},{1,13},{2,14},{3,15},{4,8},{5,9},{6,10},{7,11},{8,4},{9,5},... | collective-permute-start | bytes 49160 | tf_op jit(solution)/shard_map/ppermute | solution.py:698
  32.9 0.7 %collective-permute-start.9 = (f32[32,128]{1,0:T(8,128)S(1)}, f32[32,128]{1,0:T(8,128)S(1)}, u32[]{:S(2)}, u32[]{:S(2)}) collective-permute-start(f32[32,128]{1,0:T(8,128)S(1)} %get-tuple-element.20), channel_id=1, source_target_pairs={{0,8},{1,9},{2,10},{3,11},{4,12},{5,13},{6,14},{7,15},{8,0},{9,1},... | collective-permute-start | bytes 49160 | tf_op jit(solution)/shard_map/ppermute | solution.py:698
  33.6 2.7 %collective-permute-start.8 = (f32[32,128]{1,0:T(8,128)S(1)}, f32[32,128]{1,0:T(8,128)S(1)}, u32[]{:S(2)}, u32[]{:S(2)}) collective-permute-start(f32[32,128]{1,0:T(8,128)S(1)} %get-tuple-element.20), channel_id=1, source_target_pairs={{0,4},{1,5},{2,6},{3,7},{4,0},{5,1},{6,2},{7,3},{8,12},{9,13},{10,... | collective-permute-start | bytes 49160 | tf_op jit(solution)/shard_map/ppermute | solution.py:698
  36.3 0.3 collective-permute-start.15
  36.6 0.7 %collective-permute-start.14 = (f32[4,32,128]{2,1,0:T(8,128)S(1)}, f32[4,32,128]{2,1,0:T(8,128)S(1)}, u32[]{:S(2)}, u32[]{:S(2)}) collective-permute-start(f32[4,32,128]{2,1,0:T(8,128)S(1)} %get-tuple-element.27.rest_9_), channel_id=1, source_target_pairs={{1,2},{2,1},{3,4},{4,3},{5,6},{6,5},{7,8},{8,7},{9,10},{10,9},{11,... | collective-permute-start | bytes 196616 | tf_op jit(solution)/shard_map/ppermute | solution.py:762
  37.3 0.2 collective-permute-done.10
  37.5 2.0 %collective-permute-start.13 = (f32[4,32,128]{2,1,0:T(8,128)S(1)}, f32[4,32,128]{2,1,0:T(8,128)S(1)}, u32[]{:S(2)}, u32[]{:S(2)}) collective-permute-start(f32[4,32,128]{2,1,0:T(8,128)S(1)} %get-tuple-element.27.rest_9_), channel_id=1, source_target_pairs={{0,1},{1,0},{2,3},{3,2},{4,5},{5,4},{6,7},{7,6},{8,9},{9,8},{10,11... | collective-permute-start | bytes 196616 | tf_op jit(solution)/shard_map/ppermute | solution.py:762
  39.5 0.0 collective-permute-done.9
  39.5 0.0 collective-permute-done.8
  39.5 2.0 %collective-permute-start.11 = (f32[32,128]{1,0:T(8,128)S(1)}, f32[32,128]{1,0:T(8,128)S(1)}, u32[]{:S(2)}, u32[]{:S(2)}) collective-permute-start(f32[32,128]{1,0:T(8,128)S(1)} %add_add_fusion), channel_id=1, source_target_pairs={{0,2},{1,3},{2,0},{3,1},{4,6},{5,7},{6,4},{7,5},{8,10},{9,11},{10,... | collective-permute-start | bytes 49160 | tf_op jit(solution)/shard_map/ppermute | solution.py:698
  41.5 1.8 %collective-permute-done.11 = f32[32,128]{1,0:T(8,128)S(1)} collective-permute-done((f32[32,128]{1,0:T(8,128)S(1)}, f32[32,128]{1,0:T(8,128)S(1)}, u32[]{:S(2)}, u32[]{:S(2)}) %collective-permute-start.11) | collective-permute-done | bytes 16416 | tf_op jit(solution)/shard_map/ppermute | solution.py:698
  43.3 0.0 collective-permute-start.12
  43.3 0.0 collective-permute-done.15.rest_12_
  43.4 0.0 collective-permute-done.14.rest_11_
  43.4 0.0 collective-permute-done.13.rest_10_
  43.4 1.1 %collective-permute-done.12.rest_1_ = f32[32,128]{1,0:T(8,128)S(1)} collective-permute-done((f32[32,128]{1,0:T(8,128)S(1)}, f32[32,128]{1,0:T(8,128)S(1)}, u32[]{:S(2)}, u32[]{:S(2)}) %collective-permute-start.12) | collective-permute-done | bytes 16416 | tf_op jit(solution)/shard_map/ppermute | solution.py:698
  44.5 3.2 %gradient.1 = (f32[1,8100]{1,0:T(1,128)}, f32[30,1,8100]{2,1,0:T(1,128)}) custom-call(s32[1]{0:T(128)} %bitcast.me_ref, f32[32,128]{1,0:T(8,128)S(1)} %add.15.rest_0_, f32[32,128]{1,0:T(8,128)S(1)} %collective-permute-done.12.rest_1_, f32[256,128]{1,0:T(8,128)S(1)} %get-tuple-element.16.dense_ref.rest_2_, f32[4,64,128]{2,1,0:T(8,128)S(1)} %get-tuple-element.21.rest_3_, ...), custom_call_target="tpu_custom_call" | custom-call | flops 10000000 | bytes 4000000 | tf_op jit(solution)/shard_map/gradient/pallas_call | solution.py:735
  (8 shorter events, 0.0 us)
Async XLA Ops:
  0.6 0.8 %copy-start = (s32[1,8100]{1,0:T(1,128)S(1)}, s32[1,8100]{1,0:T(1,128)}, u32[]{:S(2)}) copy-start(s32[1,8100]{1,0:T(1,128)} %rest_6_.1) | copy-start | bytes 97204
  1.6 7.7 %collective-permute-start.2 = (f32[8,128]{1,0:T(8,128)S(1)}, f32[8,128]{1,0:T(8,128)S(1)}, u32[]{:S(2)}, u32[]{:S(2)}) collective-permute-start(f32[8,128]{1,0:T(8,128)S(1)} %depths.1.own_ref), channel_id=1, source_target_pairs={{0,8},{1,9},{2,10},{3,11},{4,12},{5,13},{6,14},{7,15},{8,0},{9,1},... | collective-permute-start | bytes 12296 | tf_op jit(solution)/shard_map/ppermute | solution.py:762
  5.7 3.6 %collective-permute-start.1 = (f32[8,128]{1,0:T(8,128)S(1)}, f32[8,128]{1,0:T(8,128)S(1)}, u32[]{:S(2)}, u32[]{:S(2)}) collective-permute-start(f32[8,128]{1,0:T(8,128)S(1)} %depths.1.own_ref), channel_id=1, source_target_pairs={{1,2},{2,1},{3,4},{4,3},{5,6},{6,5},{7,8},{8,7},{9,10},{10,9},{11,... | collective-permute-start | bytes 12296 | tf_op jit(solution)/shard_map/ppermute | solution.py:762
  6.3 3.8 %collective-permute-start = (f32[8,128]{1,0:T(8,128)S(1)}, f32[8,128]{1,0:T(8,128)S(1)}, u32[]{:S(2)}, u32[]{:S(2)}) collective-permute-start(f32[8,128]{1,0:T(8,128)S(1)} %depths.1.own_ref), channel_id=1, source_target_pairs={{0,1},{1,0},{2,3},{3,2},{4,5},{5,4},{6,7},{7,6},{8,9},{9,8},{10,11... | collective-permute-start | bytes 12296 | tf_op jit(solution)/shard_map/ppermute | solution.py:762
  14.4 6.4 %collective-permute-start.5 = (f32[48,128]{1,0:T(8,128)S(1)}, f32[48,128]{1,0:T(8,128)S(1)}, u32[]{:S(2)}, u32[]{:S(2)}) collective-permute-start(f32[48,128]{1,0:T(8,128)S(1)} %get-tuple-element.17.rest_0_), channel_id=1, source_target_pairs={{0,12},{1,13},{2,14},{3,15},{4,8},{5,9},{6,10},{7,11},{8,4},{9,5},... | collective-permute-start | bytes 73736 | tf_op jit(solution)/shard_map/ppermute | solution.py:698
  17.2 4.7 %collective-permute-start.4 = (f32[48,128]{1,0:T(8,128)S(1)}, f32[48,128]{1,0:T(8,128)S(1)}, u32[]{:S(2)}, u32[]{:S(2)}) collective-permute-start(f32[48,128]{1,0:T(8,128)S(1)} %get-tuple-element.17.rest_0_), channel_id=1, source_target_pairs={{0,8},{1,9},{2,10},{3,11},{4,12},{5,13},{6,14},{7,15},{8,0},{9,1},... | collective-permute-start | bytes 73736 | tf_op jit(solution)/shard_map/ppermute | solution.py:698
  18.9 3.8 %collective-permute-start.3 = (f32[48,128]{1,0:T(8,128)S(1)}, f32[48,128]{1,0:T(8,128)S(1)}, u32[]{:S(2)}, u32[]{:S(2)}) collective-permute-start(f32[48,128]{1,0:T(8,128)S(1)} %get-tuple-element.17.rest_0_), channel_id=1, source_target_pairs={{0,4},{1,5},{2,6},{3,7},{4,0},{5,1},{6,2},{7,3},{8,12},{9,13},{10,... | collective-permute-start | bytes 73736 | tf_op jit(solution)/shard_map/ppermute | solution.py:698
  22.7 4.7 %collective-permute-start.6 = (f32[192,128]{1,0:T(8,128)S(1)}, f32[192,128]{1,0:T(8,128)S(1)}, u32[]{:S(2)}, u32[]{:S(2)}) collective-permute-start(f32[192,128]{1,0:T(8,128)S(1)} %pad_maximum_fusion), channel_id=1, source_target_pairs={{0,2},{1,3},{2,0},{3,1},{4,6},{5,7},{6,4},{7,5},{8,10},{9,11},{10,... | collective-permute-start | bytes 294920 | tf_op jit(solution)/shard_map/ppermute | solution.py:698
  27.4 1.5 %collective-permute-start.7 = (f32[384,128]{1,0:T(8,128)S(1)}, f32[384,128]{1,0:T(8,128)S(1)}, u32[]{:S(2)}, u32[]{:S(2)}) collective-permute-start(f32[384,128]{1,0:T(8,128)S(1)} %constant_dynamic-update-slice_fusion), channel_id=1, source_target_pairs={{0,1},{1,0},{2,3},{3,2},{4,5},{5,4},{6,7},{7,6},{8,9},{9,8},{10,11... | collective-permute-start | bytes 589832 | tf_op jit(solution)/shard_map/ppermute | solution.py:698
  31.9 5.6 %collective-permute-start.10 = (f32[32,128]{1,0:T(8,128)S(1)}, f32[32,128]{1,0:T(8,128)S(1)}, u32[]{:S(2)}, u32[]{:S(2)}) collective-permute-start(f32[32,128]{1,0:T(8,128)S(1)} %get-tuple-element.20), channel_id=1, source_target_pairs={{0,12},{1,13},{2,14},{3,15},{4,8},{5,9},{6,10},{7,11},{8,4},{9,5},... | collective-permute-start | bytes 49160 | tf_op jit(solution)/shard_map/ppermute | solution.py:698
  32.9 6.6 %collective-permute-start.9 = (f32[32,128]{1,0:T(8,128)S(1)}, f32[32,128]{1,0:T(8,128)S(1)}, u32[]{:S(2)}, u32[]{:S(2)}) collective-permute-start(f32[32,128]{1,0:T(8,128)S(1)} %get-tuple-element.20), channel_id=1, source_target_pairs={{0,8},{1,9},{2,10},{3,11},{4,12},{5,13},{6,14},{7,15},{8,0},{9,1},... | collective-permute-start | bytes 49160 | tf_op jit(solution)/shard_map/ppermute | solution.py:698
  33.6 5.9 %collective-permute-start.8 = (f32[32,128]{1,0:T(8,128)S(1)}, f32[32,128]{1,0:T(8,128)S(1)}, u32[]{:S(2)}, u32[]{:S(2)}) collective-permute-start(f32[32,128]{1,0:T(8,128)S(1)} %get-tuple-element.20), channel_id=1, source_target_pairs={{0,4},{1,5},{2,6},{3,7},{4,0},{5,1},{6,2},{7,3},{8,12},{9,13},{10,... | collective-permute-start | bytes 49160 | tf_op jit(solution)/shard_map/ppermute | solution.py:698
  36.3 7.0 %collective-permute-start.15 = (f32[4,32,128]{2,1,0:T(8,128)S(1)}, f32[4,32,128]{2,1,0:T(8,128)S(1)}, u32[]{:S(2)}, u32[]{:S(2)}) collective-permute-start(f32[4,32,128]{2,1,0:T(8,128)S(1)} %get-tuple-element.27.rest_9_), channel_id=1, source_target_pairs={{0,8},{1,9},{2,10},{3,11},{4,12},{5,13},{6,14},{7,15},{8,0},{9,1},... | collective-permute-start | bytes 196616 | tf_op jit(solution)/shard_map/ppermute | solution.py:762
  36.6 6.7 %collective-permute-start.14 = (f32[4,32,128]{2,1,0:T(8,128)S(1)}, f32[4,32,128]{2,1,0:T(8,128)S(1)}, u32[]{:S(2)}, u32[]{:S(2)}) collective-permute-start(f32[4,32,128]{2,1,0:T(8,128)S(1)} %get-tuple-element.27.rest_9_), channel_id=1, source_target_pairs={{1,2},{2,1},{3,4},{4,3},{5,6},{6,5},{7,8},{8,7},{9,10},{10,9},{11,... | collective-permute-start | bytes 196616 | tf_op jit(solution)/shard_map/ppermute | solution.py:762
  37.5 5.9 %collective-permute-start.13 = (f32[4,32,128]{2,1,0:T(8,128)S(1)}, f32[4,32,128]{2,1,0:T(8,128)S(1)}, u32[]{:S(2)}, u32[]{:S(2)}) collective-permute-start(f32[4,32,128]{2,1,0:T(8,128)S(1)} %get-tuple-element.27.rest_9_), channel_id=1, source_target_pairs={{0,1},{1,0},{2,3},{3,2},{4,5},{5,4},{6,7},{7,6},{8,9},{9,8},{10,11... | collective-permute-start | bytes 196616 | tf_op jit(solution)/shard_map/ppermute | solution.py:762
  39.5 3.8 %collective-permute-start.11 = (f32[32,128]{1,0:T(8,128)S(1)}, f32[32,128]{1,0:T(8,128)S(1)}, u32[]{:S(2)}, u32[]{:S(2)}) collective-permute-start(f32[32,128]{1,0:T(8,128)S(1)} %add_add_fusion), channel_id=1, source_target_pairs={{0,2},{1,3},{2,0},{3,1},{4,6},{5,7},{6,4},{7,5},{8,10},{9,11},{10,... | collective-permute-start | bytes 49160 | tf_op jit(solution)/shard_map/ppermute | solution.py:698
  43.3 1.2 %collective-permute-start.12 = (f32[32,128]{1,0:T(8,128)S(1)}, f32[32,128]{1,0:T(8,128)S(1)}, u32[]{:S(2)}, u32[]{:S(2)}) collective-permute-start(f32[32,128]{1,0:T(8,128)S(1)} %add.15.rest_0_), channel_id=1, source_target_pairs={{0,1},{1,0},{2,3},{3,2},{4,5},{5,4},{6,7},{7,6},{8,9},{9,8},{10,11... | collective-permute-start | bytes 49160 | tf_op jit(solution)/shard_map/ppermute | solution.py:698

commit v9 on v8

--- a/solution.py
+++ b/solution.py
@@ -299,7 +299,7 @@
         flux2 = flux2 + jnp.where(across > here, xq * (ahead(t, SIDE) - t), zero)
         return xa, xq, total + xq * t, flux1, flux2
 
-    xa, xq, total, flux1, flux2 = lax.fori_loop(0, levels, up, (zero,) * 5, unroll=6)
+    xa, xq, total, flux1, flux2 = lax.fori_loop(0, levels, up, (zero,) * 5, unroll=10)
     level_scale = 1.0 / math.sqrt(levels)
     spread = (flux1 - behind(flux1, 1)) + (flux2 - behind(flux2, SIDE))
     dense_ref[3 * ROWS : 4 * ROWS, :] = jnp.where(inside, (total + SPREAD * spread) * level_scale, zero)
@@ -698,18 +698,21 @@
     return lax.ppermute(x, "tile", [(t, t ^ offset) for t in range(tiles)])
 
 
-def gather_tiles(block, tiles, beside):
+def gather_tiles(block, tiles, beside, strips, to_neighbours):
     held = [block]
     places = [(0,)]
     for stride, radix in rounds(tiles):
         whole = held[0] if len(held) == 1 else jnp.concatenate(held, axis=0)
+        if stride == 2:
+            whole, strips = lax.optimization_barrier((whole, strips))
+            strips_met = to_neighbours(strips)
         if stride == 1:
-            whole, beside = lax.optimization_barrier((whole, beside))
+            whole, beside, strips_met = lax.optimization_barrier((whole, beside, strips_met))
         covered = tuple(n for place in places for n in place)
         for number in range(1, radix):
             held.append(swap(whole, tiles, number * stride))
             places.append(tuple(n ^ (number * stride) for n in covered))
-    return held, tuple(places), beside
+    return held, tuple(places), beside, strips_met
 
 
 def sum_tiles(block, tiles):
@@ -830,8 +833,7 @@
         1e7,
         4e6,
     )
-    blocks, places, inside = gather_tiles(block, tiles, inside)
-    strips_met = to_neighbours(strips)
+    blocks, places, inside, strips_met = gather_tiles(block, tiles, inside, strips, to_neighbours)
     lines = 4 * tiles
     frame = pltpu.VMEM((4, lines, LANES), F32)
     basis = shape(ITERS, ROWS, LANES)

time: 48 us -> 51.8 us (1.079)
  waiting for transfers between devices: 11.3 us -> 14.5 us
  starting transfers between devices: 22.3 us -> 22.9 us
    ppermute x10, waiting for transfers between devices: 10.5 us -> 13.6 us  [swap(): return lax.ppermute(x, 'tile', [(t, t ^ offset) for t in range(tiles)])]
    ppermute x6, starting transfers between devices: 10.7 us -> 11.6 us  [to_neighbours(): out.append(lax.ppermute(x, 'tile', pairs))]
  transfers between devices with their start and end apart: 16 -> 16, of which waited for: 8 -> 9; matrix products, arithmetic and copies ran while one was open for 0% -> 0% of each run, Pallas kernels for 4% -> 4%
where the time goes in v9:
time: 51.8 us; the launch traced here: 51.5 us
  starting transfers between devices  22.9 us (44%)
  waiting for transfers between devices  14.5 us (28%)
  Pallas kernels  12.6 us (24%)
  local copies, waits for them, and re-layouts  0.77 us (1%)
  between operations  0.75 us (1%)
    ppermute x10, waiting for transfers between devices, swap(): return lax.ppermute(x, 'tile', [(t, t ^ offset) for t in range(tiles)])  13.6 us
    pallas_call x5, Pallas kernels, call(): pl.pallas_call(kernel, out_shape=outs, in_specs=[smem] * len(scalars) + [...  12.6 us
    ppermute x6, starting transfers between devices, to_neighbours(): out.append(lax.ppermute(x, 'tile', pairs))  11.6 us
    ppermute x10, starting transfers between devices, swap(): return lax.ppermute(x, 'tile', [(t, t ^ offset) for t in range(tiles)])  11.3 us
  transfers between devices with their start and end apart: 16, of which 9 were waited for; matrix products, arithmetic and copies ran while one was open for 0% of the time, Pallas kernels for 4%

profile of v9, /device:TPU:0, one launch (start us, length us, event | category | flops | bytes accessed | tf_op | source)
XLA Modules:
  0.0 51.5 jit_solution(7491895837704827901)
XLA Ops:
  0.6 0.0 copy-start
  0.6 0.7 %copy-done = s32[1,8100]{1,0:T(1,128)S(1)} copy-done((s32[1,8100]{1,0:T(1,128)S(1)}, s32[1,8100]{1,0:T(1,128)}, u32[]{:S(2)}) %copy-start) | copy-done | bytes 32424
  1.4 0.2 depths.1.own_ref
  1.6 4.0 %collective-permute-start.2 = (f32[8,128]{1,0:T(8,128)S(1)}, f32[8,128]{1,0:T(8,128)S(1)}, u32[]{:S(2)}, u32[]{:S(2)}) collective-permute-start(f32[8,128]{1,0:T(8,128)S(1)} %depths.1.own_ref), channel_id=1, source_target_pairs={{0,8},{1,9},{2,10},{3,11},{4,12},{5,13},{6,14},{7,15},{8,0},{9,1},... | collective-permute-start | bytes 12296 | tf_op jit(solution)/shard_map/ppermute | solution.py:765
  5.7 0.6 %collective-permute-start.1 = (f32[8,128]{1,0:T(8,128)S(1)}, f32[8,128]{1,0:T(8,128)S(1)}, u32[]{:S(2)}, u32[]{:S(2)}) collective-permute-start(f32[8,128]{1,0:T(8,128)S(1)} %depths.1.own_ref), channel_id=1, source_target_pairs={{1,2},{2,1},{3,4},{4,3},{5,6},{6,5},{7,8},{8,7},{9,10},{10,9},{11,... | collective-permute-start | bytes 12296 | tf_op jit(solution)/shard_map/ppermute | solution.py:765
  6.3 2.9 %collective-permute-start = (f32[8,128]{1,0:T(8,128)S(1)}, f32[8,128]{1,0:T(8,128)S(1)}, u32[]{:S(2)}, u32[]{:S(2)}) collective-permute-start(f32[8,128]{1,0:T(8,128)S(1)} %depths.1.own_ref), channel_id=1, source_target_pairs={{0,1},{1,0},{2,3},{3,2},{4,5},{5,4},{6,7},{7,6},{8,9},{9,8},{10,11... | collective-permute-start | bytes 12296 | tf_op jit(solution)/shard_map/ppermute | solution.py:765
  9.3 0.0 collective-permute-done.2.rest_2_
  9.3 0.0 collective-permute-done.1.rest_1_
  9.3 0.8 %collective-permute-done.rest_0_ = f32[8,128]{1,0:T(8,128)S(1)} collective-permute-done((f32[8,128]{1,0:T(8,128)S(1)}, f32[8,128]{1,0:T(8,128)S(1)}, u32[]{:S(2)}, u32[]{:S(2)}) %collective-permute-start) | collective-permute-done | bytes 4128 | tf_op jit(solution)/shard_map/ppermute | solution.py:765
  10.1 4.3 %columns.1 = (f32[1920,128]{1,0:T(8,128)S(1)}, f32[1920,128]{1,0:T(8,128)S(1)}, f32[4,32,128]{2,1,0:T(8,128)S(1)}, f32[48,128]{1,0:T(8,128)S(1)}, f32[256,128]{1,0:T(8,128)S(1)}, /*index=5*/f32[8,128]{1,0:T(8,128)S(1)}) custom-call(s32[1]{0:T(128)} %bitcast.me_ref, f32[8,128]{1,0:T(8,128)S(1)} %depths.1.own_ref, f32[8,128]{1,0:T(8,128)S(1)} %collective-permute-done.rest_0_, ...), custom_call_target="tpu_custom_call" | custom-call | flops 20000000 | bytes 8000000 | tf_op jit(solution)/shard_map/columns/pallas_call | solution.py:738
  14.4 2.8 %collective-permute-start.5 = (f32[48,128]{1,0:T(8,128)S(1)}, f32[48,128]{1,0:T(8,128)S(1)}, u32[]{:S(2)}, u32[]{:S(2)}) collective-permute-start(f32[48,128]{1,0:T(8,128)S(1)} %get-tuple-element.22.rest_0_), channel_id=1, source_target_pairs={{0,12},{1,13},{2,14},{3,15},{4,8},{5,9},{6,10},{7,11},{8,4},{9,5},... | collective-permute-start | bytes 73736 | tf_op jit(solution)/shard_map/ppermute | solution.py:698
  17.2 1.7 %collective-permute-start.4 = (f32[48,128]{1,0:T(8,128)S(1)}, f32[48,128]{1,0:T(8,128)S(1)}, u32[]{:S(2)}, u32[]{:S(2)}) collective-permute-start(f32[48,128]{1,0:T(8,128)S(1)} %get-tuple-element.22.rest_0_), channel_id=1, source_target_pairs={{0,8},{1,9},{2,10},{3,11},{4,12},{5,13},{6,14},{7,15},{8,0},{9,1},... | collective-permute-start | bytes 73736 | tf_op jit(solution)/shard_map/ppermute | solution.py:698
  18.9 0.0 collective-permute-start.3
  18.9 1.9 %interior.1.rest_7_ = f32[1920,128]{1,0:T(8,128)S(1)} custom-call(f32[256,128]{1,0:T(8,128)S(1)} %get-tuple-element.21.dense_ref.rest_2_, f32[1920,128]{1,0:T(8,128)S(1)} %get-tuple-element.25.a_ref), custom_call_target="tpu_custom_call" | custom-call | flops 10000000 | bytes 4000000 | tf_op jit(solution)/shard_map/interior/pallas_call | solution.py:738
  20.9 0.0 collective-permute-done.5.rest_3_
  20.9 1.1 %collective-permute-done.4.rest_2_ = f32[48,128]{1,0:T(8,128)S(1)} collective-permute-done((f32[48,128]{1,0:T(8,128)S(1)}, f32[48,128]{1,0:T(8,128)S(1)}, u32[]{:S(2)}, u32[]{:S(2)}) %collective-permute-start.4) | collective-permute-done | bytes 24608 | tf_op jit(solution)/shard_map/ppermute | solution.py:698
  22.0 0.8 %collective-permute-done.3.rest_1_ = f32[48,128]{1,0:T(8,128)S(1)} collective-permute-done((f32[48,128]{1,0:T(8,128)S(1)}, f32[48,128]{1,0:T(8,128)S(1)}, u32[]{:S(2)}, u32[]{:S(2)}) %collective-permute-start.3) | collective-permute-done | bytes 24608 | tf_op jit(solution)/shard_map/ppermute | solution.py:698
  22.8 1.3 %collective-permute-start.9 = (f32[4,32,128]{2,1,0:T(8,128)S(1)}, f32[4,32,128]{2,1,0:T(8,128)S(1)}, u32[]{:S(2)}, u32[]{:S(2)}) collective-permute-start(f32[4,32,128]{2,1,0:T(8,128)S(1)} %get-tuple-element.26.rest_9_), channel_id=1, source_target_pairs={{0,8},{1,9},{2,10},{3,11},{4,12},{5,13},{6,14},{7,15},{8,0},{9,1},... | collective-permute-start | bytes 196616 | tf_op jit(solution)/shard_map/ppermute | solution.py:765
  24.1 0.7 %collective-permute-start.8 = (f32[4,32,128]{2,1,0:T(8,128)S(1)}, f32[4,32,128]{2,1,0:T(8,128)S(1)}, u32[]{:S(2)}, u32[]{:S(2)}) collective-permute-start(f32[4,32,128]{2,1,0:T(8,128)S(1)} %get-tuple-element.26.rest_9_), channel_id=1, source_target_pairs={{1,2},{2,1},{3,4},{4,3},{5,6},{6,5},{7,8},{8,7},{9,10},{10,9},{11,... | collective-permute-start | bytes 196616 | tf_op jit(solution)/shard_map/ppermute | solution.py:765
  24.7 2.0 %collective-permute-start.7 = (f32[4,32,128]{2,1,0:T(8,128)S(1)}, f32[4,32,128]{2,1,0:T(8,128)S(1)}, u32[]{:S(2)}, u32[]{:S(2)}) collective-permute-start(f32[4,32,128]{2,1,0:T(8,128)S(1)} %get-tuple-element.26.rest_9_), channel_id=1, source_target_pairs={{0,1},{1,0},{2,3},{3,2},{4,5},{5,4},{6,7},{7,6},{8,9},{9,8},{10,11... | collective-permute-start | bytes 196616 | tf_op jit(solution)/shard_map/ppermute | solution.py:765
  26.8 1.1 %collective-permute-start.6 = (f32[192,128]{1,0:T(8,128)S(1)}, f32[192,128]{1,0:T(8,128)S(1)}, u32[]{:S(2)}, u32[]{:S(2)}) collective-permute-start(f32[192,128]{1,0:T(8,128)S(1)} %pad_maximum_fusion), channel_id=1, source_target_pairs={{0,2},{1,3},{2,0},{3,1},{4,6},{5,7},{6,4},{7,5},{8,10},{9,11},{10,... | collective-permute-start | bytes 294920 | tf_op jit(solution)/shard_map/ppermute | solution.py:698
  27.9 3.6 %collective-permute-done.6.rest_4_ = f32[192,128]{1,0:T(8,128)S(1)} collective-permute-done((f32[192,128]{1,0:T(8,128)S(1)}, f32[192,128]{1,0:T(8,128)S(1)}, u32[]{:S(2)}, u32[]{:S(2)}) %collective-permute-start.6) | collective-permute-done | bytes 98336 | tf_op jit(solution)/shard_map/ppermute | solution.py:698
  31.6 0.0 collective-permute-done.9.rest_12_
  31.6 0.0 collective-permute-done.8.rest_11_
  31.6 0.0 collective-permute-done.7.rest_10_
  31.6 0.1 collective-permute-start.10
  31.7 1.4 %collective-permute-done.10.rest_5_ = f32[384,128]{1,0:T(8,128)S(1)} collective-permute-done((f32[384,128]{1,0:T(8,128)S(1)}, f32[384,128]{1,0:T(8,128)S(1)}, u32[]{:S(2)}, u32[]{:S(2)}) %collective-permute-start.10) | collective-permute-done | bytes 196640 | tf_op jit(solution)/shard_map/ppermute | solution.py:698
  33.1 2.9 %krylov.1 = (f32[4,64,128]{2,1,0:T(8,128)S(1)}, f32[4,64,128]{2,1,0:T(8,128)S(1)}, f32[4,8,128]{2,1,0:T(8,128)S(1)}, f32[32,128]{1,0:T(8,128)S(1)}) custom-call(s32[1]{0:T(128)} %bitcast.me_ref, f32[256,128]{1,0:T(8,128)S(1)} %get-tuple-element.21.dense_ref.rest_2_, f32[48,128]{1,0:T(8,128)S(1)} %get-tuple-element.22.rest_0_, ...), custom_call_target="tpu_custom_call" | custom-call | flops 1000000 | bytes 1000000 | tf_op jit(solution)/shard_map/krylov/pallas_call | solution.py:738
  36.0 2.6 %collective-permute-start.13 = (f32[32,128]{1,0:T(8,128)S(1)}, f32[32,128]{1,0:T(8,128)S(1)}, u32[]{:S(2)}, u32[]{:S(2)}) collective-permute-start(f32[32,128]{1,0:T(8,128)S(1)} %get-tuple-element.28), channel_id=1, source_target_pairs={{0,12},{1,13},{2,14},{3,15},{4,8},{5,9},{6,10},{7,11},{8,4},{9,5},... | collective-permute-start | bytes 49160 | tf_op jit(solution)/shard_map/ppermute | solution.py:698
  38.6 0.3 collective-permute-start.12
  39.0 1.5 %collective-permute-start.11 = (f32[32,128]{1,0:T(8,128)S(1)}, f32[32,128]{1,0:T(8,128)S(1)}, u32[]{:S(2)}, u32[]{:S(2)}) collective-permute-start(f32[32,128]{1,0:T(8,128)S(1)} %get-tuple-element.28), channel_id=1, source_target_pairs={{0,4},{1,5},{2,6},{3,7},{4,0},{5,1},{6,2},{7,3},{8,12},{9,13},{10,... | collective-permute-start | bytes 49160 | tf_op jit(solution)/shard_map/ppermute | solution.py:698
  40.5 1.1 %collective-permute-done.13 = f32[32,128]{1,0:T(8,128)S(1)} collective-permute-done((f32[32,128]{1,0:T(8,128)S(1)}, f32[32,128]{1,0:T(8,128)S(1)}, u32[]{:S(2)}, u32[]{:S(2)}) %collective-permute-start.13) | collective-permute-done | bytes 16416 | tf_op jit(solution)/shard_map/ppermute | solution.py:698
  41.6 1.7 %collective-permute-done.12 = f32[32,128]{1,0:T(8,128)S(1)} collective-permute-done((f32[32,128]{1,0:T(8,128)S(1)}, f32[32,128]{1,0:T(8,128)S(1)}, u32[]{:S(2)}, u32[]{:S(2)}) %collective-permute-start.12) | collective-permute-done | bytes 16416 | tf_op jit(solution)/shard_map/ppermute | solution.py:698
  43.3 0.0 collective-permute-done.11
  43.3 1.1 %collective-permute-start.14 = (f32[32,128]{1,0:T(8,128)S(1)}, f32[32,128]{1,0:T(8,128)S(1)}, u32[]{:S(2)}, u32[]{:S(2)}) collective-permute-start(f32[32,128]{1,0:T(8,128)S(1)} %add_add_fusion), channel_id=1, source_target_pairs={{0,2},{1,3},{2,0},{3,1},{4,6},{5,7},{6,4},{7,5},{8,10},{9,11},{10,... | collective-permute-start | bytes 49160 | tf_op jit(solution)/shard_map/ppermute | solution.py:698
  44.4 2.7 %collective-permute-done.14 = f32[32,128]{1,0:T(8,128)S(1)} collective-permute-done((f32[32,128]{1,0:T(8,128)S(1)}, f32[32,128]{1,0:T(8,128)S(1)}, u32[]{:S(2)}, u32[]{:S(2)}) %collective-permute-start.14) | collective-permute-done | bytes 16416 | tf_op jit(solution)/shard_map/ppermute | solution.py:698
  47.1 0.0 collective-permute-start.15
  47.1 1.2 %collective-permute-done.15.rest_1_ = f32[32,128]{1,0:T(8,128)S(1)} collective-permute-done((f32[32,128]{1,0:T(8,128)S(1)}, f32[32,128]{1,0:T(8,128)S(1)}, u32[]{:S(2)}, u32[]{:S(2)}) %collective-permute-start.15) | collective-permute-done | bytes 16416 | tf_op jit(solution)/shard_map/ppermute | solution.py:698
  48.3 3.2 %gradient.1 = (f32[1,8100]{1,0:T(1,128)}, f32[30,1,8100]{2,1,0:T(1,128)}) custom-call(s32[1]{0:T(128)} %bitcast.me_ref, f32[32,128]{1,0:T(8,128)S(1)} %add.15.rest_0_, f32[32,128]{1,0:T(8,128)S(1)} %collective-permute-done.15.rest_1_, f32[256,128]{1,0:T(8,128)S(1)} %get-tuple-element.21.dense_ref.rest_2_, f32[4,64,128]{2,1,0:T(8,128)S(1)} %get-tuple-element.29.rest_3_, ...), custom_call_target="tpu_custom_call" | custom-call | flops 10000000 | bytes 4000000 | tf_op jit(solution)/shard_map/gradient/pallas_call | solution.py:738
  (8 shorter events, 0.0 us)
Async XLA Ops:
  0.6 0.8 %copy-start = (s32[1,8100]{1,0:T(1,128)S(1)}, s32[1,8100]{1,0:T(1,128)}, u32[]{:S(2)}) copy-start(s32[1,8100]{1,0:T(1,128)} %rest_6_.1) | copy-start | bytes 97204
  1.6 7.7 %collective-permute-start.2 = (f32[8,128]{1,0:T(8,128)S(1)}, f32[8,128]{1,0:T(8,128)S(1)}, u32[]{:S(2)}, u32[]{:S(2)}) collective-permute-start(f32[8,128]{1,0:T(8,128)S(1)} %depths.1.own_ref), channel_id=1, source_target_pairs={{0,8},{1,9},{2,10},{3,11},{4,12},{5,13},{6,14},{7,15},{8,0},{9,1},... | collective-permute-start | bytes 12296 | tf_op jit(solution)/shard_map/ppermute | solution.py:765
  5.7 3.6 %collective-permute-start.1 = (f32[8,128]{1,0:T(8,128)S(1)}, f32[8,128]{1,0:T(8,128)S(1)}, u32[]{:S(2)}, u32[]{:S(2)}) collective-permute-start(f32[8,128]{1,0:T(8,128)S(1)} %depths.1.own_ref), channel_id=1, source_target_pairs={{1,2},{2,1},{3,4},{4,3},{5,6},{6,5},{7,8},{8,7},{9,10},{10,9},{11,... | collective-permute-start | bytes 12296 | tf_op jit(solution)/shard_map/ppermute | solution.py:765
  6.3 3.8 %collective-permute-start = (f32[8,128]{1,0:T(8,128)S(1)}, f32[8,128]{1,0:T(8,128)S(1)}, u32[]{:S(2)}, u32[]{:S(2)}) collective-permute-start(f32[8,128]{1,0:T(8,128)S(1)} %depths.1.own_ref), channel_id=1, source_target_pairs={{0,1},{1,0},{2,3},{3,2},{4,5},{5,4},{6,7},{7,6},{8,9},{9,8},{10,11... | collective-permute-start | bytes 12296 | tf_op jit(solution)/shard_map/ppermute | solution.py:765
  14.4 6.4 %collective-permute-start.5 = (f32[48,128]{1,0:T(8,128)S(1)}, f32[48,128]{1,0:T(8,128)S(1)}, u32[]{:S(2)}, u32[]{:S(2)}) collective-permute-start(f32[48,128]{1,0:T(8,128)S(1)} %get-tuple-element.22.rest_0_), channel_id=1, source_target_pairs={{0,12},{1,13},{2,14},{3,15},{4,8},{5,9},{6,10},{7,11},{8,4},{9,5},... | collective-permute-start | bytes 73736 | tf_op jit(solution)/shard_map/ppermute | solution.py:698
  17.2 4.7 %collective-permute-start.4 = (f32[48,128]{1,0:T(8,128)S(1)}, f32[48,128]{1,0:T(8,128)S(1)}, u32[]{:S(2)}, u32[]{:S(2)}) collective-permute-start(f32[48,128]{1,0:T(8,128)S(1)} %get-tuple-element.22.rest_0_), channel_id=1, source_target_pairs={{0,8},{1,9},{2,10},{3,11},{4,12},{5,13},{6,14},{7,15},{8,0},{9,1},... | collective-permute-start | bytes 73736 | tf_op jit(solution)/shard_map/ppermute | solution.py:698
  18.9 3.8 %collective-permute-start.3 = (f32[48,128]{1,0:T(8,128)S(1)}, f32[48,128]{1,0:T(8,128)S(1)}, u32[]{:S(2)}, u32[]{:S(2)}) collective-permute-start(f32[48,128]{1,0:T(8,128)S(1)} %get-tuple-element.22.rest_0_), channel_id=1, source_target_pairs={{0,4},{1,5},{2,6},{3,7},{4,0},{5,1},{6,2},{7,3},{8,12},{9,13},{10,... | collective-permute-start | bytes 73736 | tf_op jit(solution)/shard_map/ppermute | solution.py:698
  22.8 8.8 %collective-permute-start.9 = (f32[4,32,128]{2,1,0:T(8,128)S(1)}, f32[4,32,128]{2,1,0:T(8,128)S(1)}, u32[]{:S(2)}, u32[]{:S(2)}) collective-permute-start(f32[4,32,128]{2,1,0:T(8,128)S(1)} %get-tuple-element.26.rest_9_), channel_id=1, source_target_pairs={{0,8},{1,9},{2,10},{3,11},{4,12},{5,13},{6,14},{7,15},{8,0},{9,1},... | collective-permute-start | bytes 196616 | tf_op jit(solution)/shard_map/ppermute | solution.py:765
  24.1 7.5 %collective-permute-start.8 = (f32[4,32,128]{2,1,0:T(8,128)S(1)}, f32[4,32,128]{2,1,0:T(8,128)S(1)}, u32[]{:S(2)}, u32[]{:S(2)}) collective-permute-start(f32[4,32,128]{2,1,0:T(8,128)S(1)} %get-tuple-element.26.rest_9_), channel_id=1, source_target_pairs={{1,2},{2,1},{3,4},{4,3},{5,6},{6,5},{7,8},{8,7},{9,10},{10,9},{11,... | collective-permute-start | bytes 196616 | tf_op jit(solution)/shard_map/ppermute | solution.py:765
  24.7 6.9 %collective-permute-start.7 = (f32[4,32,128]{2,1,0:T(8,128)S(1)}, f32[4,32,128]{2,1,0:T(8,128)S(1)}, u32[]{:S(2)}, u32[]{:S(2)}) collective-permute-start(f32[4,32,128]{2,1,0:T(8,128)S(1)} %get-tuple-element.26.rest_9_), channel_id=1, source_target_pairs={{0,1},{1,0},{2,3},{3,2},{4,5},{5,4},{6,7},{7,6},{8,9},{9,8},{10,11... | collective-permute-start | bytes 196616 | tf_op jit(solution)/shard_map/ppermute | solution.py:765
  26.8 4.8 %collective-permute-start.6 = (f32[192,128]{1,0:T(8,128)S(1)}, f32[192,128]{1,0:T(8,128)S(1)}, u32[]{:S(2)}, u32[]{:S(2)}) collective-permute-start(f32[192,128]{1,0:T(8,128)S(1)} %pad_maximum_fusion), channel_id=1, source_target_pairs={{0,2},{1,3},{2,0},{3,1},{4,6},{5,7},{6,4},{7,5},{8,10},{9,11},{10,... | collective-permute-start | bytes 294920 | tf_op jit(solution)/shard_map/ppermute | solution.py:698
  31.6 1.5 %collective-permute-start.10 = (f32[384,128]{1,0:T(8,128)S(1)}, f32[384,128]{1,0:T(8,128)S(1)}, u32[]{:S(2)}, u32[]{:S(2)}) collective-permute-start(f32[384,128]{1,0:T(8,128)S(1)} %constant_dynamic-update-slice_fusion), channel_id=1, source_target_pairs={{0,1},{1,0},{2,3},{3,2},{4,5},{5,4},{6,7},{7,6},{8,9},{9,8},{10,11... | collective-permute-start | bytes 589832 | tf_op jit(solution)/shard_map/ppermute | solution.py:698
  36.0 5.6 %collective-permute-start.13 = (f32[32,128]{1,0:T(8,128)S(1)}, f32[32,128]{1,0:T(8,128)S(1)}, u32[]{:S(2)}, u32[]{:S(2)}) collective-permute-start(f32[32,128]{1,0:T(8,128)S(1)} %get-tuple-element.28), channel_id=1, source_target_pairs={{0,12},{1,13},{2,14},{3,15},{4,8},{5,9},{6,10},{7,11},{8,4},{9,5},... | collective-permute-start | bytes 49160 | tf_op jit(solution)/shard_map/ppermute | solution.py:698
  38.6 4.7 %collective-permute-start.12 = (f32[32,128]{1,0:T(8,128)S(1)}, f32[32,128]{1,0:T(8,128)S(1)}, u32[]{:S(2)}, u32[]{:S(2)}) collective-permute-start(f32[32,128]{1,0:T(8,128)S(1)} %get-tuple-element.28), channel_id=1, source_target_pairs={{0,8},{1,9},{2,10},{3,11},{4,12},{5,13},{6,14},{7,15},{8,0},{9,1},... | collective-permute-start | bytes 49160 | tf_op jit(solution)/shard_map/ppermute | solution.py:698
  39.0 4.3 %collective-permute-start.11 = (f32[32,128]{1,0:T(8,128)S(1)}, f32[32,128]{1,0:T(8,128)S(1)}, u32[]{:S(2)}, u32[]{:S(2)}) collective-permute-start(f32[32,128]{1,0:T(8,128)S(1)} %get-tuple-element.28), channel_id=1, source_target_pairs={{0,4},{1,5},{2,6},{3,7},{4,0},{5,1},{6,2},{7,3},{8,12},{9,13},{10,... | collective-permute-start | bytes 49160 | tf_op jit(solution)/shard_map/ppermute | solution.py:698
  43.3 3.8 %collective-permute-start.14 = (f32[32,128]{1,0:T(8,128)S(1)}, f32[32,128]{1,0:T(8,128)S(1)}, u32[]{:S(2)}, u32[]{:S(2)}) collective-permute-start(f32[32,128]{1,0:T(8,128)S(1)} %add_add_fusion), channel_id=1, source_target_pairs={{0,2},{1,3},{2,0},{3,1},{4,6},{5,7},{6,4},{7,5},{8,10},{9,11},{10,... | collective-permute-start | bytes 49160 | tf_op jit(solution)/shard_map/ppermute | solution.py:698
  47.1 1.2 %collective-permute-start.15 = (f32[32,128]{1,0:T(8,128)S(1)}, f32[32,128]{1,0:T(8,128)S(1)}, u32[]{:S(2)}, u32[]{:S(2)}) collective-permute-start(f32[32,128]{1,0:T(8,128)S(1)} %add.15.rest_0_), channel_id=1, source_target_pairs={{0,1},{1,0},{2,3},{3,2},{4,5},{5,4},{6,7},{7,6},{8,9},{9,8},{10,11... | collective-permute-start | bytes 49160 | tf_op jit(solution)/shard_map/ppermute | solution.py:698

commit v10 on v8

--- a/solution.py
+++ b/solution.py
@@ -598,8 +598,8 @@
     rest = rest[grams:]
     dense_ref, va_ref, v_ref, line_ref, reach_ref, a_ref, q_ref, as_ref = rest[:8]
     refs = rest[8 : 8 + len(exchanges)]
-    adj_hbm, flag_hbm, height_ref, out_ref = rest[8 + len(exchanges) : 12 + len(exchanges)]
-    gram_ref, sum_ref, w_ref, h_ref, adj_ref, flag_ref, sems = rest[12 + len(exchanges) :]
+    adj_hbm, flag_hbm, height_ref, out_hbm = rest[8 + len(exchanges) : 12 + len(exchanges)]
+    gram_ref, sum_ref, w_ref, h_ref, adj_ref, flag_ref, out_ref, sems = rest[12 + len(exchanges) :]
     tables = [
         pltpu.make_async_copy(source, target, sems.at[number])
         for number, (source, target) in enumerate(((adj_hbm, adj_ref), (flag_hbm, flag_ref)))
@@ -669,7 +669,18 @@
         store_rows(out_ref.at[number], a_ref[at, :] + adjoint * q_ref[at, :] + SPREAD * spread)
         return carry
 
-    lax.fori_loop(0, levels, per_level, 0, unroll=5)
+    parts = 3
+    third = levels // parts
+    copies = []
+    for part in range(parts):
+        first = part * third
+        last = first + third if part < parts - 1 else levels
+        lax.fori_loop(first, last, per_level, 0, unroll=5)
+        at = pl.ds(first, last - first)
+        copies.append(pltpu.make_async_copy(out_ref.at[at], out_hbm.at[at], sems.at[2 + part]))
+        copies[-1].start()
+    for copy in copies:
+        copy.wait()
 
 
 def interior_kernel(levels, dense_ref, a_ref, out_ref):
@@ -731,12 +742,12 @@
 
     hbm = pl.BlockSpec(memory_space=pltpu.HBM)
 
-    def call(kernel, outs, scratch, scalars, arrays, name, flops=1e6, traffic=1e6, far=(), grant=48):
+    def call(kernel, outs, scratch, scalars, arrays, name, flops=1e6, traffic=1e6, far=(), grant=48, places=None):
         return pl.pallas_call(
             kernel,
             out_shape=outs,
             in_specs=[smem] * len(scalars) + [vmem] * len(arrays) + [hbm] * len(far),
-            out_specs=jax.tree.map(lambda _: vmem, outs),
+            out_specs=places or jax.tree.map(lambda _: vmem, outs),
             scratch_shapes=scratch,
             compiler_params=pltpu.CompilerParams(vmem_limit_bytes=grant * 1024 * 1024),
             cost_estimate=pl.CostEstimate(flops=int(flops), bytes_accessed=int(traffic), transcendentals=0),
@@ -861,7 +872,8 @@
             pltpu.VMEM((8 * ROWS, LANES), F32),
             pltpu.SMEM((1, 4), I32),
             pltpu.SMEM((1, 4), I32),
-            pltpu.SemaphoreType.DMA((2,)),
+            pltpu.VMEM((levels, 1, CELLS), F32),
+            pltpu.SemaphoreType.DMA((5,)),
         ],
         (me,),
         (
@@ -880,6 +892,7 @@
         1e7,
         4e6,
         tuple(pltpu.with_memory_space_constraint(x, pltpu.HBM) for x in (adjacent, flags)),
+        places=(vmem, hbm),
     )
     gradient = by_level(gradient)
     return height, gradient

time: 48 us -> 48.4 us (level)
  no operation moved by 1% of the time
where the time goes in v10:
time: 48.4 us; the launch traced here: 48.2 us
  starting transfers between devices  22.3 us (46%)
  Pallas kernels  13 us (27%)
  waiting for transfers between devices  11.3 us (23%)
  local copies, waits for them, and re-layouts  0.77 us (2%)
  between operations  0.75 us (2%)
    pallas_call x5, Pallas kernels, call(): pl.pallas_call(kernel, out_shape=outs, in_specs=[smem] * len(scalars) + [...  13 us
    ppermute x10, starting transfers between devices, swap(): return lax.ppermute(x, 'tile', [(t, t ^ offset) for t in range(tiles)])  11.7 us
    ppermute x6, starting transfers between devices, to_neighbours(): out.append(lax.ppermute(x, 'tile', pairs))  10.7 us
    ppermute x10, waiting for transfers between devices, swap(): return lax.ppermute(x, 'tile', [(t, t ^ offset) for t in range(tiles)])  10.5 us
  transfers between devices with their start and end apart: 16, of which 8 were waited for; matrix products, arithmetic and copies ran while one was open for 0% of the time, Pallas kernels for 4%

profile of v10, /device:TPU:0, one launch (start us, length us, event | category | flops | bytes accessed | tf_op | source)
XLA Modules:
  0.0 48.2 jit_solution(11960538157071775184)
XLA Ops:
  0.6 0.0 copy-start
  0.6 0.7 %copy-done = s32[1,8100]{1,0:T(1,128)S(1)} copy-done((s32[1,8100]{1,0:T(1,128)S(1)}, s32[1,8100]{1,0:T(1,128)}, u32[]{:S(2)}) %copy-start) | copy-done | bytes 32424
  1.4 0.2 depths.1.own_ref
  1.6 4.0 %collective-permute-start.2 = (f32[8,128]{1,0:T(8,128)S(1)}, f32[8,128]{1,0:T(8,128)S(1)}, u32[]{:S(2)}, u32[]{:S(2)}) collective-permute-start(f32[8,128]{1,0:T(8,128)S(1)} %depths.1.own_ref), channel_id=1, source_target_pairs={{0,8},{1,9},{2,10},{3,11},{4,12},{5,13},{6,14},{7,15},{8,0},{9,1},... | collective-permute-start | bytes 12296 | tf_op jit(solution)/shard_map/ppermute | solution.py:773
  5.7 0.6 %collective-permute-start.1 = (f32[8,128]{1,0:T(8,128)S(1)}, f32[8,128]{1,0:T(8,128)S(1)}, u32[]{:S(2)}, u32[]{:S(2)}) collective-permute-start(f32[8,128]{1,0:T(8,128)S(1)} %depths.1.own_ref), channel_id=1, source_target_pairs={{1,2},{2,1},{3,4},{4,3},{5,6},{6,5},{7,8},{8,7},{9,10},{10,9},{11,... | collective-permute-start | bytes 12296 | tf_op jit(solution)/shard_map/ppermute | solution.py:773
  6.3 2.9 %collective-permute-start = (f32[8,128]{1,0:T(8,128)S(1)}, f32[8,128]{1,0:T(8,128)S(1)}, u32[]{:S(2)}, u32[]{:S(2)}) collective-permute-start(f32[8,128]{1,0:T(8,128)S(1)} %depths.1.own_ref), channel_id=1, source_target_pairs={{0,1},{1,0},{2,3},{3,2},{4,5},{5,4},{6,7},{7,6},{8,9},{9,8},{10,11... | collective-permute-start | bytes 12296 | tf_op jit(solution)/shard_map/ppermute | solution.py:773
  9.3 0.0 collective-permute-done.2.rest_2_
  9.3 0.0 collective-permute-done.1.rest_1_
  9.3 0.8 %collective-permute-done.rest_0_ = f32[8,128]{1,0:T(8,128)S(1)} collective-permute-done((f32[8,128]{1,0:T(8,128)S(1)}, f32[8,128]{1,0:T(8,128)S(1)}, u32[]{:S(2)}, u32[]{:S(2)}) %collective-permute-start) | collective-permute-done | bytes 4128 | tf_op jit(solution)/shard_map/ppermute | solution.py:773
  10.1 4.3 %columns.1 = (f32[1920,128]{1,0:T(8,128)S(1)}, f32[1920,128]{1,0:T(8,128)S(1)}, f32[4,32,128]{2,1,0:T(8,128)S(1)}, f32[48,128]{1,0:T(8,128)S(1)}, f32[256,128]{1,0:T(8,128)S(1)}, /*index=5*/f32[8,128]{1,0:T(8,128)S(1)}) custom-call(s32[1]{0:T(128)} %bitcast.me_ref, f32[8,128]{1,0:T(8,128)S(1)} %depths.1.own_ref, f32[8,128]{1,0:T(8,128)S(1)} %collective-permute-done.rest_0_, ...), custom_call_target="tpu_custom_call" | custom-call | flops 20000000 | bytes 8000000 | tf_op jit(solution)/shard_map/columns/pallas_call | solution.py:746
  14.4 2.8 %collective-permute-start.5 = (f32[48,128]{1,0:T(8,128)S(1)}, f32[48,128]{1,0:T(8,128)S(1)}, u32[]{:S(2)}, u32[]{:S(2)}) collective-permute-start(f32[48,128]{1,0:T(8,128)S(1)} %get-tuple-element.17.rest_0_), channel_id=1, source_target_pairs={{0,12},{1,13},{2,14},{3,15},{4,8},{5,9},{6,10},{7,11},{8,4},{9,5},... | collective-permute-start | bytes 73736 | tf_op jit(solution)/shard_map/ppermute | solution.py:709
  17.2 1.7 %collective-permute-start.4 = (f32[48,128]{1,0:T(8,128)S(1)}, f32[48,128]{1,0:T(8,128)S(1)}, u32[]{:S(2)}, u32[]{:S(2)}) collective-permute-start(f32[48,128]{1,0:T(8,128)S(1)} %get-tuple-element.17.rest_0_), channel_id=1, source_target_pairs={{0,8},{1,9},{2,10},{3,11},{4,12},{5,13},{6,14},{7,15},{8,0},{9,1},... | collective-permute-start | bytes 73736 | tf_op jit(solution)/shard_map/ppermute | solution.py:709
  18.9 0.0 collective-permute-start.3
  18.9 1.9 %interior.1.rest_7_ = f32[1920,128]{1,0:T(8,128)S(1)} custom-call(f32[256,128]{1,0:T(8,128)S(1)} %get-tuple-element.16.dense_ref.rest_2_, f32[1920,128]{1,0:T(8,128)S(1)} %get-tuple-element.18.a_ref), custom_call_target="tpu_custom_call" | custom-call | flops 10000000 | bytes 4000000 | tf_op jit(solution)/shard_map/interior/pallas_call | solution.py:746
  20.8 0.0 collective-permute-done.5.rest_3_
  20.8 1.1 %collective-permute-done.4.rest_2_ = f32[48,128]{1,0:T(8,128)S(1)} collective-permute-done((f32[48,128]{1,0:T(8,128)S(1)}, f32[48,128]{1,0:T(8,128)S(1)}, u32[]{:S(2)}, u32[]{:S(2)}) %collective-permute-start.4) | collective-permute-done | bytes 24608 | tf_op jit(solution)/shard_map/ppermute | solution.py:709
  21.9 0.8 %collective-permute-done.3.rest_1_ = f32[48,128]{1,0:T(8,128)S(1)} collective-permute-done((f32[48,128]{1,0:T(8,128)S(1)}, f32[48,128]{1,0:T(8,128)S(1)}, u32[]{:S(2)}, u32[]{:S(2)}) %collective-permute-start.3) | collective-permute-done | bytes 24608 | tf_op jit(solution)/shard_map/ppermute | solution.py:709
  22.7 0.7 %collective-permute-start.6 = (f32[192,128]{1,0:T(8,128)S(1)}, f32[192,128]{1,0:T(8,128)S(1)}, u32[]{:S(2)}, u32[]{:S(2)}) collective-permute-start(f32[192,128]{1,0:T(8,128)S(1)} %pad_maximum_fusion), channel_id=1, source_target_pairs={{0,2},{1,3},{2,0},{3,1},{4,6},{5,7},{6,4},{7,5},{8,10},{9,11},{10,... | collective-permute-start | bytes 294920 | tf_op jit(solution)/shard_map/ppermute | solution.py:709
  23.4 4.0 %collective-permute-done.6.rest_4_ = f32[192,128]{1,0:T(8,128)S(1)} collective-permute-done((f32[192,128]{1,0:T(8,128)S(1)}, f32[192,128]{1,0:T(8,128)S(1)}, u32[]{:S(2)}, u32[]{:S(2)}) %collective-permute-start.6) | collective-permute-done | bytes 98336 | tf_op jit(solution)/shard_map/ppermute | solution.py:709
  27.4 0.1 collective-permute-start.7
  27.5 1.4 %collective-permute-done.7.rest_5_ = f32[384,128]{1,0:T(8,128)S(1)} collective-permute-done((f32[384,128]{1,0:T(8,128)S(1)}, f32[384,128]{1,0:T(8,128)S(1)}, u32[]{:S(2)}, u32[]{:S(2)}) %collective-permute-start.7) | collective-permute-done | bytes 196640 | tf_op jit(solution)/shard_map/ppermute | solution.py:709
  28.9 2.9 %krylov.1 = (f32[4,64,128]{2,1,0:T(8,128)S(1)}, f32[4,64,128]{2,1,0:T(8,128)S(1)}, f32[4,8,128]{2,1,0:T(8,128)S(1)}, f32[32,128]{1,0:T(8,128)S(1)}) custom-call(s32[1]{0:T(128)} %bitcast.me_ref, f32[256,128]{1,0:T(8,128)S(1)} %get-tuple-element.16.dense_ref.rest_2_, f32[48,128]{1,0:T(8,128)S(1)} %get-tuple-element.17.rest_0_, ...), custom_call_target="tpu_custom_call" | custom-call | flops 1000000 | bytes 1000000 | tf_op jit(solution)/shard_map/krylov/pallas_call | solution.py:746
  31.9 1.0 %collective-permute-start.10 = (f32[32,128]{1,0:T(8,128)S(1)}, f32[32,128]{1,0:T(8,128)S(1)}, u32[]{:S(2)}, u32[]{:S(2)}) collective-permute-start(f32[32,128]{1,0:T(8,128)S(1)} %get-tuple-element.20), channel_id=1, source_target_pairs={{0,12},{1,13},{2,14},{3,15},{4,8},{5,9},{6,10},{7,11},{8,4},{9,5},... | collective-permute-start | bytes 49160 | tf_op jit(solution)/shard_map/ppermute | solution.py:709
  32.9 0.7 %collective-permute-start.9 = (f32[32,128]{1,0:T(8,128)S(1)}, f32[32,128]{1,0:T(8,128)S(1)}, u32[]{:S(2)}, u32[]{:S(2)}) collective-permute-start(f32[32,128]{1,0:T(8,128)S(1)} %get-tuple-element.20), channel_id=1, source_target_pairs={{0,8},{1,9},{2,10},{3,11},{4,12},{5,13},{6,14},{7,15},{8,0},{9,1},... | collective-permute-start | bytes 49160 | tf_op jit(solution)/shard_map/ppermute | solution.py:709
  33.6 2.7 %collective-permute-start.8 = (f32[32,128]{1,0:T(8,128)S(1)}, f32[32,128]{1,0:T(8,128)S(1)}, u32[]{:S(2)}, u32[]{:S(2)}) collective-permute-start(f32[32,128]{1,0:T(8,128)S(1)} %get-tuple-element.20), channel_id=1, source_target_pairs={{0,4},{1,5},{2,6},{3,7},{4,0},{5,1},{6,2},{7,3},{8,12},{9,13},{10,... | collective-permute-start | bytes 49160 | tf_op jit(solution)/shard_map/ppermute | solution.py:709
  36.3 0.3 collective-permute-start.15
  36.6 0.7 %collective-permute-start.14 = (f32[4,32,128]{2,1,0:T(8,128)S(1)}, f32[4,32,128]{2,1,0:T(8,128)S(1)}, u32[]{:S(2)}, u32[]{:S(2)}) collective-permute-start(f32[4,32,128]{2,1,0:T(8,128)S(1)} %get-tuple-element.27.rest_9_), channel_id=1, source_target_pairs={{1,2},{2,1},{3,4},{4,3},{5,6},{6,5},{7,8},{8,7},{9,10},{10,9},{11,... | collective-permute-start | bytes 196616 | tf_op jit(solution)/shard_map/ppermute | solution.py:773
  37.3 0.2 collective-permute-done.10
  37.5 2.0 %collective-permute-start.13 = (f32[4,32,128]{2,1,0:T(8,128)S(1)}, f32[4,32,128]{2,1,0:T(8,128)S(1)}, u32[]{:S(2)}, u32[]{:S(2)}) collective-permute-start(f32[4,32,128]{2,1,0:T(8,128)S(1)} %get-tuple-element.27.rest_9_), channel_id=1, source_target_pairs={{0,1},{1,0},{2,3},{3,2},{4,5},{5,4},{6,7},{7,6},{8,9},{9,8},{10,11... | collective-permute-start | bytes 196616 | tf_op jit(solution)/shard_map/ppermute | solution.py:773
  39.5 0.0 collective-permute-done.9
  39.5 0.0 collective-permute-done.8
  39.5 2.0 %collective-permute-start.11 = (f32[32,128]{1,0:T(8,128)S(1)}, f32[32,128]{1,0:T(8,128)S(1)}, u32[]{:S(2)}, u32[]{:S(2)}) collective-permute-start(f32[32,128]{1,0:T(8,128)S(1)} %add_add_fusion), channel_id=1, source_target_pairs={{0,2},{1,3},{2,0},{3,1},{4,6},{5,7},{6,4},{7,5},{8,10},{9,11},{10,... | collective-permute-start | bytes 49160 | tf_op jit(solution)/shard_map/ppermute | solution.py:709
  41.5 1.8 %collective-permute-done.11 = f32[32,128]{1,0:T(8,128)S(1)} collective-permute-done((f32[32,128]{1,0:T(8,128)S(1)}, f32[32,128]{1,0:T(8,128)S(1)}, u32[]{:S(2)}, u32[]{:S(2)}) %collective-permute-start.11) | collective-permute-done | bytes 16416 | tf_op jit(solution)/shard_map/ppermute | solution.py:709
  43.3 0.0 collective-permute-start.12
  43.3 0.0 collective-permute-done.15.rest_12_
  43.4 0.0 collective-permute-done.14.rest_11_
  43.4 0.0 collective-permute-done.13.rest_10_
  43.4 1.1 %collective-permute-done.12.rest_1_ = f32[32,128]{1,0:T(8,128)S(1)} collective-permute-done((f32[32,128]{1,0:T(8,128)S(1)}, f32[32,128]{1,0:T(8,128)S(1)}, u32[]{:S(2)}, u32[]{:S(2)}) %collective-permute-start.12) | collective-permute-done | bytes 16416 | tf_op jit(solution)/shard_map/ppermute | solution.py:709
  44.5 3.7 %gradient.1 = (f32[1,8100]{1,0:T(1,128)}, f32[30,1,8100]{2,1,0:T(1,128)}) custom-call(s32[1]{0:T(128)} %bitcast.me_ref, f32[32,128]{1,0:T(8,128)S(1)} %add.15.rest_0_, f32[32,128]{1,0:T(8,128)S(1)} %collective-permute-done.12.rest_1_, f32[256,128]{1,0:T(8,128)S(1)} %get-tuple-element.16.dense_ref.rest_2_, f32[4,64,128]{2,1,0:T(8,128)S(1)} %get-tuple-element.21.rest_3_, ...), custom_call_target="tpu_custom_call" | custom-call | flops 10000000 | bytes 4000000 | tf_op jit(solution)/shard_map/gradient/pallas_call | solution.py:746
  (8 shorter events, 0.0 us)
Async XLA Ops:
  0.6 0.8 %copy-start = (s32[1,8100]{1,0:T(1,128)S(1)}, s32[1,8100]{1,0:T(1,128)}, u32[]{:S(2)}) copy-start(s32[1,8100]{1,0:T(1,128)} %rest_6_.1) | copy-start | bytes 97204
  1.6 7.7 %collective-permute-start.2 = (f32[8,128]{1,0:T(8,128)S(1)}, f32[8,128]{1,0:T(8,128)S(1)}, u32[]{:S(2)}, u32[]{:S(2)}) collective-permute-start(f32[8,128]{1,0:T(8,128)S(1)} %depths.1.own_ref), channel_id=1, source_target_pairs={{0,8},{1,9},{2,10},{3,11},{4,12},{5,13},{6,14},{7,15},{8,0},{9,1},... | collective-permute-start | bytes 12296 | tf_op jit(solution)/shard_map/ppermute | solution.py:773
  5.7 3.6 %collective-permute-start.1 = (f32[8,128]{1,0:T(8,128)S(1)}, f32[8,128]{1,0:T(8,128)S(1)}, u32[]{:S(2)}, u32[]{:S(2)}) collective-permute-start(f32[8,128]{1,0:T(8,128)S(1)} %depths.1.own_ref), channel_id=1, source_target_pairs={{1,2},{2,1},{3,4},{4,3},{5,6},{6,5},{7,8},{8,7},{9,10},{10,9},{11,... | collective-permute-start | bytes 12296 | tf_op jit(solution)/shard_map/ppermute | solution.py:773
  6.3 3.8 %collective-permute-start = (f32[8,128]{1,0:T(8,128)S(1)}, f32[8,128]{1,0:T(8,128)S(1)}, u32[]{:S(2)}, u32[]{:S(2)}) collective-permute-start(f32[8,128]{1,0:T(8,128)S(1)} %depths.1.own_ref), channel_id=1, source_target_pairs={{0,1},{1,0},{2,3},{3,2},{4,5},{5,4},{6,7},{7,6},{8,9},{9,8},{10,11... | collective-permute-start | bytes 12296 | tf_op jit(solution)/shard_map/ppermute | solution.py:773
  14.4 6.4 %collective-permute-start.5 = (f32[48,128]{1,0:T(8,128)S(1)}, f32[48,128]{1,0:T(8,128)S(1)}, u32[]{:S(2)}, u32[]{:S(2)}) collective-permute-start(f32[48,128]{1,0:T(8,128)S(1)} %get-tuple-element.17.rest_0_), channel_id=1, source_target_pairs={{0,12},{1,13},{2,14},{3,15},{4,8},{5,9},{6,10},{7,11},{8,4},{9,5},... | collective-permute-start | bytes 73736 | tf_op jit(solution)/shard_map/ppermute | solution.py:709
  17.2 4.7 %collective-permute-start.4 = (f32[48,128]{1,0:T(8,128)S(1)}, f32[48,128]{1,0:T(8,128)S(1)}, u32[]{:S(2)}, u32[]{:S(2)}) collective-permute-start(f32[48,128]{1,0:T(8,128)S(1)} %get-tuple-element.17.rest_0_), channel_id=1, source_target_pairs={{0,8},{1,9},{2,10},{3,11},{4,12},{5,13},{6,14},{7,15},{8,0},{9,1},... | collective-permute-start | bytes 73736 | tf_op jit(solution)/shard_map/ppermute | solution.py:709
  18.9 3.8 %collective-permute-start.3 = (f32[48,128]{1,0:T(8,128)S(1)}, f32[48,128]{1,0:T(8,128)S(1)}, u32[]{:S(2)}, u32[]{:S(2)}) collective-permute-start(f32[48,128]{1,0:T(8,128)S(1)} %get-tuple-element.17.rest_0_), channel_id=1, source_target_pairs={{0,4},{1,5},{2,6},{3,7},{4,0},{5,1},{6,2},{7,3},{8,12},{9,13},{10,... | collective-permute-start | bytes 73736 | tf_op jit(solution)/shard_map/ppermute | solution.py:709
  22.7 4.7 %collective-permute-start.6 = (f32[192,128]{1,0:T(8,128)S(1)}, f32[192,128]{1,0:T(8,128)S(1)}, u32[]{:S(2)}, u32[]{:S(2)}) collective-permute-start(f32[192,128]{1,0:T(8,128)S(1)} %pad_maximum_fusion), channel_id=1, source_target_pairs={{0,2},{1,3},{2,0},{3,1},{4,6},{5,7},{6,4},{7,5},{8,10},{9,11},{10,... | collective-permute-start | bytes 294920 | tf_op jit(solution)/shard_map/ppermute | solution.py:709
  27.4 1.5 %collective-permute-start.7 = (f32[384,128]{1,0:T(8,128)S(1)}, f32[384,128]{1,0:T(8,128)S(1)}, u32[]{:S(2)}, u32[]{:S(2)}) collective-permute-start(f32[384,128]{1,0:T(8,128)S(1)} %constant_dynamic-update-slice_fusion), channel_id=1, source_target_pairs={{0,1},{1,0},{2,3},{3,2},{4,5},{5,4},{6,7},{7,6},{8,9},{9,8},{10,11... | collective-permute-start | bytes 589832 | tf_op jit(solution)/shard_map/ppermute | solution.py:709
  31.9 5.6 %collective-permute-start.10 = (f32[32,128]{1,0:T(8,128)S(1)}, f32[32,128]{1,0:T(8,128)S(1)}, u32[]{:S(2)}, u32[]{:S(2)}) collective-permute-start(f32[32,128]{1,0:T(8,128)S(1)} %get-tuple-element.20), channel_id=1, source_target_pairs={{0,12},{1,13},{2,14},{3,15},{4,8},{5,9},{6,10},{7,11},{8,4},{9,5},... | collective-permute-start | bytes 49160 | tf_op jit(solution)/shard_map/ppermute | solution.py:709
  32.9 6.6 %collective-permute-start.9 = (f32[32,128]{1,0:T(8,128)S(1)}, f32[32,128]{1,0:T(8,128)S(1)}, u32[]{:S(2)}, u32[]{:S(2)}) collective-permute-start(f32[32,128]{1,0:T(8,128)S(1)} %get-tuple-element.20), channel_id=1, source_target_pairs={{0,8},{1,9},{2,10},{3,11},{4,12},{5,13},{6,14},{7,15},{8,0},{9,1},... | collective-permute-start | bytes 49160 | tf_op jit(solution)/shard_map/ppermute | solution.py:709
  33.6 5.9 %collective-permute-start.8 = (f32[32,128]{1,0:T(8,128)S(1)}, f32[32,128]{1,0:T(8,128)S(1)}, u32[]{:S(2)}, u32[]{:S(2)}) collective-permute-start(f32[32,128]{1,0:T(8,128)S(1)} %get-tuple-element.20), channel_id=1, source_target_pairs={{0,4},{1,5},{2,6},{3,7},{4,0},{5,1},{6,2},{7,3},{8,12},{9,13},{10,... | collective-permute-start | bytes 49160 | tf_op jit(solution)/shard_map/ppermute | solution.py:709
  36.3 7.0 %collective-permute-start.15 = (f32[4,32,128]{2,1,0:T(8,128)S(1)}, f32[4,32,128]{2,1,0:T(8,128)S(1)}, u32[]{:S(2)}, u32[]{:S(2)}) collective-permute-start(f32[4,32,128]{2,1,0:T(8,128)S(1)} %get-tuple-element.27.rest_9_), channel_id=1, source_target_pairs={{0,8},{1,9},{2,10},{3,11},{4,12},{5,13},{6,14},{7,15},{8,0},{9,1},... | collective-permute-start | bytes 196616 | tf_op jit(solution)/shard_map/ppermute | solution.py:773
  36.6 6.7 %collective-permute-start.14 = (f32[4,32,128]{2,1,0:T(8,128)S(1)}, f32[4,32,128]{2,1,0:T(8,128)S(1)}, u32[]{:S(2)}, u32[]{:S(2)}) collective-permute-start(f32[4,32,128]{2,1,0:T(8,128)S(1)} %get-tuple-element.27.rest_9_), channel_id=1, source_target_pairs={{1,2},{2,1},{3,4},{4,3},{5,6},{6,5},{7,8},{8,7},{9,10},{10,9},{11,... | collective-permute-start | bytes 196616 | tf_op jit(solution)/shard_map/ppermute | solution.py:773
  37.5 5.9 %collective-permute-start.13 = (f32[4,32,128]{2,1,0:T(8,128)S(1)}, f32[4,32,128]{2,1,0:T(8,128)S(1)}, u32[]{:S(2)}, u32[]{:S(2)}) collective-permute-start(f32[4,32,128]{2,1,0:T(8,128)S(1)} %get-tuple-element.27.rest_9_), channel_id=1, source_target_pairs={{0,1},{1,0},{2,3},{3,2},{4,5},{5,4},{6,7},{7,6},{8,9},{9,8},{10,11... | collective-permute-start | bytes 196616 | tf_op jit(solution)/shard_map/ppermute | solution.py:773
  39.5 3.8 %collective-permute-start.11 = (f32[32,128]{1,0:T(8,128)S(1)}, f32[32,128]{1,0:T(8,128)S(1)}, u32[]{:S(2)}, u32[]{:S(2)}) collective-permute-start(f32[32,128]{1,0:T(8,128)S(1)} %add_add_fusion), channel_id=1, source_target_pairs={{0,2},{1,3},{2,0},{3,1},{4,6},{5,7},{6,4},{7,5},{8,10},{9,11},{10,... | collective-permute-start | bytes 49160 | tf_op jit(solution)/shard_map/ppermute | solution.py:709
  43.3 1.2 %collective-permute-start.12 = (f32[32,128]{1,0:T(8,128)S(1)}, f32[32,128]{1,0:T(8,128)S(1)}, u32[]{:S(2)}, u32[]{:S(2)}) collective-permute-start(f32[32,128]{1,0:T(8,128)S(1)} %add.15.rest_0_), channel_id=1, source_target_pairs={{0,1},{1,0},{2,3},{3,2},{4,5},{5,4},{6,7},{7,6},{8,9},{9,8},{10,11... | collective-permute-start | bytes 49160 | tf_op jit(solution)/shard_map/ppermute | solution.py:709
